TPU v7x, 32 devices: a whole 2x2x4 slice. The times are simulated.
32 devices in a mesh: groups: 2 (over y), stem: 16 (over z, x, core).
Axes of the slice: x: 2, y: 2, z: 4, core: 2. Of those that a mesh axis runs over, the one named last changes fastest.
Arguments:
- stems: float32 [2, 2, 2097152], P('groups', None, 'stem'), parts along dimension 0, may hold values from -6 to 6
- lo_table: float32 [3, 2, 2, 256, 256], replicated, may hold values from -0.25 to 0.25
- hi_table: float32 [3, 2, 256, 256], replicated, may hold values from -0.25 to 0.25
- slice_bits: int32 [2, 3], P('groups'), parts along dimension 0, may hold values from 0 to 1
Outputs:
- window: float32 [2, 4194304], P(None, ('groups', 'stem')), parts along dimension 1
There are 2 independent parts, one for each index of `groups`. A program takes and returns all parts, laid end to end along the dimension named above; an argument that names none is the same for every part. Nothing has to cross between parts.
Inputs may be any that keep to these rules, and one draw needn't show every extreme that they name: `slice_bits`: each entry is the value of a sliced bond of two values.
All inputs are finite; a program needn't handle non-finite values.
Results may differ from a plain program's by a relative error of at most 0.00011.
Values sent between devices are 32-bit elements; how exact they have to be, the bound alone decides.
No kernel may reach another device: no remote copies, remote signals or barrier semaphores. Data moves between devices by JAX's collectives and lax.ppermute only.
A program may use at most 64 MiB of HBM per device.

v0:
```python
import jax
import jax.numpy as jnp
from jax import lax
from jax.sharding import PartitionSpec as P


def complex_block(matrices):
    real_part = matrices[..., 0, :, :]
    imag_part = matrices[..., 1, :, :]
    upper_rows = jnp.stack([real_part, -imag_part], axis=-3)
    lower_rows = jnp.stack([imag_part, real_part], axis=-3)
    return jnp.stack([upper_rows, lower_rows], axis=-4)


def select_low(lo_table, slice_bits, segment):
    chosen = slice_bits[:, segment] == 1
    return jnp.where(
        chosen[:, None, None, None], lo_table[segment, 1][None], lo_table[segment, 0][None]
    )


def apply_low(amplitudes, blocks):
    return jnp.einsum("scrhm,sdckm->sdrhk", amplitudes, blocks, precision=lax.Precision.HIGHEST)


def apply_high(amplitudes, block):
    return jnp.einsum("scrjl,dchj->sdrhl", amplitudes, block, precision=lax.Precision.HIGHEST)


def body(stems, lo_table, hi_table, slice_bits):
    slice_count = stems.shape[0]
    leading = lax.axis_size("stem")
    high_width = hi_table.shape[-1]
    low_width = lo_table.shape[-1]
    spare_count = stems.shape[2] // (high_width * low_width)
    under_count = high_width // leading
    local_shape = (slice_count, 2, spare_count, high_width, low_width)
    split_shape = (slice_count, 2, spare_count, leading, under_count, low_width)
    amplitudes = stems.reshape(local_shape)
    amplitudes = apply_low(amplitudes, complex_block(select_low(lo_table, slice_bits, 0)))
    amplitudes = apply_high(amplitudes, complex_block(hi_table[0]))
    middle_low = complex_block(select_low(lo_table, slice_bits, 1))
    middle_high = complex_block(hi_table[1])
    swapped = lax.all_to_all(
        amplitudes.reshape(split_shape), "stem", split_axis=3, concat_axis=3, tiled=True
    )
    amplitudes = apply_high(apply_low(swapped.reshape(local_shape), middle_low), middle_high)
    amplitudes = apply_low(amplitudes, complex_block(select_low(lo_table, slice_bits, 2)))
    closing = complex_block(hi_table[2])
    returned = lax.all_to_all(
        amplitudes.reshape(split_shape), "stem", split_axis=3, concat_axis=3, tiled=True
    )
    combined = jnp.sum(apply_high(returned.reshape(local_shape), closing), axis=0)
    return combined.reshape(2, spare_count * high_width * low_width)


def solution(mesh):
    placed = (P("groups", None, "stem"), P(), P(), P("groups", None))
    return jax.shard_map(
        body, mesh=mesh, in_specs=placed, out_specs=P(None, ("groups", "stem")), check_vma=False
    )
```

profile of v0, /device:TPU:0, one launch (start us, length us, event | category | flops | bytes accessed | tf_op | source)
XLA Modules:
  0.0 82.8 jit_solution(2959504869302643540)
XLA Ops:
  0.0 0.0 copy-start
  0.0 0.0 copy-start.11
  0.0 0.0 copy-start.8
  0.0 2.4 %slice_bitcast_fusion.4 = (f32[1,256,256]{2,1,0:T(8,128)S(1)}, f32[1,256,256]{2,1,0:T(8,128)}, f32[1,256,256]{2,1,0:T(8,128)}, f32[1,256,256]{2,1,0:T(8,128)}, f...) fusion(f32[3,2,256,256]{3,2,1,0:T(8,128)} %param.6), kind=kLoop, calls=%fused_computation.49 | loop fusion | bytes 3145728 | tf_op jit(solution)/shard_map/squeeze | solution.py:9
  2.4 0.0 copy-done
  2.4 0.0 copy-start.1
  2.4 0.8 %fusion.28 = (f32[1,256,256]{2,1,0:T(8,128)}, f32[1,256,256]{2,1,0:T(8,128)S(1)}, f32[1,256,256]{2,1,0:T(8,128)}) fusion(f32[3,2,256,256]{3,2,1,0:T(8,128)S(1)} %copy-done), kind=kLoop, calls=%fused_computation.57 | loop fusion | flops 196608 | bytes 1572864 | tf_op jit(solution)/shard_map/neg | solution.py:10
  3.3 0.0 copy-done.11
  3.3 0.7 fusion.31
  5.9 0.0 copy-done.8
  6.0 0.1 copy.37
  6.0 0.0 copy-done.1
  6.0 1.0 %select_bitcast_fusion.1 = (f32[1,2,256,256]{3,2,1,0:T(8,128)S(1)}, f32[1,2,256,256]{3,2,1,0:T(8,128)}, f32[1,2,256,256]{3,2,1,0:T(8,128)S(1)}) fusion(f32[3,2,2,256,256]{4,3,2,1,0:T(8,128)S(1)} %copy-done.1, pred[]{:T(512)} %bitcast.19, pred[]{:T(512)} %bitcast.6, pred[]{:T(512)} %bitcast.32), kind=kLoop, calls=%fused_computation.43 | loop fusion | flops 393216 | bytes 4718595 | tf_op jit(solution)/shard_map/jit(_where)/select_n | solution.py:17
  7.1 0.1 slice_negate_fusion
  7.2 0.1 maximum_bitcast_fusion.18
  7.3 1.9 %convolution_bitcast_fusion.3 = f32[2,2,256,256,1]{2,3,1,0,4:T(8,128)S(1)} fusion(f32[1,1,2,256,256]{4,3,2,1,0:T(8,128)S(1)} %get-tuple-element.35, f32[1,1,2,256,256]{4,3,2,1,0:T(8,128)S(1)} %get-tuple-element.34, f32[2,2,256,256]{3,2,1,0:T(8,128)S(1)} %bitcast.162), kind=kOutput, calls=%fused_computation.3 | convolution fusion | flops 1610874880 | bytes 3145728 | tf_op jit(solution)/shard_map/scrhm,sdckm->sdrhk/dot_general | solution.py:23
  9.2 0.1 maximum_bitcast_fusion.16
  9.2 1.9 %fusion = f32[2,256,2,256,1]{3,1,2,4,0:T(8,128)S(1)} fusion(f32[2,2,256,256,1]{2,3,1,0,4:T(8,128)S(1)} %convolution_bitcast_fusion.3, f32[1,2,256,256]{3,2,1,0:T(8,128)S(1)} %get-tuple-element.33, f32[1,2,256,256]{3,2,1,0:T(8,128)S(1)} %get-tuple-element.32), kind=kOutput, calls=%fused_computation.4 | convolution fusion | flops 1610874880 | bytes 3145728 | tf_op jit(solution)/shard_map/scrjl,dchj->sdrhl/dot_general | solution.py:27
  11.1 1.1 %copy.13 = f32[1,2,2,16,16,256]{5,4,2,1,0,3:T(8,128)} copy(f32[1,2,2,16,16,256]{5,4,3,2,1,0:T(8,128)S(1)} %bitcast.165) | data formatting | bytes 2097152 | tf_op jit(solution)/shard_map/reshape | solution.py:45
  12.2 7.4 %all-to-all-start = ((f32[1,2,2,16,16,256]{5,4,2,1,0,3:T(8,128)}), f32[1,2,2,16,16,256]{5,4,2,1,0,3:T(8,128)S(1)}, u32[]{:S(2)}, u32[]{:S(2)}) async-start(f32[1,2,2,16,16,256]{5,4,2,1,0,3:T(8,128)} %copy.13), calls=%async_computation | async-start | bytes 2097152 | tf_op jit(solution)/shard_map/all_to_all | solution.py:44
  19.5 0.0 copy-start.6
  19.5 0.0 copy-start.7
  19.6 0.0 copy-start.10
  19.6 0.0 copy-start.4
  19.6 0.1 maximum_bitcast_fusion.14
  19.7 0.8 copy-done.6
  20.5 0.1 copy-done.7
  20.6 0.1 copy-done.10
  20.7 0.1 maximum_bitcast_fusion.12
  20.7 0.1 copy-done.4
  20.8 0.1 slice_negate_fusion.2
  20.9 1.1 %maximum_bitcast_fusion.10 = (f32[1,1,2,256,256]{4,3,2,1,0:T(8,128)}, f32[1,1,2,256,256]{4,3,2,1,0:T(8,128)}) fusion(f32[1,1,256,256]{3,2,1,0:T(8,128)S(1)} %get-tuple-element.23, f32[1,1,256,256]{3,2,1,0:T(8,128)S(1)} %get-tuple-element.25, f32[1,1,256,256]{3,2,1,0:T(8,128)S(1)} %get-tuple-element.24), kind=kLoop, calls=%fused_computation.32 | loop fusion | flops 262144 | bytes 1835008 | tf_op jit(solution)/shard_map/stack | solution.py:12
  22.0 20.5 %all-to-all-done = f32[1,2,2,16,16,256]{5,4,2,1,0,3:T(8,128)S(1)} async-done(((f32[1,2,2,16,16,256]{5,4,2,1,0,3:T(8,128)}), f32[1,2,2,16,16,256]{5,4,2,1,0,3:T(8,128)S(1)}, u32[]{:S(2)}, u32[]{:S(2)}) %all-to-all-start) | async-done | bytes 1048608 | tf_op jit(solution)/shard_map/all_to_all | solution.py:44
  42.5 0.1 copy.14
  42.6 1.9 %convolution_bitcast_fusion.2 = f32[2,2,256,256,1]{2,3,1,0,4:T(8,128)S(1)} fusion(f32[2,2,256,256,1]{3,2,0,1,4:T(8,128)S(1)} %bitcast.163, f32[1,1,2,256,256]{4,3,2,1,0:T(8,128)S(1)} %get-tuple-element.31, f32[1,1,2,256,256]{4,3,2,1,0:T(8,128)S(1)} %get-tuple-element.30), kind=kOutput, calls=%fused_computation.2 | convolution fusion | flops 1610874880 | bytes 3145728 | tf_op jit(solution)/shard_map/scrhm,sdckm->sdrhk/dot_general | solution.py:23
  44.4 0.0 copy-start.2
  44.4 0.0 copy-start.3
  44.5 1.9 %convolution_bitcast_fusion = f32[2,2,256,256]{3,2,1,0:T(8,128)S(1)} fusion(f32[2,2,256,256,1]{2,3,1,0,4:T(8,128)S(1)} %convolution_bitcast_fusion.2, f32[1,2,256,256]{3,2,1,0:T(8,128)S(1)} %get-tuple-element.29, f32[1,2,256,256]{3,2,1,0:T(8,128)S(1)} %get-tuple-element.28), kind=kOutput, calls=%fused_computation | convolution fusion | flops 1610874880 | bytes 3145728 | tf_op jit(solution)/shard_map/scrjl,dchj->sdrhl/dot_general | solution.py:27
  46.3 0.0 copy-done.2
  46.3 0.0 copy-done.3
  46.3 1.9 %fusion.5 = f32[2,256,2,256,1]{1,3,4,2,0:T(8,128)S(1)} fusion(f32[1,1,2,256,256]{4,3,2,1,0:T(8,128)S(1)} %copy-done.3, f32[1,1,2,256,256]{4,3,2,1,0:T(8,128)S(1)} %copy-done.2, f32[2,2,256,256]{3,2,1,0:T(8,128)S(1)} %convolution_bitcast_fusion), kind=kOutput, calls=%fused_computation.11 | convolution fusion | flops 1610874880 | bytes 3145728 | tf_op jit(solution)/shard_map/scrhm,sdckm->sdrhk/dot_general | solution.py:23
  48.2 1.1 %copy.17 = f32[1,2,2,16,16,256]{5,4,2,1,0,3:T(8,128)} copy(f32[1,2,2,16,16,256]{5,4,3,2,1,0:T(8,128)S(1)} %bitcast.166) | data formatting | bytes 2097152 | tf_op jit(solution)/shard_map/reshape | solution.py:51
  49.3 0.0 copy-start.5
  49.3 0.0 copy-start.9
  49.3 7.0 %all-to-all-start.1 = ((f32[1,2,2,16,16,256]{5,4,2,1,0,3:T(8,128)}), f32[1,2,2,16,16,256]{5,4,2,1,0,3:T(8,128)S(1)}, u32[]{:S(2)}, u32[]{:S(2)}) async-start(f32[1,2,2,16,16,256]{5,4,2,1,0,3:T(8,128)} %copy.17), calls=%async_computation.1 | async-start | bytes 2097152 | tf_op jit(solution)/shard_map/all_to_all | solution.py:50
  56.3 0.0 copy-done.5
  56.3 0.0 copy-done.9
  56.3 0.1 maximum_bitcast_fusion.8
  56.4 22.8 %all-to-all-done.1 = f32[1,2,2,16,16,256]{5,4,2,1,0,3:T(8,128)S(1)} async-done(((f32[1,2,2,16,16,256]{5,4,2,1,0,3:T(8,128)}), f32[1,2,2,16,16,256]{5,4,2,1,0,3:T(8,128)S(1)}, u32[]{:S(2)}, u32[]{:S(2)}) %all-to-all-start.1) | async-done | bytes 1048608 | tf_op jit(solution)/shard_map/all_to_all | solution.py:50
  79.2 0.1 copy.18
  79.3 1.8 %convolution_bitcast_fusion.1 = f32[1,2,2,256,256]{4,3,2,1,0:T(8,128)S(1)} fusion(f32[2,2,256,256,1]{3,2,0,1,4:T(8,128)S(1)} %bitcast.164, f32[1,2,256,256]{3,2,1,0:T(8,128)S(1)} %get-tuple-element.27, f32[1,2,256,256]{3,2,1,0:T(8,128)S(1)} %get-tuple-element.26), kind=kOutput, calls=%fused_computation.1 | convolution fusion | flops 1610874880 | bytes 3145728 | tf_op jit(solution)/shard_map/scrjl,dchj->sdrhl/dot_general | solution.py:27
  81.2 1.7 %reshape.193 = f32[2,131072]{1,0:T(2,128)} reshape(f32[1,2,2,256,256]{4,3,2,1,0:T(8,128)S(1)} %convolution_bitcast_fusion.1) | data formatting | bytes 2097152 | tf_op jit(solution)/shard_map/reshape | solution.py:54
Async XLA Ops:
  0.0 2.4 %copy-start = (f32[3,2,256,256]{3,2,1,0:T(8,128)S(1)}, f32[3,2,256,256]{3,2,1,0:T(8,128)}, u32[]{:S(2)}) copy-start(f32[3,2,256,256]{3,2,1,0:T(8,128)} %param.6) | copy-start | bytes 4718596
  0.0 3.3 %copy-start.11 = (s32[1,3]{1,0:T(1,128)S(1)}, s32[1,3]{1,0:T(1,128)}, u32[]{:S(2)}) copy-start(s32[1,3]{1,0:T(1,128)} %param.7) | copy-start | bytes 40
  0.0 5.9 %copy-start.8 = (f32[1,2,131072]{2,1,0:T(2,128)S(1)}, f32[1,2,131072]{2,1,0:T(2,128)}, u32[]{:S(2)}) copy-start(f32[1,2,131072]{2,1,0:T(2,128)} %param.4) | copy-start | bytes 3145732
  2.4 3.6 %copy-start.1 = (f32[3,2,2,256,256]{4,3,2,1,0:T(8,128)S(1)}, f32[3,2,2,256,256]{4,3,2,1,0:T(8,128)}, u32[]{:S(2)}) copy-start(f32[3,2,2,256,256]{4,3,2,1,0:T(8,128)} %param.5) | copy-start | bytes 9437188
  12.2 30.3 %all-to-all-start = ((f32[1,2,2,16,16,256]{5,4,2,1,0,3:T(8,128)}), f32[1,2,2,16,16,256]{5,4,2,1,0,3:T(8,128)S(1)}, u32[]{:S(2)}, u32[]{:S(2)}) async-start(f32[1,2,2,16,16,256]{5,4,2,1,0,3:T(8,128)} %copy.13), calls=%async_computation | async-start | bytes 2097152 | tf_op jit(solution)/shard_map/all_to_all | solution.py:44
  19.5 1.0 %copy-start.6 = (f32[1,256,256]{2,1,0:T(8,128)S(1)}, f32[1,256,256]{2,1,0:T(8,128)}, u32[]{:S(2)}) copy-start(f32[1,256,256]{2,1,0:T(8,128)} %get-tuple-element.12) | copy-start | bytes 786436
  19.5 1.0 %copy-start.7 = (f32[1,256,256]{2,1,0:T(8,128)S(1)}, f32[1,256,256]{2,1,0:T(8,128)}, u32[]{:S(2)}) copy-start(f32[1,256,256]{2,1,0:T(8,128)} %get-tuple-element.13) | copy-start | bytes 786436
  19.6 1.1 %copy-start.10 = (f32[1,256,256]{2,1,0:T(8,128)S(1)}, f32[1,256,256]{2,1,0:T(8,128)}, u32[]{:S(2)}) copy-start(f32[1,256,256]{2,1,0:T(8,128)} %get-tuple-element.10) | copy-start | bytes 786436
  19.6 1.3 %copy-start.4 = (f32[1,2,256,256]{3,2,1,0:T(8,128)S(1)}, f32[1,2,256,256]{3,2,1,0:T(8,128)}, u32[]{:S(2)}) copy-start(f32[1,2,256,256]{3,2,1,0:T(8,128)} %get-tuple-element.6) | copy-start | bytes 1572868
  44.4 1.9 %copy-start.2 = (f32[1,1,2,256,256]{4,3,2,1,0:T(8,128)S(1)}, f32[1,1,2,256,256]{4,3,2,1,0:T(8,128)}, u32[]{:S(2)}) copy-start(f32[1,1,2,256,256]{4,3,2,1,0:T(8,128)} %get-tuple-element.36) | copy-start | bytes 1572868
  44.4 1.9 %copy-start.3 = (f32[1,1,2,256,256]{4,3,2,1,0:T(8,128)S(1)}, f32[1,1,2,256,256]{4,3,2,1,0:T(8,128)}, u32[]{:S(2)}) copy-start(f32[1,1,2,256,256]{4,3,2,1,0:T(8,128)} %get-tuple-element.37) | copy-start | bytes 1572868
  49.3 7.0 %copy-start.5 = (f32[1,256,256]{2,1,0:T(8,128)S(1)}, f32[1,256,256]{2,1,0:T(8,128)}, u32[]{:S(2)}) copy-start(f32[1,256,256]{2,1,0:T(8,128)} %get-tuple-element.14) | copy-start | bytes 786436
  49.3 7.0 %copy-start.9 = (f32[1,256,256]{2,1,0:T(8,128)S(1)}, f32[1,256,256]{2,1,0:T(8,128)}, u32[]{:S(2)}) copy-start(f32[1,256,256]{2,1,0:T(8,128)} %get-tuple-element.8) | copy-start | bytes 786436
  49.3 29.9 %all-to-all-start.1 = ((f32[1,2,2,16,16,256]{5,4,2,1,0,3:T(8,128)}), f32[1,2,2,16,16,256]{5,4,2,1,0,3:T(8,128)S(1)}, u32[]{:S(2)}, u32[]{:S(2)}) async-start(f32[1,2,2,16,16,256]{5,4,2,1,0,3:T(8,128)} %copy.17), calls=%async_computation.1 | async-start | bytes 2097152 | tf_op jit(solution)/shard_map/all_to_all | solution.py:50
where the time goes:
time: 84.3 us; the launch traced here: 82.8 us
  waiting for transfers between devices  43.3 us (51%)
  starting transfers between devices  14.4 us (17%)
  matrix products  11.1 us (13%)
  local copies, waits for them, and re-layouts  8.22 us (10%)
  other arithmetic  3.55 us (4%)
  between operations  2.26 us (3%)
    all_to_all x2, waiting for transfers between devices, body(): lax.all_to_all(amplitudes.reshape(split_shape), 'stem', split_axis=3, con...  43.3 us
    all_to_all x2, starting transfers between devices, body(): lax.all_to_all(amplitudes.reshape(split_shape), 'stem', split_axis=3, con...  14.4 us
    dot_general x3, matrix products, apply_low(): jnp.einsum('scrhm,sdckm->sdrhk', amplitudes, blocks, precision=lax.Precis...  5.58 us
    dot_general x3, matrix products, apply_high(): jnp.einsum('scrjl,dchj->sdrhl', amplitudes, block, precision=lax.Precisio...  5.56 us
    squeeze x1, local copies, waits for them, and re-layouts, complex_block(): imag_part = matrices[..., 1, :, :]  2.4 us
    reshape x2, local copies, waits for them, and re-layouts, body(): amplitudes.reshape(split_shape)  2.13 us
  transfers between devices with their start and end apart: 2, of which 2 were waited for; matrix products, arithmetic and copies ran while one was open for 2% of the time, Pallas kernels for 0%

commit v1 on v0

v1 whole, which is shorter than its diff:
```python
import functools

import jax
import jax.numpy as jnp
from jax import lax
from jax.experimental import pallas as pl
from jax.experimental.pallas import tpu as pltpu
from jax.sharding import PartitionSpec as P

LANES = 128
SUBLANES = 8


def halves(values):
    upper = values.astype(jnp.bfloat16)
    return upper, (values - upper.astype(jnp.float32)).astype(jnp.bfloat16)


def dot_halves(left, right):
    dot = functools.partial(jnp.dot, preferred_element_type=jnp.float32)
    small = dot(left[0], right[1]) + dot(left[1], right[0])
    return dot(left[0], right[0]) + small


def complex_left(matrix, real_part, imag_part):
    width = real_part.shape[1]
    both = halves(jnp.concatenate([real_part, imag_part], axis=1))
    by_real = dot_halves(halves(matrix[0]), both)
    by_imag = dot_halves(halves(matrix[1]), both)
    return (
        by_real[:, :width] - by_imag[:, width:],
        by_real[:, width:] + by_imag[:, :width],
    )


def complex_right(real_part, imag_part, matrix):
    height = real_part.shape[0]
    both = halves(jnp.concatenate([real_part, imag_part], axis=0))
    by_real = dot_halves(both, halves(matrix[0]))
    by_imag = dot_halves(both, halves(matrix[1]))
    return (
        by_real[:height] - by_imag[height:],
        by_real[height:] + by_imag[:height],
    )


def open_kernel(stem_ref, high_ref, out_ref):
    leading, _, _, under, low = out_ref.shape
    high = leading * under
    tiles = low // LANES
    parts = [
        jnp.concatenate(
            [stem_ref[pl.ds(2 * t + c, high, stride=2 * tiles), :] for t in range(tiles)], axis=1
        )
        for c in range(2)
    ]
    for c, value in enumerate(complex_left(high_ref[0], *parts)):
        out_ref[:, 0, c] = value.reshape(leading, under, low)


def chain_kernel(bits_ref, table_ref, out_ref, held, sems):
    segments = held.shape[0]
    copies = []
    for k in range(segments):
        entry = jnp.where(bits_ref[0, k] == 1, 1, 0)
        copies.append(pltpu.make_async_copy(table_ref.at[k, entry], held.at[k], sems.at[k]))
        copies[-1].start()
    for copy in copies:
        copy.wait()
    total = (held[0, 0], held[0, 1])
    for k in range(1, segments):
        total = complex_left(held[k], *total)
    for c in range(2):
        out_ref[c] = total[c].T


def middle_kernel(in_ref, high_ref, low_ref, out_ref):
    leading, _, _, under, low = in_ref.shape
    high = leading * under
    parts = [in_ref[:, 0, c].reshape(high, low) for c in range(2)]
    parts = complex_left(high_ref[0], *parts)
    for c, value in enumerate(complex_right(*parts, low_ref)):
        out_ref[:, 0, c] = value.reshape(leading, under, low)


def close_kernel(in_ref, high_ref, out_ref):
    leading, _, _, under, low = in_ref.shape
    high = leading * under
    tiles = low // LANES
    parts = [in_ref[:, 0, c].reshape(high, low) for c in range(2)]
    for c, value in enumerate(complex_left(high_ref[0], *parts)):
        for t in range(tiles):
            out_ref[pl.ds(2 * t + c, high, stride=2 * tiles), :] = value[
                :, t * LANES : (t + 1) * LANES
            ]


def one_slice(stem, bits, lo_table, hi_table):
    leading = lax.axis_size("stem")
    segments, _, high, _ = hi_table.shape
    low = lo_table.shape[-1]
    spare = stem.shape[1] // (high * low)
    under = high // leading
    direct = under % SUBLANES == 0
    kept = (leading, under) if direct else (1, high)
    rows = high * 2 * (low // LANES)
    split_shape = (kept[0], spare, 2, kept[1], low)
    split_spec = pl.BlockSpec((kept[0], 1, 2, kept[1], low), lambda r: (0, r, 0, 0, 0))
    split_type = jax.ShapeDtypeStruct(split_shape, jnp.float32)
    stem_spec = pl.BlockSpec((rows, LANES), lambda r: (r, 0))
    flops = 2 * 4 * 3 * spare * high * high * low
    moved = 4 * stem.size * 2
    cost = pl.CostEstimate(flops=flops, bytes_accessed=moved, transcendentals=0)

    def high_spec(segment):
        return pl.BlockSpec((1, 2, high, high), lambda r: (segment, 0, 0, 0))

    def exchange(values):
        if not direct:
            values = values.reshape(spare, 2, leading, under, low).transpose(2, 0, 1, 3, 4)
        values = lax.all_to_all(values, "stem", split_axis=0, concat_axis=0, tiled=True)
        if not direct:
            values = values.transpose(1, 2, 0, 3, 4).reshape(split_shape)
        return values

    laid = stem.reshape(2, stem.shape[1] // LANES, LANES).transpose(1, 0, 2).reshape(-1, LANES)
    chain = pl.pallas_call(
        chain_kernel,
        out_shape=jax.ShapeDtypeStruct((2, low, low), jnp.float32),
        in_specs=[pl.BlockSpec(memory_space=pltpu.SMEM), pl.BlockSpec(memory_space=pl.ANY)],
        scratch_shapes=[
            pltpu.VMEM((segments, 2, low, low), jnp.float32),
            pltpu.SemaphoreType.DMA((segments,)),
        ],
        cost_estimate=cost,
        name="low_chain",
    )(bits, lo_table)
    opened = pl.pallas_call(
        open_kernel,
        grid=(spare,),
        out_shape=split_type,
        in_specs=[stem_spec, high_spec(0)],
        out_specs=split_spec,
        cost_estimate=cost,
        name="open_high",
    )(laid, hi_table)
    middle = pl.pallas_call(
        middle_kernel,
        grid=(spare,),
        out_shape=split_type,
        in_specs=[split_spec, high_spec(1), pl.BlockSpec((2, low, low), lambda r: (0, 0, 0))],
        out_specs=split_spec,
        cost_estimate=cost,
        name="middle_high_low",
    )(exchange(opened), hi_table, chain)
    closed = pl.pallas_call(
        close_kernel,
        grid=(spare,),
        out_shape=jax.ShapeDtypeStruct(laid.shape, jnp.float32),
        in_specs=[split_spec, high_spec(2)],
        out_specs=stem_spec,
        cost_estimate=cost,
        name="close_high",
    )(exchange(middle), hi_table)
    return closed.reshape(-1, 2, LANES).transpose(1, 0, 2).reshape(stem.shape)


def body(stems, lo_table, hi_table, slice_bits):
    slices = [
        one_slice(stems[s], slice_bits[s : s + 1], lo_table, hi_table)
        for s in range(stems.shape[0])
    ]
    return functools.reduce(jnp.add, slices)


def solution(mesh):
    placed = (P("groups", None, "stem"), P(), P(), P("groups", None))
    return jax.shard_map(
        body, mesh=mesh, in_specs=placed, out_specs=P(None, ("groups", "stem")), check_vma=False
    )
```

time: 84.3 us -> 74.6 us (0.88)
  blocking collectives: 0 us -> 31.8 us
  waiting for transfers between devices: 43.3 us -> 18.8 us
  Pallas kernels: 0 us -> 14.9 us
  matrix products: 11.1 us -> 0 us
  local copies, waits for them, and re-layouts: 8.22 us -> 0.97 us
  starting transfers between devices: 14.4 us -> 7.37 us
  other arithmetic: 3.55 us -> 0 us
  between operations: 2.26 us -> 0.02 us
    all_to_all x0 -> x1, blocking collectives: none -> 31.8 us  [exchange(): lax.all_to_all(values, 'stem', split_axis=0, concat_axis=0, tiled=True)]
    all_to_all x2 -> x1, waiting for transfers between devices: 43.3 us -> 18.8 us  [exchange(): lax.all_to_all(values, 'stem', split_axis=0, concat_axis=0, tiled=True)]
    pallas_call x0 -> x4, Pallas kernels: none -> 14.9 us  [the longest x1 4.36 us: one_slice(): pl.pallas_call(middle_kernel, grid=(spare,), out_shape=split_type, in_spe...]
    dot_general x6 -> x0, matrix products: 11.1 us -> none  [the longest x3 5.58 us: apply_low(): jnp.einsum('scrhm,sdckm->sdrhk', amplitudes, blocks, precision=lax.Precis...]
    all_to_all x2 -> x1, starting transfers between devices: 14.4 us -> 7.37 us  [exchange(): lax.all_to_all(values, 'stem', split_axis=0, concat_axis=0, tiled=True)]
    reshape x3 -> x0, local copies, waits for them, and re-layouts: 3.8 us -> none  [the longest x2 2.13 us: body(): amplitudes.reshape(split_shape)]
    squeeze x1 -> x0, local copies, waits for them, and re-layouts: 2.4 us -> none  [complex_block(): imag_part = matrices[..., 1, :, :]]
    another operation x6 -> x0, other arithmetic: 1.5 us -> none  [complex_block(): return jnp.stack([upper_rows, lower_rows], axis=-4)]
  transfers between devices with their start and end apart: 2 -> 1, of which waited for: 2 -> 1; matrix products, arithmetic and copies ran while one was open for 2% -> 0% of each run, Pallas kernels for 0% -> 6%
where the time goes in v1:
time: 74.6 us; the launch traced here: 73.9 us
  blocking collectives  31.8 us (43%)
  waiting for transfers between devices  18.8 us (25%)
  Pallas kernels  14.9 us (20%)
  starting transfers between devices  7.37 us (10%)
  local copies, waits for them, and re-layouts  0.97 us (1%)
    all_to_all x1, blocking collectives, exchange(): lax.all_to_all(values, 'stem', split_axis=0, concat_axis=0, tiled=True)  31.8 us
    all_to_all x1, waiting for transfers between devices, exchange(): lax.all_to_all(values, 'stem', split_axis=0, concat_axis=0, tiled=True)  18.8 us
    all_to_all x1, starting transfers between devices, exchange(): lax.all_to_all(values, 'stem', split_axis=0, concat_axis=0, tiled=True)  7.37 us
    pallas_call x1, Pallas kernels, one_slice(): pl.pallas_call(middle_kernel, grid=(spare,), out_shape=split_type, in_spe...  4.36 us
    pallas_call x1, Pallas kernels, one_slice(): pl.pallas_call(chain_kernel, out_shape=jax.ShapeDtypeStruct((2, low, low)...  4.11 us
    pallas_call x1, Pallas kernels, one_slice(): pl.pallas_call(open_kernel, grid=(spare,), out_shape=split_type, in_specs...  3.21 us
    pallas_call x1, Pallas kernels, one_slice(): pl.pallas_call(close_kernel, grid=(spare,), out_shape=jax.ShapeDtypeStruc...  3.19 us
  transfers between devices with their start and end apart: 1, of which 1 were waited for; matrix products, arithmetic and copies ran while one was open for 0% of the time, Pallas kernels for 6%

profile of v1, /device:TPU:0, one launch (start us, length us, event | category | flops | bytes accessed | tf_op | source)
XLA Modules:
  0.0 73.9 jit_solution(15536403298597722851)
XLA Ops:
  0.0 3.2 %open_high.1 = f32[16,2,2,16,256]{4,3,2,1,0:T(8,128)} custom-call(f32[2048,128]{1,0:T(8,128)} %bitcast.10, f32[3,2,256,256]{3,2,1,0:T(8,128)} %high_ref.5), custom_call_target="tpu_custom_call" | custom-call | flops 805306368 | bytes 2097152 | tf_op jit(solution)/shard_map/open_high/pallas_call | solution.py:138
  3.2 7.4 %all-to-all-start = ((f32[16,2,2,16,256]{4,3,2,1,0:T(8,128)}), f32[16,2,2,16,256]{4,3,2,1,0:T(8,128)S(1)}, u32[]{:S(2)}, u32[]{:S(2)}) async-start(f32[16,2,2,16,256]{4,3,2,1,0:T(8,128)} %open_high.1), calls=%async_computation | async-start | bytes 2097152 | tf_op jit(solution)/shard_map/all_to_all | solution.py:121
  10.6 4.1 %low_chain.1.low_ref = f32[2,256,256]{2,1,0:T(8,128)} custom-call(s32[1,3]{1,0:T(1,128)} %bits_ref.1, f32[3,2,2,256,256]{4,3,2,1,0:T(8,128)} %table_ref.1), custom_call_target="tpu_custom_call" | custom-call | flops 805306368 | bytes 2097152 | tf_op jit(solution)/shard_map/low_chain/pallas_call | solution.py:127
  14.7 18.8 %all-to-all-done.in_ref = f32[16,2,2,16,256]{4,3,2,1,0:T(8,128)S(1)} async-done(((f32[16,2,2,16,256]{4,3,2,1,0:T(8,128)}), f32[16,2,2,16,256]{4,3,2,1,0:T(8,128)S(1)}, u32[]{:S(2)}, u32[]{:S(2)}) %all-to-all-start) | async-done | bytes 1048608 | tf_op jit(solution)/shard_map/all_to_all | solution.py:121
  33.5 0.0 copy-start
  33.5 1.0 %copy-done = f32[16,2,2,16,256]{4,3,2,1,0:T(8,128)} copy-done((f32[16,2,2,16,256]{4,3,2,1,0:T(8,128)}, f32[16,2,2,16,256]{4,3,2,1,0:T(8,128)S(1)}, u32[]{:S(2)}) %copy-start) | copy-done | bytes 1048600
  34.5 4.4 %middle_high_low.1 = f32[16,2,2,16,256]{4,3,2,1,0:T(8,128)} custom-call(f32[16,2,2,16,256]{4,3,2,1,0:T(8,128)} %copy-done, f32[3,2,256,256]{3,2,1,0:T(8,128)} %high_ref.5, f32[2,256,256]{2,1,0:T(8,128)} %low_chain.1.low_ref), custom_call_target="tpu_custom_call" | custom-call | flops 805306368 | bytes 2097152 | tf_op jit(solution)/shard_map/middle_high_low/pallas_call | solution.py:147
  38.9 31.8 %all_to_all.10.in_ref = f32[16,2,2,16,256]{4,3,2,1,0:T(8,128)} all-to-all(f32[16,2,2,16,256]{4,3,2,1,0:T(8,128)} %middle_high_low.1), channel_id=1, replica_groups=mesh['groups'=2,'stem'=16] {'stem'}, dimensions={0} | all-to-all | bytes 2097152 | tf_op jit(solution)/shard_map/all_to_all | solution.py:121
  70.7 3.2 %close_high.1 = f32[2048,128]{1,0:T(8,128)} custom-call(f32[16,2,2,16,256]{4,3,2,1,0:T(8,128)} %all_to_all.10.in_ref, f32[3,2,256,256]{3,2,1,0:T(8,128)} %high_ref.5), custom_call_target="tpu_custom_call" | custom-call | flops 805306368 | bytes 2097152 | tf_op jit(solution)/shard_map/close_high/pallas_call | solution.py:156
Async XLA Ops:
  3.2 30.3 %all-to-all-start = ((f32[16,2,2,16,256]{4,3,2,1,0:T(8,128)}), f32[16,2,2,16,256]{4,3,2,1,0:T(8,128)S(1)}, u32[]{:S(2)}, u32[]{:S(2)}) async-start(f32[16,2,2,16,256]{4,3,2,1,0:T(8,128)} %open_high.1), calls=%async_computation | async-start | bytes 2097152 | tf_op jit(solution)/shard_map/all_to_all | solution.py:121
  33.5 1.0 %copy-start = (f32[16,2,2,16,256]{4,3,2,1,0:T(8,128)}, f32[16,2,2,16,256]{4,3,2,1,0:T(8,128)S(1)}, u32[]{:S(2)}) copy-start(f32[16,2,2,16,256]{4,3,2,1,0:T(8,128)S(1)} %all-to-all-done.in_ref) | copy-start | bytes 3145732

commit v2 on v1

v2 whole, which is shorter than its diff:
```python
import jax
import jax.numpy as jnp
from jax import lax
from jax.experimental import pallas as pl
from jax.experimental.pallas import tpu as pltpu
from jax.sharding import PartitionSpec as P

LANES = 128
SUBLANES = 8
VMEM = pl.BlockSpec(memory_space=pltpu.VMEM)
SMEM = pl.BlockSpec(memory_space=pltpu.SMEM)
HBM = pl.BlockSpec(memory_space=pltpu.HBM)
SMALL = pltpu.CompilerParams(vmem_limit_bytes=20 * 1024 * 1024)
LARGE = pltpu.CompilerParams(vmem_limit_bytes=56 * 1024 * 1024)


def halves(values):
    upper = values.astype(jnp.bfloat16)
    return upper, (values - upper.astype(jnp.float32)).astype(jnp.bfloat16)


def dot_halves(left, right):
    return jnp.dot(
        jnp.concatenate([left[0], left[0], left[1]], axis=1),
        jnp.concatenate([right[0], right[1], right[0]], axis=0),
        preferred_element_type=jnp.float32,
    )


def left_block(real_part, imag_part):
    upper = jnp.concatenate([real_part, -imag_part], axis=1)
    lower = jnp.concatenate([imag_part, real_part], axis=1)
    return jnp.concatenate([upper, lower], axis=0)


def right_block(real_part, imag_part):
    upper = jnp.concatenate([real_part, imag_part], axis=1)
    lower = jnp.concatenate([-imag_part, real_part], axis=1)
    return jnp.concatenate([upper, lower], axis=0)


def read_stem(stem_ref, high):
    tiles = stem_ref.shape[0] // (2 * high)
    parts = [
        jnp.concatenate(
            [stem_ref[pl.ds(2 * t + c, high, stride=2 * tiles), :] for t in range(tiles)], axis=1
        )
        for c in range(2)
    ]
    return jnp.concatenate(parts, axis=0)


def write_stem(stem_ref, value, high):
    tiles = stem_ref.shape[0] // (2 * high)
    for c in range(2):
        for t in range(tiles):
            stem_ref[pl.ds(2 * t + c, high, stride=2 * tiles), :] = value[
                c * high : (c + 1) * high, t * LANES : (t + 1) * LANES
            ]


def open_kernel(stem_ref, high_ref, out_ref, stem, table, sems):
    leading, spare, _, under, low = out_ref.shape
    high = leading * under
    table_copy = pltpu.make_async_copy(high_ref.at[0], table, sems.at[spare])
    table_copy.start()
    copies = [
        pltpu.make_async_copy(stem_ref.at[r], stem.at[r], sems.at[r]) for r in range(spare)
    ]
    for copy in copies:
        copy.start()
    table_copy.wait()
    matrix = halves(left_block(table[0], table[1]))
    for r in range(spare):
        copies[r].wait()
        value = dot_halves(matrix, halves(read_stem(stem.at[r], high)))
        for c in range(2):
            out_ref[:, r, c] = value[c * high : (c + 1) * high].reshape(leading, under, low)


def chain_kernel(bits_ref, table_ref, out_ref, held, sems):
    segments = held.shape[0]
    copies = []
    for k in range(segments):
        entry = jnp.where(bits_ref[0, k] == 1, 1, 0)
        copies.append(pltpu.make_async_copy(table_ref.at[k, entry], held.at[k], sems.at[k]))
        copies[-1].start()
    for copy in copies:
        copy.wait()
    low = held.shape[-1]
    total = jnp.concatenate([held[0, 0], held[0, 1]], axis=0)
    for k in range(1, segments):
        total = dot_halves(halves(left_block(held[k, 0], held[k, 1])), halves(total))
    for c in range(2):
        out_ref[c] = total[c * low : (c + 1) * low].T


def middle_kernel(in_ref, high_ref, low_ref, out_ref, high_table, low_table, sems):
    leading, spare, _, under, low = in_ref.shape
    high = leading * under
    high_copy = pltpu.make_async_copy(high_ref.at[1], high_table, sems.at[0])
    low_copy = pltpu.make_async_copy(low_ref, low_table, sems.at[1])
    high_copy.start()
    low_copy.start()
    parts = [
        halves(jnp.concatenate([in_ref[:, r, c].reshape(high, low) for c in range(2)], axis=0))
        for r in range(spare)
    ]
    high_copy.wait()
    matrix = halves(left_block(high_table[0], high_table[1]))
    parts = [dot_halves(matrix, part) for part in parts]
    low_copy.wait()
    matrix = halves(right_block(low_table[0], low_table[1]))
    for r in range(spare):
        value = jnp.concatenate([parts[r][:high], parts[r][high:]], axis=1)
        value = dot_halves(halves(value), matrix)
        for c in range(2):
            out_ref[:, r, c] = value[:, c * low : (c + 1) * low].reshape(leading, under, low)


def close_kernel(in_ref, high_ref, out_ref, held, table, sems):
    leading, spare, _, under, low = in_ref.shape
    high = leading * under
    table_copy = pltpu.make_async_copy(high_ref.at[2], table, sems.at[spare])
    table_copy.start()
    parts = [
        halves(jnp.concatenate([in_ref[:, r, c].reshape(high, low) for c in range(2)], axis=0))
        for r in range(spare)
    ]
    table_copy.wait()
    matrix = halves(left_block(table[0], table[1]))
    copies = []
    for r in range(spare):
        write_stem(held.at[r], dot_halves(matrix, parts[r]), high)
        copies.append(pltpu.make_async_copy(held.at[r], out_ref.at[r], sems.at[r]))
        copies[-1].start()
    for copy in copies:
        copy.wait()


def one_slice(stem, bits, lo_table, hi_table):
    leading = lax.axis_size("stem")
    segments, _, high, _ = hi_table.shape
    low = lo_table.shape[-1]
    rows = high * 2 * (low // LANES)
    spare = stem.size // (rows * LANES)
    under = high // leading
    direct = under % SUBLANES == 0
    kept = (leading, under) if direct else (1, high)
    split_shape = (kept[0], spare, 2, kept[1], low)
    split_type = jax.ShapeDtypeStruct(split_shape, jnp.float32)
    stem_type = jax.ShapeDtypeStruct((spare, rows, LANES), jnp.float32)
    stem_scratch = pltpu.VMEM(stem_type.shape, jnp.float32)

    def exchange(values):
        if not direct:
            values = values.reshape(spare, 2, leading, under, low).transpose(2, 0, 1, 3, 4)
        values = lax.all_to_all(values, "stem", split_axis=0, concat_axis=0, tiled=True)
        if not direct:
            values = values.transpose(1, 2, 0, 3, 4).reshape(split_shape)
        return values

    laid = stem.reshape(2, stem.shape[1] // LANES, LANES).transpose(1, 0, 2)
    laid = laid.reshape(stem_type.shape)
    table_scratch = pltpu.VMEM((2, high, high), jnp.float32)
    opened = pl.pallas_call(
        open_kernel,
        out_shape=split_type,
        in_specs=[HBM, HBM],
        out_specs=VMEM,
        scratch_shapes=[stem_scratch, table_scratch, pltpu.SemaphoreType.DMA((spare + 1,))],
        compiler_params=LARGE,
        name="open_high",
    )(laid, hi_table)
    chain = pl.pallas_call(
        chain_kernel,
        out_shape=jax.ShapeDtypeStruct((2, low, low), jnp.float32),
        in_specs=[SMEM, HBM],
        out_specs=VMEM,
        scratch_shapes=[
            pltpu.VMEM((segments, 2, low, low), jnp.float32),
            pltpu.SemaphoreType.DMA((segments,)),
        ],
        compiler_params=LARGE,
        name="low_chain",
    )(bits, lo_table)
    middle = pl.pallas_call(
        middle_kernel,
        out_shape=split_type,
        in_specs=[VMEM, HBM, HBM],
        out_specs=VMEM,
        scratch_shapes=[
            table_scratch,
            pltpu.VMEM((2, low, low), jnp.float32),
            pltpu.SemaphoreType.DMA((2,)),
        ],
        compiler_params=SMALL,
        name="middle_high_low",
    )(exchange(opened), hi_table, chain)
    closed = pl.pallas_call(
        close_kernel,
        out_shape=stem_type,
        in_specs=[VMEM, HBM],
        out_specs=HBM,
        scratch_shapes=[stem_scratch, table_scratch, pltpu.SemaphoreType.DMA((spare + 1,))],
        compiler_params=SMALL,
        name="close_high",
    )(exchange(middle), hi_table)
    return closed.reshape(-1, 2, LANES).transpose(1, 0, 2).reshape(stem.shape)


def body(stems, lo_table, hi_table, slice_bits):
    total = one_slice(stems[0], slice_bits[:1], lo_table, hi_table)
    for s in range(1, stems.shape[0]):
        total = total + one_slice(stems[s], slice_bits[s : s + 1], lo_table, hi_table)
    return total


def solution(mesh):
    placed = (P("groups", None, "stem"), P(), P(), P("groups", None))
    return jax.shard_map(
        body, mesh=mesh, in_specs=placed, out_specs=P(None, ("groups", "stem")), check_vma=False
    )
```

time: 74.6 us -> 72.2 us (0.968)
  Pallas kernels: 14.9 us -> 13.3 us
    pallas_call x3, Pallas kernels: 10.8 us -> 8.53 us  [the longest x1 4.12 us: one_slice(): pl.pallas_call(open_kernel, out_shape=split_type, in_specs=[HBM, HBM], ou...]
  transfers between devices with their start and end apart: 1 -> 1, of which waited for: 1 -> 1; matrix products, arithmetic and copies ran while one was open for 0% -> 0% of each run, Pallas kernels for 6% -> 7%
where the time goes in v2:
time: 72.2 us; the launch traced here: 71.6 us
  blocking collectives  31.5 us (44%)
  waiting for transfers between devices  18.2 us (25%)
  Pallas kernels  13.3 us (18%)
  starting transfers between devices  7.5 us (10%)
  local copies, waits for them, and re-layouts  1.05 us (1%)
    all_to_all x1, blocking collectives, exchange(): lax.all_to_all(values, 'stem', split_axis=0, concat_axis=0, tiled=True)  31.5 us
    all_to_all x1, waiting for transfers between devices, exchange(): lax.all_to_all(values, 'stem', split_axis=0, concat_axis=0, tiled=True)  18.2 us
    all_to_all x1, starting transfers between devices, exchange(): lax.all_to_all(values, 'stem', split_axis=0, concat_axis=0, tiled=True)  7.5 us
    pallas_call x1, Pallas kernels, one_slice(): pl.pallas_call(chain_kernel, out_shape=jax.ShapeDtypeStruct((2, low, low)...  4.73 us
    pallas_call x1, Pallas kernels, one_slice(): pl.pallas_call(open_kernel, out_shape=split_type, in_specs=[HBM, HBM], ou...  4.12 us
    pallas_call x1, Pallas kernels, one_slice(): pl.pallas_call(middle_kernel, out_shape=split_type, in_specs=[VMEM, HBM,...  2.23 us
    pallas_call x1, Pallas kernels, one_slice(): pl.pallas_call(close_kernel, out_shape=stem_type, in_specs=[VMEM, HBM], o...  2.18 us
  transfers between devices with their start and end apart: 1, of which 1 were waited for; matrix products, arithmetic and copies ran while one was open for 0% of the time, Pallas kernels for 7%

profile of v2, /device:TPU:0, one launch (start us, length us, event | category | flops | bytes accessed | tf_op | source)
XLA Modules:
  0.0 71.6 jit_solution(10426158361669138183)
XLA Ops:
  0.0 4.1 %open_high.1 = f32[16,2,2,16,256]{4,3,2,1,0:T(8,128)} custom-call(f32[2,1024,128]{2,1,0:T(8,128)} %bitcast.10, f32[3,2,256,256]{3,2,1,0:T(8,128)} %high_ref.5), custom_call_target="tpu_custom_call" | custom-call | tf_op jit(solution)/shard_map/open_high/pallas_call | solution.py:166
  4.1 0.0 copy-start
  4.1 7.5 %all-to-all-start = ((f32[16,2,2,16,256]{4,3,2,1,0:T(8,128)}), f32[16,2,2,16,256]{4,3,2,1,0:T(8,128)S(1)}, u32[]{:S(2)}, u32[]{:S(2)}) async-start(f32[16,2,2,16,256]{4,3,2,1,0:T(8,128)} %open_high.1), calls=%async_computation | async-start | bytes 2097152 | tf_op jit(solution)/shard_map/all_to_all | solution.py:158
  11.6 4.7 %low_chain.1.low_ref = f32[2,256,256]{2,1,0:T(8,128)} custom-call(s32[1,3]{1,0:T(1,128)} %bits_ref.1, f32[3,2,2,256,256]{4,3,2,1,0:T(8,128)} %table_ref.1), custom_call_target="tpu_custom_call" | custom-call | tf_op jit(solution)/shard_map/low_chain/pallas_call | solution.py:175
  16.4 18.2 %all-to-all-done.in_ref = f32[16,2,2,16,256]{4,3,2,1,0:T(8,128)S(1)} async-done(((f32[16,2,2,16,256]{4,3,2,1,0:T(8,128)}), f32[16,2,2,16,256]{4,3,2,1,0:T(8,128)S(1)}, u32[]{:S(2)}, u32[]{:S(2)}) %all-to-all-start) | async-done | bytes 1048608 | tf_op jit(solution)/shard_map/all_to_all | solution.py:158
  34.6 0.0 copy-done
  34.6 0.0 copy-start.1
  34.6 1.0 %copy-done.1 = f32[2,256,256]{2,1,0:T(8,128)S(1)} copy-done((f32[2,256,256]{2,1,0:T(8,128)S(1)}, f32[2,256,256]{2,1,0:T(8,128)}, u32[]{:S(2)}) %copy-start.1) | copy-done | bytes 524312
  35.6 2.2 %middle_high_low.1 = f32[16,2,2,16,256]{4,3,2,1,0:T(8,128)S(1)} custom-call(f32[16,2,2,16,256]{4,3,2,1,0:T(8,128)S(1)} %all-to-all-done.in_ref, f32[3,2,256,256]{3,2,1,0:T(8,128)S(1)} %copy-done, f32[2,256,256]{2,1,0:T(8,128)S(1)} %copy-done.1), custom_call_target="tpu_custom_call" | custom-call | tf_op jit(solution)/shard_map/middle_high_low/pallas_call | solution.py:187
  37.9 31.5 %all_to_all.10.in_ref = f32[16,2,2,16,256]{4,3,2,1,0:T(8,128)S(1)} all-to-all(f32[16,2,2,16,256]{4,3,2,1,0:T(8,128)S(1)} %middle_high_low.1), channel_id=1, replica_groups=mesh['groups'=2,'stem'=16] {'stem'}, dimensions={0} | all-to-all | bytes 2097152 | tf_op jit(solution)/shard_map/all_to_all | solution.py:158
  69.4 2.2 %close_high.1 = f32[2,1024,128]{2,1,0:T(8,128)} custom-call(f32[16,2,2,16,256]{4,3,2,1,0:T(8,128)S(1)} %all_to_all.10.in_ref, f32[3,2,256,256]{3,2,1,0:T(8,128)S(1)} %copy-done), custom_call_target="tpu_custom_call" | custom-call | tf_op jit(solution)/shard_map/close_high/pallas_call | solution.py:200
Async XLA Ops:
  4.1 30.5 %copy-start = (f32[3,2,256,256]{3,2,1,0:T(8,128)S(1)}, f32[3,2,256,256]{3,2,1,0:T(8,128)}, u32[]{:S(2)}) copy-start(f32[3,2,256,256]{3,2,1,0:T(8,128)} %high_ref.5) | copy-start | bytes 4718596
  4.1 30.5 %all-to-all-start = ((f32[16,2,2,16,256]{4,3,2,1,0:T(8,128)}), f32[16,2,2,16,256]{4,3,2,1,0:T(8,128)S(1)}, u32[]{:S(2)}, u32[]{:S(2)}) async-start(f32[16,2,2,16,256]{4,3,2,1,0:T(8,128)} %open_high.1), calls=%async_computation | async-start | bytes 2097152 | tf_op jit(solution)/shard_map/all_to_all | solution.py:158
  34.6 1.0 %copy-start.1 = (f32[2,256,256]{2,1,0:T(8,128)S(1)}, f32[2,256,256]{2,1,0:T(8,128)}, u32[]{:S(2)}) copy-start(f32[2,256,256]{2,1,0:T(8,128)} %low_chain.1.low_ref) | copy-start | bytes 1572868

commit v3 on v2

--- a/solution.py
+++ b/solution.py
@@ -1,3 +1,5 @@
+import functools
+
 import jax
 import jax.numpy as jnp
 from jax import lax
@@ -138,6 +140,187 @@
         copy.wait()
 
 
+def upper_order(width):
+    return [0] + sorted(range(1, width), key=lambda t: (t.bit_count(), -t))
+
+
+def lower_order(width):
+    return [0] + sorted(range(1, width), key=lambda t: (-t.bit_length(), t))
+
+
+def distances(lists, first_is_upper):
+    width = len(lists)
+    orders = upper_order(width), lower_order(width)
+    outer, inner = orders if first_is_upper else orders[::-1]
+    for n, ref in zip(outer, lists):
+        for at, m in enumerate(inner):
+            yield ref, at, (n * width + m if first_is_upper else m * width + n)
+
+
+def rows_by_distance(table, me, under):
+    devices = table.shape[1] // under
+    starts = [pl.multiple_of((me ^ d) * under, under) for d in range(devices)]
+    return [jnp.concatenate([table[c, pl.ds(at, under), :] for at in starts]) for c in range(2)]
+
+
+def gather(in_refs, held, me, first_is_upper):
+    under = in_refs[0].shape[2]
+    for ref, m, distance in distances(in_refs, first_is_upper):
+        at = pl.ds(pl.multiple_of((me ^ distance) * under, under), under)
+        for c in range(2):
+            held[c, at, :] = ref[m, c]
+    return halves(jnp.concatenate([held[0], held[1]], axis=0))
+
+
+def open_chunk_kernel(r, upper, me_ref, stem_ref, high_ref, *refs):
+    *out_refs, stem, table, sems = refs
+    under = out_refs[0].shape[2]
+    stem_copy = pltpu.make_async_copy(stem_ref.at[r], stem, sems.at[0])
+    table_copy = pltpu.make_async_copy(high_ref.at[0], table, sems.at[1])
+    table_copy.start()
+    stem_copy.start()
+    table_copy.wait()
+    high = table.shape[-1]
+    matrix = halves(left_block(*rows_by_distance(table, me_ref[0], under)))
+    stem_copy.wait()
+    value = dot_halves(matrix, halves(read_stem(stem, high)))
+    for ref, m, distance in distances(out_refs, upper):
+        for c in range(2):
+            start = c * high + distance * under
+            ref[m, c] = value[start : start + under]
+
+
+def turn_kernel(*refs):
+    half = len(refs) // 2
+    for n, in_ref in enumerate(refs[:half]):
+        for m, out_ref in enumerate(refs[half:]):
+            out_ref[n] = in_ref[m]
+
+
+def middle_chunk_kernel(in_upper, out_upper, me_ref, high_ref, low_ref, *refs):
+    *blocks, held, high_table, low_table, sems = refs
+    in_refs, out_refs = blocks[: len(blocks) // 2], blocks[len(blocks) // 2 :]
+    _, _, under, low = in_refs[0].shape
+    high = high_table.shape[-1]
+    high_copy = pltpu.make_async_copy(high_ref.at[1], high_table, sems.at[0])
+    low_copy = pltpu.make_async_copy(low_ref, low_table, sems.at[1])
+    high_copy.start()
+    low_copy.start()
+    value = gather(in_refs, held, me_ref[0], in_upper)
+    high_copy.wait()
+    matrix = halves(left_block(*rows_by_distance(high_table, me_ref[0], under)))
+    value = dot_halves(matrix, value)
+    value = jnp.concatenate([value[:high], value[high:]], axis=1)
+    low_copy.wait()
+    value = dot_halves(halves(value), halves(right_block(low_table[0], low_table[1])))
+    for ref, m, distance in distances(out_refs, out_upper):
+        for c in range(2):
+            ref[m, c] = value[distance * under : (distance + 1) * under, c * low : (c + 1) * low]
+
+
+def close_chunk_kernel(r, upper, width, me_ref, high_ref, *refs):
+    in_refs = refs[:width]
+    out_ref, held, stem, table, sems = refs[-5:]
+    table_copy = pltpu.make_async_copy(high_ref.at[2], table, sems.at[0])
+    table_copy.start()
+    value = gather(in_refs, held, me_ref[0], upper)
+    table_copy.wait()
+    matrix = halves(left_block(table[0], table[1]))
+    write_stem(stem, dot_halves(matrix, value), table.shape[-1])
+    copy = pltpu.make_async_copy(stem, out_ref.at[r], sems.at[1])
+    copy.start()
+    copy.wait()
+
+
+def chunks_by_permutes(laid, chain, hi_table):
+    devices = lax.axis_size("stem")
+    width = 1 << ((devices.bit_length() - 1) // 2)
+    spare, rows, _ = laid.shape
+    high, low = hi_table.shape[-1], chain.shape[-1]
+    under = high // devices
+    me = lax.axis_index("stem").reshape(1)
+    block = jax.ShapeDtypeStruct((width, 2, under, low), jnp.float32)
+    blocks = (block,) * width
+    held = pltpu.VMEM((2, high, low), jnp.float32)
+    table = pltpu.VMEM((2, high, high), jnp.float32)
+    stem = pltpu.VMEM((rows, LANES), jnp.float32)
+    sems = pltpu.SemaphoreType.DMA((2,))
+
+    def tie(values, after):
+        return lax.optimization_barrier((values, after))[0]
+
+    def send(values, upper, late=None):
+        step, order = (width, upper_order(width)) if upper else (1, lower_order(width))
+        if late is not None:
+            values = [*values[:-1], tie(values[-1], late)]
+        return [values[0]] + [
+            lax.ppermute(value, "stem", [(i, i ^ (t * step)) for i in range(devices)])
+            for value, t in zip(values[1:], order[1:])
+        ]
+
+    def turn(values, name):
+        return pl.pallas_call(
+            turn_kernel,
+            out_shape=blocks,
+            in_specs=[VMEM] * width,
+            out_specs=(VMEM,) * width,
+            compiler_params=SMALL,
+            name=name,
+        )(*values)
+
+    def open_chunk(r, upper, laid):
+        return pl.pallas_call(
+            functools.partial(open_chunk_kernel, r, upper),
+            out_shape=blocks,
+            in_specs=[SMEM, HBM, HBM],
+            out_specs=(VMEM,) * width,
+            scratch_shapes=[stem, table, sems],
+            compiler_params=SMALL,
+            name=f"open_{r}",
+        )(me, laid, hi_table)
+
+    def middle_chunk(r, in_upper, out_upper, values):
+        return pl.pallas_call(
+            functools.partial(middle_chunk_kernel, in_upper, out_upper),
+            out_shape=blocks,
+            in_specs=[SMEM, HBM, HBM] + [VMEM] * width,
+            out_specs=(VMEM,) * width,
+            scratch_shapes=[held, table, pltpu.VMEM(chain.shape, jnp.float32), sems],
+            compiler_params=SMALL,
+            name=f"middle_{r}",
+        )(me, hi_table, chain, *values)
+
+    def close_chunk(r, upper, values, done=None):
+        return pl.pallas_call(
+            functools.partial(close_chunk_kernel, r, upper, width),
+            out_shape=jax.ShapeDtypeStruct(laid.shape, jnp.float32),
+            in_specs=[SMEM, HBM] + [VMEM] * width + ([] if done is None else [HBM]),
+            out_specs=HBM,
+            scratch_shapes=[held, stem, table, sems],
+            input_output_aliases={} if done is None else {2 + width: 0},
+            compiler_params=SMALL,
+            name=f"close_{r}",
+        )(me, hi_table, *values, *([] if done is None else [done]))
+
+    opened = open_chunk(0, True, laid)
+    ahead = send(opened, True)
+    behind = send(open_chunk(1, False, tie(laid, opened[0])), False, None)
+    behind = turn(behind, "turn_1")
+    behind = send(behind, True)
+    ahead = turn(ahead, "turn_0")
+    ahead = send(ahead, False, None)
+    ahead = middle_chunk(0, False, True, ahead)
+    ahead = send(ahead, True)
+    behind = middle_chunk(1, True, False, behind)
+    behind = send(behind, False, None)
+    behind = turn(behind, "back_1")
+    behind = send(behind, True)
+    ahead = turn(ahead, "back_0")
+    ahead = send(ahead, False, None)
+    done = close_chunk(0, False, ahead)
+    return close_chunk(1, True, behind, done)
+
+
 def one_slice(stem, bits, lo_table, hi_table):
     leading = lax.axis_size("stem")
     segments, _, high, _ = hi_table.shape
@@ -162,6 +345,21 @@
 
     laid = stem.reshape(2, stem.shape[1] // LANES, LANES).transpose(1, 0, 2)
     laid = laid.reshape(stem_type.shape)
+    chain = pl.pallas_call(
+        chain_kernel,
+        out_shape=jax.ShapeDtypeStruct((2, low, low), jnp.float32),
+        in_specs=[SMEM, HBM],
+        out_specs=VMEM,
+        scratch_shapes=[
+            pltpu.VMEM((segments, 2, low, low), jnp.float32),
+            pltpu.SemaphoreType.DMA((segments,)),
+        ],
+        compiler_params=SMALL,
+        name="low_chain",
+    )(bits, lo_table)
+    if direct and spare == 2 and 1 << (2 * ((leading.bit_length() - 1) // 2)) == leading:
+        closed = chunks_by_permutes(laid, chain, hi_table)
+        return closed.reshape(-1, 2, LANES).transpose(1, 0, 2).reshape(stem.shape)
     table_scratch = pltpu.VMEM((2, high, high), jnp.float32)
     opened = pl.pallas_call(
         open_kernel,
@@ -172,18 +370,6 @@
         compiler_params=LARGE,
         name="open_high",
     )(laid, hi_table)
-    chain = pl.pallas_call(
-        chain_kernel,
-        out_shape=jax.ShapeDtypeStruct((2, low, low), jnp.float32),
-        in_specs=[SMEM, HBM],
-        out_specs=VMEM,
-        scratch_shapes=[
-            pltpu.VMEM((segments, 2, low, low), jnp.float32),
-            pltpu.SemaphoreType.DMA((segments,)),
-        ],
-        compiler_params=LARGE,
-        name="low_chain",
-    )(bits, lo_table)
     middle = pl.pallas_call(
         middle_kernel,
         out_shape=split_type,

time: 72.2 us -> 65.1 us (0.902)
  blocking collectives: 31.5 us -> 0 us
  starting transfers between devices: 7.5 us -> 32.5 us
  Pallas kernels: 13.3 us -> 11.7 us
  local copies, waits for them, and re-layouts: 1.05 us -> 2.64 us
    ppermute x0 -> x24, starting transfers between devices: none -> 32.5 us  [send(): lax.ppermute(value, 'stem', [(i, i ^ t * step) for i in range(devices)])]
    all_to_all x1 -> x0, blocking collectives: 31.5 us -> none  [exchange(): lax.all_to_all(values, 'stem', split_axis=0, concat_axis=0, tiled=True)]
    all_to_all x1 -> x0, waiting for transfers between devices: 18.2 us -> none  [exchange(): lax.all_to_all(values, 'stem', split_axis=0, concat_axis=0, tiled=True)]
    ppermute x0 -> x24, waiting for transfers between devices: none -> 18 us  [send(): lax.ppermute(value, 'stem', [(i, i ^ t * step) for i in range(devices)])]
    all_to_all x1 -> x0, starting transfers between devices: 7.5 us -> none  [exchange(): lax.all_to_all(values, 'stem', split_axis=0, concat_axis=0, tiled=True)]
    pallas_call x1, Pallas kernels: 4.73 us -> 2.58 us  [one_slice(): pl.pallas_call(chain_kernel, out_shape=jax.ShapeDtypeStruct((2, low, low)...]
    unnamed x4 -> x10, local copies, waits for them, and re-layouts: 1.05 us -> 2.64 us
    pallas_call x3 -> x10, Pallas kernels: 8.53 us -> 9.09 us  [the longest x2 4.24 us: middle_chunk(): pl.pallas_call(functools.partial(middle_chunk_kernel, in_upper, out_upper...]
  transfers between devices with their start and end apart: 1 -> 24, of which waited for: 1 -> 6; matrix products, arithmetic and copies ran while one was open for 0% -> 0% of each run, Pallas kernels for 7% -> 14%
where the time goes in v3:
time: 65.1 us; the launch traced here: 65 us
  starting transfers between devices  32.5 us (50%)
  waiting for transfers between devices  18 us (28%)
  Pallas kernels  11.7 us (18%)
  local copies, waits for them, and re-layouts  2.64 us (4%)
    ppermute x24, starting transfers between devices, send(): lax.ppermute(value, 'stem', [(i, i ^ t * step) for i in range(devices)])  32.5 us
    ppermute x24, waiting for transfers between devices, send(): lax.ppermute(value, 'stem', [(i, i ^ t * step) for i in range(devices)])  18 us
    pallas_call x2, Pallas kernels, middle_chunk(): pl.pallas_call(functools.partial(middle_chunk_kernel, in_upper, out_upper...  4.24 us
    pallas_call x2, Pallas kernels, close_chunk(): pl.pallas_call(functools.partial(close_chunk_kernel, r, upper, width), ou...  3.07 us
    unnamed x10, local copies, waits for them, and re-layouts  2.64 us
    pallas_call x1, Pallas kernels, one_slice(): pl.pallas_call(chain_kernel, out_shape=jax.ShapeDtypeStruct((2, low, low)...  2.58 us
    pallas_call x2, Pallas kernels, open_chunk(): pl.pallas_call(functools.partial(open_chunk_kernel, r, upper), out_shape=...  1.64 us
  transfers between devices with their start and end apart: 24, of which 6 were waited for; matrix products, arithmetic and copies ran while one was open for 0% of the time, Pallas kernels for 14%

profile of v3, /device:TPU:0, one launch (start us, length us, event | category | flops | bytes accessed | tf_op | source)
XLA Modules:
  0.0 65.0 jit_solution(12433995063023866747)
XLA Ops:
  0.0 0.0 copy-start
  0.0 1.4 %copy-done = f32[3,2,256,256]{3,2,1,0:T(8,128)S(1)} copy-done((f32[3,2,256,256]{3,2,1,0:T(8,128)S(1)}, f32[3,2,256,256]{3,2,1,0:T(8,128)}, u32[]{:S(2)}) %copy-start) | copy-done | bytes 1572888
  1.4 0.0 copy-start.2
  1.4 1.2 %copy-done.2 = f32[1,2,131072]{2,1,0:T(2,128)S(1)} copy-done((f32[1,2,131072]{2,1,0:T(2,128)S(1)}, f32[1,2,131072]{2,1,0:T(2,128)}, u32[]{:S(2)}) %copy-start.2) | copy-done | bytes 1048600
  2.6 0.0 copy-start.3
  2.6 0.0 copy-start.4
  2.6 0.8 %open_0.1 = (f32[4,2,16,256]{3,2,1,0:T(8,128)S(1)}, f32[4,2,16,256]{3,2,1,0:T(8,128)S(1)}, f32[4,2,16,256]{3,2,1,0:T(8,128)S(1)}, f32[4,2,16,256]{3,2,1,0:T(8,128)S(1)}) custom-call(s32[1]{0:T(128)} %bitcast.me_ref, f32[2,1024,128]{2,1,0:T(8,128)S(1)} %bitcast.11, f32[3,2,256,256]{3,2,1,0:T(8,128)S(1)} %copy-done), custom_call_target="tpu_custom_call" | custom-call | tf_op jit(solution)/shard_map/open_0/pallas_call | solution.py:272
  3.5 4.1 %collective-permute-start.12 = (f32[4,2,16,256]{3,2,1,0:T(8,128)S(1)}, f32[4,2,16,256]{3,2,1,0:T(8,128)S(1)}, u32[]{:S(2)}, u32[]{:S(2)}) collective-permute-start(f32[4,2,16,256]{3,2,1,0:T(8,128)S(1)} %get-tuple-element.56), channel_id=1, source_target_pairs={{0,8},{1,9},{2,10},{3,11},{4,12},{5,13},{6,14},{7,15},{8,0},{9,1},... | collective-permute-start | bytes 393224 | tf_op jit(solution)/shard_map/ppermute | solution.py:257
  7.6 1.6 %collective-permute-start.13 = (f32[4,2,16,256]{3,2,1,0:T(8,128)S(1)}, f32[4,2,16,256]{3,2,1,0:T(8,128)S(1)}, u32[]{:S(2)}, u32[]{:S(2)}) collective-permute-start(f32[4,2,16,256]{3,2,1,0:T(8,128)S(1)} %get-tuple-element.57), channel_id=1, source_target_pairs={{0,4},{1,5},{2,6},{3,7},{4,0},{5,1},{6,2},{7,3},{8,12},{9,13},{10,... | collective-permute-start | bytes 393224 | tf_op jit(solution)/shard_map/ppermute | solution.py:257
  9.1 0.0 collective-permute-start.14
  9.1 0.8 %open_1.1 = (f32[4,2,16,256]{3,2,1,0:T(8,128)S(1)}, f32[4,2,16,256]{3,2,1,0:T(8,128)S(1)}, f32[4,2,16,256]{3,2,1,0:T(8,128)S(1)}, f32[4,2,16,256]{3,2,1,0:T(8,128)S(1)}) custom-call(s32[1]{0:T(128)} %bitcast.me_ref, f32[2,1024,128]{2,1,0:T(8,128)S(1)} %bitcast.12, f32[3,2,256,256]{3,2,1,0:T(8,128)S(1)} %copy-done), custom_call_target="tpu_custom_call" | custom-call | tf_op jit(solution)/shard_map/open_1/pallas_call | solution.py:272
  10.0 1.8 %collective-permute-start = (f32[4,2,16,256]{3,2,1,0:T(8,128)S(1)}, f32[4,2,16,256]{3,2,1,0:T(8,128)S(1)}, u32[]{:S(2)}, u32[]{:S(2)}) collective-permute-start(f32[4,2,16,256]{3,2,1,0:T(8,128)S(1)} %get-tuple-element.41), channel_id=1, source_target_pairs={{0,2},{1,3},{2,0},{3,1},{4,6},{5,7},{6,4},{7,5},{8,10},{9,11},{10,... | collective-permute-start | bytes 393224 | tf_op jit(solution)/shard_map/ppermute | solution.py:257
  11.7 0.0 collective-permute-start.1
  11.8 3.8 %collective-permute-done.12.refs_1_ = f32[4,2,16,256]{3,2,1,0:T(8,128)S(1)} collective-permute-done((f32[4,2,16,256]{3,2,1,0:T(8,128)S(1)}, f32[4,2,16,256]{3,2,1,0:T(8,128)S(1)}, u32[]{:S(2)}, u32[]{:S(2)}) %collective-permute-start.12) | collective-permute-done | bytes 131104 | tf_op jit(solution)/shard_map/ppermute | solution.py:257
  15.5 0.0 collective-permute-start.2
  15.5 0.0 collective-permute-done.13.refs_2_
  15.5 2.4 %collective-permute-done.14.refs_3_ = f32[4,2,16,256]{3,2,1,0:T(8,128)S(1)} collective-permute-done((f32[4,2,16,256]{3,2,1,0:T(8,128)S(1)}, f32[4,2,16,256]{3,2,1,0:T(8,128)S(1)}, u32[]{:S(2)}, u32[]{:S(2)}) %collective-permute-start.14) | collective-permute-done | bytes 131104 | tf_op jit(solution)/shard_map/ppermute | solution.py:257
  17.9 1.6 %collective-permute-start.15 = (f32[4,2,16,256]{3,2,1,0:T(8,128)S(1)}, f32[4,2,16,256]{3,2,1,0:T(8,128)S(1)}, u32[]{:S(2)}, u32[]{:S(2)}) collective-permute-start(f32[4,2,16,256]{3,2,1,0:T(8,128)S(1)} %get-tuple-element.60), channel_id=1, source_target_pairs={{0,2},{1,3},{2,0},{3,1},{4,6},{5,7},{6,4},{7,5},{8,10},{9,11},{10,... | collective-permute-start | bytes 393224 | tf_op jit(solution)/shard_map/ppermute | solution.py:257
  19.5 0.0 collective-permute-start.16
  19.5 0.0 collective-permute-done.refs_1_
  19.5 0.6 collective-permute-start.17
  20.1 0.0 collective-permute-done.1.refs_2_
  20.1 0.0 collective-permute-done.2.refs_3_
  20.2 4.3 %collective-permute-start.3 = (f32[4,2,16,256]{3,2,1,0:T(8,128)S(1)}, f32[4,2,16,256]{3,2,1,0:T(8,128)S(1)}, u32[]{:S(2)}, u32[]{:S(2)}) collective-permute-start(f32[4,2,16,256]{3,2,1,0:T(8,128)S(1)} %get-tuple-element.45), channel_id=1, source_target_pairs={{0,8},{1,9},{2,10},{3,11},{4,12},{5,13},{6,14},{7,15},{8,0},{9,1},... | collective-permute-start | bytes 393224 | tf_op jit(solution)/shard_map/ppermute | solution.py:257
  24.5 0.0 collective-permute-start.4
  24.5 0.0 collective-permute-done.15.refs_1_
  24.5 1.5 %collective-permute-start.5 = (f32[4,2,16,256]{3,2,1,0:T(8,128)S(1)}, f32[4,2,16,256]{3,2,1,0:T(8,128)S(1)}, u32[]{:S(2)}, u32[]{:S(2)}) collective-permute-start(f32[4,2,16,256]{3,2,1,0:T(8,128)S(1)} %get-tuple-element.47), channel_id=1, source_target_pairs={{0,12},{1,13},{2,14},{3,15},{4,8},{5,9},{6,10},{7,11},{8,4},{9,5},... | collective-permute-start | bytes 393224 | tf_op jit(solution)/shard_map/ppermute | solution.py:257
  26.0 0.0 copy-done.3
  26.0 0.0 copy-done.4
  26.0 2.6 %low_chain.1.low_ref = f32[2,256,256]{2,1,0:T(8,128)S(1)} custom-call(s32[1,3]{1,0:T(1,128)S(1)} %copy-done.4, f32[3,2,2,256,256]{4,3,2,1,0:T(8,128)S(1)} %copy-done.3), custom_call_target="tpu_custom_call" | custom-call | tf_op jit(solution)/shard_map/low_chain/pallas_call | solution.py:348
  28.6 0.0 collective-permute-done.16.refs_2_
  28.6 0.0 collective-permute-done.17.refs_3_
  28.7 0.0 copy-done.1
  28.7 2.1 %middle_0.1 = (f32[4,2,16,256]{3,2,1,0:T(8,128)S(1)}, f32[4,2,16,256]{3,2,1,0:T(8,128)S(1)}, f32[4,2,16,256]{3,2,1,0:T(8,128)S(1)}, f32[4,2,16,256]{3,2,1,0:T(8,128)S(1)}) custom-call(s32[1]{0:T(128)} %bitcast.me_ref, f32[3,2,256,256]{3,2,1,0:T(8,128)S(1)} %copy-done.1, f32[2,256,256]{2,1,0:T(8,128)S(1)} %low_chain.1.low_ref, ...), custom_call_target="tpu_custom_call" | custom-call | tf_op jit(solution)/shard_map/middle_0/pallas_call | solution.py:283
  30.8 2.6 %collective-permute-start.18 = (f32[4,2,16,256]{3,2,1,0:T(8,128)S(1)}, f32[4,2,16,256]{3,2,1,0:T(8,128)S(1)}, u32[]{:S(2)}, u32[]{:S(2)}) collective-permute-start(f32[4,2,16,256]{3,2,1,0:T(8,128)S(1)} %get-tuple-element.64), channel_id=1, source_target_pairs={{0,8},{1,9},{2,10},{3,11},{4,12},{5,13},{6,14},{7,15},{8,0},{9,1},... | collective-permute-start | bytes 393224 | tf_op jit(solution)/shard_map/ppermute | solution.py:257
  33.4 0.6 collective-permute-start.19
  34.1 0.0 collective-permute-done.3.refs_1_
  34.1 2.3 %collective-permute-start.20 = (f32[4,2,16,256]{3,2,1,0:T(8,128)S(1)}, f32[4,2,16,256]{3,2,1,0:T(8,128)S(1)}, u32[]{:S(2)}, u32[]{:S(2)}) collective-permute-start(f32[4,2,16,256]{3,2,1,0:T(8,128)S(1)} %get-tuple-element.66), channel_id=1, source_target_pairs={{0,12},{1,13},{2,14},{3,15},{4,8},{5,9},{6,10},{7,11},{8,4},{9,5},... | collective-permute-start | bytes 393224 | tf_op jit(solution)/shard_map/ppermute | solution.py:257
  36.4 0.0 collective-permute-done.4.refs_2_
  36.4 0.0 collective-permute-done.5.refs_3_
  36.4 2.1 %middle_1.1 = (f32[4,2,16,256]{3,2,1,0:T(8,128)S(1)}, f32[4,2,16,256]{3,2,1,0:T(8,128)S(1)}, f32[4,2,16,256]{3,2,1,0:T(8,128)S(1)}, f32[4,2,16,256]{3,2,1,0:T(8,128)S(1)}) custom-call(s32[1]{0:T(128)} %bitcast.me_ref, f32[3,2,256,256]{3,2,1,0:T(8,128)S(1)} %copy-done.1, f32[2,256,256]{2,1,0:T(8,128)S(1)} %low_chain.1.low_ref, ...), custom_call_target="tpu_custom_call" | custom-call | tf_op jit(solution)/shard_map/middle_1/pallas_call | solution.py:283
  38.5 1.5 %collective-permute-start.6 = (f32[4,2,16,256]{3,2,1,0:T(8,128)S(1)}, f32[4,2,16,256]{3,2,1,0:T(8,128)S(1)}, u32[]{:S(2)}, u32[]{:S(2)}) collective-permute-start(f32[4,2,16,256]{3,2,1,0:T(8,128)S(1)} %get-tuple-element.49), channel_id=1, source_target_pairs={{0,2},{1,3},{2,0},{3,1},{4,6},{5,7},{6,4},{7,5},{8,10},{9,11},{10,... | collective-permute-start | bytes 393224 | tf_op jit(solution)/shard_map/ppermute | solution.py:257
  40.0 0.0 collective-permute-start.7
  40.0 5.3 %collective-permute-done.18.refs_1_ = f32[4,2,16,256]{3,2,1,0:T(8,128)S(1)} collective-permute-done((f32[4,2,16,256]{3,2,1,0:T(8,128)S(1)}, f32[4,2,16,256]{3,2,1,0:T(8,128)S(1)}, u32[]{:S(2)}, u32[]{:S(2)}) %collective-permute-start.18) | collective-permute-done | bytes 131104 | tf_op jit(solution)/shard_map/ppermute | solution.py:257
  45.3 0.0 collective-permute-start.8
  45.3 0.0 collective-permute-done.19.refs_2_
  45.3 0.0 collective-permute-done.20.refs_3_
  45.4 1.6 %collective-permute-start.21 = (f32[4,2,16,256]{3,2,1,0:T(8,128)S(1)}, f32[4,2,16,256]{3,2,1,0:T(8,128)S(1)}, u32[]{:S(2)}, u32[]{:S(2)}) collective-permute-start(f32[4,2,16,256]{3,2,1,0:T(8,128)S(1)} %get-tuple-element.68), channel_id=1, source_target_pairs={{0,2},{1,3},{2,0},{3,1},{4,6},{5,7},{6,4},{7,5},{8,10},{9,11},{10,... | collective-permute-start | bytes 393224 | tf_op jit(solution)/shard_map/ppermute | solution.py:257
  46.9 0.0 collective-permute-done.6.refs_1_
  46.9 0.0 collective-permute-done.7.refs_2_
  46.9 0.0 collective-permute-done.8.refs_3_
  47.0 3.1 %collective-permute-start.9 = (f32[4,2,16,256]{3,2,1,0:T(8,128)S(1)}, f32[4,2,16,256]{3,2,1,0:T(8,128)S(1)}, u32[]{:S(2)}, u32[]{:S(2)}) collective-permute-start(f32[4,2,16,256]{3,2,1,0:T(8,128)S(1)} %get-tuple-element.53), channel_id=1, source_target_pairs={{0,8},{1,9},{2,10},{3,11},{4,12},{5,13},{6,14},{7,15},{8,0},{9,1},... | collective-permute-start | bytes 393224 | tf_op jit(solution)/shard_map/ppermute | solution.py:257
  50.1 1.1 %collective-permute-start.22 = (f32[4,2,16,256]{3,2,1,0:T(8,128)S(1)}, f32[4,2,16,256]{3,2,1,0:T(8,128)S(1)}, u32[]{:S(2)}, u32[]{:S(2)}) collective-permute-start(f32[4,2,16,256]{3,2,1,0:T(8,128)S(1)} %get-tuple-element.69), channel_id=1, source_target_pairs={{0,3},{1,2},{2,1},{3,0},{4,7},{5,6},{6,5},{7,4},{8,11},{9,10},{10,... | collective-permute-start | bytes 393224 | tf_op jit(solution)/shard_map/ppermute | solution.py:257
  51.2 0.0 collective-permute-start.23
  51.2 2.1 %collective-permute-start.10 = (f32[4,2,16,256]{3,2,1,0:T(8,128)S(1)}, f32[4,2,16,256]{3,2,1,0:T(8,128)S(1)}, u32[]{:S(2)}, u32[]{:S(2)}) collective-permute-start(f32[4,2,16,256]{3,2,1,0:T(8,128)S(1)} %get-tuple-element.54), channel_id=1, source_target_pairs={{0,4},{1,5},{2,6},{3,7},{4,0},{5,1},{6,2},{7,3},{8,12},{9,13},{10,... | collective-permute-start | bytes 393224 | tf_op jit(solution)/shard_map/ppermute | solution.py:257
  53.2 0.0 collective-permute-done.21.refs_1_
  53.2 2.1 %collective-permute-start.11 = (f32[4,2,16,256]{3,2,1,0:T(8,128)S(1)}, f32[4,2,16,256]{3,2,1,0:T(8,128)S(1)}, u32[]{:S(2)}, u32[]{:S(2)}) collective-permute-start(f32[4,2,16,256]{3,2,1,0:T(8,128)S(1)} %get-tuple-element.55), channel_id=1, source_target_pairs={{0,12},{1,13},{2,14},{3,15},{4,8},{5,9},{6,10},{7,11},{8,4},{9,5},... | collective-permute-start | bytes 393224 | tf_op jit(solution)/shard_map/ppermute | solution.py:257
  55.3 0.3 collective-permute-done.22.refs_2_
  55.7 0.0 collective-permute-done.23.refs_3_
  55.7 1.5 %close_0.1.refs_4_ = f32[2,1024,128]{2,1,0:T(8,128)} custom-call(s32[1]{0:T(128)} %bitcast.me_ref, f32[3,2,256,256]{3,2,1,0:T(8,128)S(1)} %copy-done.1, f32[4,2,16,256]{3,2,1,0:T(8,128)S(1)} %get-tuple-element.67.refs_0_, f32[4,2,16,256]{3,2,1,0:T(8,128)S(1)} %collective-permute-done.21.refs_1_, f32[4,2,16,256]{3,2,1,0:T(8,128)S(1)} %collective-permute-done.22.refs_2_, ...), custom_call_target="tpu_custom_call" | custom-call | tf_op jit(solution)/shard_map/close_0/pallas_call | solution.py:294
  57.2 0.0 collective-permute-done.9.refs_1_
  57.2 0.2 collective-permute-done.10.refs_2_
  57.4 6.0 %collective-permute-done.11.refs_3_ = f32[4,2,16,256]{3,2,1,0:T(8,128)S(1)} collective-permute-done((f32[4,2,16,256]{3,2,1,0:T(8,128)S(1)}, f32[4,2,16,256]{3,2,1,0:T(8,128)S(1)}, u32[]{:S(2)}, u32[]{:S(2)}) %collective-permute-start.11) | collective-permute-done | bytes 131104 | tf_op jit(solution)/shard_map/ppermute | solution.py:257
  63.4 1.5 %close_1.1 = f32[2,1024,128]{2,1,0:T(8,128)} custom-call(s32[1]{0:T(128)} %bitcast.me_ref, f32[3,2,256,256]{3,2,1,0:T(8,128)S(1)} %copy-done.1, f32[4,2,16,256]{3,2,1,0:T(8,128)S(1)} %get-tuple-element.52.refs_0_, f32[4,2,16,256]{3,2,1,0:T(8,128)S(1)} %collective-permute-done.9.refs_1_, ...), custom_call_target="tpu_custom_call", output_to_operand_aliasing={{}: (6, {})} | custom-call | tf_op jit(solution)/shard_map/close_1/pallas_call | solution.py:294
  (5 shorter events, 0.1 us)
Async XLA Ops:
  0.0 1.4 %copy-start = (f32[3,2,256,256]{3,2,1,0:T(8,128)S(1)}, f32[3,2,256,256]{3,2,1,0:T(8,128)}, u32[]{:S(2)}) copy-start(f32[3,2,256,256]{3,2,1,0:T(8,128)} %high_ref.11) | copy-start | bytes 4718596
  1.4 1.2 %copy-start.2 = (f32[1,2,131072]{2,1,0:T(2,128)S(1)}, f32[1,2,131072]{2,1,0:T(2,128)}, u32[]{:S(2)}) copy-start(f32[1,2,131072]{2,1,0:T(2,128)} %param.4) | copy-start | bytes 3145732
  2.6 23.4 %copy-start.3 = (f32[3,2,2,256,256]{4,3,2,1,0:T(8,128)S(1)}, f32[3,2,2,256,256]{4,3,2,1,0:T(8,128)}, u32[]{:S(2)}) copy-start(f32[3,2,2,256,256]{4,3,2,1,0:T(8,128)} %table_ref.1) | copy-start | bytes 9437188
  2.6 23.4 %copy-start.4 = (s32[1,3]{1,0:T(1,128)S(1)}, s32[1,3]{1,0:T(1,128)}, u32[]{:S(2)}) copy-start(s32[1,3]{1,0:T(1,128)} %bits_ref.1) | copy-start | bytes 40
  3.5 12.1 %collective-permute-start.12 = (f32[4,2,16,256]{3,2,1,0:T(8,128)S(1)}, f32[4,2,16,256]{3,2,1,0:T(8,128)S(1)}, u32[]{:S(2)}, u32[]{:S(2)}) collective-permute-start(f32[4,2,16,256]{3,2,1,0:T(8,128)S(1)} %get-tuple-element.56), channel_id=1, source_target_pairs={{0,8},{1,9},{2,10},{3,11},{4,12},{5,13},{6,14},{7,15},{8,0},{9,1},... | collective-permute-start | bytes 393224 | tf_op jit(solution)/shard_map/ppermute | solution.py:257
  7.6 8.0 %collective-permute-start.13 = (f32[4,2,16,256]{3,2,1,0:T(8,128)S(1)}, f32[4,2,16,256]{3,2,1,0:T(8,128)S(1)}, u32[]{:S(2)}, u32[]{:S(2)}) collective-permute-start(f32[4,2,16,256]{3,2,1,0:T(8,128)S(1)} %get-tuple-element.57), channel_id=1, source_target_pairs={{0,4},{1,5},{2,6},{3,7},{4,0},{5,1},{6,2},{7,3},{8,12},{9,13},{10,... | collective-permute-start | bytes 393224 | tf_op jit(solution)/shard_map/ppermute | solution.py:257
  9.1 8.8 %collective-permute-start.14 = (f32[4,2,16,256]{3,2,1,0:T(8,128)S(1)}, f32[4,2,16,256]{3,2,1,0:T(8,128)S(1)}, u32[]{:S(2)}, u32[]{:S(2)}) collective-permute-start(f32[4,2,16,256]{3,2,1,0:T(8,128)S(1)} %get-tuple-element.58), channel_id=1, source_target_pairs={{0,12},{1,13},{2,14},{3,15},{4,8},{5,9},{6,10},{7,11},{8,4},{9,5},... | collective-permute-start | bytes 393224 | tf_op jit(solution)/shard_map/ppermute | solution.py:257
  9.1 19.5 %copy-start.1 = (f32[3,2,256,256]{3,2,1,0:T(8,128)S(1)}, f32[3,2,256,256]{3,2,1,0:T(8,128)}, u32[]{:S(2)}) copy-start(f32[3,2,256,256]{3,2,1,0:T(8,128)} %high_ref.11) | copy-start | bytes 4718596
  10.0 9.5 %collective-permute-start = (f32[4,2,16,256]{3,2,1,0:T(8,128)S(1)}, f32[4,2,16,256]{3,2,1,0:T(8,128)S(1)}, u32[]{:S(2)}, u32[]{:S(2)}) collective-permute-start(f32[4,2,16,256]{3,2,1,0:T(8,128)S(1)} %get-tuple-element.41), channel_id=1, source_target_pairs={{0,2},{1,3},{2,0},{3,1},{4,6},{5,7},{6,4},{7,5},{8,10},{9,11},{10,... | collective-permute-start | bytes 393224 | tf_op jit(solution)/shard_map/ppermute | solution.py:257
  11.7 8.4 %collective-permute-start.1 = (f32[4,2,16,256]{3,2,1,0:T(8,128)S(1)}, f32[4,2,16,256]{3,2,1,0:T(8,128)S(1)}, u32[]{:S(2)}, u32[]{:S(2)}) collective-permute-start(f32[4,2,16,256]{3,2,1,0:T(8,128)S(1)} %get-tuple-element.42), channel_id=1, source_target_pairs={{0,3},{1,2},{2,1},{3,0},{4,7},{5,6},{6,5},{7,4},{8,11},{9,10},{10,... | collective-permute-start | bytes 393224 | tf_op jit(solution)/shard_map/ppermute | solution.py:257
  15.5 4.6 %collective-permute-start.2 = (f32[4,2,16,256]{3,2,1,0:T(8,128)S(1)}, f32[4,2,16,256]{3,2,1,0:T(8,128)S(1)}, u32[]{:S(2)}, u32[]{:S(2)}) collective-permute-start(f32[4,2,16,256]{3,2,1,0:T(8,128)S(1)} %get-tuple-element.43), channel_id=1, source_target_pairs={{0,1},{1,0},{2,3},{3,2},{4,5},{5,4},{6,7},{7,6},{8,9},{9,8},{10,11... | collective-permute-start | bytes 393224 | tf_op jit(solution)/shard_map/ppermute | solution.py:257
  17.9 6.6 %collective-permute-start.15 = (f32[4,2,16,256]{3,2,1,0:T(8,128)S(1)}, f32[4,2,16,256]{3,2,1,0:T(8,128)S(1)}, u32[]{:S(2)}, u32[]{:S(2)}) collective-permute-start(f32[4,2,16,256]{3,2,1,0:T(8,128)S(1)} %get-tuple-element.60), channel_id=1, source_target_pairs={{0,2},{1,3},{2,0},{3,1},{4,6},{5,7},{6,4},{7,5},{8,10},{9,11},{10,... | collective-permute-start | bytes 393224 | tf_op jit(solution)/shard_map/ppermute | solution.py:257
  19.5 9.1 %collective-permute-start.16 = (f32[4,2,16,256]{3,2,1,0:T(8,128)S(1)}, f32[4,2,16,256]{3,2,1,0:T(8,128)S(1)}, u32[]{:S(2)}, u32[]{:S(2)}) collective-permute-start(f32[4,2,16,256]{3,2,1,0:T(8,128)S(1)} %get-tuple-element.61), channel_id=1, source_target_pairs={{0,3},{1,2},{2,1},{3,0},{4,7},{5,6},{6,5},{7,4},{8,11},{9,10},{10,... | collective-permute-start | bytes 393224 | tf_op jit(solution)/shard_map/ppermute | solution.py:257
  19.5 9.1 %collective-permute-start.17 = (f32[4,2,16,256]{3,2,1,0:T(8,128)S(1)}, f32[4,2,16,256]{3,2,1,0:T(8,128)S(1)}, u32[]{:S(2)}, u32[]{:S(2)}) collective-permute-start(f32[4,2,16,256]{3,2,1,0:T(8,128)S(1)} %get-tuple-element.62), channel_id=1, source_target_pairs={{0,1},{1,0},{2,3},{3,2},{4,5},{5,4},{6,7},{7,6},{8,9},{9,8},{10,11... | collective-permute-start | bytes 393224 | tf_op jit(solution)/shard_map/ppermute | solution.py:257
  20.2 13.9 %collective-permute-start.3 = (f32[4,2,16,256]{3,2,1,0:T(8,128)S(1)}, f32[4,2,16,256]{3,2,1,0:T(8,128)S(1)}, u32[]{:S(2)}, u32[]{:S(2)}) collective-permute-start(f32[4,2,16,256]{3,2,1,0:T(8,128)S(1)} %get-tuple-element.45), channel_id=1, source_target_pairs={{0,8},{1,9},{2,10},{3,11},{4,12},{5,13},{6,14},{7,15},{8,0},{9,1},... | collective-permute-start | bytes 393224 | tf_op jit(solution)/shard_map/ppermute | solution.py:257
  24.5 11.9 %collective-permute-start.4 = (f32[4,2,16,256]{3,2,1,0:T(8,128)S(1)}, f32[4,2,16,256]{3,2,1,0:T(8,128)S(1)}, u32[]{:S(2)}, u32[]{:S(2)}) collective-permute-start(f32[4,2,16,256]{3,2,1,0:T(8,128)S(1)} %get-tuple-element.46), channel_id=1, source_target_pairs={{0,4},{1,5},{2,6},{3,7},{4,0},{5,1},{6,2},{7,3},{8,12},{9,13},{10,... | collective-permute-start | bytes 393224 | tf_op jit(solution)/shard_map/ppermute | solution.py:257
  24.5 11.9 %collective-permute-start.5 = (f32[4,2,16,256]{3,2,1,0:T(8,128)S(1)}, f32[4,2,16,256]{3,2,1,0:T(8,128)S(1)}, u32[]{:S(2)}, u32[]{:S(2)}) collective-permute-start(f32[4,2,16,256]{3,2,1,0:T(8,128)S(1)} %get-tuple-element.47), channel_id=1, source_target_pairs={{0,12},{1,13},{2,14},{3,15},{4,8},{5,9},{6,10},{7,11},{8,4},{9,5},... | collective-permute-start | bytes 393224 | tf_op jit(solution)/shard_map/ppermute | solution.py:257
  30.8 14.5 %collective-permute-start.18 = (f32[4,2,16,256]{3,2,1,0:T(8,128)S(1)}, f32[4,2,16,256]{3,2,1,0:T(8,128)S(1)}, u32[]{:S(2)}, u32[]{:S(2)}) collective-permute-start(f32[4,2,16,256]{3,2,1,0:T(8,128)S(1)} %get-tuple-element.64), channel_id=1, source_target_pairs={{0,8},{1,9},{2,10},{3,11},{4,12},{5,13},{6,14},{7,15},{8,0},{9,1},... | collective-permute-start | bytes 393224 | tf_op jit(solution)/shard_map/ppermute | solution.py:257
  33.4 11.9 %collective-permute-start.19 = (f32[4,2,16,256]{3,2,1,0:T(8,128)S(1)}, f32[4,2,16,256]{3,2,1,0:T(8,128)S(1)}, u32[]{:S(2)}, u32[]{:S(2)}) collective-permute-start(f32[4,2,16,256]{3,2,1,0:T(8,128)S(1)} %get-tuple-element.65), channel_id=1, source_target_pairs={{0,4},{1,5},{2,6},{3,7},{4,0},{5,1},{6,2},{7,3},{8,12},{9,13},{10,... | collective-permute-start | bytes 393224 | tf_op jit(solution)/shard_map/ppermute | solution.py:257
  34.1 11.2 %collective-permute-start.20 = (f32[4,2,16,256]{3,2,1,0:T(8,128)S(1)}, f32[4,2,16,256]{3,2,1,0:T(8,128)S(1)}, u32[]{:S(2)}, u32[]{:S(2)}) collective-permute-start(f32[4,2,16,256]{3,2,1,0:T(8,128)S(1)} %get-tuple-element.66), channel_id=1, source_target_pairs={{0,12},{1,13},{2,14},{3,15},{4,8},{5,9},{6,10},{7,11},{8,4},{9,5},... | collective-permute-start | bytes 393224 | tf_op jit(solution)/shard_map/ppermute | solution.py:257
  38.5 8.4 %collective-permute-start.6 = (f32[4,2,16,256]{3,2,1,0:T(8,128)S(1)}, f32[4,2,16,256]{3,2,1,0:T(8,128)S(1)}, u32[]{:S(2)}, u32[]{:S(2)}) collective-permute-start(f32[4,2,16,256]{3,2,1,0:T(8,128)S(1)} %get-tuple-element.49), channel_id=1, source_target_pairs={{0,2},{1,3},{2,0},{3,1},{4,6},{5,7},{6,4},{7,5},{8,10},{9,11},{10,... | collective-permute-start | bytes 393224 | tf_op jit(solution)/shard_map/ppermute | solution.py:257
  40.0 6.9 %collective-permute-start.7 = (f32[4,2,16,256]{3,2,1,0:T(8,128)S(1)}, f32[4,2,16,256]{3,2,1,0:T(8,128)S(1)}, u32[]{:S(2)}, u32[]{:S(2)}) collective-permute-start(f32[4,2,16,256]{3,2,1,0:T(8,128)S(1)} %get-tuple-element.50), channel_id=1, source_target_pairs={{0,3},{1,2},{2,1},{3,0},{4,7},{5,6},{6,5},{7,4},{8,11},{9,10},{10,... | collective-permute-start | bytes 393224 | tf_op jit(solution)/shard_map/ppermute | solution.py:257
  45.3 1.6 %collective-permute-start.8 = (f32[4,2,16,256]{3,2,1,0:T(8,128)S(1)}, f32[4,2,16,256]{3,2,1,0:T(8,128)S(1)}, u32[]{:S(2)}, u32[]{:S(2)}) collective-permute-start(f32[4,2,16,256]{3,2,1,0:T(8,128)S(1)} %get-tuple-element.51), channel_id=1, source_target_pairs={{0,1},{1,0},{2,3},{3,2},{4,5},{5,4},{6,7},{7,6},{8,9},{9,8},{10,11... | collective-permute-start | bytes 393224 | tf_op jit(solution)/shard_map/ppermute | solution.py:257
  45.4 7.9 %collective-permute-start.21 = (f32[4,2,16,256]{3,2,1,0:T(8,128)S(1)}, f32[4,2,16,256]{3,2,1,0:T(8,128)S(1)}, u32[]{:S(2)}, u32[]{:S(2)}) collective-permute-start(f32[4,2,16,256]{3,2,1,0:T(8,128)S(1)} %get-tuple-element.68), channel_id=1, source_target_pairs={{0,2},{1,3},{2,0},{3,1},{4,6},{5,7},{6,4},{7,5},{8,10},{9,11},{10,... | collective-permute-start | bytes 393224 | tf_op jit(solution)/shard_map/ppermute | solution.py:257
  47.0 10.2 %collective-permute-start.9 = (f32[4,2,16,256]{3,2,1,0:T(8,128)S(1)}, f32[4,2,16,256]{3,2,1,0:T(8,128)S(1)}, u32[]{:S(2)}, u32[]{:S(2)}) collective-permute-start(f32[4,2,16,256]{3,2,1,0:T(8,128)S(1)} %get-tuple-element.53), channel_id=1, source_target_pairs={{0,8},{1,9},{2,10},{3,11},{4,12},{5,13},{6,14},{7,15},{8,0},{9,1},... | collective-permute-start | bytes 393224 | tf_op jit(solution)/shard_map/ppermute | solution.py:257
  50.1 5.6 %collective-permute-start.22 = (f32[4,2,16,256]{3,2,1,0:T(8,128)S(1)}, f32[4,2,16,256]{3,2,1,0:T(8,128)S(1)}, u32[]{:S(2)}, u32[]{:S(2)}) collective-permute-start(f32[4,2,16,256]{3,2,1,0:T(8,128)S(1)} %get-tuple-element.69), channel_id=1, source_target_pairs={{0,3},{1,2},{2,1},{3,0},{4,7},{5,6},{6,5},{7,4},{8,11},{9,10},{10,... | collective-permute-start | bytes 393224 | tf_op jit(solution)/shard_map/ppermute | solution.py:257
  51.2 4.5 %collective-permute-start.23 = (f32[4,2,16,256]{3,2,1,0:T(8,128)S(1)}, f32[4,2,16,256]{3,2,1,0:T(8,128)S(1)}, u32[]{:S(2)}, u32[]{:S(2)}) collective-permute-start(f32[4,2,16,256]{3,2,1,0:T(8,128)S(1)} %get-tuple-element.70), channel_id=1, source_target_pairs={{0,1},{1,0},{2,3},{3,2},{4,5},{5,4},{6,7},{7,6},{8,9},{9,8},{10,11... | collective-permute-start | bytes 393224 | tf_op jit(solution)/shard_map/ppermute | solution.py:257
  51.2 6.2 %collective-permute-start.10 = (f32[4,2,16,256]{3,2,1,0:T(8,128)S(1)}, f32[4,2,16,256]{3,2,1,0:T(8,128)S(1)}, u32[]{:S(2)}, u32[]{:S(2)}) collective-permute-start(f32[4,2,16,256]{3,2,1,0:T(8,128)S(1)} %get-tuple-element.54), channel_id=1, source_target_pairs={{0,4},{1,5},{2,6},{3,7},{4,0},{5,1},{6,2},{7,3},{8,12},{9,13},{10,... | collective-permute-start | bytes 393224 | tf_op jit(solution)/shard_map/ppermute | solution.py:257
  53.2 10.2 %collective-permute-start.11 = (f32[4,2,16,256]{3,2,1,0:T(8,128)S(1)}, f32[4,2,16,256]{3,2,1,0:T(8,128)S(1)}, u32[]{:S(2)}, u32[]{:S(2)}) collective-permute-start(f32[4,2,16,256]{3,2,1,0:T(8,128)S(1)} %get-tuple-element.55), channel_id=1, source_target_pairs={{0,12},{1,13},{2,14},{3,15},{4,8},{5,9},{6,10},{7,11},{8,4},{9,5},... | collective-permute-start | bytes 393224 | tf_op jit(solution)/shard_map/ppermute | solution.py:257

commit v4 on v3

--- a/solution.py
+++ b/solution.py
@@ -80,19 +80,16 @@
             out_ref[:, r, c] = value[c * high : (c + 1) * high].reshape(leading, under, low)
 
 
-def chain_kernel(bits_ref, table_ref, out_ref, held, sems):
-    segments = held.shape[0]
-    copies = []
+def chain_kernel(bits_ref, table_ref, out_ref):
+    segments, _, _, low, _ = table_ref.shape
+    total = None
     for k in range(segments):
         entry = jnp.where(bits_ref[0, k] == 1, 1, 0)
-        copies.append(pltpu.make_async_copy(table_ref.at[k, entry], held.at[k], sems.at[k]))
-        copies[-1].start()
-    for copy in copies:
-        copy.wait()
-    low = held.shape[-1]
-    total = jnp.concatenate([held[0, 0], held[0, 1]], axis=0)
-    for k in range(1, segments):
-        total = dot_halves(halves(left_block(held[k, 0], held[k, 1])), halves(total))
+        parts = table_ref[k, entry, 0], table_ref[k, entry, 1]
+        if total is None:
+            total = jnp.concatenate(parts, axis=0)
+        else:
+            total = dot_halves(halves(left_block(*parts)), halves(total))
     for c in range(2):
         out_ref[c] = total[c * low : (c + 1) * low].T
 
@@ -141,11 +138,11 @@
 
 
 def upper_order(width):
-    return [0] + sorted(range(1, width), key=lambda t: (t.bit_count(), -t))
+    return [0, 1, 2, 3]
 
 
 def lower_order(width):
-    return [0] + sorted(range(1, width), key=lambda t: (-t.bit_length(), t))
+    return [0, 3, 1, 2]
 
 
 def distances(lists, first_is_upper):
@@ -172,18 +169,11 @@
     return halves(jnp.concatenate([held[0], held[1]], axis=0))
 
 
-def open_chunk_kernel(r, upper, me_ref, stem_ref, high_ref, *refs):
-    *out_refs, stem, table, sems = refs
+def open_chunk_kernel(upper, me_ref, stem_ref, table, *out_refs):
     under = out_refs[0].shape[2]
-    stem_copy = pltpu.make_async_copy(stem_ref.at[r], stem, sems.at[0])
-    table_copy = pltpu.make_async_copy(high_ref.at[0], table, sems.at[1])
-    table_copy.start()
-    stem_copy.start()
-    table_copy.wait()
     high = table.shape[-1]
     matrix = halves(left_block(*rows_by_distance(table, me_ref[0], under)))
-    stem_copy.wait()
-    value = dot_halves(matrix, halves(read_stem(stem, high)))
+    value = dot_halves(matrix, halves(read_stem(stem_ref, high)))
     for ref, m, distance in distances(out_refs, upper):
         for c in range(2):
             start = c * high + distance * under
@@ -197,37 +187,28 @@
             out_ref[n] = in_ref[m]
 
 
-def middle_chunk_kernel(in_upper, out_upper, me_ref, high_ref, low_ref, *refs):
-    *blocks, held, high_table, low_table, sems = refs
+def middle_chunk_kernel(in_upper, out_upper, me_ref, table, low_table, *refs):
+    *blocks, held = refs
     in_refs, out_refs = blocks[: len(blocks) // 2], blocks[len(blocks) // 2 :]
     _, _, under, low = in_refs[0].shape
-    high = high_table.shape[-1]
-    high_copy = pltpu.make_async_copy(high_ref.at[1], high_table, sems.at[0])
-    low_copy = pltpu.make_async_copy(low_ref, low_table, sems.at[1])
-    high_copy.start()
-    low_copy.start()
+    high = table.shape[-1]
     value = gather(in_refs, held, me_ref[0], in_upper)
-    high_copy.wait()
-    matrix = halves(left_block(*rows_by_distance(high_table, me_ref[0], under)))
+    matrix = halves(left_block(*rows_by_distance(table, me_ref[0], under)))
     value = dot_halves(matrix, value)
     value = jnp.concatenate([value[:high], value[high:]], axis=1)
-    low_copy.wait()
     value = dot_halves(halves(value), halves(right_block(low_table[0], low_table[1])))
     for ref, m, distance in distances(out_refs, out_upper):
         for c in range(2):
             ref[m, c] = value[distance * under : (distance + 1) * under, c * low : (c + 1) * low]
 
 
-def close_chunk_kernel(r, upper, width, me_ref, high_ref, *refs):
+def close_chunk_kernel(r, upper, width, me_ref, table, *refs):
     in_refs = refs[:width]
-    out_ref, held, stem, table, sems = refs[-5:]
-    table_copy = pltpu.make_async_copy(high_ref.at[2], table, sems.at[0])
-    table_copy.start()
+    out_ref, held, stem, sem = refs[-4:]
     value = gather(in_refs, held, me_ref[0], upper)
-    table_copy.wait()
     matrix = halves(left_block(table[0], table[1]))
     write_stem(stem, dot_halves(matrix, value), table.shape[-1])
-    copy = pltpu.make_async_copy(stem, out_ref.at[r], sems.at[1])
+    copy = pltpu.make_async_copy(stem, out_ref.at[r], sem)
     copy.start()
     copy.wait()
 
@@ -242,21 +223,23 @@
     block = jax.ShapeDtypeStruct((width, 2, under, low), jnp.float32)
     blocks = (block,) * width
     held = pltpu.VMEM((2, high, low), jnp.float32)
-    table = pltpu.VMEM((2, high, high), jnp.float32)
     stem = pltpu.VMEM((rows, LANES), jnp.float32)
-    sems = pltpu.SemaphoreType.DMA((2,))
 
     def tie(values, after):
         return lax.optimization_barrier((values, after))[0]
 
-    def send(values, upper, late=None):
+    def send(values, upper, ties=(None, None, None)):
         step, order = (width, upper_order(width)) if upper else (1, lower_order(width))
-        if late is not None:
-            values = [*values[:-1], tie(values[-1], late)]
+        values = [values[0]] + [
+            value if t is None else tie(value, t) for value, t in zip(values[1:], ties)
+        ]
         return [values[0]] + [
             lax.ppermute(value, "stem", [(i, i ^ (t * step)) for i in range(devices)])
             for value, t in zip(values[1:], order[1:])
         ]
+
+    def tied(values, at, after):
+        return [tie(v, after) if n == at and after is not None else v for n, v in enumerate(values)]
 
     def turn(values, name):
         return pl.pallas_call(
@@ -268,57 +251,56 @@
             name=name,
         )(*values)
 
-    def open_chunk(r, upper, laid):
+    def open_chunk(r, upper, stem):
         return pl.pallas_call(
-            functools.partial(open_chunk_kernel, r, upper),
+            functools.partial(open_chunk_kernel, upper),
             out_shape=blocks,
-            in_specs=[SMEM, HBM, HBM],
+            in_specs=[SMEM, VMEM, VMEM],
             out_specs=(VMEM,) * width,
-            scratch_shapes=[stem, table, sems],
             compiler_params=SMALL,
             name=f"open_{r}",
-        )(me, laid, hi_table)
+        )(me, stem, hi_table[0])
 
     def middle_chunk(r, in_upper, out_upper, values):
         return pl.pallas_call(
             functools.partial(middle_chunk_kernel, in_upper, out_upper),
             out_shape=blocks,
-            in_specs=[SMEM, HBM, HBM] + [VMEM] * width,
+            in_specs=[SMEM, VMEM, VMEM] + [VMEM] * width,
             out_specs=(VMEM,) * width,
-            scratch_shapes=[held, table, pltpu.VMEM(chain.shape, jnp.float32), sems],
+            scratch_shapes=[held],
             compiler_params=SMALL,
             name=f"middle_{r}",
-        )(me, hi_table, chain, *values)
+        )(me, hi_table[1], chain, *values)
 
     def close_chunk(r, upper, values, done=None):
         return pl.pallas_call(
             functools.partial(close_chunk_kernel, r, upper, width),
             out_shape=jax.ShapeDtypeStruct(laid.shape, jnp.float32),
-            in_specs=[SMEM, HBM] + [VMEM] * width + ([] if done is None else [HBM]),
+            in_specs=[SMEM, VMEM] + [VMEM] * width + ([] if done is None else [HBM]),
             out_specs=HBM,
-            scratch_shapes=[held, stem, table, sems],
+            scratch_shapes=[held, stem, pltpu.SemaphoreType.DMA],
             input_output_aliases={} if done is None else {2 + width: 0},
             compiler_params=SMALL,
             name=f"close_{r}",
-        )(me, hi_table, *values, *([] if done is None else [done]))
-
-    opened = open_chunk(0, True, laid)
-    ahead = send(opened, True)
-    behind = send(open_chunk(1, False, tie(laid, opened[0])), False, None)
-    behind = turn(behind, "turn_1")
-    behind = send(behind, True)
-    ahead = turn(ahead, "turn_0")
-    ahead = send(ahead, False, None)
-    ahead = middle_chunk(0, False, True, ahead)
-    ahead = send(ahead, True)
-    behind = middle_chunk(1, True, False, behind)
-    behind = send(behind, False, None)
-    behind = turn(behind, "back_1")
-    behind = send(behind, True)
-    ahead = turn(ahead, "back_0")
-    ahead = send(ahead, False, None)
-    done = close_chunk(0, False, ahead)
-    return close_chunk(1, True, behind, done)
+        )(me, hi_table[2], *values, *([] if done is None else [done]))
+
+    opened = open_chunk(0, True, laid[0])
+    g1 = send(opened, True)
+    g2 = send(open_chunk(1, False, tie(laid[1], opened[0])), False, (None, None, None))
+    turn_1 = turn(tied(g2, 0, ((g1[1], g1[2],), chain)), "turn_1")
+    g3 = send(turn_1, True, (None, None, None))
+    turn_0 = turn(tied(g1, 0, turn_1[0]), "turn_0")
+    g4 = send(turn_0, False, (None, None, None))
+    mid0 = middle_chunk(0, False, True, tied(g4, 0, (g3[1], g3[2],)))
+    g5 = send(mid0, True, (None, None, None))
+    mid1 = middle_chunk(1, True, False, tied(g3, 0, None))
+    g6 = send(mid1, False, (None, None, None))
+    back_1 = turn(tied(g6, 2, (g5[1], g5[2],)), "back_1")
+    g7 = send(back_1, True, (None, None, None))
+    back_0 = turn(tied(g5, 0, back_1[0]), "back_0")
+    g8 = send(back_0, False, (None, None, None))
+    done = close_chunk(0, False, tied(g8, 0, (g7[1], g7[2],)))
+    return close_chunk(1, True, g7, done)
 
 
 def one_slice(stem, bits, lo_table, hi_table):
@@ -348,12 +330,8 @@
     chain = pl.pallas_call(
         chain_kernel,
         out_shape=jax.ShapeDtypeStruct((2, low, low), jnp.float32),
-        in_specs=[SMEM, HBM],
+        in_specs=[SMEM, VMEM],
         out_specs=VMEM,
-        scratch_shapes=[
-            pltpu.VMEM((segments, 2, low, low), jnp.float32),
-            pltpu.SemaphoreType.DMA((segments,)),
-        ],
         compiler_params=SMALL,
         name="low_chain",
     )(bits, lo_table)

time: 65.1 us -> 59 us (0.906)
  waiting for transfers between devices: 18 us -> 14.9 us
  Pallas kernels: 11.7 us -> 10.2 us
  local copies, waits for them, and re-layouts: 2.64 us -> 1.77 us
    ppermute x24, waiting for transfers between devices: 18 us -> 14.9 us  [send(): lax.ppermute(value, 'stem', [(i, i ^ t * step) for i in range(devices)])]
    unnamed x10 -> x6, local copies, waits for them, and re-layouts: 2.64 us -> 0.16 us
    squeeze x0 -> x1, local copies, waits for them, and re-layouts: none -> 1.55 us  [open_chunk(): hi_table[0]]
  transfers between devices with their start and end apart: 24 -> 24, of which waited for: 6 -> 12; matrix products, arithmetic and copies ran while one was open for 0% -> 0% of each run, Pallas kernels for 14% -> 14%
where the time goes in v4:
time: 59 us; the launch traced here: 58.9 us
  starting transfers between devices  31.9 us (54%)
  waiting for transfers between devices  14.9 us (25%)
  Pallas kernels  10.2 us (17%)
  local copies, waits for them, and re-layouts  1.77 us (3%)
    ppermute x24, starting transfers between devices, send(): lax.ppermute(value, 'stem', [(i, i ^ t * step) for i in range(devices)])  31.9 us
    ppermute x24, waiting for transfers between devices, send(): lax.ppermute(value, 'stem', [(i, i ^ t * step) for i in range(devices)])  14.9 us
    pallas_call x2, Pallas kernels, middle_chunk(): pl.pallas_call(functools.partial(middle_chunk_kernel, in_upper, out_upper...  3.6 us
    pallas_call x2, Pallas kernels, close_chunk(): pl.pallas_call(functools.partial(close_chunk_kernel, r, upper, width), ou...  2.85 us
    pallas_call x1, Pallas kernels, one_slice(): pl.pallas_call(chain_kernel, out_shape=jax.ShapeDtypeStruct((2, low, low)...  2.43 us
    squeeze x1, local copies, waits for them, and re-layouts, open_chunk(): hi_table[0]  1.55 us
  transfers between devices with their start and end apart: 24, of which 12 were waited for; matrix products, arithmetic and copies ran while one was open for 0% of the time, Pallas kernels for 14%

profile of v4, /device:TPU:0, one launch (start us, length us, event | category | flops | bytes accessed | tf_op | source)
XLA Modules:
  0.0 58.9 jit_solution(1003258762720691907)
XLA Ops:
  0.0 0.0 copy-start.2
  0.0 1.5 %slice_bitcast_fusion = (f32[2,256,256]{2,1,0:T(8,128)S(1)}, f32[2,256,256]{2,1,0:T(8,128)S(1)}, f32[2,256,256]{2,1,0:T(8,128)S(1)}) fusion(f32[3,2,256,256]{3,2,1,0:T(8,128)} %param.6), kind=kLoop, calls=%fused_computation | loop fusion | bytes 3145728 | tf_op jit(solution)/shard_map/squeeze | solution.py:262
  1.6 0.1 copy-done.2
  1.7 0.0 copy-start
  1.7 0.1 fusion
  1.8 0.0 copy-start.1
  1.8 0.6 %open_0.1 = (f32[4,2,16,256]{3,2,1,0:T(8,128)S(1)}, f32[4,2,16,256]{3,2,1,0:T(8,128)S(1)}, f32[4,2,16,256]{3,2,1,0:T(8,128)S(1)}, f32[4,2,16,256]{3,2,1,0:T(8,128)S(1)}) custom-call(s32[1]{0:T(128)} %bitcast.me_ref, f32[1024,128]{1,0:T(8,128)S(1)} %bitcast.18, f32[2,256,256]{2,1,0:T(8,128)S(1)} %get-tuple-element.83.table), custom_call_target="tpu_custom_call" | custom-call | tf_op jit(solution)/shard_map/open_0/pallas_call | solution.py:255
  2.4 3.1 %collective-permute-start = (f32[4,2,16,256]{3,2,1,0:T(8,128)S(1)}, f32[4,2,16,256]{3,2,1,0:T(8,128)S(1)}, u32[]{:S(2)}, u32[]{:S(2)}) collective-permute-start(f32[4,2,16,256]{3,2,1,0:T(8,128)S(1)} %get-tuple-element.47), channel_id=1, source_target_pairs={{0,4},{1,5},{2,6},{3,7},{4,0},{5,1},{6,2},{7,3},{8,12},{9,13},{10,... | collective-permute-start | bytes 393224 | tf_op jit(solution)/shard_map/ppermute | solution.py:237
  5.5 2.6 %collective-permute-start.1 = (f32[4,2,16,256]{3,2,1,0:T(8,128)S(1)}, f32[4,2,16,256]{3,2,1,0:T(8,128)S(1)}, u32[]{:S(2)}, u32[]{:S(2)}) collective-permute-start(f32[4,2,16,256]{3,2,1,0:T(8,128)S(1)} %get-tuple-element.48), channel_id=1, source_target_pairs={{0,8},{1,9},{2,10},{3,11},{4,12},{5,13},{6,14},{7,15},{8,0},{9,1},... | collective-permute-start | bytes 393224 | tf_op jit(solution)/shard_map/ppermute | solution.py:237
  8.1 0.6 open_1.1
  8.7 0.4 collective-permute-start.2
  9.1 1.2 %collective-permute-start.3 = (f32[4,2,16,256]{3,2,1,0:T(8,128)S(1)}, f32[4,2,16,256]{3,2,1,0:T(8,128)S(1)}, u32[]{:S(2)}, u32[]{:S(2)}) collective-permute-start(f32[4,2,16,256]{3,2,1,0:T(8,128)S(1)} %get-tuple-element.51), channel_id=1, source_target_pairs={{0,1},{1,0},{2,3},{3,2},{4,5},{5,4},{6,7},{7,6},{8,9},{9,8},{10,11... | collective-permute-start | bytes 393224 | tf_op jit(solution)/shard_map/ppermute | solution.py:237
  10.3 0.5 collective-permute-start.4
  10.9 0.0 collective-permute-done.refs_1_
  10.9 3.4 %collective-permute-start.10 = (f32[4,2,16,256]{3,2,1,0:T(8,128)S(1)}, f32[4,2,16,256]{3,2,1,0:T(8,128)S(1)}, u32[]{:S(2)}, u32[]{:S(2)}) collective-permute-start(f32[4,2,16,256]{3,2,1,0:T(8,128)S(1)} %get-tuple-element.61), channel_id=1, source_target_pairs={{0,12},{1,13},{2,14},{3,15},{4,8},{5,9},{6,10},{7,11},{8,4},{9,5},... | collective-permute-start | bytes 393224 | tf_op jit(solution)/shard_map/ppermute | solution.py:237
  14.3 0.0 copy-done
  14.3 0.0 copy-done.1
  14.3 2.4 %low_chain.1.low_table = f32[2,256,256]{2,1,0:T(8,128)S(1)} custom-call(s32[1,3]{1,0:T(1,128)S(1)} %copy-done.1, f32[3,2,2,256,256]{4,3,2,1,0:T(8,128)S(1)} %copy-done), custom_call_target="tpu_custom_call" | custom-call | tf_op jit(solution)/shard_map/low_chain/pallas_call | solution.py:330
  16.7 0.0 collective-permute-done.1.refs_2_
  16.8 0.0 collective-permute-done.2.refs_1_
  16.8 0.0 collective-permute-done.3.refs_2_
  16.8 0.6 collective-permute-done.4.refs_3_
  17.4 0.5 collective-permute-start.5
  17.9 2.1 %collective-permute-start.6 = (f32[4,2,16,256]{3,2,1,0:T(8,128)S(1)}, f32[4,2,16,256]{3,2,1,0:T(8,128)S(1)}, u32[]{:S(2)}, u32[]{:S(2)}) collective-permute-start(f32[4,2,16,256]{3,2,1,0:T(8,128)S(1)} %get-tuple-element.55), channel_id=1, source_target_pairs={{0,8},{1,9},{2,10},{3,11},{4,12},{5,13},{6,14},{7,15},{8,0},{9,1},... | collective-permute-start | bytes 393224 | tf_op jit(solution)/shard_map/ppermute | solution.py:237
  20.0 0.0 collective-permute-done.10.refs_3_
  20.0 0.1 collective-permute-start.11
  20.1 1.6 %collective-permute-start.12 = (f32[4,2,16,256]{3,2,1,0:T(8,128)S(1)}, f32[4,2,16,256]{3,2,1,0:T(8,128)S(1)}, u32[]{:S(2)}, u32[]{:S(2)}) collective-permute-start(f32[4,2,16,256]{3,2,1,0:T(8,128)S(1)} %get-tuple-element.65), channel_id=1, source_target_pairs={{0,1},{1,0},{2,3},{3,2},{4,5},{5,4},{6,7},{7,6},{8,9},{9,8},{10,11... | collective-permute-start | bytes 393224 | tf_op jit(solution)/shard_map/ppermute | solution.py:237
  21.7 0.5 collective-permute-start.13
  22.2 2.2 %collective-permute-done.5.refs_1_ = f32[4,2,16,256]{3,2,1,0:T(8,128)S(1)} collective-permute-done((f32[4,2,16,256]{3,2,1,0:T(8,128)S(1)}, f32[4,2,16,256]{3,2,1,0:T(8,128)S(1)}, u32[]{:S(2)}, u32[]{:S(2)}) %collective-permute-start.5) | collective-permute-done | bytes 131104 | tf_op jit(solution)/shard_map/ppermute | solution.py:237
  24.5 2.2 %collective-permute-start.7 = (f32[4,2,16,256]{3,2,1,0:T(8,128)S(1)}, f32[4,2,16,256]{3,2,1,0:T(8,128)S(1)}, u32[]{:S(2)}, u32[]{:S(2)}) collective-permute-start(f32[4,2,16,256]{3,2,1,0:T(8,128)S(1)} %get-tuple-element.56), channel_id=1, source_target_pairs={{0,12},{1,13},{2,14},{3,15},{4,8},{5,9},{6,10},{7,11},{8,4},{9,5},... | collective-permute-start | bytes 393224 | tf_op jit(solution)/shard_map/ppermute | solution.py:237
  26.7 1.2 %collective-permute-done.6.refs_2_ = f32[4,2,16,256]{3,2,1,0:T(8,128)S(1)} collective-permute-done((f32[4,2,16,256]{3,2,1,0:T(8,128)S(1)}, f32[4,2,16,256]{3,2,1,0:T(8,128)S(1)}, u32[]{:S(2)}, u32[]{:S(2)}) %collective-permute-start.6) | collective-permute-done | bytes 131104 | tf_op jit(solution)/shard_map/ppermute | solution.py:237
  27.9 0.0 collective-permute-done.11.refs_1_
  27.9 0.0 collective-permute-done.12.refs_2_
  27.9 0.8 %collective-permute-done.13.refs_3_ = f32[4,2,16,256]{3,2,1,0:T(8,128)S(1)} collective-permute-done((f32[4,2,16,256]{3,2,1,0:T(8,128)S(1)}, f32[4,2,16,256]{3,2,1,0:T(8,128)S(1)}, u32[]{:S(2)}, u32[]{:S(2)}) %collective-permute-start.13) | collective-permute-done | bytes 131104 | tf_op jit(solution)/shard_map/ppermute | solution.py:237
  28.7 1.8 %middle_0.1 = (f32[4,2,16,256]{3,2,1,0:T(8,128)S(1)}, f32[4,2,16,256]{3,2,1,0:T(8,128)S(1)}, f32[4,2,16,256]{3,2,1,0:T(8,128)S(1)}, f32[4,2,16,256]{3,2,1,0:T(8,128)S(1)}) custom-call(s32[1]{0:T(128)} %bitcast.me_ref, f32[2,256,256]{2,1,0:T(8,128)S(1)} %get-tuple-element.85.table, f32[2,256,256]{2,1,0:T(8,128)S(1)} %low_chain.1.low_table, ...), custom_call_target="tpu_custom_call" | custom-call | tf_op jit(solution)/shard_map/middle_0/pallas_call | solution.py:265
  30.5 0.5 collective-permute-start.14
  30.9 1.4 %collective-permute-start.15 = (f32[4,2,16,256]{3,2,1,0:T(8,128)S(1)}, f32[4,2,16,256]{3,2,1,0:T(8,128)S(1)}, u32[]{:S(2)}, u32[]{:S(2)}) collective-permute-start(f32[4,2,16,256]{3,2,1,0:T(8,128)S(1)} %get-tuple-element.68), channel_id=1, source_target_pairs={{0,8},{1,9},{2,10},{3,11},{4,12},{5,13},{6,14},{7,15},{8,0},{9,1},... | collective-permute-start | bytes 393224 | tf_op jit(solution)/shard_map/ppermute | solution.py:237
  32.4 0.0 collective-permute-done.7.refs_3_
  32.4 1.8 %middle_1.1 = (f32[4,2,16,256]{3,2,1,0:T(8,128)S(1)}, f32[4,2,16,256]{3,2,1,0:T(8,128)S(1)}, f32[4,2,16,256]{3,2,1,0:T(8,128)S(1)}, f32[4,2,16,256]{3,2,1,0:T(8,128)S(1)}) custom-call(s32[1]{0:T(128)} %bitcast.me_ref, f32[2,256,256]{2,1,0:T(8,128)S(1)} %get-tuple-element.85.table, f32[2,256,256]{2,1,0:T(8,128)S(1)} %low_chain.1.low_table, ...), custom_call_target="tpu_custom_call" | custom-call | tf_op jit(solution)/shard_map/middle_1/pallas_call | solution.py:265
  34.2 0.1 collective-permute-start.9
  34.2 1.1 %collective-permute-start.16 = (f32[4,2,16,256]{3,2,1,0:T(8,128)S(1)}, f32[4,2,16,256]{3,2,1,0:T(8,128)S(1)}, u32[]{:S(2)}, u32[]{:S(2)}) collective-permute-start(f32[4,2,16,256]{3,2,1,0:T(8,128)S(1)} %get-tuple-element.70), channel_id=1, source_target_pairs={{0,2},{1,3},{2,0},{3,1},{4,6},{5,7},{6,4},{7,5},{8,10},{9,11},{10,... | collective-permute-start | bytes 393224 | tf_op jit(solution)/shard_map/ppermute | solution.py:237
  35.3 0.8 %collective-permute-start.8 = (f32[4,2,16,256]{3,2,1,0:T(8,128)S(1)}, f32[4,2,16,256]{3,2,1,0:T(8,128)S(1)}, u32[]{:S(2)}, u32[]{:S(2)}) collective-permute-start(f32[4,2,16,256]{3,2,1,0:T(8,128)S(1)} %get-tuple-element.58), channel_id=1, source_target_pairs={{0,3},{1,2},{2,1},{3,0},{4,7},{5,6},{6,5},{7,4},{8,11},{9,10},{10,... | collective-permute-start | bytes 393224 | tf_op jit(solution)/shard_map/ppermute | solution.py:237
  36.1 2.4 %collective-permute-done.14.refs_1_ = f32[4,2,16,256]{3,2,1,0:T(8,128)S(1)} collective-permute-done((f32[4,2,16,256]{3,2,1,0:T(8,128)S(1)}, f32[4,2,16,256]{3,2,1,0:T(8,128)S(1)}, u32[]{:S(2)}, u32[]{:S(2)}) %collective-permute-start.14) | collective-permute-done | bytes 131104 | tf_op jit(solution)/shard_map/ppermute | solution.py:237
  38.5 0.5 collective-permute-start.20
  39.0 0.9 %collective-permute-done.15.refs_2_ = f32[4,2,16,256]{3,2,1,0:T(8,128)S(1)} collective-permute-done((f32[4,2,16,256]{3,2,1,0:T(8,128)S(1)}, f32[4,2,16,256]{3,2,1,0:T(8,128)S(1)}, u32[]{:S(2)}, u32[]{:S(2)}) %collective-permute-start.15) | collective-permute-done | bytes 131104 | tf_op jit(solution)/shard_map/ppermute | solution.py:237
  39.9 0.0 collective-permute-done.9.refs_2_
  39.9 0.7 %collective-permute-done.16.refs_3_ = f32[4,2,16,256]{3,2,1,0:T(8,128)S(1)} collective-permute-done((f32[4,2,16,256]{3,2,1,0:T(8,128)S(1)}, f32[4,2,16,256]{3,2,1,0:T(8,128)S(1)}, u32[]{:S(2)}, u32[]{:S(2)}) %collective-permute-start.16) | collective-permute-done | bytes 131104 | tf_op jit(solution)/shard_map/ppermute | solution.py:237
  40.6 1.9 %collective-permute-done.8.refs_1_ = f32[4,2,16,256]{3,2,1,0:T(8,128)S(1)} collective-permute-done((f32[4,2,16,256]{3,2,1,0:T(8,128)S(1)}, f32[4,2,16,256]{3,2,1,0:T(8,128)S(1)}, u32[]{:S(2)}, u32[]{:S(2)}) %collective-permute-start.8) | collective-permute-done | bytes 131104 | tf_op jit(solution)/shard_map/ppermute | solution.py:237
  42.5 1.7 %collective-permute-start.17 = (f32[4,2,16,256]{3,2,1,0:T(8,128)S(1)}, f32[4,2,16,256]{3,2,1,0:T(8,128)S(1)}, u32[]{:S(2)}, u32[]{:S(2)}) collective-permute-start(f32[4,2,16,256]{3,2,1,0:T(8,128)S(1)} %get-tuple-element.72), channel_id=1, source_target_pairs={{0,4},{1,5},{2,6},{3,7},{4,0},{5,1},{6,2},{7,3},{8,12},{9,13},{10,... | collective-permute-start | bytes 393224 | tf_op jit(solution)/shard_map/ppermute | solution.py:237
  44.2 1.5 %collective-permute-start.18 = (f32[4,2,16,256]{3,2,1,0:T(8,128)S(1)}, f32[4,2,16,256]{3,2,1,0:T(8,128)S(1)}, u32[]{:S(2)}, u32[]{:S(2)}) collective-permute-start(f32[4,2,16,256]{3,2,1,0:T(8,128)S(1)} %get-tuple-element.73), channel_id=1, source_target_pairs={{0,8},{1,9},{2,10},{3,11},{4,12},{5,13},{6,14},{7,15},{8,0},{9,1},... | collective-permute-start | bytes 393224 | tf_op jit(solution)/shard_map/ppermute | solution.py:237
  45.8 0.0 collective-permute-done.20.refs_3_
  45.8 0.1 collective-permute-start.21
  45.9 0.6 collective-permute-start.22
  46.5 1.6 %collective-permute-start.23 = (f32[4,2,16,256]{3,2,1,0:T(8,128)S(1)}, f32[4,2,16,256]{3,2,1,0:T(8,128)S(1)}, u32[]{:S(2)}, u32[]{:S(2)}) collective-permute-start(f32[4,2,16,256]{3,2,1,0:T(8,128)S(1)} %get-tuple-element.82), channel_id=1, source_target_pairs={{0,2},{1,3},{2,0},{3,1},{4,6},{5,7},{6,4},{7,5},{8,10},{9,11},{10,... | collective-permute-start | bytes 393224 | tf_op jit(solution)/shard_map/ppermute | solution.py:237
  48.0 2.0 %collective-permute-done.17.refs_1_ = f32[4,2,16,256]{3,2,1,0:T(8,128)S(1)} collective-permute-done((f32[4,2,16,256]{3,2,1,0:T(8,128)S(1)}, f32[4,2,16,256]{3,2,1,0:T(8,128)S(1)}, u32[]{:S(2)}, u32[]{:S(2)}) %collective-permute-start.17) | collective-permute-done | bytes 131104 | tf_op jit(solution)/shard_map/ppermute | solution.py:237
  50.0 3.8 %collective-permute-start.19 = (f32[4,2,16,256]{3,2,1,0:T(8,128)S(1)}, f32[4,2,16,256]{3,2,1,0:T(8,128)S(1)}, u32[]{:S(2)}, u32[]{:S(2)}) collective-permute-start(f32[4,2,16,256]{3,2,1,0:T(8,128)S(1)} %get-tuple-element.74), channel_id=1, source_target_pairs={{0,12},{1,13},{2,14},{3,15},{4,8},{5,9},{6,10},{7,11},{8,4},{9,5},... | collective-permute-start | bytes 393224 | tf_op jit(solution)/shard_map/ppermute | solution.py:237
  53.9 0.4 collective-permute-done.18.refs_2_
  54.3 0.0 collective-permute-done.21.refs_1_
  54.3 0.0 collective-permute-done.22.refs_2_
  54.3 0.2 collective-permute-done.23.refs_3_
  54.5 1.4 %close_0.1.refs_4_ = f32[2,1024,128]{2,1,0:T(8,128)} custom-call(s32[1]{0:T(128)} %bitcast.me_ref, f32[2,256,256]{2,1,0:T(8,128)S(1)} %get-tuple-element.84.table, f32[4,2,16,256]{3,2,1,0:T(8,128)S(1)} %get-tuple-element.79.refs_0_, f32[4,2,16,256]{3,2,1,0:T(8,128)S(1)} %collective-permute-done.21.refs_1_, ...), custom_call_target="tpu_custom_call" | custom-call | tf_op jit(solution)/shard_map/close_0/pallas_call | solution.py:276
  55.9 1.5 %collective-permute-done.19.refs_3_ = f32[4,2,16,256]{3,2,1,0:T(8,128)S(1)} collective-permute-done((f32[4,2,16,256]{3,2,1,0:T(8,128)S(1)}, f32[4,2,16,256]{3,2,1,0:T(8,128)S(1)}, u32[]{:S(2)}, u32[]{:S(2)}) %collective-permute-start.19) | collective-permute-done | bytes 131104 | tf_op jit(solution)/shard_map/ppermute | solution.py:237
  57.4 1.4 %close_1.1 = f32[2,1024,128]{2,1,0:T(8,128)} custom-call(s32[1]{0:T(128)} %bitcast.me_ref, f32[2,256,256]{2,1,0:T(8,128)S(1)} %get-tuple-element.84.table, f32[4,2,16,256]{3,2,1,0:T(8,128)S(1)} %get-tuple-element.71.refs_0_, f32[4,2,16,256]{3,2,1,0:T(8,128)S(1)} %collective-permute-done.17.refs_1_, ...), custom_call_target="tpu_custom_call", output_to_operand_aliasing={{}: (6, {})} | custom-call | tf_op jit(solution)/shard_map/close_1/pallas_call | solution.py:276
  (4 shorter events, 0.1 us)
Async XLA Ops:
  0.0 1.7 %copy-start.2 = (f32[1,2,131072]{2,1,0:T(2,128)S(1)}, f32[1,2,131072]{2,1,0:T(2,128)}, u32[]{:S(2)}) copy-start(f32[1,2,131072]{2,1,0:T(2,128)} %param.4) | copy-start | bytes 3145732
  1.7 12.6 %copy-start = (f32[3,2,2,256,256]{4,3,2,1,0:T(8,128)S(1)}, f32[3,2,2,256,256]{4,3,2,1,0:T(8,128)}, u32[]{:S(2)}) copy-start(f32[3,2,2,256,256]{4,3,2,1,0:T(8,128)} %table_ref.1) | copy-start | bytes 9437188
  1.8 12.5 %copy-start.1 = (s32[1,3]{1,0:T(1,128)S(1)}, s32[1,3]{1,0:T(1,128)}, u32[]{:S(2)}) copy-start(s32[1,3]{1,0:T(1,128)} %bits_ref.1) | copy-start | bytes 40
  2.4 8.5 %collective-permute-start = (f32[4,2,16,256]{3,2,1,0:T(8,128)S(1)}, f32[4,2,16,256]{3,2,1,0:T(8,128)S(1)}, u32[]{:S(2)}, u32[]{:S(2)}) collective-permute-start(f32[4,2,16,256]{3,2,1,0:T(8,128)S(1)} %get-tuple-element.47), channel_id=1, source_target_pairs={{0,4},{1,5},{2,6},{3,7},{4,0},{5,1},{6,2},{7,3},{8,12},{9,13},{10,... | collective-permute-start | bytes 393224 | tf_op jit(solution)/shard_map/ppermute | solution.py:237
  5.5 11.3 %collective-permute-start.1 = (f32[4,2,16,256]{3,2,1,0:T(8,128)S(1)}, f32[4,2,16,256]{3,2,1,0:T(8,128)S(1)}, u32[]{:S(2)}, u32[]{:S(2)}) collective-permute-start(f32[4,2,16,256]{3,2,1,0:T(8,128)S(1)} %get-tuple-element.48), channel_id=1, source_target_pairs={{0,8},{1,9},{2,10},{3,11},{4,12},{5,13},{6,14},{7,15},{8,0},{9,1},... | collective-permute-start | bytes 393224 | tf_op jit(solution)/shard_map/ppermute | solution.py:237
  8.7 8.1 %collective-permute-start.2 = (f32[4,2,16,256]{3,2,1,0:T(8,128)S(1)}, f32[4,2,16,256]{3,2,1,0:T(8,128)S(1)}, u32[]{:S(2)}, u32[]{:S(2)}) collective-permute-start(f32[4,2,16,256]{3,2,1,0:T(8,128)S(1)} %get-tuple-element.50), channel_id=1, source_target_pairs={{0,3},{1,2},{2,1},{3,0},{4,7},{5,6},{6,5},{7,4},{8,11},{9,10},{10,... | collective-permute-start | bytes 393224 | tf_op jit(solution)/shard_map/ppermute | solution.py:237
  9.1 7.7 %collective-permute-start.3 = (f32[4,2,16,256]{3,2,1,0:T(8,128)S(1)}, f32[4,2,16,256]{3,2,1,0:T(8,128)S(1)}, u32[]{:S(2)}, u32[]{:S(2)}) collective-permute-start(f32[4,2,16,256]{3,2,1,0:T(8,128)S(1)} %get-tuple-element.51), channel_id=1, source_target_pairs={{0,1},{1,0},{2,3},{3,2},{4,5},{5,4},{6,7},{7,6},{8,9},{9,8},{10,11... | collective-permute-start | bytes 393224 | tf_op jit(solution)/shard_map/ppermute | solution.py:237
  10.3 7.0 %collective-permute-start.4 = (f32[4,2,16,256]{3,2,1,0:T(8,128)S(1)}, f32[4,2,16,256]{3,2,1,0:T(8,128)S(1)}, u32[]{:S(2)}, u32[]{:S(2)}) collective-permute-start(f32[4,2,16,256]{3,2,1,0:T(8,128)S(1)} %get-tuple-element.52), channel_id=1, source_target_pairs={{0,2},{1,3},{2,0},{3,1},{4,6},{5,7},{6,4},{7,5},{8,10},{9,11},{10,... | collective-permute-start | bytes 393224 | tf_op jit(solution)/shard_map/ppermute | solution.py:237
  10.9 9.1 %collective-permute-start.10 = (f32[4,2,16,256]{3,2,1,0:T(8,128)S(1)}, f32[4,2,16,256]{3,2,1,0:T(8,128)S(1)}, u32[]{:S(2)}, u32[]{:S(2)}) collective-permute-start(f32[4,2,16,256]{3,2,1,0:T(8,128)S(1)} %get-tuple-element.61), channel_id=1, source_target_pairs={{0,12},{1,13},{2,14},{3,15},{4,8},{5,9},{6,10},{7,11},{8,4},{9,5},... | collective-permute-start | bytes 393224 | tf_op jit(solution)/shard_map/ppermute | solution.py:237
  17.4 7.1 %collective-permute-start.5 = (f32[4,2,16,256]{3,2,1,0:T(8,128)S(1)}, f32[4,2,16,256]{3,2,1,0:T(8,128)S(1)}, u32[]{:S(2)}, u32[]{:S(2)}) collective-permute-start(f32[4,2,16,256]{3,2,1,0:T(8,128)S(1)} %get-tuple-element.54), channel_id=1, source_target_pairs={{0,4},{1,5},{2,6},{3,7},{4,0},{5,1},{6,2},{7,3},{8,12},{9,13},{10,... | collective-permute-start | bytes 393224 | tf_op jit(solution)/shard_map/ppermute | solution.py:237
  17.9 10.0 %collective-permute-start.6 = (f32[4,2,16,256]{3,2,1,0:T(8,128)S(1)}, f32[4,2,16,256]{3,2,1,0:T(8,128)S(1)}, u32[]{:S(2)}, u32[]{:S(2)}) collective-permute-start(f32[4,2,16,256]{3,2,1,0:T(8,128)S(1)} %get-tuple-element.55), channel_id=1, source_target_pairs={{0,8},{1,9},{2,10},{3,11},{4,12},{5,13},{6,14},{7,15},{8,0},{9,1},... | collective-permute-start | bytes 393224 | tf_op jit(solution)/shard_map/ppermute | solution.py:237
  20.0 7.9 %collective-permute-start.11 = (f32[4,2,16,256]{3,2,1,0:T(8,128)S(1)}, f32[4,2,16,256]{3,2,1,0:T(8,128)S(1)}, u32[]{:S(2)}, u32[]{:S(2)}) collective-permute-start(f32[4,2,16,256]{3,2,1,0:T(8,128)S(1)} %get-tuple-element.64), channel_id=1, source_target_pairs={{0,3},{1,2},{2,1},{3,0},{4,7},{5,6},{6,5},{7,4},{8,11},{9,10},{10,... | collective-permute-start | bytes 393224 | tf_op jit(solution)/shard_map/ppermute | solution.py:237
  20.1 7.8 %collective-permute-start.12 = (f32[4,2,16,256]{3,2,1,0:T(8,128)S(1)}, f32[4,2,16,256]{3,2,1,0:T(8,128)S(1)}, u32[]{:S(2)}, u32[]{:S(2)}) collective-permute-start(f32[4,2,16,256]{3,2,1,0:T(8,128)S(1)} %get-tuple-element.65), channel_id=1, source_target_pairs={{0,1},{1,0},{2,3},{3,2},{4,5},{5,4},{6,7},{7,6},{8,9},{9,8},{10,11... | collective-permute-start | bytes 393224 | tf_op jit(solution)/shard_map/ppermute | solution.py:237
  21.7 7.0 %collective-permute-start.13 = (f32[4,2,16,256]{3,2,1,0:T(8,128)S(1)}, f32[4,2,16,256]{3,2,1,0:T(8,128)S(1)}, u32[]{:S(2)}, u32[]{:S(2)}) collective-permute-start(f32[4,2,16,256]{3,2,1,0:T(8,128)S(1)} %get-tuple-element.66), channel_id=1, source_target_pairs={{0,2},{1,3},{2,0},{3,1},{4,6},{5,7},{6,4},{7,5},{8,10},{9,11},{10,... | collective-permute-start | bytes 393224 | tf_op jit(solution)/shard_map/ppermute | solution.py:237
  24.5 7.9 %collective-permute-start.7 = (f32[4,2,16,256]{3,2,1,0:T(8,128)S(1)}, f32[4,2,16,256]{3,2,1,0:T(8,128)S(1)}, u32[]{:S(2)}, u32[]{:S(2)}) collective-permute-start(f32[4,2,16,256]{3,2,1,0:T(8,128)S(1)} %get-tuple-element.56), channel_id=1, source_target_pairs={{0,12},{1,13},{2,14},{3,15},{4,8},{5,9},{6,10},{7,11},{8,4},{9,5},... | collective-permute-start | bytes 393224 | tf_op jit(solution)/shard_map/ppermute | solution.py:237
  30.5 8.0 %collective-permute-start.14 = (f32[4,2,16,256]{3,2,1,0:T(8,128)S(1)}, f32[4,2,16,256]{3,2,1,0:T(8,128)S(1)}, u32[]{:S(2)}, u32[]{:S(2)}) collective-permute-start(f32[4,2,16,256]{3,2,1,0:T(8,128)S(1)} %get-tuple-element.67), channel_id=1, source_target_pairs={{0,4},{1,5},{2,6},{3,7},{4,0},{5,1},{6,2},{7,3},{8,12},{9,13},{10,... | collective-permute-start | bytes 393224 | tf_op jit(solution)/shard_map/ppermute | solution.py:237
  30.9 8.9 %collective-permute-start.15 = (f32[4,2,16,256]{3,2,1,0:T(8,128)S(1)}, f32[4,2,16,256]{3,2,1,0:T(8,128)S(1)}, u32[]{:S(2)}, u32[]{:S(2)}) collective-permute-start(f32[4,2,16,256]{3,2,1,0:T(8,128)S(1)} %get-tuple-element.68), channel_id=1, source_target_pairs={{0,8},{1,9},{2,10},{3,11},{4,12},{5,13},{6,14},{7,15},{8,0},{9,1},... | collective-permute-start | bytes 393224 | tf_op jit(solution)/shard_map/ppermute | solution.py:237
  34.2 5.7 %collective-permute-start.9 = (f32[4,2,16,256]{3,2,1,0:T(8,128)S(1)}, f32[4,2,16,256]{3,2,1,0:T(8,128)S(1)}, u32[]{:S(2)}, u32[]{:S(2)}) collective-permute-start(f32[4,2,16,256]{3,2,1,0:T(8,128)S(1)} %get-tuple-element.59), channel_id=1, source_target_pairs={{0,1},{1,0},{2,3},{3,2},{4,5},{5,4},{6,7},{7,6},{8,9},{9,8},{10,11... | collective-permute-start | bytes 393224 | tf_op jit(solution)/shard_map/ppermute | solution.py:237
  34.2 6.4 %collective-permute-start.16 = (f32[4,2,16,256]{3,2,1,0:T(8,128)S(1)}, f32[4,2,16,256]{3,2,1,0:T(8,128)S(1)}, u32[]{:S(2)}, u32[]{:S(2)}) collective-permute-start(f32[4,2,16,256]{3,2,1,0:T(8,128)S(1)} %get-tuple-element.70), channel_id=1, source_target_pairs={{0,2},{1,3},{2,0},{3,1},{4,6},{5,7},{6,4},{7,5},{8,10},{9,11},{10,... | collective-permute-start | bytes 393224 | tf_op jit(solution)/shard_map/ppermute | solution.py:237
  35.3 7.2 %collective-permute-start.8 = (f32[4,2,16,256]{3,2,1,0:T(8,128)S(1)}, f32[4,2,16,256]{3,2,1,0:T(8,128)S(1)}, u32[]{:S(2)}, u32[]{:S(2)}) collective-permute-start(f32[4,2,16,256]{3,2,1,0:T(8,128)S(1)} %get-tuple-element.58), channel_id=1, source_target_pairs={{0,3},{1,2},{2,1},{3,0},{4,7},{5,6},{6,5},{7,4},{8,11},{9,10},{10,... | collective-permute-start | bytes 393224 | tf_op jit(solution)/shard_map/ppermute | solution.py:237
  38.5 7.3 %collective-permute-start.20 = (f32[4,2,16,256]{3,2,1,0:T(8,128)S(1)}, f32[4,2,16,256]{3,2,1,0:T(8,128)S(1)}, u32[]{:S(2)}, u32[]{:S(2)}) collective-permute-start(f32[4,2,16,256]{3,2,1,0:T(8,128)S(1)} %get-tuple-element.77), channel_id=1, source_target_pairs={{0,12},{1,13},{2,14},{3,15},{4,8},{5,9},{6,10},{7,11},{8,4},{9,5},... | collective-permute-start | bytes 393224 | tf_op jit(solution)/shard_map/ppermute | solution.py:237
  42.5 7.5 %collective-permute-start.17 = (f32[4,2,16,256]{3,2,1,0:T(8,128)S(1)}, f32[4,2,16,256]{3,2,1,0:T(8,128)S(1)}, u32[]{:S(2)}, u32[]{:S(2)}) collective-permute-start(f32[4,2,16,256]{3,2,1,0:T(8,128)S(1)} %get-tuple-element.72), channel_id=1, source_target_pairs={{0,4},{1,5},{2,6},{3,7},{4,0},{5,1},{6,2},{7,3},{8,12},{9,13},{10,... | collective-permute-start | bytes 393224 | tf_op jit(solution)/shard_map/ppermute | solution.py:237
  44.2 10.1 %collective-permute-start.18 = (f32[4,2,16,256]{3,2,1,0:T(8,128)S(1)}, f32[4,2,16,256]{3,2,1,0:T(8,128)S(1)}, u32[]{:S(2)}, u32[]{:S(2)}) collective-permute-start(f32[4,2,16,256]{3,2,1,0:T(8,128)S(1)} %get-tuple-element.73), channel_id=1, source_target_pairs={{0,8},{1,9},{2,10},{3,11},{4,12},{5,13},{6,14},{7,15},{8,0},{9,1},... | collective-permute-start | bytes 393224 | tf_op jit(solution)/shard_map/ppermute | solution.py:237
  45.8 8.5 %collective-permute-start.21 = (f32[4,2,16,256]{3,2,1,0:T(8,128)S(1)}, f32[4,2,16,256]{3,2,1,0:T(8,128)S(1)}, u32[]{:S(2)}, u32[]{:S(2)}) collective-permute-start(f32[4,2,16,256]{3,2,1,0:T(8,128)S(1)} %get-tuple-element.80), channel_id=1, source_target_pairs={{0,3},{1,2},{2,1},{3,0},{4,7},{5,6},{6,5},{7,4},{8,11},{9,10},{10,... | collective-permute-start | bytes 393224 | tf_op jit(solution)/shard_map/ppermute | solution.py:237
  45.9 8.4 %collective-permute-start.22 = (f32[4,2,16,256]{3,2,1,0:T(8,128)S(1)}, f32[4,2,16,256]{3,2,1,0:T(8,128)S(1)}, u32[]{:S(2)}, u32[]{:S(2)}) collective-permute-start(f32[4,2,16,256]{3,2,1,0:T(8,128)S(1)} %get-tuple-element.81), channel_id=1, source_target_pairs={{0,1},{1,0},{2,3},{3,2},{4,5},{5,4},{6,7},{7,6},{8,9},{9,8},{10,11... | collective-permute-start | bytes 393224 | tf_op jit(solution)/shard_map/ppermute | solution.py:237
  46.5 8.0 %collective-permute-start.23 = (f32[4,2,16,256]{3,2,1,0:T(8,128)S(1)}, f32[4,2,16,256]{3,2,1,0:T(8,128)S(1)}, u32[]{:S(2)}, u32[]{:S(2)}) collective-permute-start(f32[4,2,16,256]{3,2,1,0:T(8,128)S(1)} %get-tuple-element.82), channel_id=1, source_target_pairs={{0,2},{1,3},{2,0},{3,1},{4,6},{5,7},{6,4},{7,5},{8,10},{9,11},{10,... | collective-permute-start | bytes 393224 | tf_op jit(solution)/shard_map/ppermute | solution.py:237
  50.0 7.4 %collective-permute-start.19 = (f32[4,2,16,256]{3,2,1,0:T(8,128)S(1)}, f32[4,2,16,256]{3,2,1,0:T(8,128)S(1)}, u32[]{:S(2)}, u32[]{:S(2)}) collective-permute-start(f32[4,2,16,256]{3,2,1,0:T(8,128)S(1)} %get-tuple-element.74), channel_id=1, source_target_pairs={{0,12},{1,13},{2,14},{3,15},{4,8},{5,9},{6,10},{7,11},{8,4},{9,5},... | collective-permute-start | bytes 393224 | tf_op jit(solution)/shard_map/ppermute | solution.py:237

commit v5 on v2

--- a/solution.py
+++ b/solution.py
@@ -1,3 +1,5 @@
+import functools
+
 import jax
 import jax.numpy as jnp
 from jax import lax
@@ -7,6 +9,7 @@
 
 LANES = 128
 SUBLANES = 8
+PIECES = 1
 VMEM = pl.BlockSpec(memory_space=pltpu.VMEM)
 SMEM = pl.BlockSpec(memory_space=pltpu.SMEM)
 HBM = pl.BlockSpec(memory_space=pltpu.HBM)
@@ -33,10 +36,18 @@
     return jnp.concatenate([upper, lower], axis=0)
 
 
-def right_block(real_part, imag_part):
-    upper = jnp.concatenate([real_part, imag_part], axis=1)
-    lower = jnp.concatenate([-imag_part, real_part], axis=1)
-    return jnp.concatenate([upper, lower], axis=0)
+def left_halves(real_part, imag_part):
+    return [left_block(*parts) for parts in zip(halves(real_part), halves(imag_part))]
+
+
+def times_right(value, real_part, imag_part):
+    high, low = value.shape[0] // 2, value.shape[1]
+    sides = [jnp.concatenate(parts, axis=1) for parts in zip(halves(real_part), halves(imag_part))]
+    value = dot_halves(halves(value), sides)
+    return (
+        value[:high, :low] - value[high:, low:],
+        value[high:, :low] + value[:high, low:],
+    )
 
 
 def read_stem(stem_ref, high):
@@ -70,7 +81,7 @@
     for copy in copies:
         copy.start()
     table_copy.wait()
-    matrix = halves(left_block(table[0], table[1]))
+    matrix = left_halves(table[0], table[1])
     for r in range(spare):
         copies[r].wait()
         value = dot_halves(matrix, halves(read_stem(stem.at[r], high)))
@@ -78,19 +89,20 @@
             out_ref[:, r, c] = value[c * high : (c + 1) * high].reshape(leading, under, low)
 
 
-def chain_kernel(bits_ref, table_ref, out_ref, held, sems):
-    segments = held.shape[0]
-    copies = []
-    for k in range(segments):
-        entry = jnp.where(bits_ref[0, k] == 1, 1, 0)
-        copies.append(pltpu.make_async_copy(table_ref.at[k, entry], held.at[k], sems.at[k]))
-        copies[-1].start()
-    for copy in copies:
-        copy.wait()
-    low = held.shape[-1]
-    total = jnp.concatenate([held[0, 0], held[0, 1]], axis=0)
-    for k in range(1, segments):
-        total = dot_halves(halves(left_block(held[k, 0], held[k, 1])), halves(total))
+def chain_kernel(bits_ref, table_ref, out_ref, total):
+    segments, _, _, low, _ = table_ref.shape
+
+    def chosen(k):
+        return table_ref.at[k, jnp.where(bits_ref[0, k] == 1, 1, 0)]
+
+    def step(k, carry):
+        table = chosen(k)
+        total[...] = dot_halves(left_halves(table[0], table[1]), halves(total[...]))
+        return carry
+
+    for c in range(2):
+        total[c * low : (c + 1) * low] = chosen(0)[c]
+    lax.fori_loop(1, segments, step, 0)
     for c in range(2):
         out_ref[c] = total[c * low : (c + 1) * low].T
 
@@ -107,15 +119,12 @@
         for r in range(spare)
     ]
     high_copy.wait()
-    matrix = halves(left_block(high_table[0], high_table[1]))
+    matrix = left_halves(high_table[0], high_table[1])
     parts = [dot_halves(matrix, part) for part in parts]
     low_copy.wait()
-    matrix = halves(right_block(low_table[0], low_table[1]))
     for r in range(spare):
-        value = jnp.concatenate([parts[r][:high], parts[r][high:]], axis=1)
-        value = dot_halves(halves(value), matrix)
-        for c in range(2):
-            out_ref[:, r, c] = value[:, c * low : (c + 1) * low].reshape(leading, under, low)
+        for c, part in enumerate(times_right(parts[r], low_table[0], low_table[1])):
+            out_ref[:, r, c] = part.reshape(leading, under, low)
 
 
 def close_kernel(in_ref, high_ref, out_ref, held, table, sems):
@@ -128,7 +137,7 @@
         for r in range(spare)
     ]
     table_copy.wait()
-    matrix = halves(left_block(table[0], table[1]))
+    matrix = left_halves(table[0], table[1])
     copies = []
     for r in range(spare):
         write_stem(held.at[r], dot_halves(matrix, parts[r]), high)
@@ -136,6 +145,208 @@
         copies[-1].start()
     for copy in copies:
         copy.wait()
+
+
+def layout_over(values, others):
+    return tuple(tuple(value + other for other in others) for value in values)
+
+
+def distances(layout):
+    for n, array in enumerate(layout):
+        for m, distance in enumerate(array):
+            yield n, m, distance
+
+
+def rows_by_distance(table, me, under):
+    devices = table.shape[1] // under
+    starts = [pl.multiple_of((me ^ d) * under, under) for d in range(devices)]
+    return [jnp.concatenate([table[c, pl.ds(at, under), :] for at in starts]) for c in range(2)]
+
+
+def gather(in_refs, held, me, layout):
+    under = in_refs[0].shape[2]
+    for n, m, distance in distances(layout):
+        at = pl.ds(pl.multiple_of((me ^ distance) * under, under), under)
+        for c in range(2):
+            held[c, at, :] = in_refs[n][m, c]
+    return halves(jnp.concatenate([held[0], held[1]], axis=0))
+
+
+def open_chunk_kernel(layout, me_ref, stem_ref, table, *out_refs):
+    under = out_refs[0].shape[2]
+    high = table.shape[-1]
+    matrix = left_halves(*rows_by_distance(table, me_ref[0], under))
+    value = dot_halves(matrix, halves(read_stem(stem_ref, high)))
+    for n, m, distance in distances(layout):
+        for c in range(2):
+            start = c * high + distance * under
+            out_refs[n][m, c] = value[start : start + under]
+
+
+def turn_kernel(old, new, *refs):
+    place = {distance: (n, m) for n, m, distance in distances(old)}
+    for n, m, distance in distances(new):
+        at = place[distance]
+        refs[len(old) + n][m] = refs[at[0]][at[1]]
+
+
+def middle_chunk_kernel(old, new, me_ref, table, low_table, *refs):
+    *blocks, held, between = refs
+    in_refs, out_refs = blocks[: len(old)], blocks[len(old) :]
+    under = in_refs[0].shape[2]
+
+    def stage(n, carry):
+        @pl.when(n == 0)
+        def high_modes():
+            value = gather(in_refs, held, me_ref[0], old)
+            matrix = left_halves(*rows_by_distance(table, me_ref[0], under))
+            between[...] = dot_halves(matrix, value)
+
+        @pl.when(n == 1)
+        def low_modes():
+            parts = times_right(between[...], low_table[0], low_table[1])
+            for n, m, distance in distances(new):
+                for c in range(2):
+                    out_refs[n][m, c] = parts[c][distance * under : (distance + 1) * under]
+
+        return carry
+
+    lax.fori_loop(0, 2, stage, 0)
+
+
+def close_chunk_kernel(r, layout, me_ref, table, *refs):
+    in_refs = refs[: len(layout)]
+    out_ref, held, stem, sems = refs[-4:]
+    pieces = sems.shape[0]
+    high, rows = table.shape[-1] // pieces, stem.shape[0] // pieces
+    gather(in_refs, held, me_ref[0], layout)
+
+    def copy(n):
+        at = pl.ds(n * rows, rows)
+        return pltpu.make_async_copy(stem.at[at], out_ref.at[r, at], sems.at[n])
+
+    def piece(n, carry):
+        some = pl.ds(n * high, high)
+        matrix = left_halves(table[0, some], table[1, some])
+        value = halves(jnp.concatenate([held[0], held[1]], axis=0))
+        write_stem(stem.at[pl.ds(n * rows, rows)], dot_halves(matrix, value), high)
+        copy(n).start()
+        return carry
+
+    lax.fori_loop(0, pieces, piece, 0)
+    for n in range(pieces):
+        copy(n).wait()
+
+
+def chunks_by_permutes(laid, chain, hi_table):
+    devices = lax.axis_size("stem")
+    width = 1 << ((devices.bit_length() - 1) // 2)
+    spare, rows, _ = laid.shape
+    high, low = hi_table.shape[-1], chain.shape[-1]
+    under = high // devices
+    me = lax.axis_index("stem").reshape(1)
+    held = pltpu.VMEM((2, high, low), jnp.float32)
+    stem = pltpu.VMEM((rows, LANES), jnp.float32)
+
+    def tie(values, after):
+        return lax.optimization_barrier((values, after))[0]
+
+    def blocks(layout):
+        shapes = [(len(array), 2, under, low) for array in layout]
+        return tuple(jax.ShapeDtypeStruct(shape, jnp.float32) for shape in shapes)
+
+    def swap(value, step, after=None):
+        value = value if after is None else tie(value, after)
+        return lax.ppermute(value, "stem", [(i, i ^ step) for i in range(devices)])
+
+    def tied(values, at, after):
+        return [tie(v, after) if n == at else v for n, v in enumerate(values)]
+
+    def turn(old, new, values, name):
+        return pl.pallas_call(
+            functools.partial(turn_kernel, old, new),
+            out_shape=blocks(new),
+            in_specs=[VMEM] * len(old),
+            out_specs=(VMEM,) * len(new),
+            compiler_params=SMALL,
+            name=name,
+        )(*values)
+
+    def open_chunk(r, layout, stem):
+        return pl.pallas_call(
+            functools.partial(open_chunk_kernel, layout),
+            out_shape=blocks(layout),
+            in_specs=[SMEM, VMEM, VMEM],
+            out_specs=(VMEM,) * len(layout),
+            compiler_params=SMALL,
+            name=f"open_{r}",
+        )(me, stem, hi_table[0])
+
+    def middle_chunk(r, old, new, values):
+        return pl.pallas_call(
+            functools.partial(middle_chunk_kernel, old, new),
+            out_shape=blocks(new),
+            in_specs=[SMEM, VMEM, VMEM] + [VMEM] * len(old),
+            out_specs=(VMEM,) * len(new),
+            scratch_shapes=[held, pltpu.VMEM((2 * high, low), jnp.float32)],
+            compiler_params=SMALL,
+            name=f"middle_{r}",
+        )(me, hi_table[1], chain, *values)
+
+    def close_chunk(r, layout, values, done=None):
+        return pl.pallas_call(
+            functools.partial(close_chunk_kernel, r, layout),
+            out_shape=jax.ShapeDtypeStruct(laid.shape, jnp.float32),
+            in_specs=[SMEM, VMEM] + [VMEM] * len(layout) + ([] if done is None else [HBM]),
+            out_specs=HBM,
+            scratch_shapes=[held, stem, pltpu.SemaphoreType.DMA((PIECES,))],
+            input_output_aliases={} if done is None else {2 + len(layout): 0},
+            compiler_params=SMALL,
+            name=f"close_{r}",
+        )(me, hi_table[2], *values, *([] if done is None else [done]))
+
+    L00z = layout_over((0, 4, 8, 12), (0, 1, 3, 2))
+    L00p = layout_over((0, 1, 3, 2), (0, 4, 8, 12))
+    L01z = layout_over((0, 4, 8, 12), (0, 1, 3, 2))
+    L01p = layout_over((0, 1, 3, 2), (0, 4, 8, 12))
+    L10p = layout_over((0, 1, 3, 2), (0, 4, 8, 12))
+    L10z = layout_over((0, 4, 8, 12), (0, 1, 3, 2))
+    L11p = layout_over((0, 1, 3, 2), (0, 4, 8, 12))
+    L11z = layout_over((0, 4, 8, 12), (0, 1, 3, 2))
+    open_0 = open_chunk(0, L00z, laid[0])
+    open_1 = open_chunk(1, L10p, tie(laid[1], open_0[0]))
+    open_0_1 = swap(open_0[1], 4)
+    open_0_2 = swap(open_0[2], 8)
+    open_0_3 = swap(open_0[3], 12)
+    open_1_1 = swap(open_1[1], 1)
+    open_1_2 = swap(open_1[2], 3)
+    open_1_3 = swap(open_1[3], 2)
+    turn_101 = turn(L10p, L10z, tied([open_1[0], open_1_1, open_1_2, open_1_3], 0, (open_0_1, open_0_2, chain)), "turn_101")
+    turn_001 = turn(L00z, L00p, tied([open_0[0], open_0_1, open_0_2, open_0_3], 0, turn_101[0]), "turn_001")
+    turn_001_1 = swap(turn_001[1], 1)
+    turn_001_2 = swap(turn_001[2], 3)
+    turn_001_3 = swap(turn_001[3], 2)
+    turn_101_1 = swap(turn_101[1], 4)
+    turn_101_2 = swap(turn_101[2], 8)
+    middle_0 = middle_chunk(0, L00p, L01z, tied([turn_001[0], turn_001_1, turn_001_2, turn_001_3], 0, (turn_101_1, turn_101_2)))
+    middle_0_1 = swap(middle_0[1], 4)
+    middle_0_2 = swap(middle_0[2], 8)
+    middle_0_3 = swap(middle_0[3], 12)
+    turn_101_3 = swap(turn_101[3], 12)
+    middle_1 = middle_chunk(1, L10z, L11p, [turn_101[0], turn_101_1, turn_101_2, turn_101_3])
+    middle_1_1 = swap(middle_1[1], 1)
+    middle_1_2 = swap(middle_1[2], 3)
+    middle_1_3 = swap(middle_1[3], 2)
+    turn_111 = turn(L11p, L11z, tied([middle_1[0], middle_1_1, middle_1_2, middle_1_3], 2, (middle_0_1, middle_0_2)), "turn_111")
+    turn_011 = turn(L01z, L01p, tied([middle_0[0], middle_0_1, middle_0_2, middle_0_3], 0, turn_111[0]), "turn_011")
+    turn_011_1 = swap(turn_011[1], 1)
+    turn_011_2 = swap(turn_011[2], 3)
+    turn_011_3 = swap(turn_011[3], 2)
+    turn_111_1 = swap(turn_111[1], 4)
+    turn_111_2 = swap(turn_111[2], 8)
+    close_0 = close_chunk(0, L01p, tied([turn_011[0], turn_011_1, turn_011_2, turn_011_3], 0, (turn_111_1, turn_111_2)))
+    turn_111_3 = swap(turn_111[3], 12)
+    return close_chunk(1, L11z, [turn_111[0], turn_111_1, turn_111_2, turn_111_3], close_0)
 
 
 def one_slice(stem, bits, lo_table, hi_table):
@@ -162,6 +373,18 @@
 
     laid = stem.reshape(2, stem.shape[1] // LANES, LANES).transpose(1, 0, 2)
     laid = laid.reshape(stem_type.shape)
+    chain = pl.pallas_call(
+        chain_kernel,
+        out_shape=jax.ShapeDtypeStruct((2, low, low), jnp.float32),
+        in_specs=[SMEM, VMEM],
+        out_specs=VMEM,
+        scratch_shapes=[pltpu.VMEM((2 * low, low), jnp.float32)],
+        compiler_params=SMALL,
+        name="low_chain",
+    )(bits, lo_table)
+    if direct and spare == 2 and 1 << (2 * ((leading.bit_length() - 1) // 2)) == leading:
+        closed = chunks_by_permutes(laid, chain, hi_table)
+        return closed.reshape(-1, 2, LANES).transpose(1, 0, 2).reshape(stem.shape)
     table_scratch = pltpu.VMEM((2, high, high), jnp.float32)
     opened = pl.pallas_call(
         open_kernel,
@@ -172,18 +395,6 @@
         compiler_params=LARGE,
         name="open_high",
     )(laid, hi_table)
-    chain = pl.pallas_call(
-        chain_kernel,
-        out_shape=jax.ShapeDtypeStruct((2, low, low), jnp.float32),
-        in_specs=[SMEM, HBM],
-        out_specs=VMEM,
-        scratch_shapes=[
-            pltpu.VMEM((segments, 2, low, low), jnp.float32),
-            pltpu.SemaphoreType.DMA((segments,)),
-        ],
-        compiler_params=LARGE,
-        name="low_chain",
-    )(bits, lo_table)
     middle = pl.pallas_call(
         middle_kernel,
         out_shape=split_type,

time: 72.2 us -> 58.1 us (0.80)
  blocking collectives: 31.5 us -> 0 us
  starting transfers between devices: 7.5 us -> 31.6 us
  Pallas kernels: 13.3 us -> 8.59 us
  waiting for transfers between devices: 18.2 us -> 15.8 us
    ppermute x0 -> x24, starting transfers between devices: none -> 31.6 us  [swap(): return lax.ppermute(value, 'stem', [(i, i ^ step) for i in range(devices)])]
    all_to_all x1 -> x0, blocking collectives: 31.5 us -> none  [exchange(): lax.all_to_all(values, 'stem', split_axis=0, concat_axis=0, tiled=True)]
    all_to_all x1 -> x0, waiting for transfers between devices: 18.2 us -> none  [exchange(): lax.all_to_all(values, 'stem', split_axis=0, concat_axis=0, tiled=True)]
    ppermute x0 -> x24, waiting for transfers between devices: none -> 15.8 us  [swap(): return lax.ppermute(value, 'stem', [(i, i ^ step) for i in range(devices)])]
    all_to_all x1 -> x0, starting transfers between devices: 7.5 us -> none  [exchange(): lax.all_to_all(values, 'stem', split_axis=0, concat_axis=0, tiled=True)]
    pallas_call x1, Pallas kernels: 4.73 us -> 1.94 us  [one_slice(): pl.pallas_call(chain_kernel, out_shape=jax.ShapeDtypeStruct((2, low, low)...]
    pallas_call x3 -> x10, Pallas kernels: 8.53 us -> 6.65 us  [the longest x2 2.85 us: close_chunk(): pl.pallas_call(functools.partial(close_chunk_kernel, r, layout), out_shap...]
    squeeze x0 -> x1, local copies, waits for them, and re-layouts: none -> 1.55 us  [open_chunk(): hi_table[0]]
  transfers between devices with their start and end apart: 1 -> 24, of which waited for: 1 -> 10; matrix products, arithmetic and copies ran while one was open for 0% -> 0% of each run, Pallas kernels for 7% -> 11%
where the time goes in v5:
time: 58.1 us; the launch traced here: 58 us
  starting transfers between devices  31.6 us (54%)
  waiting for transfers between devices  15.8 us (27%)
  Pallas kernels  8.59 us (15%)
  local copies, waits for them, and re-layouts  1.77 us (3%)
    ppermute x24, starting transfers between devices, swap(): return lax.ppermute(value, 'stem', [(i, i ^ step) for i in range(devices)])  31.6 us
    ppermute x24, waiting for transfers between devices, swap(): return lax.ppermute(value, 'stem', [(i, i ^ step) for i in range(devices)])  15.8 us
    pallas_call x2, Pallas kernels, close_chunk(): pl.pallas_call(functools.partial(close_chunk_kernel, r, layout), out_shap...  2.85 us
    pallas_call x2, Pallas kernels, middle_chunk(): pl.pallas_call(functools.partial(middle_chunk_kernel, old, new), out_shap...  2.47 us
    pallas_call x1, Pallas kernels, one_slice(): pl.pallas_call(chain_kernel, out_shape=jax.ShapeDtypeStruct((2, low, low)...  1.94 us
    squeeze x1, local copies, waits for them, and re-layouts, open_chunk(): hi_table[0]  1.55 us
    pallas_call x2, Pallas kernels, open_chunk(): pl.pallas_call(functools.partial(open_chunk_kernel, layout), out_shape=bl...  1.19 us
  transfers between devices with their start and end apart: 24, of which 10 were waited for; matrix products, arithmetic and copies ran while one was open for 0% of the time, Pallas kernels for 11%

profile of v5, /device:TPU:0, one launch (start us, length us, event | category | flops | bytes accessed | tf_op | source)
XLA Modules:
  0.0 58.0 jit_solution(5884167897634980451)
XLA Ops:
  0.0 0.0 copy-start.2
  0.0 1.5 %slice_bitcast_fusion = (f32[2,256,256]{2,1,0:T(8,128)S(1)}, f32[2,256,256]{2,1,0:T(8,128)S(1)}, f32[2,256,256]{2,1,0:T(8,128)S(1)}) fusion(f32[3,2,256,256]{3,2,1,0:T(8,128)} %param.6), kind=kLoop, calls=%fused_computation | loop fusion | bytes 3145728 | tf_op jit(solution)/shard_map/squeeze | solution.py:283
  1.6 0.1 copy-done.2
  1.7 0.0 copy-start
  1.7 0.1 fusion
  1.8 0.0 copy-start.1
  1.8 0.6 %open_0.1 = (f32[4,2,16,256]{3,2,1,0:T(8,128)S(1)}, f32[4,2,16,256]{3,2,1,0:T(8,128)S(1)}, f32[4,2,16,256]{3,2,1,0:T(8,128)S(1)}, f32[4,2,16,256]{3,2,1,0:T(8,128)S(1)}) custom-call(s32[1]{0:T(128)} %bitcast.me_ref, f32[1024,128]{1,0:T(8,128)S(1)} %bitcast.18, f32[2,256,256]{2,1,0:T(8,128)S(1)} %get-tuple-element.83.table), custom_call_target="tpu_custom_call" | custom-call | tf_op jit(solution)/shard_map/open_0/pallas_call | solution.py:276
  2.4 3.1 %collective-permute-start = (f32[4,2,16,256]{3,2,1,0:T(8,128)S(1)}, f32[4,2,16,256]{3,2,1,0:T(8,128)S(1)}, u32[]{:S(2)}, u32[]{:S(2)}) collective-permute-start(f32[4,2,16,256]{3,2,1,0:T(8,128)S(1)} %get-tuple-element.47), channel_id=1, source_target_pairs={{0,4},{1,5},{2,6},{3,7},{4,0},{5,1},{6,2},{7,3},{8,12},{9,13},{10,... | collective-permute-start | bytes 393224 | tf_op jit(solution)/shard_map/ppermute | solution.py:260
  5.5 2.6 %collective-permute-start.1 = (f32[4,2,16,256]{3,2,1,0:T(8,128)S(1)}, f32[4,2,16,256]{3,2,1,0:T(8,128)S(1)}, u32[]{:S(2)}, u32[]{:S(2)}) collective-permute-start(f32[4,2,16,256]{3,2,1,0:T(8,128)S(1)} %get-tuple-element.48), channel_id=1, source_target_pairs={{0,8},{1,9},{2,10},{3,11},{4,12},{5,13},{6,14},{7,15},{8,0},{9,1},... | collective-permute-start | bytes 393224 | tf_op jit(solution)/shard_map/ppermute | solution.py:260
  8.1 0.6 %open_1.1 = (f32[4,2,16,256]{3,2,1,0:T(8,128)S(1)}, f32[4,2,16,256]{3,2,1,0:T(8,128)S(1)}, f32[4,2,16,256]{3,2,1,0:T(8,128)S(1)}, f32[4,2,16,256]{3,2,1,0:T(8,128)S(1)}) custom-call(s32[1]{0:T(128)} %bitcast.me_ref, f32[1024,128]{1,0:T(8,128)S(1)} %bitcast.17, f32[2,256,256]{2,1,0:T(8,128)S(1)} %get-tuple-element.83.table), custom_call_target="tpu_custom_call" | custom-call | tf_op jit(solution)/shard_map/open_1/pallas_call | solution.py:276
  8.7 0.1 collective-permute-start.2
  8.7 1.6 %collective-permute-start.3 = (f32[4,2,16,256]{3,2,1,0:T(8,128)S(1)}, f32[4,2,16,256]{3,2,1,0:T(8,128)S(1)}, u32[]{:S(2)}, u32[]{:S(2)}) collective-permute-start(f32[4,2,16,256]{3,2,1,0:T(8,128)S(1)} %get-tuple-element.51), channel_id=1, source_target_pairs={{0,3},{1,2},{2,1},{3,0},{4,7},{5,6},{6,5},{7,4},{8,11},{9,10},{10,... | collective-permute-start | bytes 393224 | tf_op jit(solution)/shard_map/ppermute | solution.py:260
  10.3 0.5 collective-permute-start.4
  10.9 0.0 collective-permute-done.refs_1_
  10.9 3.4 %collective-permute-start.10 = (f32[4,2,16,256]{3,2,1,0:T(8,128)S(1)}, f32[4,2,16,256]{3,2,1,0:T(8,128)S(1)}, u32[]{:S(2)}, u32[]{:S(2)}) collective-permute-start(f32[4,2,16,256]{3,2,1,0:T(8,128)S(1)} %get-tuple-element.61), channel_id=1, source_target_pairs={{0,12},{1,13},{2,14},{3,15},{4,8},{5,9},{6,10},{7,11},{8,4},{9,5},... | collective-permute-start | bytes 393224 | tf_op jit(solution)/shard_map/ppermute | solution.py:260
  14.3 0.0 copy-done
  14.3 0.0 copy-done.1
  14.3 1.9 %low_chain.1.low_table = f32[2,256,256]{2,1,0:T(8,128)S(1)} custom-call(s32[1,3]{1,0:T(1,128)S(1)} %copy-done.1, f32[3,2,2,256,256]{4,3,2,1,0:T(8,128)S(1)} %copy-done), custom_call_target="tpu_custom_call" | custom-call | tf_op jit(solution)/shard_map/low_chain/pallas_call | solution.py:376
  16.3 0.0 collective-permute-done.1.refs_2_
  16.3 0.0 collective-permute-done.2.refs_1_
  16.3 0.0 collective-permute-done.3.refs_2_
  16.3 1.1 %collective-permute-done.4.refs_3_ = f32[4,2,16,256]{3,2,1,0:T(8,128)S(1)} collective-permute-done((f32[4,2,16,256]{3,2,1,0:T(8,128)S(1)}, f32[4,2,16,256]{3,2,1,0:T(8,128)S(1)}, u32[]{:S(2)}, u32[]{:S(2)}) %collective-permute-start.4) | collective-permute-done | bytes 131104 | tf_op jit(solution)/shard_map/ppermute | solution.py:260
  17.5 0.5 collective-permute-start.5
  18.0 2.0 %collective-permute-start.6 = (f32[4,2,16,256]{3,2,1,0:T(8,128)S(1)}, f32[4,2,16,256]{3,2,1,0:T(8,128)S(1)}, u32[]{:S(2)}, u32[]{:S(2)}) collective-permute-start(f32[4,2,16,256]{3,2,1,0:T(8,128)S(1)} %get-tuple-element.55), channel_id=1, source_target_pairs={{0,8},{1,9},{2,10},{3,11},{4,12},{5,13},{6,14},{7,15},{8,0},{9,1},... | collective-permute-start | bytes 393224 | tf_op jit(solution)/shard_map/ppermute | solution.py:260
  20.0 0.0 collective-permute-done.10.refs_3_
  20.0 0.1 collective-permute-start.11
  20.1 1.6 %collective-permute-start.12 = (f32[4,2,16,256]{3,2,1,0:T(8,128)S(1)}, f32[4,2,16,256]{3,2,1,0:T(8,128)S(1)}, u32[]{:S(2)}, u32[]{:S(2)}) collective-permute-start(f32[4,2,16,256]{3,2,1,0:T(8,128)S(1)} %get-tuple-element.65), channel_id=1, source_target_pairs={{0,3},{1,2},{2,1},{3,0},{4,7},{5,6},{6,5},{7,4},{8,11},{9,10},{10,... | collective-permute-start | bytes 393224 | tf_op jit(solution)/shard_map/ppermute | solution.py:260
  21.7 0.5 collective-permute-start.13
  22.3 1.8 %collective-permute-done.5.refs_1_ = f32[4,2,16,256]{3,2,1,0:T(8,128)S(1)} collective-permute-done((f32[4,2,16,256]{3,2,1,0:T(8,128)S(1)}, f32[4,2,16,256]{3,2,1,0:T(8,128)S(1)}, u32[]{:S(2)}, u32[]{:S(2)}) %collective-permute-start.5) | collective-permute-done | bytes 131104 | tf_op jit(solution)/shard_map/ppermute | solution.py:260
  24.1 2.4 %collective-permute-start.7 = (f32[4,2,16,256]{3,2,1,0:T(8,128)S(1)}, f32[4,2,16,256]{3,2,1,0:T(8,128)S(1)}, u32[]{:S(2)}, u32[]{:S(2)}) collective-permute-start(f32[4,2,16,256]{3,2,1,0:T(8,128)S(1)} %get-tuple-element.56), channel_id=1, source_target_pairs={{0,12},{1,13},{2,14},{3,15},{4,8},{5,9},{6,10},{7,11},{8,4},{9,5},... | collective-permute-start | bytes 393224 | tf_op jit(solution)/shard_map/ppermute | solution.py:260
  26.4 2.6 %collective-permute-done.6.refs_2_ = f32[4,2,16,256]{3,2,1,0:T(8,128)S(1)} collective-permute-done((f32[4,2,16,256]{3,2,1,0:T(8,128)S(1)}, f32[4,2,16,256]{3,2,1,0:T(8,128)S(1)}, u32[]{:S(2)}, u32[]{:S(2)}) %collective-permute-start.6) | collective-permute-done | bytes 131104 | tf_op jit(solution)/shard_map/ppermute | solution.py:260
  29.0 0.0 collective-permute-done.11.refs_1_
  29.0 0.0 collective-permute-done.12.refs_2_
  29.0 0.0 collective-permute-done.13.refs_3_
  29.0 1.2 %middle_0.1 = (f32[4,2,16,256]{3,2,1,0:T(8,128)S(1)}, f32[4,2,16,256]{3,2,1,0:T(8,128)S(1)}, f32[4,2,16,256]{3,2,1,0:T(8,128)S(1)}, f32[4,2,16,256]{3,2,1,0:T(8,128)S(1)}) custom-call(s32[1]{0:T(128)} %bitcast.me_ref, f32[2,256,256]{2,1,0:T(8,128)S(1)} %get-tuple-element.85.table, f32[2,256,256]{2,1,0:T(8,128)S(1)} %low_chain.1.low_table, ...), custom_call_target="tpu_custom_call" | custom-call | tf_op jit(solution)/shard_map/middle_0/pallas_call | solution.py:286
  30.3 0.2 collective-permute-start.14
  30.5 2.1 %collective-permute-start.15 = (f32[4,2,16,256]{3,2,1,0:T(8,128)S(1)}, f32[4,2,16,256]{3,2,1,0:T(8,128)S(1)}, u32[]{:S(2)}, u32[]{:S(2)}) collective-permute-start(f32[4,2,16,256]{3,2,1,0:T(8,128)S(1)} %get-tuple-element.68), channel_id=1, source_target_pairs={{0,8},{1,9},{2,10},{3,11},{4,12},{5,13},{6,14},{7,15},{8,0},{9,1},... | collective-permute-start | bytes 393224 | tf_op jit(solution)/shard_map/ppermute | solution.py:260
  32.6 0.0 collective-permute-done.7.refs_3_
  32.6 1.2 %middle_1.1 = (f32[4,2,16,256]{3,2,1,0:T(8,128)S(1)}, f32[4,2,16,256]{3,2,1,0:T(8,128)S(1)}, f32[4,2,16,256]{3,2,1,0:T(8,128)S(1)}, f32[4,2,16,256]{3,2,1,0:T(8,128)S(1)}) custom-call(s32[1]{0:T(128)} %bitcast.me_ref, f32[2,256,256]{2,1,0:T(8,128)S(1)} %get-tuple-element.85.table, f32[2,256,256]{2,1,0:T(8,128)S(1)} %low_chain.1.low_table, ...), custom_call_target="tpu_custom_call" | custom-call | tf_op jit(solution)/shard_map/middle_1/pallas_call | solution.py:286
  33.8 0.1 collective-permute-start.9
  34.0 1.5 %collective-permute-start.16 = (f32[4,2,16,256]{3,2,1,0:T(8,128)S(1)}, f32[4,2,16,256]{3,2,1,0:T(8,128)S(1)}, u32[]{:S(2)}, u32[]{:S(2)}) collective-permute-start(f32[4,2,16,256]{3,2,1,0:T(8,128)S(1)} %get-tuple-element.70), channel_id=1, source_target_pairs={{0,2},{1,3},{2,0},{3,1},{4,6},{5,7},{6,4},{7,5},{8,10},{9,11},{10,... | collective-permute-start | bytes 393224 | tf_op jit(solution)/shard_map/ppermute | solution.py:260
  35.4 0.3 collective-permute-start.8
  35.7 2.0 %collective-permute-done.14.refs_1_ = f32[4,2,16,256]{3,2,1,0:T(8,128)S(1)} collective-permute-done((f32[4,2,16,256]{3,2,1,0:T(8,128)S(1)}, f32[4,2,16,256]{3,2,1,0:T(8,128)S(1)}, u32[]{:S(2)}, u32[]{:S(2)}) %collective-permute-start.14) | collective-permute-done | bytes 131104 | tf_op jit(solution)/shard_map/ppermute | solution.py:260
  37.7 0.7 %collective-permute-start.20 = (f32[4,2,16,256]{3,2,1,0:T(8,128)S(1)}, f32[4,2,16,256]{3,2,1,0:T(8,128)S(1)}, u32[]{:S(2)}, u32[]{:S(2)}) collective-permute-start(f32[4,2,16,256]{3,2,1,0:T(8,128)S(1)} %get-tuple-element.77), channel_id=1, source_target_pairs={{0,12},{1,13},{2,14},{3,15},{4,8},{5,9},{6,10},{7,11},{8,4},{9,5},... | collective-permute-start | bytes 393224 | tf_op jit(solution)/shard_map/ppermute | solution.py:260
  38.4 0.5 collective-permute-done.15.refs_2_
  38.9 0.7 %collective-permute-done.9.refs_2_ = f32[4,2,16,256]{3,2,1,0:T(8,128)S(1)} collective-permute-done((f32[4,2,16,256]{3,2,1,0:T(8,128)S(1)}, f32[4,2,16,256]{3,2,1,0:T(8,128)S(1)}, u32[]{:S(2)}, u32[]{:S(2)}) %collective-permute-start.9) | collective-permute-done | bytes 131104 | tf_op jit(solution)/shard_map/ppermute | solution.py:260
  39.6 2.8 %collective-permute-done.16.refs_3_ = f32[4,2,16,256]{3,2,1,0:T(8,128)S(1)} collective-permute-done((f32[4,2,16,256]{3,2,1,0:T(8,128)S(1)}, f32[4,2,16,256]{3,2,1,0:T(8,128)S(1)}, u32[]{:S(2)}, u32[]{:S(2)}) %collective-permute-start.16) | collective-permute-done | bytes 131104 | tf_op jit(solution)/shard_map/ppermute | solution.py:260
  42.5 0.0 collective-permute-done.8.refs_1_
  42.5 1.1 %collective-permute-start.17 = (f32[4,2,16,256]{3,2,1,0:T(8,128)S(1)}, f32[4,2,16,256]{3,2,1,0:T(8,128)S(1)}, u32[]{:S(2)}, u32[]{:S(2)}) collective-permute-start(f32[4,2,16,256]{3,2,1,0:T(8,128)S(1)} %get-tuple-element.72), channel_id=1, source_target_pairs={{0,4},{1,5},{2,6},{3,7},{4,0},{5,1},{6,2},{7,3},{8,12},{9,13},{10,... | collective-permute-start | bytes 393224 | tf_op jit(solution)/shard_map/ppermute | solution.py:260
  43.7 1.6 %collective-permute-start.18 = (f32[4,2,16,256]{3,2,1,0:T(8,128)S(1)}, f32[4,2,16,256]{3,2,1,0:T(8,128)S(1)}, u32[]{:S(2)}, u32[]{:S(2)}) collective-permute-start(f32[4,2,16,256]{3,2,1,0:T(8,128)S(1)} %get-tuple-element.73), channel_id=1, source_target_pairs={{0,8},{1,9},{2,10},{3,11},{4,12},{5,13},{6,14},{7,15},{8,0},{9,1},... | collective-permute-start | bytes 393224 | tf_op jit(solution)/shard_map/ppermute | solution.py:260
  45.3 0.0 collective-permute-done.20.refs_3_
  45.3 0.1 collective-permute-start.21
  45.4 2.3 %collective-permute-start.22 = (f32[4,2,16,256]{3,2,1,0:T(8,128)S(1)}, f32[4,2,16,256]{3,2,1,0:T(8,128)S(1)}, u32[]{:S(2)}, u32[]{:S(2)}) collective-permute-start(f32[4,2,16,256]{3,2,1,0:T(8,128)S(1)} %get-tuple-element.81), channel_id=1, source_target_pairs={{0,3},{1,2},{2,1},{3,0},{4,7},{5,6},{6,5},{7,4},{8,11},{9,10},{10,... | collective-permute-start | bytes 393224 | tf_op jit(solution)/shard_map/ppermute | solution.py:260
  47.7 0.0 collective-permute-start.23
  47.8 1.9 %collective-permute-done.17.refs_1_ = f32[4,2,16,256]{3,2,1,0:T(8,128)S(1)} collective-permute-done((f32[4,2,16,256]{3,2,1,0:T(8,128)S(1)}, f32[4,2,16,256]{3,2,1,0:T(8,128)S(1)}, u32[]{:S(2)}, u32[]{:S(2)}) %collective-permute-start.17) | collective-permute-done | bytes 131104 | tf_op jit(solution)/shard_map/ppermute | solution.py:260
  49.7 3.1 %collective-permute-start.19 = (f32[4,2,16,256]{3,2,1,0:T(8,128)S(1)}, f32[4,2,16,256]{3,2,1,0:T(8,128)S(1)}, u32[]{:S(2)}, u32[]{:S(2)}) collective-permute-start(f32[4,2,16,256]{3,2,1,0:T(8,128)S(1)} %get-tuple-element.74), channel_id=1, source_target_pairs={{0,12},{1,13},{2,14},{3,15},{4,8},{5,9},{6,10},{7,11},{8,4},{9,5},... | collective-permute-start | bytes 393224 | tf_op jit(solution)/shard_map/ppermute | solution.py:260
  52.8 2.1 %collective-permute-done.18.refs_2_ = f32[4,2,16,256]{3,2,1,0:T(8,128)S(1)} collective-permute-done((f32[4,2,16,256]{3,2,1,0:T(8,128)S(1)}, f32[4,2,16,256]{3,2,1,0:T(8,128)S(1)}, u32[]{:S(2)}, u32[]{:S(2)}) %collective-permute-start.18) | collective-permute-done | bytes 131104 | tf_op jit(solution)/shard_map/ppermute | solution.py:260
  55.0 0.0 collective-permute-done.21.refs_1_
  55.0 0.0 collective-permute-done.22.refs_2_
  55.0 0.0 collective-permute-done.23.refs_3_
  55.0 1.4 %close_0.1.refs_4_ = f32[2,1024,128]{2,1,0:T(8,128)} custom-call(s32[1]{0:T(128)} %bitcast.me_ref, f32[2,256,256]{2,1,0:T(8,128)S(1)} %get-tuple-element.84.table, f32[4,2,16,256]{3,2,1,0:T(8,128)S(1)} %get-tuple-element.79.refs_0_, f32[4,2,16,256]{3,2,1,0:T(8,128)S(1)} %collective-permute-done.21.refs_1_, ...), custom_call_target="tpu_custom_call" | custom-call | tf_op jit(solution)/shard_map/close_0/pallas_call | solution.py:297
  56.4 0.2 collective-permute-done.19.refs_3_
  56.6 1.4 %close_1.1 = f32[2,1024,128]{2,1,0:T(8,128)} custom-call(s32[1]{0:T(128)} %bitcast.me_ref, f32[2,256,256]{2,1,0:T(8,128)S(1)} %get-tuple-element.84.table, f32[4,2,16,256]{3,2,1,0:T(8,128)S(1)} %get-tuple-element.71.refs_0_, f32[4,2,16,256]{3,2,1,0:T(8,128)S(1)} %collective-permute-done.17.refs_1_, ...), custom_call_target="tpu_custom_call", output_to_operand_aliasing={{}: (6, {})} | custom-call | tf_op jit(solution)/shard_map/close_1/pallas_call | solution.py:297
  (4 shorter events, 0.1 us)
Async XLA Ops:
  0.0 1.7 %copy-start.2 = (f32[1,2,131072]{2,1,0:T(2,128)S(1)}, f32[1,2,131072]{2,1,0:T(2,128)}, u32[]{:S(2)}) copy-start(f32[1,2,131072]{2,1,0:T(2,128)} %param.4) | copy-start | bytes 3145732
  1.7 12.6 %copy-start = (f32[3,2,2,256,256]{4,3,2,1,0:T(8,128)S(1)}, f32[3,2,2,256,256]{4,3,2,1,0:T(8,128)}, u32[]{:S(2)}) copy-start(f32[3,2,2,256,256]{4,3,2,1,0:T(8,128)} %table_ref.1) | copy-start | bytes 9437188
  1.8 12.5 %copy-start.1 = (s32[1,3]{1,0:T(1,128)S(1)}, s32[1,3]{1,0:T(1,128)}, u32[]{:S(2)}) copy-start(s32[1,3]{1,0:T(1,128)} %bits_ref.1) | copy-start | bytes 40
  2.4 8.5 %collective-permute-start = (f32[4,2,16,256]{3,2,1,0:T(8,128)S(1)}, f32[4,2,16,256]{3,2,1,0:T(8,128)S(1)}, u32[]{:S(2)}, u32[]{:S(2)}) collective-permute-start(f32[4,2,16,256]{3,2,1,0:T(8,128)S(1)} %get-tuple-element.47), channel_id=1, source_target_pairs={{0,4},{1,5},{2,6},{3,7},{4,0},{5,1},{6,2},{7,3},{8,12},{9,13},{10,... | collective-permute-start | bytes 393224 | tf_op jit(solution)/shard_map/ppermute | solution.py:260
  5.5 10.8 %collective-permute-start.1 = (f32[4,2,16,256]{3,2,1,0:T(8,128)S(1)}, f32[4,2,16,256]{3,2,1,0:T(8,128)S(1)}, u32[]{:S(2)}, u32[]{:S(2)}) collective-permute-start(f32[4,2,16,256]{3,2,1,0:T(8,128)S(1)} %get-tuple-element.48), channel_id=1, source_target_pairs={{0,8},{1,9},{2,10},{3,11},{4,12},{5,13},{6,14},{7,15},{8,0},{9,1},... | collective-permute-start | bytes 393224 | tf_op jit(solution)/shard_map/ppermute | solution.py:260
  8.7 7.6 %collective-permute-start.2 = (f32[4,2,16,256]{3,2,1,0:T(8,128)S(1)}, f32[4,2,16,256]{3,2,1,0:T(8,128)S(1)}, u32[]{:S(2)}, u32[]{:S(2)}) collective-permute-start(f32[4,2,16,256]{3,2,1,0:T(8,128)S(1)} %get-tuple-element.50), channel_id=1, source_target_pairs={{0,1},{1,0},{2,3},{3,2},{4,5},{5,4},{6,7},{7,6},{8,9},{9,8},{10,11... | collective-permute-start | bytes 393224 | tf_op jit(solution)/shard_map/ppermute | solution.py:260
  8.7 7.5 %collective-permute-start.3 = (f32[4,2,16,256]{3,2,1,0:T(8,128)S(1)}, f32[4,2,16,256]{3,2,1,0:T(8,128)S(1)}, u32[]{:S(2)}, u32[]{:S(2)}) collective-permute-start(f32[4,2,16,256]{3,2,1,0:T(8,128)S(1)} %get-tuple-element.51), channel_id=1, source_target_pairs={{0,3},{1,2},{2,1},{3,0},{4,7},{5,6},{6,5},{7,4},{8,11},{9,10},{10,... | collective-permute-start | bytes 393224 | tf_op jit(solution)/shard_map/ppermute | solution.py:260
  10.3 7.1 %collective-permute-start.4 = (f32[4,2,16,256]{3,2,1,0:T(8,128)S(1)}, f32[4,2,16,256]{3,2,1,0:T(8,128)S(1)}, u32[]{:S(2)}, u32[]{:S(2)}) collective-permute-start(f32[4,2,16,256]{3,2,1,0:T(8,128)S(1)} %get-tuple-element.52), channel_id=1, source_target_pairs={{0,2},{1,3},{2,0},{3,1},{4,6},{5,7},{6,4},{7,5},{8,10},{9,11},{10,... | collective-permute-start | bytes 393224 | tf_op jit(solution)/shard_map/ppermute | solution.py:260
  10.9 9.1 %collective-permute-start.10 = (f32[4,2,16,256]{3,2,1,0:T(8,128)S(1)}, f32[4,2,16,256]{3,2,1,0:T(8,128)S(1)}, u32[]{:S(2)}, u32[]{:S(2)}) collective-permute-start(f32[4,2,16,256]{3,2,1,0:T(8,128)S(1)} %get-tuple-element.61), channel_id=1, source_target_pairs={{0,12},{1,13},{2,14},{3,15},{4,8},{5,9},{6,10},{7,11},{8,4},{9,5},... | collective-permute-start | bytes 393224 | tf_op jit(solution)/shard_map/ppermute | solution.py:260
  17.5 6.6 %collective-permute-start.5 = (f32[4,2,16,256]{3,2,1,0:T(8,128)S(1)}, f32[4,2,16,256]{3,2,1,0:T(8,128)S(1)}, u32[]{:S(2)}, u32[]{:S(2)}) collective-permute-start(f32[4,2,16,256]{3,2,1,0:T(8,128)S(1)} %get-tuple-element.54), channel_id=1, source_target_pairs={{0,4},{1,5},{2,6},{3,7},{4,0},{5,1},{6,2},{7,3},{8,12},{9,13},{10,... | collective-permute-start | bytes 393224 | tf_op jit(solution)/shard_map/ppermute | solution.py:260
  18.0 11.0 %collective-permute-start.6 = (f32[4,2,16,256]{3,2,1,0:T(8,128)S(1)}, f32[4,2,16,256]{3,2,1,0:T(8,128)S(1)}, u32[]{:S(2)}, u32[]{:S(2)}) collective-permute-start(f32[4,2,16,256]{3,2,1,0:T(8,128)S(1)} %get-tuple-element.55), channel_id=1, source_target_pairs={{0,8},{1,9},{2,10},{3,11},{4,12},{5,13},{6,14},{7,15},{8,0},{9,1},... | collective-permute-start | bytes 393224 | tf_op jit(solution)/shard_map/ppermute | solution.py:260
  20.0 9.0 %collective-permute-start.11 = (f32[4,2,16,256]{3,2,1,0:T(8,128)S(1)}, f32[4,2,16,256]{3,2,1,0:T(8,128)S(1)}, u32[]{:S(2)}, u32[]{:S(2)}) collective-permute-start(f32[4,2,16,256]{3,2,1,0:T(8,128)S(1)} %get-tuple-element.64), channel_id=1, source_target_pairs={{0,1},{1,0},{2,3},{3,2},{4,5},{5,4},{6,7},{7,6},{8,9},{9,8},{10,11... | collective-permute-start | bytes 393224 | tf_op jit(solution)/shard_map/ppermute | solution.py:260
  20.1 8.9 %collective-permute-start.12 = (f32[4,2,16,256]{3,2,1,0:T(8,128)S(1)}, f32[4,2,16,256]{3,2,1,0:T(8,128)S(1)}, u32[]{:S(2)}, u32[]{:S(2)}) collective-permute-start(f32[4,2,16,256]{3,2,1,0:T(8,128)S(1)} %get-tuple-element.65), channel_id=1, source_target_pairs={{0,3},{1,2},{2,1},{3,0},{4,7},{5,6},{6,5},{7,4},{8,11},{9,10},{10,... | collective-permute-start | bytes 393224 | tf_op jit(solution)/shard_map/ppermute | solution.py:260
  21.7 7.3 %collective-permute-start.13 = (f32[4,2,16,256]{3,2,1,0:T(8,128)S(1)}, f32[4,2,16,256]{3,2,1,0:T(8,128)S(1)}, u32[]{:S(2)}, u32[]{:S(2)}) collective-permute-start(f32[4,2,16,256]{3,2,1,0:T(8,128)S(1)} %get-tuple-element.66), channel_id=1, source_target_pairs={{0,2},{1,3},{2,0},{3,1},{4,6},{5,7},{6,4},{7,5},{8,10},{9,11},{10,... | collective-permute-start | bytes 393224 | tf_op jit(solution)/shard_map/ppermute | solution.py:260
  24.1 8.5 %collective-permute-start.7 = (f32[4,2,16,256]{3,2,1,0:T(8,128)S(1)}, f32[4,2,16,256]{3,2,1,0:T(8,128)S(1)}, u32[]{:S(2)}, u32[]{:S(2)}) collective-permute-start(f32[4,2,16,256]{3,2,1,0:T(8,128)S(1)} %get-tuple-element.56), channel_id=1, source_target_pairs={{0,12},{1,13},{2,14},{3,15},{4,8},{5,9},{6,10},{7,11},{8,4},{9,5},... | collective-permute-start | bytes 393224 | tf_op jit(solution)/shard_map/ppermute | solution.py:260
  30.3 7.4 %collective-permute-start.14 = (f32[4,2,16,256]{3,2,1,0:T(8,128)S(1)}, f32[4,2,16,256]{3,2,1,0:T(8,128)S(1)}, u32[]{:S(2)}, u32[]{:S(2)}) collective-permute-start(f32[4,2,16,256]{3,2,1,0:T(8,128)S(1)} %get-tuple-element.67), channel_id=1, source_target_pairs={{0,4},{1,5},{2,6},{3,7},{4,0},{5,1},{6,2},{7,3},{8,12},{9,13},{10,... | collective-permute-start | bytes 393224 | tf_op jit(solution)/shard_map/ppermute | solution.py:260
  30.5 8.5 %collective-permute-start.15 = (f32[4,2,16,256]{3,2,1,0:T(8,128)S(1)}, f32[4,2,16,256]{3,2,1,0:T(8,128)S(1)}, u32[]{:S(2)}, u32[]{:S(2)}) collective-permute-start(f32[4,2,16,256]{3,2,1,0:T(8,128)S(1)} %get-tuple-element.68), channel_id=1, source_target_pairs={{0,8},{1,9},{2,10},{3,11},{4,12},{5,13},{6,14},{7,15},{8,0},{9,1},... | collective-permute-start | bytes 393224 | tf_op jit(solution)/shard_map/ppermute | solution.py:260
  33.8 5.8 %collective-permute-start.9 = (f32[4,2,16,256]{3,2,1,0:T(8,128)S(1)}, f32[4,2,16,256]{3,2,1,0:T(8,128)S(1)}, u32[]{:S(2)}, u32[]{:S(2)}) collective-permute-start(f32[4,2,16,256]{3,2,1,0:T(8,128)S(1)} %get-tuple-element.59), channel_id=1, source_target_pairs={{0,3},{1,2},{2,1},{3,0},{4,7},{5,6},{6,5},{7,4},{8,11},{9,10},{10,... | collective-permute-start | bytes 393224 | tf_op jit(solution)/shard_map/ppermute | solution.py:260
  34.0 8.5 %collective-permute-start.16 = (f32[4,2,16,256]{3,2,1,0:T(8,128)S(1)}, f32[4,2,16,256]{3,2,1,0:T(8,128)S(1)}, u32[]{:S(2)}, u32[]{:S(2)}) collective-permute-start(f32[4,2,16,256]{3,2,1,0:T(8,128)S(1)} %get-tuple-element.70), channel_id=1, source_target_pairs={{0,2},{1,3},{2,0},{3,1},{4,6},{5,7},{6,4},{7,5},{8,10},{9,11},{10,... | collective-permute-start | bytes 393224 | tf_op jit(solution)/shard_map/ppermute | solution.py:260
  35.4 7.0 %collective-permute-start.8 = (f32[4,2,16,256]{3,2,1,0:T(8,128)S(1)}, f32[4,2,16,256]{3,2,1,0:T(8,128)S(1)}, u32[]{:S(2)}, u32[]{:S(2)}) collective-permute-start(f32[4,2,16,256]{3,2,1,0:T(8,128)S(1)} %get-tuple-element.58), channel_id=1, source_target_pairs={{0,1},{1,0},{2,3},{3,2},{4,5},{5,4},{6,7},{7,6},{8,9},{9,8},{10,11... | collective-permute-start | bytes 393224 | tf_op jit(solution)/shard_map/ppermute | solution.py:260
  37.7 7.6 %collective-permute-start.20 = (f32[4,2,16,256]{3,2,1,0:T(8,128)S(1)}, f32[4,2,16,256]{3,2,1,0:T(8,128)S(1)}, u32[]{:S(2)}, u32[]{:S(2)}) collective-permute-start(f32[4,2,16,256]{3,2,1,0:T(8,128)S(1)} %get-tuple-element.77), channel_id=1, source_target_pairs={{0,12},{1,13},{2,14},{3,15},{4,8},{5,9},{6,10},{7,11},{8,4},{9,5},... | collective-permute-start | bytes 393224 | tf_op jit(solution)/shard_map/ppermute | solution.py:260
  42.5 7.2 %collective-permute-start.17 = (f32[4,2,16,256]{3,2,1,0:T(8,128)S(1)}, f32[4,2,16,256]{3,2,1,0:T(8,128)S(1)}, u32[]{:S(2)}, u32[]{:S(2)}) collective-permute-start(f32[4,2,16,256]{3,2,1,0:T(8,128)S(1)} %get-tuple-element.72), channel_id=1, source_target_pairs={{0,4},{1,5},{2,6},{3,7},{4,0},{5,1},{6,2},{7,3},{8,12},{9,13},{10,... | collective-permute-start | bytes 393224 | tf_op jit(solution)/shard_map/ppermute | solution.py:260
  43.7 11.3 %collective-permute-start.18 = (f32[4,2,16,256]{3,2,1,0:T(8,128)S(1)}, f32[4,2,16,256]{3,2,1,0:T(8,128)S(1)}, u32[]{:S(2)}, u32[]{:S(2)}) collective-permute-start(f32[4,2,16,256]{3,2,1,0:T(8,128)S(1)} %get-tuple-element.73), channel_id=1, source_target_pairs={{0,8},{1,9},{2,10},{3,11},{4,12},{5,13},{6,14},{7,15},{8,0},{9,1},... | collective-permute-start | bytes 393224 | tf_op jit(solution)/shard_map/ppermute | solution.py:260
  45.3 9.6 %collective-permute-start.21 = (f32[4,2,16,256]{3,2,1,0:T(8,128)S(1)}, f32[4,2,16,256]{3,2,1,0:T(8,128)S(1)}, u32[]{:S(2)}, u32[]{:S(2)}) collective-permute-start(f32[4,2,16,256]{3,2,1,0:T(8,128)S(1)} %get-tuple-element.80), channel_id=1, source_target_pairs={{0,1},{1,0},{2,3},{3,2},{4,5},{5,4},{6,7},{7,6},{8,9},{9,8},{10,11... | collective-permute-start | bytes 393224 | tf_op jit(solution)/shard_map/ppermute | solution.py:260
  45.4 9.5 %collective-permute-start.22 = (f32[4,2,16,256]{3,2,1,0:T(8,128)S(1)}, f32[4,2,16,256]{3,2,1,0:T(8,128)S(1)}, u32[]{:S(2)}, u32[]{:S(2)}) collective-permute-start(f32[4,2,16,256]{3,2,1,0:T(8,128)S(1)} %get-tuple-element.81), channel_id=1, source_target_pairs={{0,3},{1,2},{2,1},{3,0},{4,7},{5,6},{6,5},{7,4},{8,11},{9,10},{10,... | collective-permute-start | bytes 393224 | tf_op jit(solution)/shard_map/ppermute | solution.py:260
  47.7 7.2 %collective-permute-start.23 = (f32[4,2,16,256]{3,2,1,0:T(8,128)S(1)}, f32[4,2,16,256]{3,2,1,0:T(8,128)S(1)}, u32[]{:S(2)}, u32[]{:S(2)}) collective-permute-start(f32[4,2,16,256]{3,2,1,0:T(8,128)S(1)} %get-tuple-element.82), channel_id=1, source_target_pairs={{0,2},{1,3},{2,0},{3,1},{4,6},{5,7},{6,4},{7,5},{8,10},{9,11},{10,... | collective-permute-start | bytes 393224 | tf_op jit(solution)/shard_map/ppermute | solution.py:260
  49.7 6.9 %collective-permute-start.19 = (f32[4,2,16,256]{3,2,1,0:T(8,128)S(1)}, f32[4,2,16,256]{3,2,1,0:T(8,128)S(1)}, u32[]{:S(2)}, u32[]{:S(2)}) collective-permute-start(f32[4,2,16,256]{3,2,1,0:T(8,128)S(1)} %get-tuple-element.74), channel_id=1, source_target_pairs={{0,12},{1,13},{2,14},{3,15},{4,8},{5,9},{6,10},{7,11},{8,4},{9,5},... | collective-permute-start | bytes 393224 | tf_op jit(solution)/shard_map/ppermute | solution.py:260

commit v6 on v5

--- a/solution.py
+++ b/solution.py
@@ -9,7 +9,6 @@
 
 LANES = 128
 SUBLANES = 8
-PIECES = 1
 VMEM = pl.BlockSpec(memory_space=pltpu.VMEM)
 SMEM = pl.BlockSpec(memory_space=pltpu.SMEM)
 HBM = pl.BlockSpec(memory_space=pltpu.HBM)
@@ -157,10 +156,12 @@
             yield n, m, distance
 
 
-def rows_by_distance(table, me, under):
-    devices = table.shape[1] // under
+def rows_by_distance(parts, me, under):
+    devices = parts[0].shape[0] // under
     starts = [pl.multiple_of((me ^ d) * under, under) for d in range(devices)]
-    return [jnp.concatenate([table[c, pl.ds(at, under), :] for at in starts]) for c in range(2)]
+    return [
+        jnp.concatenate([part[pl.ds(at, under), :] for at in starts], axis=0) for part in parts
+    ]
 
 
 def gather(in_refs, held, me, layout):
@@ -172,10 +173,10 @@
     return halves(jnp.concatenate([held[0], held[1]], axis=0))
 
 
-def open_chunk_kernel(layout, me_ref, stem_ref, table, *out_refs):
+def open_chunk(layout, me_ref, stem_ref, parts, out_refs):
     under = out_refs[0].shape[2]
-    high = table.shape[-1]
-    matrix = left_halves(*rows_by_distance(table, me_ref[0], under))
+    high = parts[0].shape[0]
+    matrix = left_halves(*rows_by_distance(parts, me_ref[0], under))
     value = dot_halves(matrix, halves(read_stem(stem_ref, high)))
     for n, m, distance in distances(layout):
         for c in range(2):
@@ -183,6 +184,24 @@
             out_refs[n][m, c] = value[start : start + under]
 
 
+def open_chunk_kernel(layout, me_ref, stem_ref, table, *out_refs):
+    open_chunk(layout, me_ref, stem_ref, (table.at[0], table.at[1]), out_refs)
+
+
+def open_first_kernel(layout, me_ref, packed_ref, *refs):
+    *out_refs, table = refs
+    _, high, _ = table.shape
+    tiles = high // LANES
+    rows = packed_ref.shape[0] - 2 * high * tiles
+    matrix = packed_ref[rows:].reshape(2, high // SUBLANES, tiles, SUBLANES, LANES)
+    for c in range(2):
+        for t in range(tiles):
+            part = matrix[c, :, t].reshape(high, LANES)
+            table[c, :, t * LANES : (t + 1) * LANES] = part
+    parts = table.at[0], table.at[1]
+    open_chunk(layout, me_ref, packed_ref.at[pl.ds(0, rows)], parts, out_refs)
+
+
 def turn_kernel(old, new, *refs):
     place = {distance: (n, m) for n, m, distance in distances(old)}
     for n, m, distance in distances(new):
@@ -199,7 +218,7 @@
         @pl.when(n == 0)
         def high_modes():
             value = gather(in_refs, held, me_ref[0], old)
-            matrix = left_halves(*rows_by_distance(table, me_ref[0], under))
+            matrix = left_halves(*rows_by_distance((table.at[0], table.at[1]), me_ref[0], under))
             between[...] = dot_halves(matrix, value)
 
         @pl.when(n == 1)
@@ -214,28 +233,28 @@
     lax.fori_loop(0, 2, stage, 0)
 
 
-def close_chunk_kernel(r, layout, me_ref, table, *refs):
-    in_refs = refs[: len(layout)]
-    out_ref, held, stem, sems = refs[-4:]
-    pieces = sems.shape[0]
-    high, rows = table.shape[-1] // pieces, stem.shape[0] // pieces
-    gather(in_refs, held, me_ref[0], layout)
-
-    def copy(n):
-        at = pl.ds(n * rows, rows)
-        return pltpu.make_async_copy(stem.at[at], out_ref.at[r, at], sems.at[n])
-
-    def piece(n, carry):
-        some = pl.ds(n * high, high)
-        matrix = left_halves(table[0, some], table[1, some])
-        value = halves(jnp.concatenate([held[0], held[1]], axis=0))
-        write_stem(stem.at[pl.ds(n * rows, rows)], dot_halves(matrix, value), high)
-        copy(n).start()
-        return carry
-
-    lax.fori_loop(0, pieces, piece, 0)
-    for n in range(pieces):
-        copy(n).wait()
+def close_chunk(layout, me_ref, table, in_refs, held, stem):
+    value = gather(in_refs, held, me_ref[0], layout)
+    matrix = left_halves(table[0], table[1])
+    write_stem(stem, dot_halves(matrix, value), table.shape[-1])
+
+
+def close_first_kernel(layout, me_ref, table, *refs):
+    *in_refs, out_ref, held = refs
+    close_chunk(layout, me_ref, table, in_refs, held, out_ref)
+
+
+def close_last_kernel(layout, me_ref, table, *refs):
+    *in_refs, first_ref, out_ref, held, stem, sems = refs
+    copies = [
+        pltpu.make_async_copy(first_ref, out_ref.at[0], sems.at[0]),
+        pltpu.make_async_copy(stem, out_ref.at[1], sems.at[1]),
+    ]
+    copies[0].start()
+    close_chunk(layout, me_ref, table, in_refs, held, stem)
+    copies[1].start()
+    for copy in copies:
+        copy.wait()
 
 
 def chunks_by_permutes(laid, chain, hi_table):
@@ -272,15 +291,29 @@
             name=name,
         )(*values)
 
-    def open_chunk(r, layout, stem):
+    def open_chunk_0(layout):
+        tiles = high // LANES
+        matrix = hi_table[0].reshape(2, high // SUBLANES, SUBLANES, tiles, LANES)
+        matrix = matrix.transpose(0, 1, 3, 2, 4).reshape(-1, LANES)
+        return pl.pallas_call(
+            functools.partial(open_first_kernel, layout),
+            out_shape=blocks(layout),
+            in_specs=[SMEM, VMEM],
+            out_specs=(VMEM,) * len(layout),
+            scratch_shapes=[pltpu.VMEM((2, high, high), jnp.float32)],
+            compiler_params=SMALL,
+            name="open_0",
+        )(me, jnp.concatenate([laid[0], matrix], axis=0))
+
+    def open_chunk_1(layout, stem, table):
         return pl.pallas_call(
             functools.partial(open_chunk_kernel, layout),
             out_shape=blocks(layout),
             in_specs=[SMEM, VMEM, VMEM],
             out_specs=(VMEM,) * len(layout),
             compiler_params=SMALL,
-            name=f"open_{r}",
-        )(me, stem, hi_table[0])
+            name="open_1",
+        )(me, stem, table)
 
     def middle_chunk(r, old, new, values):
         return pl.pallas_call(
@@ -291,57 +324,67 @@
             scratch_shapes=[held, pltpu.VMEM((2 * high, low), jnp.float32)],
             compiler_params=SMALL,
             name=f"middle_{r}",
-        )(me, hi_table[1], chain, *values)
-
-    def close_chunk(r, layout, values, done=None):
+        )(me, later[1][1], chain, *values)
+
+    def close_chunk(r, layout, values, first=None):
+        if first is None:
+            return pl.pallas_call(
+                functools.partial(close_first_kernel, layout),
+                out_shape=jax.ShapeDtypeStruct(laid.shape[1:], jnp.float32),
+                in_specs=[SMEM, VMEM] + [VMEM] * len(layout),
+                out_specs=VMEM,
+                scratch_shapes=[held],
+                compiler_params=SMALL,
+                name=f"close_{r}",
+            )(me, later[1][2], *values)
         return pl.pallas_call(
-            functools.partial(close_chunk_kernel, r, layout),
+            functools.partial(close_last_kernel, layout),
             out_shape=jax.ShapeDtypeStruct(laid.shape, jnp.float32),
-            in_specs=[SMEM, VMEM] + [VMEM] * len(layout) + ([] if done is None else [HBM]),
+            in_specs=[SMEM, VMEM] + [VMEM] * len(layout) + [VMEM],
             out_specs=HBM,
-            scratch_shapes=[held, stem, pltpu.SemaphoreType.DMA((PIECES,))],
-            input_output_aliases={} if done is None else {2 + len(layout): 0},
+            scratch_shapes=[held, stem, pltpu.SemaphoreType.DMA((2,))],
             compiler_params=SMALL,
             name=f"close_{r}",
-        )(me, hi_table[2], *values, *([] if done is None else [done]))
-
-    L00z = layout_over((0, 4, 8, 12), (0, 1, 3, 2))
-    L00p = layout_over((0, 1, 3, 2), (0, 4, 8, 12))
-    L01z = layout_over((0, 4, 8, 12), (0, 1, 3, 2))
-    L01p = layout_over((0, 1, 3, 2), (0, 4, 8, 12))
-    L10p = layout_over((0, 1, 3, 2), (0, 4, 8, 12))
-    L10z = layout_over((0, 4, 8, 12), (0, 1, 3, 2))
+        )(me, later[1][2], *values, first)
+
+    L00z = layout_over((0, 4, 8, 12), (0, 3, 1, 2))
+    L00p = layout_over((0, 3, 1, 2), (0, 4, 8, 12))
+    L01z = layout_over((0, 4, 8, 12), (0, 1, 2, 3))
+    L01p = layout_over((0, 1, 2, 3), (0, 4, 8, 12))
+    L10p = layout_over((0, 2, 1, 3), (0, 4, 8, 12))
+    L10z = layout_over((0, 4, 8, 12), (0, 2, 1, 3))
     L11p = layout_over((0, 1, 3, 2), (0, 4, 8, 12))
     L11z = layout_over((0, 4, 8, 12), (0, 1, 3, 2))
-    open_0 = open_chunk(0, L00z, laid[0])
-    open_1 = open_chunk(1, L10p, tie(laid[1], open_0[0]))
+    open_0 = open_chunk_0(L00z)
+    later = tie((laid, hi_table), open_0[0])
+    open_1 = open_chunk_1(L10p, later[0][1], later[1][0])
     open_0_1 = swap(open_0[1], 4)
     open_0_2 = swap(open_0[2], 8)
     open_0_3 = swap(open_0[3], 12)
-    open_1_1 = swap(open_1[1], 1)
-    open_1_2 = swap(open_1[2], 3)
-    open_1_3 = swap(open_1[3], 2)
+    turn_001 = turn(L00z, L00p, [open_0[0], open_0_1, open_0_2, open_0_3], "turn_001")
+    turn_001_1 = swap(turn_001[1], 3)
+    turn_001_2 = swap(turn_001[2], 1)
+    turn_001_3 = swap(turn_001[3], 2)
+    open_1_1 = swap(open_1[1], 2)
+    open_1_2 = swap(open_1[2], 1)
+    open_1_3 = swap(open_1[3], 3)
     turn_101 = turn(L10p, L10z, tied([open_1[0], open_1_1, open_1_2, open_1_3], 0, (open_0_1, open_0_2, chain)), "turn_101")
-    turn_001 = turn(L00z, L00p, tied([open_0[0], open_0_1, open_0_2, open_0_3], 0, turn_101[0]), "turn_001")
-    turn_001_1 = swap(turn_001[1], 1)
-    turn_001_2 = swap(turn_001[2], 3)
-    turn_001_3 = swap(turn_001[3], 2)
     turn_101_1 = swap(turn_101[1], 4)
     turn_101_2 = swap(turn_101[2], 8)
     middle_0 = middle_chunk(0, L00p, L01z, tied([turn_001[0], turn_001_1, turn_001_2, turn_001_3], 0, (turn_101_1, turn_101_2)))
     middle_0_1 = swap(middle_0[1], 4)
     middle_0_2 = swap(middle_0[2], 8)
     middle_0_3 = swap(middle_0[3], 12)
+    turn_011 = turn(L01z, L01p, [middle_0[0], middle_0_1, middle_0_2, middle_0_3], "turn_011")
+    turn_011_1 = swap(turn_011[1], 1)
+    turn_011_2 = swap(turn_011[2], 2)
+    turn_011_3 = swap(turn_011[3], 3)
     turn_101_3 = swap(turn_101[3], 12)
     middle_1 = middle_chunk(1, L10z, L11p, [turn_101[0], turn_101_1, turn_101_2, turn_101_3])
     middle_1_1 = swap(middle_1[1], 1)
     middle_1_2 = swap(middle_1[2], 3)
     middle_1_3 = swap(middle_1[3], 2)
     turn_111 = turn(L11p, L11z, tied([middle_1[0], middle_1_1, middle_1_2, middle_1_3], 2, (middle_0_1, middle_0_2)), "turn_111")
-    turn_011 = turn(L01z, L01p, tied([middle_0[0], middle_0_1, middle_0_2, middle_0_3], 0, turn_111[0]), "turn_011")
-    turn_011_1 = swap(turn_011[1], 1)
-    turn_011_2 = swap(turn_011[2], 3)
-    turn_011_3 = swap(turn_011[3], 2)
     turn_111_1 = swap(turn_111[1], 4)
     turn_111_2 = swap(turn_111[2], 8)
     close_0 = close_chunk(0, L01p, tied([turn_011[0], turn_011_1, turn_011_2, turn_011_3], 0, (turn_111_1, turn_111_2)))

time: 58.1 us -> 57 us (0.981)
  waiting for transfers between devices: 15.8 us -> 14.5 us
  starting transfers between devices: 31.6 us -> 32.9 us
  Pallas kernels: 8.59 us -> 7.81 us
    squeeze x1 -> x2, local copies, waits for them, and re-layouts: 1.55 us -> 0.21 us  [chunks_by_permutes(): open_1 = open_chunk_1(L10p, later[0][1], later[1][0])]
    ppermute x24, waiting for transfers between devices: 15.8 us -> 14.5 us  [swap(): return lax.ppermute(value, 'stem', [(i, i ^ step) for i in range(devices)])]
    ppermute x24, starting transfers between devices: 31.6 us -> 32.9 us  [swap(): return lax.ppermute(value, 'stem', [(i, i ^ step) for i in range(devices)])]
    slice x1 -> x3, local copies, waits for them, and re-layouts: 0.07 us -> 1.2 us  [the longest x1 1.13 us: open_chunk_0(): laid[0]]
    pallas_call x4, Pallas kernels: 4.04 us -> 3.27 us  [the longest x1 1.43 us: close_chunk(): pl.pallas_call(functools.partial(close_last_kernel, layout), out_shape=ja...]
  transfers between devices with their start and end apart: 24 -> 24, of which waited for: 10 -> 11; matrix products, arithmetic and copies ran while one was open for 0% -> 0% of each run, Pallas kernels for 11% -> 10%
where the time goes in v6:
time: 57 us; the launch traced here: 56.9 us
  starting transfers between devices  32.9 us (58%)
  waiting for transfers between devices  14.5 us (25%)
  Pallas kernels  7.81 us (14%)
  local copies, waits for them, and re-layouts  1.43 us (3%)
    ppermute x24, starting transfers between devices, swap(): return lax.ppermute(value, 'stem', [(i, i ^ step) for i in range(devices)])  32.9 us
    ppermute x24, waiting for transfers between devices, swap(): return lax.ppermute(value, 'stem', [(i, i ^ step) for i in range(devices)])  14.5 us
    pallas_call x2, Pallas kernels, middle_chunk(): pl.pallas_call(functools.partial(middle_chunk_kernel, old, new), out_shap...  2.46 us
    pallas_call x1, Pallas kernels, one_slice(): pl.pallas_call(chain_kernel, out_shape=jax.ShapeDtypeStruct((2, low, low)...  1.94 us
    pallas_call x1, Pallas kernels, close_chunk(): pl.pallas_call(functools.partial(close_last_kernel, layout), out_shape=ja...  1.43 us
  transfers between devices with their start and end apart: 24, of which 11 were waited for; matrix products, arithmetic and copies ran while one was open for 0% of the time, Pallas kernels for 10%

profile of v6, /device:TPU:0, one launch (start us, length us, event | category | flops | bytes accessed | tf_op | source)
XLA Modules:
  0.0 56.9 jit_solution(16764357509573713982)
XLA Ops:
  0.0 1.1 %slice.27 = f32[512,2,128]{2,1,0:T(2,128)S(1)} slice(f32[1024,2,128]{2,1,0:T(2,128)} %bitcast.27), slice={[0:512], [0:2], [0:128]} | slice | bytes 1048576 | tf_op jit(solution)/shard_map/slice | solution.py:306
  1.1 0.1 slice-done
  1.2 0.1 pad_maximum_fusion.packed_ref
  1.3 0.0 copy-start.3
  1.3 0.6 %open_0.1 = (f32[4,2,16,256]{3,2,1,0:T(8,128)S(1)}, f32[4,2,16,256]{3,2,1,0:T(8,128)S(1)}, f32[4,2,16,256]{3,2,1,0:T(8,128)S(1)}, f32[4,2,16,256]{3,2,1,0:T(8,128)S(1)}) custom-call(s32[1]{0:T(128)} %bitcast.me_ref, f32[2048,128]{1,0:T(8,128)S(1)} %pad_maximum_fusion.packed_ref), custom_call_target="tpu_custom_call" | custom-call | tf_op jit(solution)/shard_map/open_0/pallas_call | solution.py:298
  1.9 3.1 %collective-permute-start = (f32[4,2,16,256]{3,2,1,0:T(8,128)S(1)}, f32[4,2,16,256]{3,2,1,0:T(8,128)S(1)}, u32[]{:S(2)}, u32[]{:S(2)}) collective-permute-start(f32[4,2,16,256]{3,2,1,0:T(8,128)S(1)} %get-tuple-element.47), channel_id=1, source_target_pairs={{0,4},{1,5},{2,6},{3,7},{4,0},{5,1},{6,2},{7,3},{8,12},{9,13},{10,... | collective-permute-start | bytes 393224 | tf_op jit(solution)/shard_map/ppermute | solution.py:279
  5.0 2.6 %collective-permute-start.1 = (f32[4,2,16,256]{3,2,1,0:T(8,128)S(1)}, f32[4,2,16,256]{3,2,1,0:T(8,128)S(1)}, u32[]{:S(2)}, u32[]{:S(2)}) collective-permute-start(f32[4,2,16,256]{3,2,1,0:T(8,128)S(1)} %get-tuple-element.48), channel_id=1, source_target_pairs={{0,8},{1,9},{2,10},{3,11},{4,12},{5,13},{6,14},{7,15},{8,0},{9,1},... | collective-permute-start | bytes 393224 | tf_op jit(solution)/shard_map/ppermute | solution.py:279
  7.6 0.0 copy-done.2
  7.6 0.2 slice_bitcast_fusion
  7.8 0.0 copy-done.3
  7.8 0.0 copy-start.1
  7.8 0.6 %open_1.1 = (f32[4,2,16,256]{3,2,1,0:T(8,128)S(1)}, f32[4,2,16,256]{3,2,1,0:T(8,128)S(1)}, f32[4,2,16,256]{3,2,1,0:T(8,128)S(1)}, f32[4,2,16,256]{3,2,1,0:T(8,128)S(1)}) custom-call(s32[1]{0:T(128)} %bitcast.me_ref, f32[1024,128]{1,0:T(8,128)S(1)} %slice_bitcast_fusion.1.stem_ref, f32[2,256,256]{2,1,0:T(8,128)S(1)} %get-tuple-element.81.table), custom_call_target="tpu_custom_call" | custom-call | tf_op jit(solution)/shard_map/open_1/pallas_call | solution.py:309
  8.4 1.6 %collective-permute-start.2 = (f32[4,2,16,256]{3,2,1,0:T(8,128)S(1)}, f32[4,2,16,256]{3,2,1,0:T(8,128)S(1)}, u32[]{:S(2)}, u32[]{:S(2)}) collective-permute-start(f32[4,2,16,256]{3,2,1,0:T(8,128)S(1)} %get-tuple-element.50), channel_id=1, source_target_pairs={{0,2},{1,3},{2,0},{3,1},{4,6},{5,7},{6,4},{7,5},{8,10},{9,11},{10,... | collective-permute-start | bytes 393224 | tf_op jit(solution)/shard_map/ppermute | solution.py:279
  10.0 0.0 collective-permute-start.3
  10.0 0.6 %collective-permute-start.4 = (f32[4,2,16,256]{3,2,1,0:T(8,128)S(1)}, f32[4,2,16,256]{3,2,1,0:T(8,128)S(1)}, u32[]{:S(2)}, u32[]{:S(2)}) collective-permute-start(f32[4,2,16,256]{3,2,1,0:T(8,128)S(1)} %get-tuple-element.52), channel_id=1, source_target_pairs={{0,3},{1,2},{2,1},{3,0},{4,7},{5,6},{6,5},{7,4},{8,11},{9,10},{10,... | collective-permute-start | bytes 393224 | tf_op jit(solution)/shard_map/ppermute | solution.py:279
  10.7 0.0 collective-permute-done.refs_1_
  10.7 3.2 %collective-permute-start.10 = (f32[4,2,16,256]{3,2,1,0:T(8,128)S(1)}, f32[4,2,16,256]{3,2,1,0:T(8,128)S(1)}, u32[]{:S(2)}, u32[]{:S(2)}) collective-permute-start(f32[4,2,16,256]{3,2,1,0:T(8,128)S(1)} %get-tuple-element.60), channel_id=1, source_target_pairs={{0,12},{1,13},{2,14},{3,15},{4,8},{5,9},{6,10},{7,11},{8,4},{9,5},... | collective-permute-start | bytes 393224 | tf_op jit(solution)/shard_map/ppermute | solution.py:279
  13.8 0.0 copy-done
  13.8 1.9 %low_chain.1.low_table = f32[2,256,256]{2,1,0:T(8,128)S(1)} custom-call(s32[1,3]{1,0:T(1,128)S(1)} %copy-done.1, f32[3,2,2,256,256]{4,3,2,1,0:T(8,128)S(1)} %copy-done), custom_call_target="tpu_custom_call" | custom-call | tf_op jit(solution)/shard_map/low_chain/pallas_call | solution.py:419
  15.8 0.0 collective-permute-done.1.refs_2_
  15.8 0.0 collective-permute-done.2.refs_1_
  15.8 0.0 collective-permute-done.3.refs_2_
  15.8 0.0 collective-permute-done.4.refs_3_
  15.9 0.5 collective-permute-start.5
  16.3 3.2 %collective-permute-start.6 = (f32[4,2,16,256]{3,2,1,0:T(8,128)S(1)}, f32[4,2,16,256]{3,2,1,0:T(8,128)S(1)}, u32[]{:S(2)}, u32[]{:S(2)}) collective-permute-start(f32[4,2,16,256]{3,2,1,0:T(8,128)S(1)} %get-tuple-element.55), channel_id=1, source_target_pairs={{0,8},{1,9},{2,10},{3,11},{4,12},{5,13},{6,14},{7,15},{8,0},{9,1},... | collective-permute-start | bytes 393224 | tf_op jit(solution)/shard_map/ppermute | solution.py:279
  19.5 0.0 collective-permute-done.10.refs_3_
  19.6 0.1 collective-permute-start.11
  19.6 1.6 %collective-permute-start.12 = (f32[4,2,16,256]{3,2,1,0:T(8,128)S(1)}, f32[4,2,16,256]{3,2,1,0:T(8,128)S(1)}, u32[]{:S(2)}, u32[]{:S(2)}) collective-permute-start(f32[4,2,16,256]{3,2,1,0:T(8,128)S(1)} %get-tuple-element.64), channel_id=1, source_target_pairs={{0,1},{1,0},{2,3},{3,2},{4,5},{5,4},{6,7},{7,6},{8,9},{9,8},{10,11... | collective-permute-start | bytes 393224 | tf_op jit(solution)/shard_map/ppermute | solution.py:279
  21.2 0.5 collective-permute-start.13
  21.8 1.8 %collective-permute-done.5.refs_1_ = f32[4,2,16,256]{3,2,1,0:T(8,128)S(1)} collective-permute-done((f32[4,2,16,256]{3,2,1,0:T(8,128)S(1)}, f32[4,2,16,256]{3,2,1,0:T(8,128)S(1)}, u32[]{:S(2)}, u32[]{:S(2)}) %collective-permute-start.5) | collective-permute-done | bytes 131104 | tf_op jit(solution)/shard_map/ppermute | solution.py:279
  23.6 2.1 %collective-permute-start.7 = (f32[4,2,16,256]{3,2,1,0:T(8,128)S(1)}, f32[4,2,16,256]{3,2,1,0:T(8,128)S(1)}, u32[]{:S(2)}, u32[]{:S(2)}) collective-permute-start(f32[4,2,16,256]{3,2,1,0:T(8,128)S(1)} %get-tuple-element.56), channel_id=1, source_target_pairs={{0,12},{1,13},{2,14},{3,15},{4,8},{5,9},{6,10},{7,11},{8,4},{9,5},... | collective-permute-start | bytes 393224 | tf_op jit(solution)/shard_map/ppermute | solution.py:279
  25.7 1.0 %collective-permute-done.6.refs_2_ = f32[4,2,16,256]{3,2,1,0:T(8,128)S(1)} collective-permute-done((f32[4,2,16,256]{3,2,1,0:T(8,128)S(1)}, f32[4,2,16,256]{3,2,1,0:T(8,128)S(1)}, u32[]{:S(2)}, u32[]{:S(2)}) %collective-permute-start.6) | collective-permute-done | bytes 131104 | tf_op jit(solution)/shard_map/ppermute | solution.py:279
  26.7 0.0 collective-permute-done.11.refs_1_
  26.7 0.0 collective-permute-done.12.refs_2_
  26.7 1.5 %collective-permute-done.13.refs_3_ = f32[4,2,16,256]{3,2,1,0:T(8,128)S(1)} collective-permute-done((f32[4,2,16,256]{3,2,1,0:T(8,128)S(1)}, f32[4,2,16,256]{3,2,1,0:T(8,128)S(1)}, u32[]{:S(2)}, u32[]{:S(2)}) %collective-permute-start.13) | collective-permute-done | bytes 131104 | tf_op jit(solution)/shard_map/ppermute | solution.py:279
  28.2 1.2 %middle_0.1 = (f32[4,2,16,256]{3,2,1,0:T(8,128)S(1)}, f32[4,2,16,256]{3,2,1,0:T(8,128)S(1)}, f32[4,2,16,256]{3,2,1,0:T(8,128)S(1)}, f32[4,2,16,256]{3,2,1,0:T(8,128)S(1)}) custom-call(s32[1]{0:T(128)} %bitcast.me_ref, f32[2,256,256]{2,1,0:T(8,128)S(1)} %get-tuple-element.82.table, f32[2,256,256]{2,1,0:T(8,128)S(1)} %low_chain.1.low_table, ...), custom_call_target="tpu_custom_call" | custom-call | tf_op jit(solution)/shard_map/middle_0/pallas_call | solution.py:319
  29.5 0.4 collective-permute-start.14
  29.9 1.5 %collective-permute-start.15 = (f32[4,2,16,256]{3,2,1,0:T(8,128)S(1)}, f32[4,2,16,256]{3,2,1,0:T(8,128)S(1)}, u32[]{:S(2)}, u32[]{:S(2)}) collective-permute-start(f32[4,2,16,256]{3,2,1,0:T(8,128)S(1)} %get-tuple-element.67), channel_id=1, source_target_pairs={{0,8},{1,9},{2,10},{3,11},{4,12},{5,13},{6,14},{7,15},{8,0},{9,1},... | collective-permute-start | bytes 393224 | tf_op jit(solution)/shard_map/ppermute | solution.py:279
  31.4 0.0 collective-permute-done.7.refs_3_
  31.4 1.2 %middle_1.1 = (f32[4,2,16,256]{3,2,1,0:T(8,128)S(1)}, f32[4,2,16,256]{3,2,1,0:T(8,128)S(1)}, f32[4,2,16,256]{3,2,1,0:T(8,128)S(1)}, f32[4,2,16,256]{3,2,1,0:T(8,128)S(1)}) custom-call(s32[1]{0:T(128)} %bitcast.me_ref, f32[2,256,256]{2,1,0:T(8,128)S(1)} %get-tuple-element.82.table, f32[2,256,256]{2,1,0:T(8,128)S(1)} %low_chain.1.low_table, ...), custom_call_target="tpu_custom_call" | custom-call | tf_op jit(solution)/shard_map/middle_1/pallas_call | solution.py:319
  32.6 0.1 collective-permute-start.9
  32.7 1.2 %collective-permute-start.16 = (f32[4,2,16,256]{3,2,1,0:T(8,128)S(1)}, f32[4,2,16,256]{3,2,1,0:T(8,128)S(1)}, u32[]{:S(2)}, u32[]{:S(2)}) collective-permute-start(f32[4,2,16,256]{3,2,1,0:T(8,128)S(1)} %get-tuple-element.69), channel_id=1, source_target_pairs={{0,2},{1,3},{2,0},{3,1},{4,6},{5,7},{6,4},{7,5},{8,10},{9,11},{10,... | collective-permute-start | bytes 393224 | tf_op jit(solution)/shard_map/ppermute | solution.py:279
  33.9 0.6 %collective-permute-start.8 = (f32[4,2,16,256]{3,2,1,0:T(8,128)S(1)}, f32[4,2,16,256]{3,2,1,0:T(8,128)S(1)}, u32[]{:S(2)}, u32[]{:S(2)}) collective-permute-start(f32[4,2,16,256]{3,2,1,0:T(8,128)S(1)} %get-tuple-element.58), channel_id=1, source_target_pairs={{0,1},{1,0},{2,3},{3,2},{4,5},{5,4},{6,7},{7,6},{8,9},{9,8},{10,11... | collective-permute-start | bytes 393224 | tf_op jit(solution)/shard_map/ppermute | solution.py:279
  34.5 3.3 %collective-permute-done.14.refs_1_ = f32[4,2,16,256]{3,2,1,0:T(8,128)S(1)} collective-permute-done((f32[4,2,16,256]{3,2,1,0:T(8,128)S(1)}, f32[4,2,16,256]{3,2,1,0:T(8,128)S(1)}, u32[]{:S(2)}, u32[]{:S(2)}) %collective-permute-start.14) | collective-permute-done | bytes 131104 | tf_op jit(solution)/shard_map/ppermute | solution.py:279
  37.8 0.0 collective-permute-start.20
  37.8 0.0 collective-permute-done.15.refs_2_
  37.8 0.7 %collective-permute-done.9.refs_2_ = f32[4,2,16,256]{3,2,1,0:T(8,128)S(1)} collective-permute-done((f32[4,2,16,256]{3,2,1,0:T(8,128)S(1)}, f32[4,2,16,256]{3,2,1,0:T(8,128)S(1)}, u32[]{:S(2)}, u32[]{:S(2)}) %collective-permute-start.9) | collective-permute-done | bytes 131104 | tf_op jit(solution)/shard_map/ppermute | solution.py:279
  38.5 2.4 %collective-permute-done.16.refs_3_ = f32[4,2,16,256]{3,2,1,0:T(8,128)S(1)} collective-permute-done((f32[4,2,16,256]{3,2,1,0:T(8,128)S(1)}, f32[4,2,16,256]{3,2,1,0:T(8,128)S(1)}, u32[]{:S(2)}, u32[]{:S(2)}) %collective-permute-start.16) | collective-permute-done | bytes 131104 | tf_op jit(solution)/shard_map/ppermute | solution.py:279
  40.9 0.0 collective-permute-done.8.refs_1_
  40.9 1.7 %collective-permute-start.17 = (f32[4,2,16,256]{3,2,1,0:T(8,128)S(1)}, f32[4,2,16,256]{3,2,1,0:T(8,128)S(1)}, u32[]{:S(2)}, u32[]{:S(2)}) collective-permute-start(f32[4,2,16,256]{3,2,1,0:T(8,128)S(1)} %get-tuple-element.71), channel_id=1, source_target_pairs={{0,4},{1,5},{2,6},{3,7},{4,0},{5,1},{6,2},{7,3},{8,12},{9,13},{10,... | collective-permute-start | bytes 393224 | tf_op jit(solution)/shard_map/ppermute | solution.py:279
  42.6 3.2 %collective-permute-start.18 = (f32[4,2,16,256]{3,2,1,0:T(8,128)S(1)}, f32[4,2,16,256]{3,2,1,0:T(8,128)S(1)}, u32[]{:S(2)}, u32[]{:S(2)}) collective-permute-start(f32[4,2,16,256]{3,2,1,0:T(8,128)S(1)} %get-tuple-element.72), channel_id=1, source_target_pairs={{0,8},{1,9},{2,10},{3,11},{4,12},{5,13},{6,14},{7,15},{8,0},{9,1},... | collective-permute-start | bytes 393224 | tf_op jit(solution)/shard_map/ppermute | solution.py:279
  45.8 0.0 collective-permute-done.20.refs_3_
  45.9 0.1 collective-permute-start.21
  46.0 0.1 collective-permute-start.22
  46.0 1.8 %collective-permute-start.23 = (f32[4,2,16,256]{3,2,1,0:T(8,128)S(1)}, f32[4,2,16,256]{3,2,1,0:T(8,128)S(1)}, u32[]{:S(2)}, u32[]{:S(2)}) collective-permute-start(f32[4,2,16,256]{3,2,1,0:T(8,128)S(1)} %get-tuple-element.80), channel_id=1, source_target_pairs={{0,3},{1,2},{2,1},{3,0},{4,7},{5,6},{6,5},{7,4},{8,11},{9,10},{10,... | collective-permute-start | bytes 393224 | tf_op jit(solution)/shard_map/ppermute | solution.py:279
  47.8 0.1 collective-permute-done.17.refs_1_
  47.9 3.2 %collective-permute-start.19 = (f32[4,2,16,256]{3,2,1,0:T(8,128)S(1)}, f32[4,2,16,256]{3,2,1,0:T(8,128)S(1)}, u32[]{:S(2)}, u32[]{:S(2)}) collective-permute-start(f32[4,2,16,256]{3,2,1,0:T(8,128)S(1)} %get-tuple-element.73), channel_id=1, source_target_pairs={{0,12},{1,13},{2,14},{3,15},{4,8},{5,9},{6,10},{7,11},{8,4},{9,5},... | collective-permute-start | bytes 393224 | tf_op jit(solution)/shard_map/ppermute | solution.py:279
  51.1 0.9 %collective-permute-done.18.refs_2_ = f32[4,2,16,256]{3,2,1,0:T(8,128)S(1)} collective-permute-done((f32[4,2,16,256]{3,2,1,0:T(8,128)S(1)}, f32[4,2,16,256]{3,2,1,0:T(8,128)S(1)}, u32[]{:S(2)}, u32[]{:S(2)}) %collective-permute-start.18) | collective-permute-done | bytes 131104 | tf_op jit(solution)/shard_map/ppermute | solution.py:279
  52.0 0.0 collective-permute-done.21.refs_1_
  52.0 0.3 collective-permute-done.22.refs_2_
  52.3 1.9 %collective-permute-done.23.refs_3_ = f32[4,2,16,256]{3,2,1,0:T(8,128)S(1)} collective-permute-done((f32[4,2,16,256]{3,2,1,0:T(8,128)S(1)}, f32[4,2,16,256]{3,2,1,0:T(8,128)S(1)}, u32[]{:S(2)}, u32[]{:S(2)}) %collective-permute-start.23) | collective-permute-done | bytes 131104 | tf_op jit(solution)/shard_map/ppermute | solution.py:279
  54.2 0.6 %close_0.1.refs_4_ = f32[1024,128]{1,0:T(8,128)S(1)} custom-call(s32[1]{0:T(128)} %bitcast.me_ref, f32[2,256,256]{2,1,0:T(8,128)S(1)} %get-tuple-element.83.table, f32[4,2,16,256]{3,2,1,0:T(8,128)S(1)} %get-tuple-element.77.refs_0_, f32[4,2,16,256]{3,2,1,0:T(8,128)S(1)} %collective-permute-done.21.refs_1_, ...), custom_call_target="tpu_custom_call" | custom-call | tf_op jit(solution)/shard_map/close_0/pallas_call | solution.py:331
  54.8 0.6 %collective-permute-done.19.refs_3_ = f32[4,2,16,256]{3,2,1,0:T(8,128)S(1)} collective-permute-done((f32[4,2,16,256]{3,2,1,0:T(8,128)S(1)}, f32[4,2,16,256]{3,2,1,0:T(8,128)S(1)}, u32[]{:S(2)}, u32[]{:S(2)}) %collective-permute-start.19) | collective-permute-done | bytes 131104 | tf_op jit(solution)/shard_map/ppermute | solution.py:279
  55.5 1.4 %close_1.1 = f32[2,1024,128]{2,1,0:T(8,128)} custom-call(s32[1]{0:T(128)} %bitcast.me_ref, f32[2,256,256]{2,1,0:T(8,128)S(1)} %get-tuple-element.83.table, f32[4,2,16,256]{3,2,1,0:T(8,128)S(1)} %get-tuple-element.70.refs_0_, f32[4,2,16,256]{3,2,1,0:T(8,128)S(1)} %collective-permute-done.17.refs_1_, f32[4,2,16,256]{3,2,1,0:T(8,128)S(1)} %collective-permute-done.18.refs_2_, ...), custom_call_target="tpu_custom_call" | custom-call | tf_op jit(solution)/shard_map/close_1/pallas_call | solution.py:340
  (9 shorter events, 0.2 us)
Async XLA Ops:
  0.0 1.2 %slice-start = ((f32[3,2,256,256]{3,2,1,0:T(8,128)}), f32[1,2,256,256]{3,2,1,0:T(8,128)S(1)}, s32[]{:S(2)}) async-start(f32[3,2,256,256]{3,2,1,0:T(8,128)} %param.6), calls=%async_computation | async-start | bytes 1048576 | tf_op jit(solution)/shard_map/slice | solution.py:296
  1.2 6.4 %copy-start.2 = (f32[3,2,256,256]{3,2,1,0:T(8,128)S(1)}, f32[3,2,256,256]{3,2,1,0:T(8,128)}, u32[]{:S(2)}) copy-start(f32[3,2,256,256]{3,2,1,0:T(8,128)} %param.6) | copy-start | bytes 4718596
  1.3 6.5 %copy-start.3 = (f32[1,2,131072]{2,1,0:T(2,128)S(1)}, f32[1,2,131072]{2,1,0:T(2,128)}, u32[]{:S(2)}) copy-start(f32[1,2,131072]{2,1,0:T(2,128)} %param.4) | copy-start | bytes 3145732
  1.9 8.7 %collective-permute-start = (f32[4,2,16,256]{3,2,1,0:T(8,128)S(1)}, f32[4,2,16,256]{3,2,1,0:T(8,128)S(1)}, u32[]{:S(2)}, u32[]{:S(2)}) collective-permute-start(f32[4,2,16,256]{3,2,1,0:T(8,128)S(1)} %get-tuple-element.47), channel_id=1, source_target_pairs={{0,4},{1,5},{2,6},{3,7},{4,0},{5,1},{6,2},{7,3},{8,12},{9,13},{10,... | collective-permute-start | bytes 393224 | tf_op jit(solution)/shard_map/ppermute | solution.py:279
  5.0 10.8 %collective-permute-start.1 = (f32[4,2,16,256]{3,2,1,0:T(8,128)S(1)}, f32[4,2,16,256]{3,2,1,0:T(8,128)S(1)}, u32[]{:S(2)}, u32[]{:S(2)}) collective-permute-start(f32[4,2,16,256]{3,2,1,0:T(8,128)S(1)} %get-tuple-element.48), channel_id=1, source_target_pairs={{0,8},{1,9},{2,10},{3,11},{4,12},{5,13},{6,14},{7,15},{8,0},{9,1},... | collective-permute-start | bytes 393224 | tf_op jit(solution)/shard_map/ppermute | solution.py:279
  7.6 6.2 %copy-start = (f32[3,2,2,256,256]{4,3,2,1,0:T(8,128)S(1)}, f32[3,2,2,256,256]{4,3,2,1,0:T(8,128)}, u32[]{:S(2)}) copy-start(f32[3,2,2,256,256]{4,3,2,1,0:T(8,128)} %table_ref.1) | copy-start | bytes 9437188
  7.8 6.1 %copy-start.1 = (s32[1,3]{1,0:T(1,128)S(1)}, s32[1,3]{1,0:T(1,128)}, u32[]{:S(2)}) copy-start(s32[1,3]{1,0:T(1,128)} %bits_ref.1) | copy-start | bytes 40
  8.4 7.3 %collective-permute-start.2 = (f32[4,2,16,256]{3,2,1,0:T(8,128)S(1)}, f32[4,2,16,256]{3,2,1,0:T(8,128)S(1)}, u32[]{:S(2)}, u32[]{:S(2)}) collective-permute-start(f32[4,2,16,256]{3,2,1,0:T(8,128)S(1)} %get-tuple-element.50), channel_id=1, source_target_pairs={{0,2},{1,3},{2,0},{3,1},{4,6},{5,7},{6,4},{7,5},{8,10},{9,11},{10,... | collective-permute-start | bytes 393224 | tf_op jit(solution)/shard_map/ppermute | solution.py:279
  10.0 5.8 %collective-permute-start.3 = (f32[4,2,16,256]{3,2,1,0:T(8,128)S(1)}, f32[4,2,16,256]{3,2,1,0:T(8,128)S(1)}, u32[]{:S(2)}, u32[]{:S(2)}) collective-permute-start(f32[4,2,16,256]{3,2,1,0:T(8,128)S(1)} %get-tuple-element.51), channel_id=1, source_target_pairs={{0,1},{1,0},{2,3},{3,2},{4,5},{5,4},{6,7},{7,6},{8,9},{9,8},{10,11... | collective-permute-start | bytes 393224 | tf_op jit(solution)/shard_map/ppermute | solution.py:279
  10.0 5.8 %collective-permute-start.4 = (f32[4,2,16,256]{3,2,1,0:T(8,128)S(1)}, f32[4,2,16,256]{3,2,1,0:T(8,128)S(1)}, u32[]{:S(2)}, u32[]{:S(2)}) collective-permute-start(f32[4,2,16,256]{3,2,1,0:T(8,128)S(1)} %get-tuple-element.52), channel_id=1, source_target_pairs={{0,3},{1,2},{2,1},{3,0},{4,7},{5,6},{6,5},{7,4},{8,11},{9,10},{10,... | collective-permute-start | bytes 393224 | tf_op jit(solution)/shard_map/ppermute | solution.py:279
  10.7 8.9 %collective-permute-start.10 = (f32[4,2,16,256]{3,2,1,0:T(8,128)S(1)}, f32[4,2,16,256]{3,2,1,0:T(8,128)S(1)}, u32[]{:S(2)}, u32[]{:S(2)}) collective-permute-start(f32[4,2,16,256]{3,2,1,0:T(8,128)S(1)} %get-tuple-element.60), channel_id=1, source_target_pairs={{0,12},{1,13},{2,14},{3,15},{4,8},{5,9},{6,10},{7,11},{8,4},{9,5},... | collective-permute-start | bytes 393224 | tf_op jit(solution)/shard_map/ppermute | solution.py:279
  15.9 7.7 %collective-permute-start.5 = (f32[4,2,16,256]{3,2,1,0:T(8,128)S(1)}, f32[4,2,16,256]{3,2,1,0:T(8,128)S(1)}, u32[]{:S(2)}, u32[]{:S(2)}) collective-permute-start(f32[4,2,16,256]{3,2,1,0:T(8,128)S(1)} %get-tuple-element.54), channel_id=1, source_target_pairs={{0,4},{1,5},{2,6},{3,7},{4,0},{5,1},{6,2},{7,3},{8,12},{9,13},{10,... | collective-permute-start | bytes 393224 | tf_op jit(solution)/shard_map/ppermute | solution.py:279
  16.3 10.4 %collective-permute-start.6 = (f32[4,2,16,256]{3,2,1,0:T(8,128)S(1)}, f32[4,2,16,256]{3,2,1,0:T(8,128)S(1)}, u32[]{:S(2)}, u32[]{:S(2)}) collective-permute-start(f32[4,2,16,256]{3,2,1,0:T(8,128)S(1)} %get-tuple-element.55), channel_id=1, source_target_pairs={{0,8},{1,9},{2,10},{3,11},{4,12},{5,13},{6,14},{7,15},{8,0},{9,1},... | collective-permute-start | bytes 393224 | tf_op jit(solution)/shard_map/ppermute | solution.py:279
  19.6 7.1 %collective-permute-start.11 = (f32[4,2,16,256]{3,2,1,0:T(8,128)S(1)}, f32[4,2,16,256]{3,2,1,0:T(8,128)S(1)}, u32[]{:S(2)}, u32[]{:S(2)}) collective-permute-start(f32[4,2,16,256]{3,2,1,0:T(8,128)S(1)} %get-tuple-element.63), channel_id=1, source_target_pairs={{0,3},{1,2},{2,1},{3,0},{4,7},{5,6},{6,5},{7,4},{8,11},{9,10},{10,... | collective-permute-start | bytes 393224 | tf_op jit(solution)/shard_map/ppermute | solution.py:279
  19.6 7.1 %collective-permute-start.12 = (f32[4,2,16,256]{3,2,1,0:T(8,128)S(1)}, f32[4,2,16,256]{3,2,1,0:T(8,128)S(1)}, u32[]{:S(2)}, u32[]{:S(2)}) collective-permute-start(f32[4,2,16,256]{3,2,1,0:T(8,128)S(1)} %get-tuple-element.64), channel_id=1, source_target_pairs={{0,1},{1,0},{2,3},{3,2},{4,5},{5,4},{6,7},{7,6},{8,9},{9,8},{10,11... | collective-permute-start | bytes 393224 | tf_op jit(solution)/shard_map/ppermute | solution.py:279
  21.2 7.0 %collective-permute-start.13 = (f32[4,2,16,256]{3,2,1,0:T(8,128)S(1)}, f32[4,2,16,256]{3,2,1,0:T(8,128)S(1)}, u32[]{:S(2)}, u32[]{:S(2)}) collective-permute-start(f32[4,2,16,256]{3,2,1,0:T(8,128)S(1)} %get-tuple-element.65), channel_id=1, source_target_pairs={{0,2},{1,3},{2,0},{3,1},{4,6},{5,7},{6,4},{7,5},{8,10},{9,11},{10,... | collective-permute-start | bytes 393224 | tf_op jit(solution)/shard_map/ppermute | solution.py:279
  23.6 7.8 %collective-permute-start.7 = (f32[4,2,16,256]{3,2,1,0:T(8,128)S(1)}, f32[4,2,16,256]{3,2,1,0:T(8,128)S(1)}, u32[]{:S(2)}, u32[]{:S(2)}) collective-permute-start(f32[4,2,16,256]{3,2,1,0:T(8,128)S(1)} %get-tuple-element.56), channel_id=1, source_target_pairs={{0,12},{1,13},{2,14},{3,15},{4,8},{5,9},{6,10},{7,11},{8,4},{9,5},... | collective-permute-start | bytes 393224 | tf_op jit(solution)/shard_map/ppermute | solution.py:279
  29.5 8.3 %collective-permute-start.14 = (f32[4,2,16,256]{3,2,1,0:T(8,128)S(1)}, f32[4,2,16,256]{3,2,1,0:T(8,128)S(1)}, u32[]{:S(2)}, u32[]{:S(2)}) collective-permute-start(f32[4,2,16,256]{3,2,1,0:T(8,128)S(1)} %get-tuple-element.66), channel_id=1, source_target_pairs={{0,4},{1,5},{2,6},{3,7},{4,0},{5,1},{6,2},{7,3},{8,12},{9,13},{10,... | collective-permute-start | bytes 393224 | tf_op jit(solution)/shard_map/ppermute | solution.py:279
  29.9 7.9 %collective-permute-start.15 = (f32[4,2,16,256]{3,2,1,0:T(8,128)S(1)}, f32[4,2,16,256]{3,2,1,0:T(8,128)S(1)}, u32[]{:S(2)}, u32[]{:S(2)}) collective-permute-start(f32[4,2,16,256]{3,2,1,0:T(8,128)S(1)} %get-tuple-element.67), channel_id=1, source_target_pairs={{0,8},{1,9},{2,10},{3,11},{4,12},{5,13},{6,14},{7,15},{8,0},{9,1},... | collective-permute-start | bytes 393224 | tf_op jit(solution)/shard_map/ppermute | solution.py:279
  32.6 5.9 %collective-permute-start.9 = (f32[4,2,16,256]{3,2,1,0:T(8,128)S(1)}, f32[4,2,16,256]{3,2,1,0:T(8,128)S(1)}, u32[]{:S(2)}, u32[]{:S(2)}) collective-permute-start(f32[4,2,16,256]{3,2,1,0:T(8,128)S(1)} %get-tuple-element.59), channel_id=1, source_target_pairs={{0,3},{1,2},{2,1},{3,0},{4,7},{5,6},{6,5},{7,4},{8,11},{9,10},{10,... | collective-permute-start | bytes 393224 | tf_op jit(solution)/shard_map/ppermute | solution.py:279
  32.7 8.1 %collective-permute-start.16 = (f32[4,2,16,256]{3,2,1,0:T(8,128)S(1)}, f32[4,2,16,256]{3,2,1,0:T(8,128)S(1)}, u32[]{:S(2)}, u32[]{:S(2)}) collective-permute-start(f32[4,2,16,256]{3,2,1,0:T(8,128)S(1)} %get-tuple-element.69), channel_id=1, source_target_pairs={{0,2},{1,3},{2,0},{3,1},{4,6},{5,7},{6,4},{7,5},{8,10},{9,11},{10,... | collective-permute-start | bytes 393224 | tf_op jit(solution)/shard_map/ppermute | solution.py:279
  33.9 6.9 %collective-permute-start.8 = (f32[4,2,16,256]{3,2,1,0:T(8,128)S(1)}, f32[4,2,16,256]{3,2,1,0:T(8,128)S(1)}, u32[]{:S(2)}, u32[]{:S(2)}) collective-permute-start(f32[4,2,16,256]{3,2,1,0:T(8,128)S(1)} %get-tuple-element.58), channel_id=1, source_target_pairs={{0,1},{1,0},{2,3},{3,2},{4,5},{5,4},{6,7},{7,6},{8,9},{9,8},{10,11... | collective-permute-start | bytes 393224 | tf_op jit(solution)/shard_map/ppermute | solution.py:279
  37.8 8.0 %collective-permute-start.20 = (f32[4,2,16,256]{3,2,1,0:T(8,128)S(1)}, f32[4,2,16,256]{3,2,1,0:T(8,128)S(1)}, u32[]{:S(2)}, u32[]{:S(2)}) collective-permute-start(f32[4,2,16,256]{3,2,1,0:T(8,128)S(1)} %get-tuple-element.75), channel_id=1, source_target_pairs={{0,12},{1,13},{2,14},{3,15},{4,8},{5,9},{6,10},{7,11},{8,4},{9,5},... | collective-permute-start | bytes 393224 | tf_op jit(solution)/shard_map/ppermute | solution.py:279
  40.9 7.0 %collective-permute-start.17 = (f32[4,2,16,256]{3,2,1,0:T(8,128)S(1)}, f32[4,2,16,256]{3,2,1,0:T(8,128)S(1)}, u32[]{:S(2)}, u32[]{:S(2)}) collective-permute-start(f32[4,2,16,256]{3,2,1,0:T(8,128)S(1)} %get-tuple-element.71), channel_id=1, source_target_pairs={{0,4},{1,5},{2,6},{3,7},{4,0},{5,1},{6,2},{7,3},{8,12},{9,13},{10,... | collective-permute-start | bytes 393224 | tf_op jit(solution)/shard_map/ppermute | solution.py:279
  42.6 9.4 %collective-permute-start.18 = (f32[4,2,16,256]{3,2,1,0:T(8,128)S(1)}, f32[4,2,16,256]{3,2,1,0:T(8,128)S(1)}, u32[]{:S(2)}, u32[]{:S(2)}) collective-permute-start(f32[4,2,16,256]{3,2,1,0:T(8,128)S(1)} %get-tuple-element.72), channel_id=1, source_target_pairs={{0,8},{1,9},{2,10},{3,11},{4,12},{5,13},{6,14},{7,15},{8,0},{9,1},... | collective-permute-start | bytes 393224 | tf_op jit(solution)/shard_map/ppermute | solution.py:279
  45.9 6.1 %collective-permute-start.21 = (f32[4,2,16,256]{3,2,1,0:T(8,128)S(1)}, f32[4,2,16,256]{3,2,1,0:T(8,128)S(1)}, u32[]{:S(2)}, u32[]{:S(2)}) collective-permute-start(f32[4,2,16,256]{3,2,1,0:T(8,128)S(1)} %get-tuple-element.78), channel_id=1, source_target_pairs={{0,1},{1,0},{2,3},{3,2},{4,5},{5,4},{6,7},{7,6},{8,9},{9,8},{10,11... | collective-permute-start | bytes 393224 | tf_op jit(solution)/shard_map/ppermute | solution.py:279
  46.0 6.4 %collective-permute-start.22 = (f32[4,2,16,256]{3,2,1,0:T(8,128)S(1)}, f32[4,2,16,256]{3,2,1,0:T(8,128)S(1)}, u32[]{:S(2)}, u32[]{:S(2)}) collective-permute-start(f32[4,2,16,256]{3,2,1,0:T(8,128)S(1)} %get-tuple-element.79), channel_id=1, source_target_pairs={{0,2},{1,3},{2,0},{3,1},{4,6},{5,7},{6,4},{7,5},{8,10},{9,11},{10,... | collective-permute-start | bytes 393224 | tf_op jit(solution)/shard_map/ppermute | solution.py:279
  46.0 8.2 %collective-permute-start.23 = (f32[4,2,16,256]{3,2,1,0:T(8,128)S(1)}, f32[4,2,16,256]{3,2,1,0:T(8,128)S(1)}, u32[]{:S(2)}, u32[]{:S(2)}) collective-permute-start(f32[4,2,16,256]{3,2,1,0:T(8,128)S(1)} %get-tuple-element.80), channel_id=1, source_target_pairs={{0,3},{1,2},{2,1},{3,0},{4,7},{5,6},{6,5},{7,4},{8,11},{9,10},{10,... | collective-permute-start | bytes 393224 | tf_op jit(solution)/shard_map/ppermute | solution.py:279
  47.9 7.6 %collective-permute-start.19 = (f32[4,2,16,256]{3,2,1,0:T(8,128)S(1)}, f32[4,2,16,256]{3,2,1,0:T(8,128)S(1)}, u32[]{:S(2)}, u32[]{:S(2)}) collective-permute-start(f32[4,2,16,256]{3,2,1,0:T(8,128)S(1)} %get-tuple-element.73), channel_id=1, source_target_pairs={{0,12},{1,13},{2,14},{3,15},{4,8},{5,9},{6,10},{7,11},{8,4},{9,5},... | collective-permute-start | bytes 393224 | tf_op jit(solution)/shard_map/ppermute | solution.py:279

commit v7 on v6

--- a/solution.py
+++ b/solution.py
@@ -257,139 +257,111 @@
         copy.wait()
 
 
-def chunks_by_permutes(laid, chain, hi_table):
+def chunks_by_permutes(laid, chain, hi_table, width):
     devices = lax.axis_size("stem")
-    width = 1 << ((devices.bit_length() - 1) // 2)
-    spare, rows, _ = laid.shape
+    _, rows, _ = laid.shape
     high, low = hi_table.shape[-1], chain.shape[-1]
     under = high // devices
     me = lax.axis_index("stem").reshape(1)
     held = pltpu.VMEM((2, high, low), jnp.float32)
-    stem = pltpu.VMEM((rows, LANES), jnp.float32)
+    upper = tuple(t * width for t in range(width))
+
+    def lower(*first):
+        return (0, *first, *(q for q in range(1, width) if q not in first))
 
     def tie(values, after):
         return lax.optimization_barrier((values, after))[0]
+
+    def tied(values, at, after):
+        return [tie(v, tuple(after)) if n == at else v for n, v in enumerate(values)]
 
     def blocks(layout):
         shapes = [(len(array), 2, under, low) for array in layout]
         return tuple(jax.ShapeDtypeStruct(shape, jnp.float32) for shape in shapes)
 
-    def swap(value, step, after=None):
-        value = value if after is None else tie(value, after)
-        return lax.ppermute(value, "stem", [(i, i ^ step) for i in range(devices)])
-
-    def tied(values, at, after):
-        return [tie(v, after) if n == at else v for n, v in enumerate(values)]
-
-    def turn(old, new, values, name):
+    def call(kernel, name, values, tables=(), out=None, scratch=()):
+        specs = [SMEM] * bool(tables) + [VMEM] * (len(tables) + len(values))
         return pl.pallas_call(
-            functools.partial(turn_kernel, old, new),
-            out_shape=blocks(new),
-            in_specs=[VMEM] * len(old),
-            out_specs=(VMEM,) * len(new),
+            kernel,
+            out_shape=blocks(out) if isinstance(out, tuple) else out,
+            in_specs=specs,
+            out_specs=(VMEM,) * len(out) if isinstance(out, tuple) else VMEM,
+            scratch_shapes=list(scratch),
             compiler_params=SMALL,
             name=name,
-        )(*values)
-
-    def open_chunk_0(layout):
+        )(*[me] * bool(tables), *tables, *values)
+
+    def send(values, layout):
+        steps = [array[0] for array in layout]
+        return [values[0]] + [
+            lax.ppermute(value, "stem", [(i, i ^ step) for i in range(devices)])
+            for value, step in zip(values[1:], steps[1:])
+        ]
+
+    def turn(old, new, values, name):
+        return call(functools.partial(turn_kernel, old, new), name, values, out=new)
+
+    def open_first(layout):
         tiles = high // LANES
         matrix = hi_table[0].reshape(2, high // SUBLANES, SUBLANES, tiles, LANES)
         matrix = matrix.transpose(0, 1, 3, 2, 4).reshape(-1, LANES)
-        return pl.pallas_call(
-            functools.partial(open_first_kernel, layout),
-            out_shape=blocks(layout),
-            in_specs=[SMEM, VMEM],
-            out_specs=(VMEM,) * len(layout),
-            scratch_shapes=[pltpu.VMEM((2, high, high), jnp.float32)],
-            compiler_params=SMALL,
-            name="open_0",
-        )(me, jnp.concatenate([laid[0], matrix], axis=0))
-
-    def open_chunk_1(layout, stem, table):
-        return pl.pallas_call(
-            functools.partial(open_chunk_kernel, layout),
-            out_shape=blocks(layout),
-            in_specs=[SMEM, VMEM, VMEM],
-            out_specs=(VMEM,) * len(layout),
-            compiler_params=SMALL,
-            name="open_1",
-        )(me, stem, table)
-
-    def middle_chunk(r, old, new, values):
-        return pl.pallas_call(
-            functools.partial(middle_chunk_kernel, old, new),
-            out_shape=blocks(new),
-            in_specs=[SMEM, VMEM, VMEM] + [VMEM] * len(old),
-            out_specs=(VMEM,) * len(new),
-            scratch_shapes=[held, pltpu.VMEM((2 * high, low), jnp.float32)],
-            compiler_params=SMALL,
-            name=f"middle_{r}",
-        )(me, later[1][1], chain, *values)
-
-    def close_chunk(r, layout, values, first=None):
-        if first is None:
-            return pl.pallas_call(
-                functools.partial(close_first_kernel, layout),
-                out_shape=jax.ShapeDtypeStruct(laid.shape[1:], jnp.float32),
-                in_specs=[SMEM, VMEM] + [VMEM] * len(layout),
-                out_specs=VMEM,
-                scratch_shapes=[held],
-                compiler_params=SMALL,
-                name=f"close_{r}",
-            )(me, later[1][2], *values)
+        packed = jnp.concatenate([laid[0], matrix], axis=0)
+        kernel = functools.partial(open_first_kernel, layout)
+        scratch = [pltpu.VMEM((2, high, high), jnp.float32)]
+        return call(kernel, "open_0", [], [packed], layout, scratch)
+
+    def open_last(layout):
+        kernel = functools.partial(open_chunk_kernel, layout)
+        return call(kernel, "open_1", [], [stems[1], tables[0]], layout)
+
+    def middle(old, new, values, name):
+        kernel = functools.partial(middle_chunk_kernel, old, new)
+        scratch = [held, pltpu.VMEM((2 * high, low), jnp.float32)]
+        return call(kernel, name, values, [tables[1], chain], new, scratch)
+
+    def close_first(layout, values):
+        kernel = functools.partial(close_first_kernel, layout)
+        out = jax.ShapeDtypeStruct(laid.shape[1:], jnp.float32)
+        return call(kernel, "close_0", values, [tables[2]], out, [held])
+
+    def close_last(layout, values, first):
         return pl.pallas_call(
             functools.partial(close_last_kernel, layout),
             out_shape=jax.ShapeDtypeStruct(laid.shape, jnp.float32),
-            in_specs=[SMEM, VMEM] + [VMEM] * len(layout) + [VMEM],
+            in_specs=[SMEM] + [VMEM] * (2 + len(layout)),
             out_specs=HBM,
-            scratch_shapes=[held, stem, pltpu.SemaphoreType.DMA((2,))],
+            scratch_shapes=[
+                held,
+                pltpu.VMEM((rows, LANES), jnp.float32),
+                pltpu.SemaphoreType.DMA((2,)),
+            ],
             compiler_params=SMALL,
-            name=f"close_{r}",
-        )(me, later[1][2], *values, first)
-
-    L00z = layout_over((0, 4, 8, 12), (0, 3, 1, 2))
-    L00p = layout_over((0, 3, 1, 2), (0, 4, 8, 12))
-    L01z = layout_over((0, 4, 8, 12), (0, 1, 2, 3))
-    L01p = layout_over((0, 1, 2, 3), (0, 4, 8, 12))
-    L10p = layout_over((0, 2, 1, 3), (0, 4, 8, 12))
-    L10z = layout_over((0, 4, 8, 12), (0, 2, 1, 3))
-    L11p = layout_over((0, 1, 3, 2), (0, 4, 8, 12))
-    L11z = layout_over((0, 4, 8, 12), (0, 1, 3, 2))
-    open_0 = open_chunk_0(L00z)
-    later = tie((laid, hi_table), open_0[0])
-    open_1 = open_chunk_1(L10p, later[0][1], later[1][0])
-    open_0_1 = swap(open_0[1], 4)
-    open_0_2 = swap(open_0[2], 8)
-    open_0_3 = swap(open_0[3], 12)
-    turn_001 = turn(L00z, L00p, [open_0[0], open_0_1, open_0_2, open_0_3], "turn_001")
-    turn_001_1 = swap(turn_001[1], 3)
-    turn_001_2 = swap(turn_001[2], 1)
-    turn_001_3 = swap(turn_001[3], 2)
-    open_1_1 = swap(open_1[1], 2)
-    open_1_2 = swap(open_1[2], 1)
-    open_1_3 = swap(open_1[3], 3)
-    turn_101 = turn(L10p, L10z, tied([open_1[0], open_1_1, open_1_2, open_1_3], 0, (open_0_1, open_0_2, chain)), "turn_101")
-    turn_101_1 = swap(turn_101[1], 4)
-    turn_101_2 = swap(turn_101[2], 8)
-    middle_0 = middle_chunk(0, L00p, L01z, tied([turn_001[0], turn_001_1, turn_001_2, turn_001_3], 0, (turn_101_1, turn_101_2)))
-    middle_0_1 = swap(middle_0[1], 4)
-    middle_0_2 = swap(middle_0[2], 8)
-    middle_0_3 = swap(middle_0[3], 12)
-    turn_011 = turn(L01z, L01p, [middle_0[0], middle_0_1, middle_0_2, middle_0_3], "turn_011")
-    turn_011_1 = swap(turn_011[1], 1)
-    turn_011_2 = swap(turn_011[2], 2)
-    turn_011_3 = swap(turn_011[3], 3)
-    turn_101_3 = swap(turn_101[3], 12)
-    middle_1 = middle_chunk(1, L10z, L11p, [turn_101[0], turn_101_1, turn_101_2, turn_101_3])
-    middle_1_1 = swap(middle_1[1], 1)
-    middle_1_2 = swap(middle_1[2], 3)
-    middle_1_3 = swap(middle_1[3], 2)
-    turn_111 = turn(L11p, L11z, tied([middle_1[0], middle_1_1, middle_1_2, middle_1_3], 2, (middle_0_1, middle_0_2)), "turn_111")
-    turn_111_1 = swap(turn_111[1], 4)
-    turn_111_2 = swap(turn_111[2], 8)
-    close_0 = close_chunk(0, L01p, tied([turn_011[0], turn_011_1, turn_011_2, turn_011_3], 0, (turn_111_1, turn_111_2)))
-    turn_111_3 = swap(turn_111[3], 12)
-    return close_chunk(1, L11z, [turn_111[0], turn_111_1, turn_111_2, turn_111_3], close_0)
+            name="close_1",
+        )(me, tables[2], *values, first)
+
+    orders = [lower(width // 2), lower(width // 2), lower(), lower(width // 2)]
+    uppers = [layout_over(upper, order) for order in orders]
+    lowers = [layout_over(order, upper) for order in orders]
+
+    ahead = open_first(uppers[0])
+    stems, tables = tie((laid, hi_table), ahead[0])
+    behind = open_last(lowers[1])
+    ahead = send(ahead, uppers[0])
+    behind = send(behind, lowers[1])
+    behind = turn(lowers[1], uppers[1], tied(behind, 0, [*ahead[1:3], chain]), "turn_1_in")
+    behind = send(behind, uppers[1])
+    ahead = turn(uppers[0], lowers[0], ahead, "turn_0_in")
+    ahead = send(ahead, lowers[0])
+    ahead = middle(lowers[0], uppers[2], tied(ahead, 0, behind[1:3]), "middle_0")
+    ahead = send(ahead, uppers[2])
+    behind = middle(uppers[1], lowers[3], behind, "middle_1")
+    behind = send(behind, lowers[3])
+    behind = turn(lowers[3], uppers[3], tied(behind, 2, ahead[1:3]), "turn_1_out")
+    behind = send(behind, uppers[3])
+    ahead = turn(uppers[2], lowers[2], ahead, "turn_0_out")
+    ahead = send(ahead, lowers[2])
+    first = close_first(lowers[2], tied(ahead, 0, behind[1:3]))
+    return close_last(uppers[3], behind, first)
 
 
 def one_slice(stem, bits, lo_table, hi_table):
@@ -425,8 +397,9 @@
         compiler_params=SMALL,
         name="low_chain",
     )(bits, lo_table)
-    if direct and spare == 2 and 1 << (2 * ((leading.bit_length() - 1) // 2)) == leading:
-        closed = chunks_by_permutes(laid, chain, hi_table)
+    width = 1 << ((leading.bit_length() - 1) // 2)
+    if direct and spare == 2 and width > 1 and width * width == leading:
+        closed = chunks_by_permutes(laid, chain, hi_table, width)
         return closed.reshape(-1, 2, LANES).transpose(1, 0, 2).reshape(stem.shape)
     table_scratch = pltpu.VMEM((2, high, high), jnp.float32)
     opened = pl.pallas_call(

time: 57 us -> 56.3 us (0.988)
  transfers between devices with their start and end apart: 24 -> 24, of which waited for: 11 -> 12; matrix products, arithmetic and copies ran while one was open for 0% -> 0% of each run, Pallas kernels for 10% -> 10%
where the time goes in v7:
time: 56.3 us; the launch traced here: 56.2 us
  starting transfers between devices  32.4 us (58%)
  waiting for transfers between devices  14.2 us (25%)
  Pallas kernels  7.81 us (14%)
  local copies, waits for them, and re-layouts  1.43 us (3%)
    ppermute x24, starting transfers between devices, send(): lax.ppermute(value, 'stem', [(i, i ^ step) for i in range(devices)])  32.4 us
    ppermute x24, waiting for transfers between devices, send(): lax.ppermute(value, 'stem', [(i, i ^ step) for i in range(devices)])  14.2 us
    pallas_call x9, Pallas kernels, call(): pl.pallas_call(kernel, out_shape=blocks(out) if isinstance(out, tuple) el...  4.45 us
    pallas_call x1, Pallas kernels, one_slice(): pl.pallas_call(chain_kernel, out_shape=jax.ShapeDtypeStruct((2, low, low)...  1.94 us
    pallas_call x1, Pallas kernels, close_last(): pl.pallas_call(functools.partial(close_last_kernel, layout), out_shape=ja...  1.43 us
    slice x1, local copies, waits for them, and re-layouts, open_first(): packed = jnp.concatenate([laid[0], matrix], axis=0)  1.13 us
  transfers between devices with their start and end apart: 24, of which 12 were waited for; matrix products, arithmetic and copies ran while one was open for 0% of the time, Pallas kernels for 10%

profile of v7, /device:TPU:0, one launch (start us, length us, event | category | flops | bytes accessed | tf_op | source)
XLA Modules:
  0.0 56.2 jit_solution(3581808830816147791)
XLA Ops:
  0.0 1.1 %slice.27 = f32[512,2,128]{2,1,0:T(2,128)S(1)} slice(f32[1024,2,128]{2,1,0:T(2,128)} %bitcast.27), slice={[0:512], [0:2], [0:128]} | slice | bytes 1048576 | tf_op jit(solution)/shard_map/slice | solution.py:308
  1.1 0.1 slice-done
  1.2 0.1 pad_maximum_fusion.packed_ref
  1.3 0.0 copy-start.3
  1.3 0.6 %open_0.1 = (f32[4,2,16,256]{3,2,1,0:T(8,128)S(1)}, f32[4,2,16,256]{3,2,1,0:T(8,128)S(1)}, f32[4,2,16,256]{3,2,1,0:T(8,128)S(1)}, f32[4,2,16,256]{3,2,1,0:T(8,128)S(1)}) custom-call(s32[1]{0:T(128)} %bitcast.me_ref, f32[2048,128]{1,0:T(8,128)S(1)} %pad_maximum_fusion.packed_ref), custom_call_target="tpu_custom_call" | custom-call | tf_op jit(solution)/shard_map/open_0/pallas_call | solution.py:284
  1.9 3.1 %collective-permute-start = (f32[4,2,16,256]{3,2,1,0:T(8,128)S(1)}, f32[4,2,16,256]{3,2,1,0:T(8,128)S(1)}, u32[]{:S(2)}, u32[]{:S(2)}) collective-permute-start(f32[4,2,16,256]{3,2,1,0:T(8,128)S(1)} %get-tuple-element.47), channel_id=1, source_target_pairs={{0,4},{1,5},{2,6},{3,7},{4,0},{5,1},{6,2},{7,3},{8,12},{9,13},{10,... | collective-permute-start | bytes 393224 | tf_op jit(solution)/shard_map/ppermute | solution.py:297
  5.0 2.6 %collective-permute-start.1 = (f32[4,2,16,256]{3,2,1,0:T(8,128)S(1)}, f32[4,2,16,256]{3,2,1,0:T(8,128)S(1)}, u32[]{:S(2)}, u32[]{:S(2)}) collective-permute-start(f32[4,2,16,256]{3,2,1,0:T(8,128)S(1)} %get-tuple-element.48), channel_id=1, source_target_pairs={{0,8},{1,9},{2,10},{3,11},{4,12},{5,13},{6,14},{7,15},{8,0},{9,1},... | collective-permute-start | bytes 393224 | tf_op jit(solution)/shard_map/ppermute | solution.py:297
  7.6 0.0 copy-done.2
  7.6 0.2 slice_bitcast_fusion
  7.8 0.0 copy-done.3
  7.8 0.0 copy-start.1
  7.8 0.6 %open_1.1 = (f32[4,2,16,256]{3,2,1,0:T(8,128)S(1)}, f32[4,2,16,256]{3,2,1,0:T(8,128)S(1)}, f32[4,2,16,256]{3,2,1,0:T(8,128)S(1)}, f32[4,2,16,256]{3,2,1,0:T(8,128)S(1)}) custom-call(s32[1]{0:T(128)} %bitcast.me_ref, f32[1024,128]{1,0:T(8,128)S(1)} %slice_bitcast_fusion.1.stem_ref, f32[2,256,256]{2,1,0:T(8,128)S(1)} %get-tuple-element.81.table), custom_call_target="tpu_custom_call" | custom-call | tf_op jit(solution)/shard_map/open_1/pallas_call | solution.py:284
  8.4 1.6 %collective-permute-start.2 = (f32[4,2,16,256]{3,2,1,0:T(8,128)S(1)}, f32[4,2,16,256]{3,2,1,0:T(8,128)S(1)}, u32[]{:S(2)}, u32[]{:S(2)}) collective-permute-start(f32[4,2,16,256]{3,2,1,0:T(8,128)S(1)} %get-tuple-element.50), channel_id=1, source_target_pairs={{0,2},{1,3},{2,0},{3,1},{4,6},{5,7},{6,4},{7,5},{8,10},{9,11},{10,... | collective-permute-start | bytes 393224 | tf_op jit(solution)/shard_map/ppermute | solution.py:297
  10.0 0.0 collective-permute-start.3
  10.0 0.6 %collective-permute-start.4 = (f32[4,2,16,256]{3,2,1,0:T(8,128)S(1)}, f32[4,2,16,256]{3,2,1,0:T(8,128)S(1)}, u32[]{:S(2)}, u32[]{:S(2)}) collective-permute-start(f32[4,2,16,256]{3,2,1,0:T(8,128)S(1)} %get-tuple-element.52), channel_id=1, source_target_pairs={{0,3},{1,2},{2,1},{3,0},{4,7},{5,6},{6,5},{7,4},{8,11},{9,10},{10,... | collective-permute-start | bytes 393224 | tf_op jit(solution)/shard_map/ppermute | solution.py:297
  10.7 0.0 collective-permute-done.refs_1_
  10.7 3.2 %collective-permute-start.10 = (f32[4,2,16,256]{3,2,1,0:T(8,128)S(1)}, f32[4,2,16,256]{3,2,1,0:T(8,128)S(1)}, u32[]{:S(2)}, u32[]{:S(2)}) collective-permute-start(f32[4,2,16,256]{3,2,1,0:T(8,128)S(1)} %get-tuple-element.60), channel_id=1, source_target_pairs={{0,12},{1,13},{2,14},{3,15},{4,8},{5,9},{6,10},{7,11},{8,4},{9,5},... | collective-permute-start | bytes 393224 | tf_op jit(solution)/shard_map/ppermute | solution.py:297
  13.8 0.0 copy-done
  13.8 1.9 %low_chain.1.low_table = f32[2,256,256]{2,1,0:T(8,128)S(1)} custom-call(s32[1,3]{1,0:T(1,128)S(1)} %copy-done.1, f32[3,2,2,256,256]{4,3,2,1,0:T(8,128)S(1)} %copy-done), custom_call_target="tpu_custom_call" | custom-call | tf_op jit(solution)/shard_map/low_chain/pallas_call | solution.py:391
  15.8 0.0 collective-permute-done.1.refs_2_
  15.8 0.0 collective-permute-done.2.refs_1_
  15.8 0.0 collective-permute-done.3.refs_2_
  15.8 0.0 collective-permute-done.4.refs_3_
  15.9 0.5 collective-permute-start.5
  16.3 3.2 %collective-permute-start.6 = (f32[4,2,16,256]{3,2,1,0:T(8,128)S(1)}, f32[4,2,16,256]{3,2,1,0:T(8,128)S(1)}, u32[]{:S(2)}, u32[]{:S(2)}) collective-permute-start(f32[4,2,16,256]{3,2,1,0:T(8,128)S(1)} %get-tuple-element.55), channel_id=1, source_target_pairs={{0,8},{1,9},{2,10},{3,11},{4,12},{5,13},{6,14},{7,15},{8,0},{9,1},... | collective-permute-start | bytes 393224 | tf_op jit(solution)/shard_map/ppermute | solution.py:297
  19.5 0.0 collective-permute-done.10.refs_3_
  19.6 1.6 %collective-permute-start.11 = (f32[4,2,16,256]{3,2,1,0:T(8,128)S(1)}, f32[4,2,16,256]{3,2,1,0:T(8,128)S(1)}, u32[]{:S(2)}, u32[]{:S(2)}) collective-permute-start(f32[4,2,16,256]{3,2,1,0:T(8,128)S(1)} %get-tuple-element.63), channel_id=1, source_target_pairs={{0,2},{1,3},{2,0},{3,1},{4,6},{5,7},{6,4},{7,5},{8,10},{9,11},{10,... | collective-permute-start | bytes 393224 | tf_op jit(solution)/shard_map/ppermute | solution.py:297
  21.1 0.0 collective-permute-start.12
  21.1 0.6 %collective-permute-start.13 = (f32[4,2,16,256]{3,2,1,0:T(8,128)S(1)}, f32[4,2,16,256]{3,2,1,0:T(8,128)S(1)}, u32[]{:S(2)}, u32[]{:S(2)}) collective-permute-start(f32[4,2,16,256]{3,2,1,0:T(8,128)S(1)} %get-tuple-element.65), channel_id=1, source_target_pairs={{0,3},{1,2},{2,1},{3,0},{4,7},{5,6},{6,5},{7,4},{8,11},{9,10},{10,... | collective-permute-start | bytes 393224 | tf_op jit(solution)/shard_map/ppermute | solution.py:297
  21.8 1.8 %collective-permute-done.5.refs_1_ = f32[4,2,16,256]{3,2,1,0:T(8,128)S(1)} collective-permute-done((f32[4,2,16,256]{3,2,1,0:T(8,128)S(1)}, f32[4,2,16,256]{3,2,1,0:T(8,128)S(1)}, u32[]{:S(2)}, u32[]{:S(2)}) %collective-permute-start.5) | collective-permute-done | bytes 131104 | tf_op jit(solution)/shard_map/ppermute | solution.py:297
  23.6 2.1 %collective-permute-start.7 = (f32[4,2,16,256]{3,2,1,0:T(8,128)S(1)}, f32[4,2,16,256]{3,2,1,0:T(8,128)S(1)}, u32[]{:S(2)}, u32[]{:S(2)}) collective-permute-start(f32[4,2,16,256]{3,2,1,0:T(8,128)S(1)} %get-tuple-element.56), channel_id=1, source_target_pairs={{0,12},{1,13},{2,14},{3,15},{4,8},{5,9},{6,10},{7,11},{8,4},{9,5},... | collective-permute-start | bytes 393224 | tf_op jit(solution)/shard_map/ppermute | solution.py:297
  25.7 1.0 %collective-permute-done.6.refs_2_ = f32[4,2,16,256]{3,2,1,0:T(8,128)S(1)} collective-permute-done((f32[4,2,16,256]{3,2,1,0:T(8,128)S(1)}, f32[4,2,16,256]{3,2,1,0:T(8,128)S(1)}, u32[]{:S(2)}, u32[]{:S(2)}) %collective-permute-start.6) | collective-permute-done | bytes 131104 | tf_op jit(solution)/shard_map/ppermute | solution.py:297
  26.7 0.0 collective-permute-done.11.refs_1_
  26.7 0.0 collective-permute-done.12.refs_2_
  26.7 0.2 collective-permute-done.13.refs_3_
  26.9 1.2 %middle_0.1 = (f32[4,2,16,256]{3,2,1,0:T(8,128)S(1)}, f32[4,2,16,256]{3,2,1,0:T(8,128)S(1)}, f32[4,2,16,256]{3,2,1,0:T(8,128)S(1)}, f32[4,2,16,256]{3,2,1,0:T(8,128)S(1)}) custom-call(s32[1]{0:T(128)} %bitcast.me_ref, f32[2,256,256]{2,1,0:T(8,128)S(1)} %get-tuple-element.82.table, f32[2,256,256]{2,1,0:T(8,128)S(1)} %low_chain.1.low_table, ...), custom_call_target="tpu_custom_call" | custom-call | tf_op jit(solution)/shard_map/middle_0/pallas_call | solution.py:284
  28.1 0.4 collective-permute-start.14
  28.6 1.6 %collective-permute-start.15 = (f32[4,2,16,256]{3,2,1,0:T(8,128)S(1)}, f32[4,2,16,256]{3,2,1,0:T(8,128)S(1)}, u32[]{:S(2)}, u32[]{:S(2)}) collective-permute-start(f32[4,2,16,256]{3,2,1,0:T(8,128)S(1)} %get-tuple-element.67), channel_id=1, source_target_pairs={{0,8},{1,9},{2,10},{3,11},{4,12},{5,13},{6,14},{7,15},{8,0},{9,1},... | collective-permute-start | bytes 393224 | tf_op jit(solution)/shard_map/ppermute | solution.py:297
  30.2 0.5 collective-permute-done.7.refs_3_
  30.7 1.2 %middle_1.1 = (f32[4,2,16,256]{3,2,1,0:T(8,128)S(1)}, f32[4,2,16,256]{3,2,1,0:T(8,128)S(1)}, f32[4,2,16,256]{3,2,1,0:T(8,128)S(1)}, f32[4,2,16,256]{3,2,1,0:T(8,128)S(1)}) custom-call(s32[1]{0:T(128)} %bitcast.me_ref, f32[2,256,256]{2,1,0:T(8,128)S(1)} %get-tuple-element.82.table, f32[2,256,256]{2,1,0:T(8,128)S(1)} %low_chain.1.low_table, ...), custom_call_target="tpu_custom_call" | custom-call | tf_op jit(solution)/shard_map/middle_1/pallas_call | solution.py:284
  31.9 0.1 collective-permute-start.9
  32.0 1.6 %collective-permute-start.16 = (f32[4,2,16,256]{3,2,1,0:T(8,128)S(1)}, f32[4,2,16,256]{3,2,1,0:T(8,128)S(1)}, u32[]{:S(2)}, u32[]{:S(2)}) collective-permute-start(f32[4,2,16,256]{3,2,1,0:T(8,128)S(1)} %get-tuple-element.69), channel_id=1, source_target_pairs={{0,3},{1,2},{2,1},{3,0},{4,7},{5,6},{6,5},{7,4},{8,11},{9,10},{10,... | collective-permute-start | bytes 393224 | tf_op jit(solution)/shard_map/ppermute | solution.py:297
  33.6 0.6 %collective-permute-start.8 = (f32[4,2,16,256]{3,2,1,0:T(8,128)S(1)}, f32[4,2,16,256]{3,2,1,0:T(8,128)S(1)}, u32[]{:S(2)}, u32[]{:S(2)}) collective-permute-start(f32[4,2,16,256]{3,2,1,0:T(8,128)S(1)} %get-tuple-element.58), channel_id=1, source_target_pairs={{0,2},{1,3},{2,0},{3,1},{4,6},{5,7},{6,4},{7,5},{8,10},{9,11},{10,... | collective-permute-start | bytes 393224 | tf_op jit(solution)/shard_map/ppermute | solution.py:297
  34.2 2.6 %collective-permute-done.14.refs_1_ = f32[4,2,16,256]{3,2,1,0:T(8,128)S(1)} collective-permute-done((f32[4,2,16,256]{3,2,1,0:T(8,128)S(1)}, f32[4,2,16,256]{3,2,1,0:T(8,128)S(1)}, u32[]{:S(2)}, u32[]{:S(2)}) %collective-permute-start.14) | collective-permute-done | bytes 131104 | tf_op jit(solution)/shard_map/ppermute | solution.py:297
  36.7 0.3 collective-permute-start.20
  37.1 1.2 %collective-permute-done.15.refs_2_ = f32[4,2,16,256]{3,2,1,0:T(8,128)S(1)} collective-permute-done((f32[4,2,16,256]{3,2,1,0:T(8,128)S(1)}, f32[4,2,16,256]{3,2,1,0:T(8,128)S(1)}, u32[]{:S(2)}, u32[]{:S(2)}) %collective-permute-start.15) | collective-permute-done | bytes 131104 | tf_op jit(solution)/shard_map/ppermute | solution.py:297
  38.2 0.0 collective-permute-done.9.refs_2_
  38.2 0.0 collective-permute-done.16.refs_3_
  38.2 2.5 %collective-permute-done.8.refs_1_ = f32[4,2,16,256]{3,2,1,0:T(8,128)S(1)} collective-permute-done((f32[4,2,16,256]{3,2,1,0:T(8,128)S(1)}, f32[4,2,16,256]{3,2,1,0:T(8,128)S(1)}, u32[]{:S(2)}, u32[]{:S(2)}) %collective-permute-start.8) | collective-permute-done | bytes 131104 | tf_op jit(solution)/shard_map/ppermute | solution.py:297
  40.7 1.4 %collective-permute-start.17 = (f32[4,2,16,256]{3,2,1,0:T(8,128)S(1)}, f32[4,2,16,256]{3,2,1,0:T(8,128)S(1)}, u32[]{:S(2)}, u32[]{:S(2)}) collective-permute-start(f32[4,2,16,256]{3,2,1,0:T(8,128)S(1)} %get-tuple-element.71), channel_id=1, source_target_pairs={{0,4},{1,5},{2,6},{3,7},{4,0},{5,1},{6,2},{7,3},{8,12},{9,13},{10,... | collective-permute-start | bytes 393224 | tf_op jit(solution)/shard_map/ppermute | solution.py:297
  42.1 2.8 %collective-permute-start.18 = (f32[4,2,16,256]{3,2,1,0:T(8,128)S(1)}, f32[4,2,16,256]{3,2,1,0:T(8,128)S(1)}, u32[]{:S(2)}, u32[]{:S(2)}) collective-permute-start(f32[4,2,16,256]{3,2,1,0:T(8,128)S(1)} %get-tuple-element.72), channel_id=1, source_target_pairs={{0,8},{1,9},{2,10},{3,11},{4,12},{5,13},{6,14},{7,15},{8,0},{9,1},... | collective-permute-start | bytes 393224 | tf_op jit(solution)/shard_map/ppermute | solution.py:297
  44.9 0.0 collective-permute-done.20.refs_3_
  45.0 0.1 collective-permute-start.21
  45.1 0.1 collective-permute-start.22
  45.1 1.8 %collective-permute-start.23 = (f32[4,2,16,256]{3,2,1,0:T(8,128)S(1)}, f32[4,2,16,256]{3,2,1,0:T(8,128)S(1)}, u32[]{:S(2)}, u32[]{:S(2)}) collective-permute-start(f32[4,2,16,256]{3,2,1,0:T(8,128)S(1)} %get-tuple-element.80), channel_id=1, source_target_pairs={{0,3},{1,2},{2,1},{3,0},{4,7},{5,6},{6,5},{7,4},{8,11},{9,10},{10,... | collective-permute-start | bytes 393224 | tf_op jit(solution)/shard_map/ppermute | solution.py:297
  46.9 1.0 %collective-permute-done.17.refs_1_ = f32[4,2,16,256]{3,2,1,0:T(8,128)S(1)} collective-permute-done((f32[4,2,16,256]{3,2,1,0:T(8,128)S(1)}, f32[4,2,16,256]{3,2,1,0:T(8,128)S(1)}, u32[]{:S(2)}, u32[]{:S(2)}) %collective-permute-start.17) | collective-permute-done | bytes 131104 | tf_op jit(solution)/shard_map/ppermute | solution.py:297
  47.9 2.7 %collective-permute-start.19 = (f32[4,2,16,256]{3,2,1,0:T(8,128)S(1)}, f32[4,2,16,256]{3,2,1,0:T(8,128)S(1)}, u32[]{:S(2)}, u32[]{:S(2)}) collective-permute-start(f32[4,2,16,256]{3,2,1,0:T(8,128)S(1)} %get-tuple-element.73), channel_id=1, source_target_pairs={{0,12},{1,13},{2,14},{3,15},{4,8},{5,9},{6,10},{7,11},{8,4},{9,5},... | collective-permute-start | bytes 393224 | tf_op jit(solution)/shard_map/ppermute | solution.py:297
  50.6 0.5 collective-permute-done.18.refs_2_
  51.1 0.0 collective-permute-done.21.refs_1_
  51.1 0.3 collective-permute-done.22.refs_2_
  51.4 1.9 %collective-permute-done.23.refs_3_ = f32[4,2,16,256]{3,2,1,0:T(8,128)S(1)} collective-permute-done((f32[4,2,16,256]{3,2,1,0:T(8,128)S(1)}, f32[4,2,16,256]{3,2,1,0:T(8,128)S(1)}, u32[]{:S(2)}, u32[]{:S(2)}) %collective-permute-start.23) | collective-permute-done | bytes 131104 | tf_op jit(solution)/shard_map/ppermute | solution.py:297
  53.3 0.6 %close_0.1.refs_4_ = f32[1024,128]{1,0:T(8,128)S(1)} custom-call(s32[1]{0:T(128)} %bitcast.me_ref, f32[2,256,256]{2,1,0:T(8,128)S(1)} %get-tuple-element.83.table, f32[4,2,16,256]{3,2,1,0:T(8,128)S(1)} %get-tuple-element.77.refs_0_, f32[4,2,16,256]{3,2,1,0:T(8,128)S(1)} %collective-permute-done.21.refs_1_, ...), custom_call_target="tpu_custom_call" | custom-call | tf_op jit(solution)/shard_map/close_0/pallas_call | solution.py:284
  54.0 0.8 %collective-permute-done.19.refs_3_ = f32[4,2,16,256]{3,2,1,0:T(8,128)S(1)} collective-permute-done((f32[4,2,16,256]{3,2,1,0:T(8,128)S(1)}, f32[4,2,16,256]{3,2,1,0:T(8,128)S(1)}, u32[]{:S(2)}, u32[]{:S(2)}) %collective-permute-start.19) | collective-permute-done | bytes 131104 | tf_op jit(solution)/shard_map/ppermute | solution.py:297
  54.7 1.4 %close_1.1 = f32[2,1024,128]{2,1,0:T(8,128)} custom-call(s32[1]{0:T(128)} %bitcast.me_ref, f32[2,256,256]{2,1,0:T(8,128)S(1)} %get-tuple-element.83.table, f32[4,2,16,256]{3,2,1,0:T(8,128)S(1)} %get-tuple-element.70.refs_0_, f32[4,2,16,256]{3,2,1,0:T(8,128)S(1)} %collective-permute-done.17.refs_1_, f32[4,2,16,256]{3,2,1,0:T(8,128)S(1)} %collective-permute-done.18.refs_2_, ...), custom_call_target="tpu_custom_call" | custom-call | tf_op jit(solution)/shard_map/close_1/pallas_call | solution.py:328
  (9 shorter events, 0.2 us)
Async XLA Ops:
  0.0 1.2 %slice-start = ((f32[3,2,256,256]{3,2,1,0:T(8,128)}), f32[1,2,256,256]{3,2,1,0:T(8,128)S(1)}, s32[]{:S(2)}) async-start(f32[3,2,256,256]{3,2,1,0:T(8,128)} %param.6), calls=%async_computation | async-start | bytes 1048576 | tf_op jit(solution)/shard_map/slice | solution.py:306
  1.2 6.4 %copy-start.2 = (f32[3,2,256,256]{3,2,1,0:T(8,128)S(1)}, f32[3,2,256,256]{3,2,1,0:T(8,128)}, u32[]{:S(2)}) copy-start(f32[3,2,256,256]{3,2,1,0:T(8,128)} %param.6) | copy-start | bytes 4718596
  1.3 6.5 %copy-start.3 = (f32[1,2,131072]{2,1,0:T(2,128)S(1)}, f32[1,2,131072]{2,1,0:T(2,128)}, u32[]{:S(2)}) copy-start(f32[1,2,131072]{2,1,0:T(2,128)} %param.4) | copy-start | bytes 3145732
  1.9 8.7 %collective-permute-start = (f32[4,2,16,256]{3,2,1,0:T(8,128)S(1)}, f32[4,2,16,256]{3,2,1,0:T(8,128)S(1)}, u32[]{:S(2)}, u32[]{:S(2)}) collective-permute-start(f32[4,2,16,256]{3,2,1,0:T(8,128)S(1)} %get-tuple-element.47), channel_id=1, source_target_pairs={{0,4},{1,5},{2,6},{3,7},{4,0},{5,1},{6,2},{7,3},{8,12},{9,13},{10,... | collective-permute-start | bytes 393224 | tf_op jit(solution)/shard_map/ppermute | solution.py:297
  5.0 10.8 %collective-permute-start.1 = (f32[4,2,16,256]{3,2,1,0:T(8,128)S(1)}, f32[4,2,16,256]{3,2,1,0:T(8,128)S(1)}, u32[]{:S(2)}, u32[]{:S(2)}) collective-permute-start(f32[4,2,16,256]{3,2,1,0:T(8,128)S(1)} %get-tuple-element.48), channel_id=1, source_target_pairs={{0,8},{1,9},{2,10},{3,11},{4,12},{5,13},{6,14},{7,15},{8,0},{9,1},... | collective-permute-start | bytes 393224 | tf_op jit(solution)/shard_map/ppermute | solution.py:297
  7.6 6.2 %copy-start = (f32[3,2,2,256,256]{4,3,2,1,0:T(8,128)S(1)}, f32[3,2,2,256,256]{4,3,2,1,0:T(8,128)}, u32[]{:S(2)}) copy-start(f32[3,2,2,256,256]{4,3,2,1,0:T(8,128)} %table_ref.1) | copy-start | bytes 9437188
  7.8 6.1 %copy-start.1 = (s32[1,3]{1,0:T(1,128)S(1)}, s32[1,3]{1,0:T(1,128)}, u32[]{:S(2)}) copy-start(s32[1,3]{1,0:T(1,128)} %bits_ref.1) | copy-start | bytes 40
  8.4 7.3 %collective-permute-start.2 = (f32[4,2,16,256]{3,2,1,0:T(8,128)S(1)}, f32[4,2,16,256]{3,2,1,0:T(8,128)S(1)}, u32[]{:S(2)}, u32[]{:S(2)}) collective-permute-start(f32[4,2,16,256]{3,2,1,0:T(8,128)S(1)} %get-tuple-element.50), channel_id=1, source_target_pairs={{0,2},{1,3},{2,0},{3,1},{4,6},{5,7},{6,4},{7,5},{8,10},{9,11},{10,... | collective-permute-start | bytes 393224 | tf_op jit(solution)/shard_map/ppermute | solution.py:297
  10.0 5.8 %collective-permute-start.3 = (f32[4,2,16,256]{3,2,1,0:T(8,128)S(1)}, f32[4,2,16,256]{3,2,1,0:T(8,128)S(1)}, u32[]{:S(2)}, u32[]{:S(2)}) collective-permute-start(f32[4,2,16,256]{3,2,1,0:T(8,128)S(1)} %get-tuple-element.51), channel_id=1, source_target_pairs={{0,1},{1,0},{2,3},{3,2},{4,5},{5,4},{6,7},{7,6},{8,9},{9,8},{10,11... | collective-permute-start | bytes 393224 | tf_op jit(solution)/shard_map/ppermute | solution.py:297
  10.0 5.8 %collective-permute-start.4 = (f32[4,2,16,256]{3,2,1,0:T(8,128)S(1)}, f32[4,2,16,256]{3,2,1,0:T(8,128)S(1)}, u32[]{:S(2)}, u32[]{:S(2)}) collective-permute-start(f32[4,2,16,256]{3,2,1,0:T(8,128)S(1)} %get-tuple-element.52), channel_id=1, source_target_pairs={{0,3},{1,2},{2,1},{3,0},{4,7},{5,6},{6,5},{7,4},{8,11},{9,10},{10,... | collective-permute-start | bytes 393224 | tf_op jit(solution)/shard_map/ppermute | solution.py:297
  10.7 8.9 %collective-permute-start.10 = (f32[4,2,16,256]{3,2,1,0:T(8,128)S(1)}, f32[4,2,16,256]{3,2,1,0:T(8,128)S(1)}, u32[]{:S(2)}, u32[]{:S(2)}) collective-permute-start(f32[4,2,16,256]{3,2,1,0:T(8,128)S(1)} %get-tuple-element.60), channel_id=1, source_target_pairs={{0,12},{1,13},{2,14},{3,15},{4,8},{5,9},{6,10},{7,11},{8,4},{9,5},... | collective-permute-start | bytes 393224 | tf_op jit(solution)/shard_map/ppermute | solution.py:297
  15.9 7.7 %collective-permute-start.5 = (f32[4,2,16,256]{3,2,1,0:T(8,128)S(1)}, f32[4,2,16,256]{3,2,1,0:T(8,128)S(1)}, u32[]{:S(2)}, u32[]{:S(2)}) collective-permute-start(f32[4,2,16,256]{3,2,1,0:T(8,128)S(1)} %get-tuple-element.54), channel_id=1, source_target_pairs={{0,4},{1,5},{2,6},{3,7},{4,0},{5,1},{6,2},{7,3},{8,12},{9,13},{10,... | collective-permute-start | bytes 393224 | tf_op jit(solution)/shard_map/ppermute | solution.py:297
  16.3 10.4 %collective-permute-start.6 = (f32[4,2,16,256]{3,2,1,0:T(8,128)S(1)}, f32[4,2,16,256]{3,2,1,0:T(8,128)S(1)}, u32[]{:S(2)}, u32[]{:S(2)}) collective-permute-start(f32[4,2,16,256]{3,2,1,0:T(8,128)S(1)} %get-tuple-element.55), channel_id=1, source_target_pairs={{0,8},{1,9},{2,10},{3,11},{4,12},{5,13},{6,14},{7,15},{8,0},{9,1},... | collective-permute-start | bytes 393224 | tf_op jit(solution)/shard_map/ppermute | solution.py:297
  19.6 7.1 %collective-permute-start.11 = (f32[4,2,16,256]{3,2,1,0:T(8,128)S(1)}, f32[4,2,16,256]{3,2,1,0:T(8,128)S(1)}, u32[]{:S(2)}, u32[]{:S(2)}) collective-permute-start(f32[4,2,16,256]{3,2,1,0:T(8,128)S(1)} %get-tuple-element.63), channel_id=1, source_target_pairs={{0,2},{1,3},{2,0},{3,1},{4,6},{5,7},{6,4},{7,5},{8,10},{9,11},{10,... | collective-permute-start | bytes 393224 | tf_op jit(solution)/shard_map/ppermute | solution.py:297
  21.1 5.6 %collective-permute-start.12 = (f32[4,2,16,256]{3,2,1,0:T(8,128)S(1)}, f32[4,2,16,256]{3,2,1,0:T(8,128)S(1)}, u32[]{:S(2)}, u32[]{:S(2)}) collective-permute-start(f32[4,2,16,256]{3,2,1,0:T(8,128)S(1)} %get-tuple-element.64), channel_id=1, source_target_pairs={{0,1},{1,0},{2,3},{3,2},{4,5},{5,4},{6,7},{7,6},{8,9},{9,8},{10,11... | collective-permute-start | bytes 393224 | tf_op jit(solution)/shard_map/ppermute | solution.py:297
  21.1 5.8 %collective-permute-start.13 = (f32[4,2,16,256]{3,2,1,0:T(8,128)S(1)}, f32[4,2,16,256]{3,2,1,0:T(8,128)S(1)}, u32[]{:S(2)}, u32[]{:S(2)}) collective-permute-start(f32[4,2,16,256]{3,2,1,0:T(8,128)S(1)} %get-tuple-element.65), channel_id=1, source_target_pairs={{0,3},{1,2},{2,1},{3,0},{4,7},{5,6},{6,5},{7,4},{8,11},{9,10},{10,... | collective-permute-start | bytes 393224 | tf_op jit(solution)/shard_map/ppermute | solution.py:297
  23.6 7.1 %collective-permute-start.7 = (f32[4,2,16,256]{3,2,1,0:T(8,128)S(1)}, f32[4,2,16,256]{3,2,1,0:T(8,128)S(1)}, u32[]{:S(2)}, u32[]{:S(2)}) collective-permute-start(f32[4,2,16,256]{3,2,1,0:T(8,128)S(1)} %get-tuple-element.56), channel_id=1, source_target_pairs={{0,12},{1,13},{2,14},{3,15},{4,8},{5,9},{6,10},{7,11},{8,4},{9,5},... | collective-permute-start | bytes 393224 | tf_op jit(solution)/shard_map/ppermute | solution.py:297
  28.1 8.6 %collective-permute-start.14 = (f32[4,2,16,256]{3,2,1,0:T(8,128)S(1)}, f32[4,2,16,256]{3,2,1,0:T(8,128)S(1)}, u32[]{:S(2)}, u32[]{:S(2)}) collective-permute-start(f32[4,2,16,256]{3,2,1,0:T(8,128)S(1)} %get-tuple-element.66), channel_id=1, source_target_pairs={{0,4},{1,5},{2,6},{3,7},{4,0},{5,1},{6,2},{7,3},{8,12},{9,13},{10,... | collective-permute-start | bytes 393224 | tf_op jit(solution)/shard_map/ppermute | solution.py:297
  28.6 9.6 %collective-permute-start.15 = (f32[4,2,16,256]{3,2,1,0:T(8,128)S(1)}, f32[4,2,16,256]{3,2,1,0:T(8,128)S(1)}, u32[]{:S(2)}, u32[]{:S(2)}) collective-permute-start(f32[4,2,16,256]{3,2,1,0:T(8,128)S(1)} %get-tuple-element.67), channel_id=1, source_target_pairs={{0,8},{1,9},{2,10},{3,11},{4,12},{5,13},{6,14},{7,15},{8,0},{9,1},... | collective-permute-start | bytes 393224 | tf_op jit(solution)/shard_map/ppermute | solution.py:297
  31.9 6.3 %collective-permute-start.9 = (f32[4,2,16,256]{3,2,1,0:T(8,128)S(1)}, f32[4,2,16,256]{3,2,1,0:T(8,128)S(1)}, u32[]{:S(2)}, u32[]{:S(2)}) collective-permute-start(f32[4,2,16,256]{3,2,1,0:T(8,128)S(1)} %get-tuple-element.59), channel_id=1, source_target_pairs={{0,1},{1,0},{2,3},{3,2},{4,5},{5,4},{6,7},{7,6},{8,9},{9,8},{10,11... | collective-permute-start | bytes 393224 | tf_op jit(solution)/shard_map/ppermute | solution.py:297
  32.0 6.2 %collective-permute-start.16 = (f32[4,2,16,256]{3,2,1,0:T(8,128)S(1)}, f32[4,2,16,256]{3,2,1,0:T(8,128)S(1)}, u32[]{:S(2)}, u32[]{:S(2)}) collective-permute-start(f32[4,2,16,256]{3,2,1,0:T(8,128)S(1)} %get-tuple-element.69), channel_id=1, source_target_pairs={{0,3},{1,2},{2,1},{3,0},{4,7},{5,6},{6,5},{7,4},{8,11},{9,10},{10,... | collective-permute-start | bytes 393224 | tf_op jit(solution)/shard_map/ppermute | solution.py:297
  33.6 7.1 %collective-permute-start.8 = (f32[4,2,16,256]{3,2,1,0:T(8,128)S(1)}, f32[4,2,16,256]{3,2,1,0:T(8,128)S(1)}, u32[]{:S(2)}, u32[]{:S(2)}) collective-permute-start(f32[4,2,16,256]{3,2,1,0:T(8,128)S(1)} %get-tuple-element.58), channel_id=1, source_target_pairs={{0,2},{1,3},{2,0},{3,1},{4,6},{5,7},{6,4},{7,5},{8,10},{9,11},{10,... | collective-permute-start | bytes 393224 | tf_op jit(solution)/shard_map/ppermute | solution.py:297
  36.7 8.2 %collective-permute-start.20 = (f32[4,2,16,256]{3,2,1,0:T(8,128)S(1)}, f32[4,2,16,256]{3,2,1,0:T(8,128)S(1)}, u32[]{:S(2)}, u32[]{:S(2)}) collective-permute-start(f32[4,2,16,256]{3,2,1,0:T(8,128)S(1)} %get-tuple-element.75), channel_id=1, source_target_pairs={{0,12},{1,13},{2,14},{3,15},{4,8},{5,9},{6,10},{7,11},{8,4},{9,5},... | collective-permute-start | bytes 393224 | tf_op jit(solution)/shard_map/ppermute | solution.py:297
  40.7 7.2 %collective-permute-start.17 = (f32[4,2,16,256]{3,2,1,0:T(8,128)S(1)}, f32[4,2,16,256]{3,2,1,0:T(8,128)S(1)}, u32[]{:S(2)}, u32[]{:S(2)}) collective-permute-start(f32[4,2,16,256]{3,2,1,0:T(8,128)S(1)} %get-tuple-element.71), channel_id=1, source_target_pairs={{0,4},{1,5},{2,6},{3,7},{4,0},{5,1},{6,2},{7,3},{8,12},{9,13},{10,... | collective-permute-start | bytes 393224 | tf_op jit(solution)/shard_map/ppermute | solution.py:297
  42.1 9.0 %collective-permute-start.18 = (f32[4,2,16,256]{3,2,1,0:T(8,128)S(1)}, f32[4,2,16,256]{3,2,1,0:T(8,128)S(1)}, u32[]{:S(2)}, u32[]{:S(2)}) collective-permute-start(f32[4,2,16,256]{3,2,1,0:T(8,128)S(1)} %get-tuple-element.72), channel_id=1, source_target_pairs={{0,8},{1,9},{2,10},{3,11},{4,12},{5,13},{6,14},{7,15},{8,0},{9,1},... | collective-permute-start | bytes 393224 | tf_op jit(solution)/shard_map/ppermute | solution.py:297
  45.0 6.1 %collective-permute-start.21 = (f32[4,2,16,256]{3,2,1,0:T(8,128)S(1)}, f32[4,2,16,256]{3,2,1,0:T(8,128)S(1)}, u32[]{:S(2)}, u32[]{:S(2)}) collective-permute-start(f32[4,2,16,256]{3,2,1,0:T(8,128)S(1)} %get-tuple-element.78), channel_id=1, source_target_pairs={{0,1},{1,0},{2,3},{3,2},{4,5},{5,4},{6,7},{7,6},{8,9},{9,8},{10,11... | collective-permute-start | bytes 393224 | tf_op jit(solution)/shard_map/ppermute | solution.py:297
  45.1 6.4 %collective-permute-start.22 = (f32[4,2,16,256]{3,2,1,0:T(8,128)S(1)}, f32[4,2,16,256]{3,2,1,0:T(8,128)S(1)}, u32[]{:S(2)}, u32[]{:S(2)}) collective-permute-start(f32[4,2,16,256]{3,2,1,0:T(8,128)S(1)} %get-tuple-element.79), channel_id=1, source_target_pairs={{0,2},{1,3},{2,0},{3,1},{4,6},{5,7},{6,4},{7,5},{8,10},{9,11},{10,... | collective-permute-start | bytes 393224 | tf_op jit(solution)/shard_map/ppermute | solution.py:297
  45.1 8.2 %collective-permute-start.23 = (f32[4,2,16,256]{3,2,1,0:T(8,128)S(1)}, f32[4,2,16,256]{3,2,1,0:T(8,128)S(1)}, u32[]{:S(2)}, u32[]{:S(2)}) collective-permute-start(f32[4,2,16,256]{3,2,1,0:T(8,128)S(1)} %get-tuple-element.80), channel_id=1, source_target_pairs={{0,3},{1,2},{2,1},{3,0},{4,7},{5,6},{6,5},{7,4},{8,11},{9,10},{10,... | collective-permute-start | bytes 393224 | tf_op jit(solution)/shard_map/ppermute | solution.py:297
  47.9 6.8 %collective-permute-start.19 = (f32[4,2,16,256]{3,2,1,0:T(8,128)S(1)}, f32[4,2,16,256]{3,2,1,0:T(8,128)S(1)}, u32[]{:S(2)}, u32[]{:S(2)}) collective-permute-start(f32[4,2,16,256]{3,2,1,0:T(8,128)S(1)} %get-tuple-element.73), channel_id=1, source_target_pairs={{0,12},{1,13},{2,14},{3,15},{4,8},{5,9},{6,10},{7,11},{8,4},{9,5},... | collective-permute-start | bytes 393224 | tf_op jit(solution)/shard_map/ppermute | solution.py:297

commit v8 on v7

--- a/solution.py
+++ b/solution.py
@@ -339,7 +339,7 @@
             name="close_1",
         )(me, tables[2], *values, first)
 
-    orders = [lower(width // 2), lower(width // 2), lower(), lower(width // 2)]
+    orders = [lower(width // 2), lower(width // 2), lower(1, width - 1), lower(width // 2)]
     uppers = [layout_over(upper, order) for order in orders]
     lowers = [layout_over(order, upper) for order in orders]
 
@@ -352,11 +352,11 @@
     behind = send(behind, uppers[1])
     ahead = turn(uppers[0], lowers[0], ahead, "turn_0_in")
     ahead = send(ahead, lowers[0])
-    ahead = middle(lowers[0], uppers[2], tied(ahead, 0, behind[1:3]), "middle_0")
+    ahead = middle(lowers[0], uppers[2], tied(ahead, 1, behind[1:3]), "middle_0")
     ahead = send(ahead, uppers[2])
     behind = middle(uppers[1], lowers[3], behind, "middle_1")
     behind = send(behind, lowers[3])
-    behind = turn(lowers[3], uppers[3], tied(behind, 2, ahead[1:3]), "turn_1_out")
+    behind = turn(lowers[3], uppers[3], tied(behind, 1, ahead[1:3]), "turn_1_out")
     behind = send(behind, uppers[3])
     ahead = turn(uppers[2], lowers[2], ahead, "turn_0_out")
     ahead = send(ahead, lowers[2])

time: 56.3 us -> 56 us (level)
  waiting for transfers between devices: 14.2 us -> 12.7 us
  starting transfers between devices: 32.4 us -> 33.6 us
    ppermute x24, waiting for transfers between devices: 14.2 us -> 12.7 us  [send(): lax.ppermute(value, 'stem', [(i, i ^ step) for i in range(devices)])]
    ppermute x24, starting transfers between devices: 32.4 us -> 33.6 us  [send(): lax.ppermute(value, 'stem', [(i, i ^ step) for i in range(devices)])]
  transfers between devices with their start and end apart: 24 -> 24, of which waited for: 12 -> 9; matrix products, arithmetic and copies ran while one was open for 0% -> 0% of each run, Pallas kernels for 10% -> 10%
where the time goes in v8:
time: 56 us; the launch traced here: 55.8 us
  starting transfers between devices  33.6 us (60%)
  waiting for transfers between devices  12.7 us (23%)
  Pallas kernels  7.82 us (14%)
  local copies, waits for them, and re-layouts  1.43 us (3%)
    ppermute x24, starting transfers between devices, send(): lax.ppermute(value, 'stem', [(i, i ^ step) for i in range(devices)])  33.6 us
    ppermute x24, waiting for transfers between devices, send(): lax.ppermute(value, 'stem', [(i, i ^ step) for i in range(devices)])  12.7 us
    pallas_call x9, Pallas kernels, call(): pl.pallas_call(kernel, out_shape=blocks(out) if isinstance(out, tuple) el...  4.45 us
    pallas_call x1, Pallas kernels, one_slice(): pl.pallas_call(chain_kernel, out_shape=jax.ShapeDtypeStruct((2, low, low)...  1.94 us
    pallas_call x1, Pallas kernels, close_last(): pl.pallas_call(functools.partial(close_last_kernel, layout), out_shape=ja...  1.44 us
    slice x1, local copies, waits for them, and re-layouts, open_first(): packed = jnp.concatenate([laid[0], matrix], axis=0)  1.13 us
  transfers between devices with their start and end apart: 24, of which 9 were waited for; matrix products, arithmetic and copies ran while one was open for 0% of the time, Pallas kernels for 10%

profile of v8, /device:TPU:0, one launch (start us, length us, event | category | flops | bytes accessed | tf_op | source)
XLA Modules:
  0.0 55.8 jit_solution(5838347246404153896)
XLA Ops:
  0.0 1.1 %slice.27 = f32[512,2,128]{2,1,0:T(2,128)S(1)} slice(f32[1024,2,128]{2,1,0:T(2,128)} %bitcast.27), slice={[0:512], [0:2], [0:128]} | slice | bytes 1048576 | tf_op jit(solution)/shard_map/slice | solution.py:308
  1.1 0.1 slice-done
  1.2 0.1 pad_maximum_fusion.packed_ref
  1.3 0.0 copy-start.3
  1.3 0.6 %open_0.1 = (f32[4,2,16,256]{3,2,1,0:T(8,128)S(1)}, f32[4,2,16,256]{3,2,1,0:T(8,128)S(1)}, f32[4,2,16,256]{3,2,1,0:T(8,128)S(1)}, f32[4,2,16,256]{3,2,1,0:T(8,128)S(1)}) custom-call(s32[1]{0:T(128)} %bitcast.me_ref, f32[2048,128]{1,0:T(8,128)S(1)} %pad_maximum_fusion.packed_ref), custom_call_target="tpu_custom_call" | custom-call | tf_op jit(solution)/shard_map/open_0/pallas_call | solution.py:284
  1.9 3.1 %collective-permute-start = (f32[4,2,16,256]{3,2,1,0:T(8,128)S(1)}, f32[4,2,16,256]{3,2,1,0:T(8,128)S(1)}, u32[]{:S(2)}, u32[]{:S(2)}) collective-permute-start(f32[4,2,16,256]{3,2,1,0:T(8,128)S(1)} %get-tuple-element.47), channel_id=1, source_target_pairs={{0,4},{1,5},{2,6},{3,7},{4,0},{5,1},{6,2},{7,3},{8,12},{9,13},{10,... | collective-permute-start | bytes 393224 | tf_op jit(solution)/shard_map/ppermute | solution.py:297
  5.0 2.6 %collective-permute-start.1 = (f32[4,2,16,256]{3,2,1,0:T(8,128)S(1)}, f32[4,2,16,256]{3,2,1,0:T(8,128)S(1)}, u32[]{:S(2)}, u32[]{:S(2)}) collective-permute-start(f32[4,2,16,256]{3,2,1,0:T(8,128)S(1)} %get-tuple-element.48), channel_id=1, source_target_pairs={{0,8},{1,9},{2,10},{3,11},{4,12},{5,13},{6,14},{7,15},{8,0},{9,1},... | collective-permute-start | bytes 393224 | tf_op jit(solution)/shard_map/ppermute | solution.py:297
  7.6 0.0 copy-done.2
  7.6 0.2 slice_bitcast_fusion
  7.8 0.0 copy-done.3
  7.8 0.0 copy-start.1
  7.8 0.6 %open_1.1 = (f32[4,2,16,256]{3,2,1,0:T(8,128)S(1)}, f32[4,2,16,256]{3,2,1,0:T(8,128)S(1)}, f32[4,2,16,256]{3,2,1,0:T(8,128)S(1)}, f32[4,2,16,256]{3,2,1,0:T(8,128)S(1)}) custom-call(s32[1]{0:T(128)} %bitcast.me_ref, f32[1024,128]{1,0:T(8,128)S(1)} %slice_bitcast_fusion.1.stem_ref, f32[2,256,256]{2,1,0:T(8,128)S(1)} %get-tuple-element.81.table), custom_call_target="tpu_custom_call" | custom-call | tf_op jit(solution)/shard_map/open_1/pallas_call | solution.py:284
  8.4 1.6 %collective-permute-start.2 = (f32[4,2,16,256]{3,2,1,0:T(8,128)S(1)}, f32[4,2,16,256]{3,2,1,0:T(8,128)S(1)}, u32[]{:S(2)}, u32[]{:S(2)}) collective-permute-start(f32[4,2,16,256]{3,2,1,0:T(8,128)S(1)} %get-tuple-element.50), channel_id=1, source_target_pairs={{0,2},{1,3},{2,0},{3,1},{4,6},{5,7},{6,4},{7,5},{8,10},{9,11},{10,... | collective-permute-start | bytes 393224 | tf_op jit(solution)/shard_map/ppermute | solution.py:297
  10.0 0.0 collective-permute-start.3
  10.0 0.6 %collective-permute-start.4 = (f32[4,2,16,256]{3,2,1,0:T(8,128)S(1)}, f32[4,2,16,256]{3,2,1,0:T(8,128)S(1)}, u32[]{:S(2)}, u32[]{:S(2)}) collective-permute-start(f32[4,2,16,256]{3,2,1,0:T(8,128)S(1)} %get-tuple-element.52), channel_id=1, source_target_pairs={{0,3},{1,2},{2,1},{3,0},{4,7},{5,6},{6,5},{7,4},{8,11},{9,10},{10,... | collective-permute-start | bytes 393224 | tf_op jit(solution)/shard_map/ppermute | solution.py:297
  10.7 0.0 collective-permute-done.refs_1_
  10.7 3.2 %collective-permute-start.9 = (f32[4,2,16,256]{3,2,1,0:T(8,128)S(1)}, f32[4,2,16,256]{3,2,1,0:T(8,128)S(1)}, u32[]{:S(2)}, u32[]{:S(2)}) collective-permute-start(f32[4,2,16,256]{3,2,1,0:T(8,128)S(1)} %get-tuple-element.59), channel_id=1, source_target_pairs={{0,12},{1,13},{2,14},{3,15},{4,8},{5,9},{6,10},{7,11},{8,4},{9,5},... | collective-permute-start | bytes 393224 | tf_op jit(solution)/shard_map/ppermute | solution.py:297
  13.8 0.0 copy-done.1
  13.8 1.9 %low_chain.1.low_table = f32[2,256,256]{2,1,0:T(8,128)S(1)} custom-call(s32[1,3]{1,0:T(1,128)S(1)} %copy-done.1, f32[3,2,2,256,256]{4,3,2,1,0:T(8,128)S(1)} %copy-done), custom_call_target="tpu_custom_call" | custom-call | tf_op jit(solution)/shard_map/low_chain/pallas_call | solution.py:391
  15.8 0.0 collective-permute-done.1.refs_2_
  15.8 0.0 collective-permute-done.2.refs_1_
  15.8 0.0 collective-permute-done.3.refs_2_
  15.8 0.0 collective-permute-done.4.refs_3_
  15.9 0.5 collective-permute-start.5
  16.3 3.2 %collective-permute-start.6 = (f32[4,2,16,256]{3,2,1,0:T(8,128)S(1)}, f32[4,2,16,256]{3,2,1,0:T(8,128)S(1)}, u32[]{:S(2)}, u32[]{:S(2)}) collective-permute-start(f32[4,2,16,256]{3,2,1,0:T(8,128)S(1)} %get-tuple-element.55), channel_id=1, source_target_pairs={{0,8},{1,9},{2,10},{3,11},{4,12},{5,13},{6,14},{7,15},{8,0},{9,1},... | collective-permute-start | bytes 393224 | tf_op jit(solution)/shard_map/ppermute | solution.py:297
  19.5 0.0 collective-permute-done.9.refs_3_
  19.6 1.6 %collective-permute-start.10 = (f32[4,2,16,256]{3,2,1,0:T(8,128)S(1)}, f32[4,2,16,256]{3,2,1,0:T(8,128)S(1)}, u32[]{:S(2)}, u32[]{:S(2)}) collective-permute-start(f32[4,2,16,256]{3,2,1,0:T(8,128)S(1)} %get-tuple-element.61), channel_id=1, source_target_pairs={{0,2},{1,3},{2,0},{3,1},{4,6},{5,7},{6,4},{7,5},{8,10},{9,11},{10,... | collective-permute-start | bytes 393224 | tf_op jit(solution)/shard_map/ppermute | solution.py:297
  21.1 0.0 collective-permute-start.11
  21.1 0.6 %collective-permute-start.12 = (f32[4,2,16,256]{3,2,1,0:T(8,128)S(1)}, f32[4,2,16,256]{3,2,1,0:T(8,128)S(1)}, u32[]{:S(2)}, u32[]{:S(2)}) collective-permute-start(f32[4,2,16,256]{3,2,1,0:T(8,128)S(1)} %get-tuple-element.64), channel_id=1, source_target_pairs={{0,3},{1,2},{2,1},{3,0},{4,7},{5,6},{6,5},{7,4},{8,11},{9,10},{10,... | collective-permute-start | bytes 393224 | tf_op jit(solution)/shard_map/ppermute | solution.py:297
  21.8 1.8 %collective-permute-done.5.refs_1_ = f32[4,2,16,256]{3,2,1,0:T(8,128)S(1)} collective-permute-done((f32[4,2,16,256]{3,2,1,0:T(8,128)S(1)}, f32[4,2,16,256]{3,2,1,0:T(8,128)S(1)}, u32[]{:S(2)}, u32[]{:S(2)}) %collective-permute-start.5) | collective-permute-done | bytes 131104 | tf_op jit(solution)/shard_map/ppermute | solution.py:297
  23.6 2.1 %collective-permute-start.7 = (f32[4,2,16,256]{3,2,1,0:T(8,128)S(1)}, f32[4,2,16,256]{3,2,1,0:T(8,128)S(1)}, u32[]{:S(2)}, u32[]{:S(2)}) collective-permute-start(f32[4,2,16,256]{3,2,1,0:T(8,128)S(1)} %get-tuple-element.56), channel_id=1, source_target_pairs={{0,12},{1,13},{2,14},{3,15},{4,8},{5,9},{6,10},{7,11},{8,4},{9,5},... | collective-permute-start | bytes 393224 | tf_op jit(solution)/shard_map/ppermute | solution.py:297
  25.7 1.0 %collective-permute-done.6.refs_2_ = f32[4,2,16,256]{3,2,1,0:T(8,128)S(1)} collective-permute-done((f32[4,2,16,256]{3,2,1,0:T(8,128)S(1)}, f32[4,2,16,256]{3,2,1,0:T(8,128)S(1)}, u32[]{:S(2)}, u32[]{:S(2)}) %collective-permute-start.6) | collective-permute-done | bytes 131104 | tf_op jit(solution)/shard_map/ppermute | solution.py:297
  26.7 0.0 collective-permute-done.10.refs_1_
  26.7 0.0 collective-permute-done.11.refs_2_
  26.7 0.2 collective-permute-done.12.refs_3_
  26.9 1.2 %middle_0.1 = (f32[4,2,16,256]{3,2,1,0:T(8,128)S(1)}, f32[4,2,16,256]{3,2,1,0:T(8,128)S(1)}, f32[4,2,16,256]{3,2,1,0:T(8,128)S(1)}, f32[4,2,16,256]{3,2,1,0:T(8,128)S(1)}) custom-call(s32[1]{0:T(128)} %bitcast.me_ref, f32[2,256,256]{2,1,0:T(8,128)S(1)} %get-tuple-element.82.table, f32[2,256,256]{2,1,0:T(8,128)S(1)} %low_chain.1.low_table, ...), custom_call_target="tpu_custom_call" | custom-call | tf_op jit(solution)/shard_map/middle_0/pallas_call | solution.py:284
  28.1 0.4 collective-permute-start.13
  28.6 1.6 %collective-permute-start.14 = (f32[4,2,16,256]{3,2,1,0:T(8,128)S(1)}, f32[4,2,16,256]{3,2,1,0:T(8,128)S(1)}, u32[]{:S(2)}, u32[]{:S(2)}) collective-permute-start(f32[4,2,16,256]{3,2,1,0:T(8,128)S(1)} %get-tuple-element.66), channel_id=1, source_target_pairs={{0,8},{1,9},{2,10},{3,11},{4,12},{5,13},{6,14},{7,15},{8,0},{9,1},... | collective-permute-start | bytes 393224 | tf_op jit(solution)/shard_map/ppermute | solution.py:297
  30.2 0.5 collective-permute-done.7.refs_3_
  30.7 1.2 %middle_1.1 = (f32[4,2,16,256]{3,2,1,0:T(8,128)S(1)}, f32[4,2,16,256]{3,2,1,0:T(8,128)S(1)}, f32[4,2,16,256]{3,2,1,0:T(8,128)S(1)}, f32[4,2,16,256]{3,2,1,0:T(8,128)S(1)}) custom-call(s32[1]{0:T(128)} %bitcast.me_ref, f32[2,256,256]{2,1,0:T(8,128)S(1)} %get-tuple-element.82.table, f32[2,256,256]{2,1,0:T(8,128)S(1)} %low_chain.1.low_table, ...), custom_call_target="tpu_custom_call" | custom-call | tf_op jit(solution)/shard_map/middle_1/pallas_call | solution.py:284
  31.9 1.5 %collective-permute-start.8 = (f32[4,2,16,256]{3,2,1,0:T(8,128)S(1)}, f32[4,2,16,256]{3,2,1,0:T(8,128)S(1)}, u32[]{:S(2)}, u32[]{:S(2)}) collective-permute-start(f32[4,2,16,256]{3,2,1,0:T(8,128)S(1)} %get-tuple-element.58), channel_id=1, source_target_pairs={{0,2},{1,3},{2,0},{3,1},{4,6},{5,7},{6,4},{7,5},{8,10},{9,11},{10,... | collective-permute-start | bytes 393224 | tf_op jit(solution)/shard_map/ppermute | solution.py:297
  33.5 0.0 collective-permute-start.15
  33.5 0.7 %collective-permute-start.16 = (f32[4,2,16,256]{3,2,1,0:T(8,128)S(1)}, f32[4,2,16,256]{3,2,1,0:T(8,128)S(1)}, u32[]{:S(2)}, u32[]{:S(2)}) collective-permute-start(f32[4,2,16,256]{3,2,1,0:T(8,128)S(1)} %get-tuple-element.69), channel_id=1, source_target_pairs={{0,3},{1,2},{2,1},{3,0},{4,7},{5,6},{6,5},{7,4},{8,11},{9,10},{10,... | collective-permute-start | bytes 393224 | tf_op jit(solution)/shard_map/ppermute | solution.py:297
  34.1 2.6 %collective-permute-done.13.refs_1_ = f32[4,2,16,256]{3,2,1,0:T(8,128)S(1)} collective-permute-done((f32[4,2,16,256]{3,2,1,0:T(8,128)S(1)}, f32[4,2,16,256]{3,2,1,0:T(8,128)S(1)}, u32[]{:S(2)}, u32[]{:S(2)}) %collective-permute-start.13) | collective-permute-done | bytes 131104 | tf_op jit(solution)/shard_map/ppermute | solution.py:297
  36.7 0.3 collective-permute-start.20
  37.1 1.2 %collective-permute-done.14.refs_2_ = f32[4,2,16,256]{3,2,1,0:T(8,128)S(1)} collective-permute-done((f32[4,2,16,256]{3,2,1,0:T(8,128)S(1)}, f32[4,2,16,256]{3,2,1,0:T(8,128)S(1)}, u32[]{:S(2)}, u32[]{:S(2)}) %collective-permute-start.14) | collective-permute-done | bytes 131104 | tf_op jit(solution)/shard_map/ppermute | solution.py:297
  38.2 0.0 collective-permute-done.8.refs_1_
  38.2 0.0 collective-permute-done.15.refs_2_
  38.2 1.0 %collective-permute-done.16.refs_3_ = f32[4,2,16,256]{3,2,1,0:T(8,128)S(1)} collective-permute-done((f32[4,2,16,256]{3,2,1,0:T(8,128)S(1)}, f32[4,2,16,256]{3,2,1,0:T(8,128)S(1)}, u32[]{:S(2)}, u32[]{:S(2)}) %collective-permute-start.16) | collective-permute-done | bytes 131104 | tf_op jit(solution)/shard_map/ppermute | solution.py:297
  39.3 1.4 %collective-permute-start.17 = (f32[4,2,16,256]{3,2,1,0:T(8,128)S(1)}, f32[4,2,16,256]{3,2,1,0:T(8,128)S(1)}, u32[]{:S(2)}, u32[]{:S(2)}) collective-permute-start(f32[4,2,16,256]{3,2,1,0:T(8,128)S(1)} %get-tuple-element.71), channel_id=1, source_target_pairs={{0,4},{1,5},{2,6},{3,7},{4,0},{5,1},{6,2},{7,3},{8,12},{9,13},{10,... | collective-permute-start | bytes 393224 | tf_op jit(solution)/shard_map/ppermute | solution.py:297
  40.7 4.3 %collective-permute-start.18 = (f32[4,2,16,256]{3,2,1,0:T(8,128)S(1)}, f32[4,2,16,256]{3,2,1,0:T(8,128)S(1)}, u32[]{:S(2)}, u32[]{:S(2)}) collective-permute-start(f32[4,2,16,256]{3,2,1,0:T(8,128)S(1)} %get-tuple-element.72), channel_id=1, source_target_pairs={{0,8},{1,9},{2,10},{3,11},{4,12},{5,13},{6,14},{7,15},{8,0},{9,1},... | collective-permute-start | bytes 393224 | tf_op jit(solution)/shard_map/ppermute | solution.py:297
  44.9 0.0 collective-permute-done.20.refs_3_
  45.0 0.1 collective-permute-start.21
  45.1 0.1 collective-permute-start.22
  45.1 2.1 %collective-permute-start.23 = (f32[4,2,16,256]{3,2,1,0:T(8,128)S(1)}, f32[4,2,16,256]{3,2,1,0:T(8,128)S(1)}, u32[]{:S(2)}, u32[]{:S(2)}) collective-permute-start(f32[4,2,16,256]{3,2,1,0:T(8,128)S(1)} %get-tuple-element.80), channel_id=1, source_target_pairs={{0,2},{1,3},{2,0},{3,1},{4,6},{5,7},{6,4},{7,5},{8,10},{9,11},{10,... | collective-permute-start | bytes 393224 | tf_op jit(solution)/shard_map/ppermute | solution.py:297
  47.2 0.0 collective-permute-done.17.refs_1_
  47.2 2.2 %collective-permute-start.19 = (f32[4,2,16,256]{3,2,1,0:T(8,128)S(1)}, f32[4,2,16,256]{3,2,1,0:T(8,128)S(1)}, u32[]{:S(2)}, u32[]{:S(2)}) collective-permute-start(f32[4,2,16,256]{3,2,1,0:T(8,128)S(1)} %get-tuple-element.73), channel_id=1, source_target_pairs={{0,12},{1,13},{2,14},{3,15},{4,8},{5,9},{6,10},{7,11},{8,4},{9,5},... | collective-permute-start | bytes 393224 | tf_op jit(solution)/shard_map/ppermute | solution.py:297
  49.4 1.4 %collective-permute-done.18.refs_2_ = f32[4,2,16,256]{3,2,1,0:T(8,128)S(1)} collective-permute-done((f32[4,2,16,256]{3,2,1,0:T(8,128)S(1)}, f32[4,2,16,256]{3,2,1,0:T(8,128)S(1)}, u32[]{:S(2)}, u32[]{:S(2)}) %collective-permute-start.18) | collective-permute-done | bytes 131104 | tf_op jit(solution)/shard_map/ppermute | solution.py:297
  50.8 0.0 collective-permute-done.21.refs_1_
  50.8 0.0 collective-permute-done.22.refs_2_
  50.8 2.9 %collective-permute-done.23.refs_3_ = f32[4,2,16,256]{3,2,1,0:T(8,128)S(1)} collective-permute-done((f32[4,2,16,256]{3,2,1,0:T(8,128)S(1)}, f32[4,2,16,256]{3,2,1,0:T(8,128)S(1)}, u32[]{:S(2)}, u32[]{:S(2)}) %collective-permute-start.23) | collective-permute-done | bytes 131104 | tf_op jit(solution)/shard_map/ppermute | solution.py:297
  53.7 0.6 %close_0.1.refs_4_ = f32[1024,128]{1,0:T(8,128)S(1)} custom-call(s32[1]{0:T(128)} %bitcast.me_ref, f32[2,256,256]{2,1,0:T(8,128)S(1)} %get-tuple-element.83.table, f32[4,2,16,256]{3,2,1,0:T(8,128)S(1)} %get-tuple-element.77.refs_0_, f32[4,2,16,256]{3,2,1,0:T(8,128)S(1)} %collective-permute-done.21.refs_1_, ...), custom_call_target="tpu_custom_call" | custom-call | tf_op jit(solution)/shard_map/close_0/pallas_call | solution.py:284
  54.4 0.0 collective-permute-done.19.refs_3_
  54.4 1.4 %close_1.1 = f32[2,1024,128]{2,1,0:T(8,128)} custom-call(s32[1]{0:T(128)} %bitcast.me_ref, f32[2,256,256]{2,1,0:T(8,128)S(1)} %get-tuple-element.83.table, f32[4,2,16,256]{3,2,1,0:T(8,128)S(1)} %get-tuple-element.70.refs_0_, f32[4,2,16,256]{3,2,1,0:T(8,128)S(1)} %collective-permute-done.17.refs_1_, f32[4,2,16,256]{3,2,1,0:T(8,128)S(1)} %collective-permute-done.18.refs_2_, ...), custom_call_target="tpu_custom_call" | custom-call | tf_op jit(solution)/shard_map/close_1/pallas_call | solution.py:328
  (9 shorter events, 0.2 us)
Async XLA Ops:
  0.0 1.2 %slice-start = ((f32[3,2,256,256]{3,2,1,0:T(8,128)}), f32[1,2,256,256]{3,2,1,0:T(8,128)S(1)}, s32[]{:S(2)}) async-start(f32[3,2,256,256]{3,2,1,0:T(8,128)} %param.6), calls=%async_computation | async-start | bytes 1048576 | tf_op jit(solution)/shard_map/slice | solution.py:306
  1.2 6.4 %copy-start.2 = (f32[3,2,256,256]{3,2,1,0:T(8,128)S(1)}, f32[3,2,256,256]{3,2,1,0:T(8,128)}, u32[]{:S(2)}) copy-start(f32[3,2,256,256]{3,2,1,0:T(8,128)} %param.6) | copy-start | bytes 4718596
  1.3 6.5 %copy-start.3 = (f32[1,2,131072]{2,1,0:T(2,128)S(1)}, f32[1,2,131072]{2,1,0:T(2,128)}, u32[]{:S(2)}) copy-start(f32[1,2,131072]{2,1,0:T(2,128)} %param.4) | copy-start | bytes 3145732
  1.9 8.7 %collective-permute-start = (f32[4,2,16,256]{3,2,1,0:T(8,128)S(1)}, f32[4,2,16,256]{3,2,1,0:T(8,128)S(1)}, u32[]{:S(2)}, u32[]{:S(2)}) collective-permute-start(f32[4,2,16,256]{3,2,1,0:T(8,128)S(1)} %get-tuple-element.47), channel_id=1, source_target_pairs={{0,4},{1,5},{2,6},{3,7},{4,0},{5,1},{6,2},{7,3},{8,12},{9,13},{10,... | collective-permute-start | bytes 393224 | tf_op jit(solution)/shard_map/ppermute | solution.py:297
  5.0 10.8 %collective-permute-start.1 = (f32[4,2,16,256]{3,2,1,0:T(8,128)S(1)}, f32[4,2,16,256]{3,2,1,0:T(8,128)S(1)}, u32[]{:S(2)}, u32[]{:S(2)}) collective-permute-start(f32[4,2,16,256]{3,2,1,0:T(8,128)S(1)} %get-tuple-element.48), channel_id=1, source_target_pairs={{0,8},{1,9},{2,10},{3,11},{4,12},{5,13},{6,14},{7,15},{8,0},{9,1},... | collective-permute-start | bytes 393224 | tf_op jit(solution)/shard_map/ppermute | solution.py:297
  7.6 6.2 %copy-start = (f32[3,2,2,256,256]{4,3,2,1,0:T(8,128)S(1)}, f32[3,2,2,256,256]{4,3,2,1,0:T(8,128)}, u32[]{:S(2)}) copy-start(f32[3,2,2,256,256]{4,3,2,1,0:T(8,128)} %table_ref.1) | copy-start | bytes 9437188
  7.8 6.1 %copy-start.1 = (s32[1,3]{1,0:T(1,128)S(1)}, s32[1,3]{1,0:T(1,128)}, u32[]{:S(2)}) copy-start(s32[1,3]{1,0:T(1,128)} %bits_ref.1) | copy-start | bytes 40
  8.4 7.3 %collective-permute-start.2 = (f32[4,2,16,256]{3,2,1,0:T(8,128)S(1)}, f32[4,2,16,256]{3,2,1,0:T(8,128)S(1)}, u32[]{:S(2)}, u32[]{:S(2)}) collective-permute-start(f32[4,2,16,256]{3,2,1,0:T(8,128)S(1)} %get-tuple-element.50), channel_id=1, source_target_pairs={{0,2},{1,3},{2,0},{3,1},{4,6},{5,7},{6,4},{7,5},{8,10},{9,11},{10,... | collective-permute-start | bytes 393224 | tf_op jit(solution)/shard_map/ppermute | solution.py:297
  10.0 5.8 %collective-permute-start.3 = (f32[4,2,16,256]{3,2,1,0:T(8,128)S(1)}, f32[4,2,16,256]{3,2,1,0:T(8,128)S(1)}, u32[]{:S(2)}, u32[]{:S(2)}) collective-permute-start(f32[4,2,16,256]{3,2,1,0:T(8,128)S(1)} %get-tuple-element.51), channel_id=1, source_target_pairs={{0,1},{1,0},{2,3},{3,2},{4,5},{5,4},{6,7},{7,6},{8,9},{9,8},{10,11... | collective-permute-start | bytes 393224 | tf_op jit(solution)/shard_map/ppermute | solution.py:297
  10.0 5.8 %collective-permute-start.4 = (f32[4,2,16,256]{3,2,1,0:T(8,128)S(1)}, f32[4,2,16,256]{3,2,1,0:T(8,128)S(1)}, u32[]{:S(2)}, u32[]{:S(2)}) collective-permute-start(f32[4,2,16,256]{3,2,1,0:T(8,128)S(1)} %get-tuple-element.52), channel_id=1, source_target_pairs={{0,3},{1,2},{2,1},{3,0},{4,7},{5,6},{6,5},{7,4},{8,11},{9,10},{10,... | collective-permute-start | bytes 393224 | tf_op jit(solution)/shard_map/ppermute | solution.py:297
  10.7 8.9 %collective-permute-start.9 = (f32[4,2,16,256]{3,2,1,0:T(8,128)S(1)}, f32[4,2,16,256]{3,2,1,0:T(8,128)S(1)}, u32[]{:S(2)}, u32[]{:S(2)}) collective-permute-start(f32[4,2,16,256]{3,2,1,0:T(8,128)S(1)} %get-tuple-element.59), channel_id=1, source_target_pairs={{0,12},{1,13},{2,14},{3,15},{4,8},{5,9},{6,10},{7,11},{8,4},{9,5},... | collective-permute-start | bytes 393224 | tf_op jit(solution)/shard_map/ppermute | solution.py:297
  15.9 7.7 %collective-permute-start.5 = (f32[4,2,16,256]{3,2,1,0:T(8,128)S(1)}, f32[4,2,16,256]{3,2,1,0:T(8,128)S(1)}, u32[]{:S(2)}, u32[]{:S(2)}) collective-permute-start(f32[4,2,16,256]{3,2,1,0:T(8,128)S(1)} %get-tuple-element.54), channel_id=1, source_target_pairs={{0,4},{1,5},{2,6},{3,7},{4,0},{5,1},{6,2},{7,3},{8,12},{9,13},{10,... | collective-permute-start | bytes 393224 | tf_op jit(solution)/shard_map/ppermute | solution.py:297
  16.3 10.4 %collective-permute-start.6 = (f32[4,2,16,256]{3,2,1,0:T(8,128)S(1)}, f32[4,2,16,256]{3,2,1,0:T(8,128)S(1)}, u32[]{:S(2)}, u32[]{:S(2)}) collective-permute-start(f32[4,2,16,256]{3,2,1,0:T(8,128)S(1)} %get-tuple-element.55), channel_id=1, source_target_pairs={{0,8},{1,9},{2,10},{3,11},{4,12},{5,13},{6,14},{7,15},{8,0},{9,1},... | collective-permute-start | bytes 393224 | tf_op jit(solution)/shard_map/ppermute | solution.py:297
  19.6 7.1 %collective-permute-start.10 = (f32[4,2,16,256]{3,2,1,0:T(8,128)S(1)}, f32[4,2,16,256]{3,2,1,0:T(8,128)S(1)}, u32[]{:S(2)}, u32[]{:S(2)}) collective-permute-start(f32[4,2,16,256]{3,2,1,0:T(8,128)S(1)} %get-tuple-element.61), channel_id=1, source_target_pairs={{0,2},{1,3},{2,0},{3,1},{4,6},{5,7},{6,4},{7,5},{8,10},{9,11},{10,... | collective-permute-start | bytes 393224 | tf_op jit(solution)/shard_map/ppermute | solution.py:297
  21.1 5.6 %collective-permute-start.11 = (f32[4,2,16,256]{3,2,1,0:T(8,128)S(1)}, f32[4,2,16,256]{3,2,1,0:T(8,128)S(1)}, u32[]{:S(2)}, u32[]{:S(2)}) collective-permute-start(f32[4,2,16,256]{3,2,1,0:T(8,128)S(1)} %get-tuple-element.63), channel_id=1, source_target_pairs={{0,1},{1,0},{2,3},{3,2},{4,5},{5,4},{6,7},{7,6},{8,9},{9,8},{10,11... | collective-permute-start | bytes 393224 | tf_op jit(solution)/shard_map/ppermute | solution.py:297
  21.1 5.8 %collective-permute-start.12 = (f32[4,2,16,256]{3,2,1,0:T(8,128)S(1)}, f32[4,2,16,256]{3,2,1,0:T(8,128)S(1)}, u32[]{:S(2)}, u32[]{:S(2)}) collective-permute-start(f32[4,2,16,256]{3,2,1,0:T(8,128)S(1)} %get-tuple-element.64), channel_id=1, source_target_pairs={{0,3},{1,2},{2,1},{3,0},{4,7},{5,6},{6,5},{7,4},{8,11},{9,10},{10,... | collective-permute-start | bytes 393224 | tf_op jit(solution)/shard_map/ppermute | solution.py:297
  23.6 7.1 %collective-permute-start.7 = (f32[4,2,16,256]{3,2,1,0:T(8,128)S(1)}, f32[4,2,16,256]{3,2,1,0:T(8,128)S(1)}, u32[]{:S(2)}, u32[]{:S(2)}) collective-permute-start(f32[4,2,16,256]{3,2,1,0:T(8,128)S(1)} %get-tuple-element.56), channel_id=1, source_target_pairs={{0,12},{1,13},{2,14},{3,15},{4,8},{5,9},{6,10},{7,11},{8,4},{9,5},... | collective-permute-start | bytes 393224 | tf_op jit(solution)/shard_map/ppermute | solution.py:297
  28.1 8.6 %collective-permute-start.13 = (f32[4,2,16,256]{3,2,1,0:T(8,128)S(1)}, f32[4,2,16,256]{3,2,1,0:T(8,128)S(1)}, u32[]{:S(2)}, u32[]{:S(2)}) collective-permute-start(f32[4,2,16,256]{3,2,1,0:T(8,128)S(1)} %get-tuple-element.65), channel_id=1, source_target_pairs={{0,4},{1,5},{2,6},{3,7},{4,0},{5,1},{6,2},{7,3},{8,12},{9,13},{10,... | collective-permute-start | bytes 393224 | tf_op jit(solution)/shard_map/ppermute | solution.py:297
  28.6 9.6 %collective-permute-start.14 = (f32[4,2,16,256]{3,2,1,0:T(8,128)S(1)}, f32[4,2,16,256]{3,2,1,0:T(8,128)S(1)}, u32[]{:S(2)}, u32[]{:S(2)}) collective-permute-start(f32[4,2,16,256]{3,2,1,0:T(8,128)S(1)} %get-tuple-element.66), channel_id=1, source_target_pairs={{0,8},{1,9},{2,10},{3,11},{4,12},{5,13},{6,14},{7,15},{8,0},{9,1},... | collective-permute-start | bytes 393224 | tf_op jit(solution)/shard_map/ppermute | solution.py:297
  31.9 6.3 %collective-permute-start.8 = (f32[4,2,16,256]{3,2,1,0:T(8,128)S(1)}, f32[4,2,16,256]{3,2,1,0:T(8,128)S(1)}, u32[]{:S(2)}, u32[]{:S(2)}) collective-permute-start(f32[4,2,16,256]{3,2,1,0:T(8,128)S(1)} %get-tuple-element.58), channel_id=1, source_target_pairs={{0,2},{1,3},{2,0},{3,1},{4,6},{5,7},{6,4},{7,5},{8,10},{9,11},{10,... | collective-permute-start | bytes 393224 | tf_op jit(solution)/shard_map/ppermute | solution.py:297
  33.5 4.8 %collective-permute-start.15 = (f32[4,2,16,256]{3,2,1,0:T(8,128)S(1)}, f32[4,2,16,256]{3,2,1,0:T(8,128)S(1)}, u32[]{:S(2)}, u32[]{:S(2)}) collective-permute-start(f32[4,2,16,256]{3,2,1,0:T(8,128)S(1)} %get-tuple-element.68), channel_id=1, source_target_pairs={{0,1},{1,0},{2,3},{3,2},{4,5},{5,4},{6,7},{7,6},{8,9},{9,8},{10,11... | collective-permute-start | bytes 393224 | tf_op jit(solution)/shard_map/ppermute | solution.py:297
  33.5 5.8 %collective-permute-start.16 = (f32[4,2,16,256]{3,2,1,0:T(8,128)S(1)}, f32[4,2,16,256]{3,2,1,0:T(8,128)S(1)}, u32[]{:S(2)}, u32[]{:S(2)}) collective-permute-start(f32[4,2,16,256]{3,2,1,0:T(8,128)S(1)} %get-tuple-element.69), channel_id=1, source_target_pairs={{0,3},{1,2},{2,1},{3,0},{4,7},{5,6},{6,5},{7,4},{8,11},{9,10},{10,... | collective-permute-start | bytes 393224 | tf_op jit(solution)/shard_map/ppermute | solution.py:297
  36.7 8.2 %collective-permute-start.20 = (f32[4,2,16,256]{3,2,1,0:T(8,128)S(1)}, f32[4,2,16,256]{3,2,1,0:T(8,128)S(1)}, u32[]{:S(2)}, u32[]{:S(2)}) collective-permute-start(f32[4,2,16,256]{3,2,1,0:T(8,128)S(1)} %get-tuple-element.75), channel_id=1, source_target_pairs={{0,12},{1,13},{2,14},{3,15},{4,8},{5,9},{6,10},{7,11},{8,4},{9,5},... | collective-permute-start | bytes 393224 | tf_op jit(solution)/shard_map/ppermute | solution.py:297
  39.3 7.9 %collective-permute-start.17 = (f32[4,2,16,256]{3,2,1,0:T(8,128)S(1)}, f32[4,2,16,256]{3,2,1,0:T(8,128)S(1)}, u32[]{:S(2)}, u32[]{:S(2)}) collective-permute-start(f32[4,2,16,256]{3,2,1,0:T(8,128)S(1)} %get-tuple-element.71), channel_id=1, source_target_pairs={{0,4},{1,5},{2,6},{3,7},{4,0},{5,1},{6,2},{7,3},{8,12},{9,13},{10,... | collective-permute-start | bytes 393224 | tf_op jit(solution)/shard_map/ppermute | solution.py:297
  40.7 10.2 %collective-permute-start.18 = (f32[4,2,16,256]{3,2,1,0:T(8,128)S(1)}, f32[4,2,16,256]{3,2,1,0:T(8,128)S(1)}, u32[]{:S(2)}, u32[]{:S(2)}) collective-permute-start(f32[4,2,16,256]{3,2,1,0:T(8,128)S(1)} %get-tuple-element.72), channel_id=1, source_target_pairs={{0,8},{1,9},{2,10},{3,11},{4,12},{5,13},{6,14},{7,15},{8,0},{9,1},... | collective-permute-start | bytes 393224 | tf_op jit(solution)/shard_map/ppermute | solution.py:297
  45.0 5.8 %collective-permute-start.21 = (f32[4,2,16,256]{3,2,1,0:T(8,128)S(1)}, f32[4,2,16,256]{3,2,1,0:T(8,128)S(1)}, u32[]{:S(2)}, u32[]{:S(2)}) collective-permute-start(f32[4,2,16,256]{3,2,1,0:T(8,128)S(1)} %get-tuple-element.78), channel_id=1, source_target_pairs={{0,1},{1,0},{2,3},{3,2},{4,5},{5,4},{6,7},{7,6},{8,9},{9,8},{10,11... | collective-permute-start | bytes 393224 | tf_op jit(solution)/shard_map/ppermute | solution.py:297
  45.1 5.8 %collective-permute-start.22 = (f32[4,2,16,256]{3,2,1,0:T(8,128)S(1)}, f32[4,2,16,256]{3,2,1,0:T(8,128)S(1)}, u32[]{:S(2)}, u32[]{:S(2)}) collective-permute-start(f32[4,2,16,256]{3,2,1,0:T(8,128)S(1)} %get-tuple-element.79), channel_id=1, source_target_pairs={{0,3},{1,2},{2,1},{3,0},{4,7},{5,6},{6,5},{7,4},{8,11},{9,10},{10,... | collective-permute-start | bytes 393224 | tf_op jit(solution)/shard_map/ppermute | solution.py:297
  45.1 8.6 %collective-permute-start.23 = (f32[4,2,16,256]{3,2,1,0:T(8,128)S(1)}, f32[4,2,16,256]{3,2,1,0:T(8,128)S(1)}, u32[]{:S(2)}, u32[]{:S(2)}) collective-permute-start(f32[4,2,16,256]{3,2,1,0:T(8,128)S(1)} %get-tuple-element.80), channel_id=1, source_target_pairs={{0,2},{1,3},{2,0},{3,1},{4,6},{5,7},{6,4},{7,5},{8,10},{9,11},{10,... | collective-permute-start | bytes 393224 | tf_op jit(solution)/shard_map/ppermute | solution.py:297
  47.2 7.2 %collective-permute-start.19 = (f32[4,2,16,256]{3,2,1,0:T(8,128)S(1)}, f32[4,2,16,256]{3,2,1,0:T(8,128)S(1)}, u32[]{:S(2)}, u32[]{:S(2)}) collective-permute-start(f32[4,2,16,256]{3,2,1,0:T(8,128)S(1)} %get-tuple-element.73), channel_id=1, source_target_pairs={{0,12},{1,13},{2,14},{3,15},{4,8},{5,9},{6,10},{7,11},{8,4},{9,5},... | collective-permute-start | bytes 393224 | tf_op jit(solution)/shard_map/ppermute | solution.py:297

commit v9 on v8

--- a/solution.py
+++ b/solution.py
@@ -37,6 +37,15 @@
 
 def left_halves(real_part, imag_part):
     return [left_block(*parts) for parts in zip(halves(real_part), halves(imag_part))]
+
+
+def times_left(real_part, imag_part, value):
+    high = value.shape[0] // 2
+    upper, lower = value[:high], value[high:]
+    by_real = dot_halves(halves(real_part), halves(upper))
+    by_imag = dot_halves(halves(imag_part), halves(lower))
+    by_sums = dot_halves(halves(real_part + imag_part), halves(upper + lower))
+    return jnp.concatenate([by_real - by_imag, by_sums - by_real - by_imag], axis=0)
 
 
 def times_right(value, real_part, imag_part):
@@ -96,7 +105,7 @@
 
     def step(k, carry):
         table = chosen(k)
-        total[...] = dot_halves(left_halves(table[0], table[1]), halves(total[...]))
+        total[...] = times_left(table[0], table[1], total[...])
         return carry
 
     for c in range(2):
@@ -170,14 +179,13 @@
         at = pl.ds(pl.multiple_of((me ^ distance) * under, under), under)
         for c in range(2):
             held[c, at, :] = in_refs[n][m, c]
-    return halves(jnp.concatenate([held[0], held[1]], axis=0))
+    return jnp.concatenate([held[0], held[1]], axis=0)
 
 
 def open_chunk(layout, me_ref, stem_ref, parts, out_refs):
     under = out_refs[0].shape[2]
     high = parts[0].shape[0]
-    matrix = left_halves(*rows_by_distance(parts, me_ref[0], under))
-    value = dot_halves(matrix, halves(read_stem(stem_ref, high)))
+    value = times_left(*rows_by_distance(parts, me_ref[0], under), read_stem(stem_ref, high))
     for n, m, distance in distances(layout):
         for c in range(2):
             start = c * high + distance * under
@@ -218,8 +226,8 @@
         @pl.when(n == 0)
         def high_modes():
             value = gather(in_refs, held, me_ref[0], old)
-            matrix = left_halves(*rows_by_distance((table.at[0], table.at[1]), me_ref[0], under))
-            between[...] = dot_halves(matrix, value)
+            parts = rows_by_distance((table.at[0], table.at[1]), me_ref[0], under)
+            between[...] = times_left(*parts, value)
 
         @pl.when(n == 1)
         def low_modes():
@@ -235,8 +243,7 @@
 
 def close_chunk(layout, me_ref, table, in_refs, held, stem):
     value = gather(in_refs, held, me_ref[0], layout)
-    matrix = left_halves(table[0], table[1])
-    write_stem(stem, dot_halves(matrix, value), table.shape[-1])
+    write_stem(stem, times_left(table[0], table[1], value), table.shape[-1])
 
 
 def close_first_kernel(layout, me_ref, table, *refs):

time: 56 us -> 55.7 us (level)
  Pallas kernels: 7.82 us -> 7.24 us
where the time goes in v9:
time: 55.7 us; the launch traced here: 55.6 us
  starting transfers between devices  33.9 us (61%)
  waiting for transfers between devices  12.8 us (23%)
  Pallas kernels  7.24 us (13%)
  local copies, waits for them, and re-layouts  1.43 us (3%)
    ppermute x24, starting transfers between devices, send(): lax.ppermute(value, 'stem', [(i, i ^ step) for i in range(devices)])  33.9 us
    ppermute x24, waiting for transfers between devices, send(): lax.ppermute(value, 'stem', [(i, i ^ step) for i in range(devices)])  12.8 us
    pallas_call x9, Pallas kernels, call(): pl.pallas_call(kernel, out_shape=blocks(out) if isinstance(out, tuple) el...  4.07 us
    pallas_call x1, Pallas kernels, one_slice(): pl.pallas_call(chain_kernel, out_shape=jax.ShapeDtypeStruct((2, low, low)...  1.81 us
    pallas_call x1, Pallas kernels, close_last(): pl.pallas_call(functools.partial(close_last_kernel, layout), out_shape=ja...  1.36 us
    slice x1, local copies, waits for them, and re-layouts, open_first(): packed = jnp.concatenate([laid[0], matrix], axis=0)  1.13 us
  transfers between devices with their start and end apart: 24, of which 9 were waited for; matrix products, arithmetic and copies ran while one was open for 0% of the time, Pallas kernels for 10%

profile of v9, /device:TPU:0, one launch (start us, length us, event | category | flops | bytes accessed | tf_op | source)
XLA Modules:
  0.0 55.6 jit_solution(16459724660654223439)
XLA Ops:
  0.0 1.1 %slice.27 = f32[512,2,128]{2,1,0:T(2,128)S(1)} slice(f32[1024,2,128]{2,1,0:T(2,128)} %bitcast.27), slice={[0:512], [0:2], [0:128]} | slice | bytes 1048576 | tf_op jit(solution)/shard_map/slice | solution.py:315
  1.1 0.1 slice-done
  1.2 0.1 pad_maximum_fusion.packed_ref
  1.3 0.0 copy-start.3
  1.3 0.5 open_0.1
  1.8 3.1 %collective-permute-start = (f32[4,2,16,256]{3,2,1,0:T(8,128)S(1)}, f32[4,2,16,256]{3,2,1,0:T(8,128)S(1)}, u32[]{:S(2)}, u32[]{:S(2)}) collective-permute-start(f32[4,2,16,256]{3,2,1,0:T(8,128)S(1)} %get-tuple-element.47), channel_id=1, source_target_pairs={{0,4},{1,5},{2,6},{3,7},{4,0},{5,1},{6,2},{7,3},{8,12},{9,13},{10,... | collective-permute-start | bytes 393224 | tf_op jit(solution)/shard_map/ppermute | solution.py:304
  4.9 2.6 %collective-permute-start.1 = (f32[4,2,16,256]{3,2,1,0:T(8,128)S(1)}, f32[4,2,16,256]{3,2,1,0:T(8,128)S(1)}, u32[]{:S(2)}, u32[]{:S(2)}) collective-permute-start(f32[4,2,16,256]{3,2,1,0:T(8,128)S(1)} %get-tuple-element.48), channel_id=1, source_target_pairs={{0,8},{1,9},{2,10},{3,11},{4,12},{5,13},{6,14},{7,15},{8,0},{9,1},... | collective-permute-start | bytes 393224 | tf_op jit(solution)/shard_map/ppermute | solution.py:304
  7.5 0.0 copy-done.2
  7.5 0.2 slice_bitcast_fusion
  7.7 0.0 copy-done.3
  7.7 0.0 copy-start.1
  7.8 0.5 open_1.1
  8.3 1.6 %collective-permute-start.2 = (f32[4,2,16,256]{3,2,1,0:T(8,128)S(1)}, f32[4,2,16,256]{3,2,1,0:T(8,128)S(1)}, u32[]{:S(2)}, u32[]{:S(2)}) collective-permute-start(f32[4,2,16,256]{3,2,1,0:T(8,128)S(1)} %get-tuple-element.50), channel_id=1, source_target_pairs={{0,2},{1,3},{2,0},{3,1},{4,6},{5,7},{6,4},{7,5},{8,10},{9,11},{10,... | collective-permute-start | bytes 393224 | tf_op jit(solution)/shard_map/ppermute | solution.py:304
  9.8 0.0 collective-permute-start.3
  9.9 0.6 %collective-permute-start.4 = (f32[4,2,16,256]{3,2,1,0:T(8,128)S(1)}, f32[4,2,16,256]{3,2,1,0:T(8,128)S(1)}, u32[]{:S(2)}, u32[]{:S(2)}) collective-permute-start(f32[4,2,16,256]{3,2,1,0:T(8,128)S(1)} %get-tuple-element.52), channel_id=1, source_target_pairs={{0,3},{1,2},{2,1},{3,0},{4,7},{5,6},{6,5},{7,4},{8,11},{9,10},{10,... | collective-permute-start | bytes 393224 | tf_op jit(solution)/shard_map/ppermute | solution.py:304
  10.5 0.0 collective-permute-done.refs_1_
  10.5 3.2 %collective-permute-start.9 = (f32[4,2,16,256]{3,2,1,0:T(8,128)S(1)}, f32[4,2,16,256]{3,2,1,0:T(8,128)S(1)}, u32[]{:S(2)}, u32[]{:S(2)}) collective-permute-start(f32[4,2,16,256]{3,2,1,0:T(8,128)S(1)} %get-tuple-element.59), channel_id=1, source_target_pairs={{0,12},{1,13},{2,14},{3,15},{4,8},{5,9},{6,10},{7,11},{8,4},{9,5},... | collective-permute-start | bytes 393224 | tf_op jit(solution)/shard_map/ppermute | solution.py:304
  13.7 0.0 copy-done
  13.7 1.8 %low_chain.1.low_table = f32[2,256,256]{2,1,0:T(8,128)S(1)} custom-call(s32[1,3]{1,0:T(1,128)S(1)} %copy-done.1, f32[3,2,2,256,256]{4,3,2,1,0:T(8,128)S(1)} %copy-done), custom_call_target="tpu_custom_call" | custom-call | tf_op jit(solution)/shard_map/low_chain/pallas_call | solution.py:398
  15.6 0.0 collective-permute-done.1.refs_2_
  15.6 0.0 collective-permute-done.2.refs_1_
  15.6 0.0 collective-permute-done.3.refs_2_
  15.6 0.0 collective-permute-done.4.refs_3_
  15.7 0.5 collective-permute-start.5
  16.2 3.2 %collective-permute-start.6 = (f32[4,2,16,256]{3,2,1,0:T(8,128)S(1)}, f32[4,2,16,256]{3,2,1,0:T(8,128)S(1)}, u32[]{:S(2)}, u32[]{:S(2)}) collective-permute-start(f32[4,2,16,256]{3,2,1,0:T(8,128)S(1)} %get-tuple-element.55), channel_id=1, source_target_pairs={{0,8},{1,9},{2,10},{3,11},{4,12},{5,13},{6,14},{7,15},{8,0},{9,1},... | collective-permute-start | bytes 393224 | tf_op jit(solution)/shard_map/ppermute | solution.py:304
  19.4 0.0 collective-permute-done.9.refs_3_
  19.5 1.6 %collective-permute-start.10 = (f32[4,2,16,256]{3,2,1,0:T(8,128)S(1)}, f32[4,2,16,256]{3,2,1,0:T(8,128)S(1)}, u32[]{:S(2)}, u32[]{:S(2)}) collective-permute-start(f32[4,2,16,256]{3,2,1,0:T(8,128)S(1)} %get-tuple-element.61), channel_id=1, source_target_pairs={{0,2},{1,3},{2,0},{3,1},{4,6},{5,7},{6,4},{7,5},{8,10},{9,11},{10,... | collective-permute-start | bytes 393224 | tf_op jit(solution)/shard_map/ppermute | solution.py:304
  21.0 0.0 collective-permute-start.11
  21.0 0.6 %collective-permute-start.12 = (f32[4,2,16,256]{3,2,1,0:T(8,128)S(1)}, f32[4,2,16,256]{3,2,1,0:T(8,128)S(1)}, u32[]{:S(2)}, u32[]{:S(2)}) collective-permute-start(f32[4,2,16,256]{3,2,1,0:T(8,128)S(1)} %get-tuple-element.64), channel_id=1, source_target_pairs={{0,3},{1,2},{2,1},{3,0},{4,7},{5,6},{6,5},{7,4},{8,11},{9,10},{10,... | collective-permute-start | bytes 393224 | tf_op jit(solution)/shard_map/ppermute | solution.py:304
  21.7 1.8 %collective-permute-done.5.refs_1_ = f32[4,2,16,256]{3,2,1,0:T(8,128)S(1)} collective-permute-done((f32[4,2,16,256]{3,2,1,0:T(8,128)S(1)}, f32[4,2,16,256]{3,2,1,0:T(8,128)S(1)}, u32[]{:S(2)}, u32[]{:S(2)}) %collective-permute-start.5) | collective-permute-done | bytes 131104 | tf_op jit(solution)/shard_map/ppermute | solution.py:304
  23.5 2.0 %collective-permute-start.7 = (f32[4,2,16,256]{3,2,1,0:T(8,128)S(1)}, f32[4,2,16,256]{3,2,1,0:T(8,128)S(1)}, u32[]{:S(2)}, u32[]{:S(2)}) collective-permute-start(f32[4,2,16,256]{3,2,1,0:T(8,128)S(1)} %get-tuple-element.56), channel_id=1, source_target_pairs={{0,12},{1,13},{2,14},{3,15},{4,8},{5,9},{6,10},{7,11},{8,4},{9,5},... | collective-permute-start | bytes 393224 | tf_op jit(solution)/shard_map/ppermute | solution.py:304
  25.5 1.0 %collective-permute-done.6.refs_2_ = f32[4,2,16,256]{3,2,1,0:T(8,128)S(1)} collective-permute-done((f32[4,2,16,256]{3,2,1,0:T(8,128)S(1)}, f32[4,2,16,256]{3,2,1,0:T(8,128)S(1)}, u32[]{:S(2)}, u32[]{:S(2)}) %collective-permute-start.6) | collective-permute-done | bytes 131104 | tf_op jit(solution)/shard_map/ppermute | solution.py:304
  26.5 0.0 collective-permute-done.10.refs_1_
  26.5 0.0 collective-permute-done.11.refs_2_
  26.5 0.3 collective-permute-done.12.refs_3_
  26.8 1.2 %middle_0.1 = (f32[4,2,16,256]{3,2,1,0:T(8,128)S(1)}, f32[4,2,16,256]{3,2,1,0:T(8,128)S(1)}, f32[4,2,16,256]{3,2,1,0:T(8,128)S(1)}, f32[4,2,16,256]{3,2,1,0:T(8,128)S(1)}) custom-call(s32[1]{0:T(128)} %bitcast.me_ref, f32[2,256,256]{2,1,0:T(8,128)S(1)} %get-tuple-element.82.table, f32[2,256,256]{2,1,0:T(8,128)S(1)} %low_chain.1.low_table, ...), custom_call_target="tpu_custom_call" | custom-call | tf_op jit(solution)/shard_map/middle_0/pallas_call | solution.py:291
  28.0 0.4 collective-permute-start.13
  28.4 1.7 %collective-permute-start.14 = (f32[4,2,16,256]{3,2,1,0:T(8,128)S(1)}, f32[4,2,16,256]{3,2,1,0:T(8,128)S(1)}, u32[]{:S(2)}, u32[]{:S(2)}) collective-permute-start(f32[4,2,16,256]{3,2,1,0:T(8,128)S(1)} %get-tuple-element.66), channel_id=1, source_target_pairs={{0,8},{1,9},{2,10},{3,11},{4,12},{5,13},{6,14},{7,15},{8,0},{9,1},... | collective-permute-start | bytes 393224 | tf_op jit(solution)/shard_map/ppermute | solution.py:304
  30.1 0.6 %collective-permute-done.7.refs_3_ = f32[4,2,16,256]{3,2,1,0:T(8,128)S(1)} collective-permute-done((f32[4,2,16,256]{3,2,1,0:T(8,128)S(1)}, f32[4,2,16,256]{3,2,1,0:T(8,128)S(1)}, u32[]{:S(2)}, u32[]{:S(2)}) %collective-permute-start.7) | collective-permute-done | bytes 131104 | tf_op jit(solution)/shard_map/ppermute | solution.py:304
  30.7 1.2 %middle_1.1 = (f32[4,2,16,256]{3,2,1,0:T(8,128)S(1)}, f32[4,2,16,256]{3,2,1,0:T(8,128)S(1)}, f32[4,2,16,256]{3,2,1,0:T(8,128)S(1)}, f32[4,2,16,256]{3,2,1,0:T(8,128)S(1)}) custom-call(s32[1]{0:T(128)} %bitcast.me_ref, f32[2,256,256]{2,1,0:T(8,128)S(1)} %get-tuple-element.82.table, f32[2,256,256]{2,1,0:T(8,128)S(1)} %low_chain.1.low_table, ...), custom_call_target="tpu_custom_call" | custom-call | tf_op jit(solution)/shard_map/middle_1/pallas_call | solution.py:291
  31.8 1.5 %collective-permute-start.8 = (f32[4,2,16,256]{3,2,1,0:T(8,128)S(1)}, f32[4,2,16,256]{3,2,1,0:T(8,128)S(1)}, u32[]{:S(2)}, u32[]{:S(2)}) collective-permute-start(f32[4,2,16,256]{3,2,1,0:T(8,128)S(1)} %get-tuple-element.58), channel_id=1, source_target_pairs={{0,2},{1,3},{2,0},{3,1},{4,6},{5,7},{6,4},{7,5},{8,10},{9,11},{10,... | collective-permute-start | bytes 393224 | tf_op jit(solution)/shard_map/ppermute | solution.py:304
  33.4 0.0 collective-permute-start.15
  33.4 0.7 %collective-permute-start.16 = (f32[4,2,16,256]{3,2,1,0:T(8,128)S(1)}, f32[4,2,16,256]{3,2,1,0:T(8,128)S(1)}, u32[]{:S(2)}, u32[]{:S(2)}) collective-permute-start(f32[4,2,16,256]{3,2,1,0:T(8,128)S(1)} %get-tuple-element.69), channel_id=1, source_target_pairs={{0,3},{1,2},{2,1},{3,0},{4,7},{5,6},{6,5},{7,4},{8,11},{9,10},{10,... | collective-permute-start | bytes 393224 | tf_op jit(solution)/shard_map/ppermute | solution.py:304
  34.0 2.5 %collective-permute-done.13.refs_1_ = f32[4,2,16,256]{3,2,1,0:T(8,128)S(1)} collective-permute-done((f32[4,2,16,256]{3,2,1,0:T(8,128)S(1)}, f32[4,2,16,256]{3,2,1,0:T(8,128)S(1)}, u32[]{:S(2)}, u32[]{:S(2)}) %collective-permute-start.13) | collective-permute-done | bytes 131104 | tf_op jit(solution)/shard_map/ppermute | solution.py:304
  36.6 0.4 collective-permute-start.20
  37.0 1.2 %collective-permute-done.14.refs_2_ = f32[4,2,16,256]{3,2,1,0:T(8,128)S(1)} collective-permute-done((f32[4,2,16,256]{3,2,1,0:T(8,128)S(1)}, f32[4,2,16,256]{3,2,1,0:T(8,128)S(1)}, u32[]{:S(2)}, u32[]{:S(2)}) %collective-permute-start.14) | collective-permute-done | bytes 131104 | tf_op jit(solution)/shard_map/ppermute | solution.py:304
  38.1 0.0 collective-permute-done.8.refs_1_
  38.1 0.0 collective-permute-done.15.refs_2_
  38.1 1.0 %collective-permute-done.16.refs_3_ = f32[4,2,16,256]{3,2,1,0:T(8,128)S(1)} collective-permute-done((f32[4,2,16,256]{3,2,1,0:T(8,128)S(1)}, f32[4,2,16,256]{3,2,1,0:T(8,128)S(1)}, u32[]{:S(2)}, u32[]{:S(2)}) %collective-permute-start.16) | collective-permute-done | bytes 131104 | tf_op jit(solution)/shard_map/ppermute | solution.py:304
  39.2 1.2 %collective-permute-start.17 = (f32[4,2,16,256]{3,2,1,0:T(8,128)S(1)}, f32[4,2,16,256]{3,2,1,0:T(8,128)S(1)}, u32[]{:S(2)}, u32[]{:S(2)}) collective-permute-start(f32[4,2,16,256]{3,2,1,0:T(8,128)S(1)} %get-tuple-element.71), channel_id=1, source_target_pairs={{0,4},{1,5},{2,6},{3,7},{4,0},{5,1},{6,2},{7,3},{8,12},{9,13},{10,... | collective-permute-start | bytes 393224 | tf_op jit(solution)/shard_map/ppermute | solution.py:304
  40.4 4.4 %collective-permute-start.18 = (f32[4,2,16,256]{3,2,1,0:T(8,128)S(1)}, f32[4,2,16,256]{3,2,1,0:T(8,128)S(1)}, u32[]{:S(2)}, u32[]{:S(2)}) collective-permute-start(f32[4,2,16,256]{3,2,1,0:T(8,128)S(1)} %get-tuple-element.72), channel_id=1, source_target_pairs={{0,8},{1,9},{2,10},{3,11},{4,12},{5,13},{6,14},{7,15},{8,0},{9,1},... | collective-permute-start | bytes 393224 | tf_op jit(solution)/shard_map/ppermute | solution.py:304
  44.8 0.0 collective-permute-done.20.refs_3_
  44.9 0.1 collective-permute-start.21
  45.0 0.1 collective-permute-start.22
  45.0 2.1 %collective-permute-start.23 = (f32[4,2,16,256]{3,2,1,0:T(8,128)S(1)}, f32[4,2,16,256]{3,2,1,0:T(8,128)S(1)}, u32[]{:S(2)}, u32[]{:S(2)}) collective-permute-start(f32[4,2,16,256]{3,2,1,0:T(8,128)S(1)} %get-tuple-element.80), channel_id=1, source_target_pairs={{0,2},{1,3},{2,0},{3,1},{4,6},{5,7},{6,4},{7,5},{8,10},{9,11},{10,... | collective-permute-start | bytes 393224 | tf_op jit(solution)/shard_map/ppermute | solution.py:304
  47.1 0.0 collective-permute-done.17.refs_1_
  47.1 2.2 %collective-permute-start.19 = (f32[4,2,16,256]{3,2,1,0:T(8,128)S(1)}, f32[4,2,16,256]{3,2,1,0:T(8,128)S(1)}, u32[]{:S(2)}, u32[]{:S(2)}) collective-permute-start(f32[4,2,16,256]{3,2,1,0:T(8,128)S(1)} %get-tuple-element.73), channel_id=1, source_target_pairs={{0,12},{1,13},{2,14},{3,15},{4,8},{5,9},{6,10},{7,11},{8,4},{9,5},... | collective-permute-start | bytes 393224 | tf_op jit(solution)/shard_map/ppermute | solution.py:304
  49.3 1.4 %collective-permute-done.18.refs_2_ = f32[4,2,16,256]{3,2,1,0:T(8,128)S(1)} collective-permute-done((f32[4,2,16,256]{3,2,1,0:T(8,128)S(1)}, f32[4,2,16,256]{3,2,1,0:T(8,128)S(1)}, u32[]{:S(2)}, u32[]{:S(2)}) %collective-permute-start.18) | collective-permute-done | bytes 131104 | tf_op jit(solution)/shard_map/ppermute | solution.py:304
  50.6 0.0 collective-permute-done.21.refs_1_
  50.7 0.0 collective-permute-done.22.refs_2_
  50.7 3.0 %collective-permute-done.23.refs_3_ = f32[4,2,16,256]{3,2,1,0:T(8,128)S(1)} collective-permute-done((f32[4,2,16,256]{3,2,1,0:T(8,128)S(1)}, f32[4,2,16,256]{3,2,1,0:T(8,128)S(1)}, u32[]{:S(2)}, u32[]{:S(2)}) %collective-permute-start.23) | collective-permute-done | bytes 131104 | tf_op jit(solution)/shard_map/ppermute | solution.py:304
  53.6 0.5 close_0.1.refs_4_
  54.2 0.0 collective-permute-done.19.refs_3_
  54.2 1.4 %close_1.1 = f32[2,1024,128]{2,1,0:T(8,128)} custom-call(s32[1]{0:T(128)} %bitcast.me_ref, f32[2,256,256]{2,1,0:T(8,128)S(1)} %get-tuple-element.83.table, f32[4,2,16,256]{3,2,1,0:T(8,128)S(1)} %get-tuple-element.70.refs_0_, f32[4,2,16,256]{3,2,1,0:T(8,128)S(1)} %collective-permute-done.17.refs_1_, f32[4,2,16,256]{3,2,1,0:T(8,128)S(1)} %collective-permute-done.18.refs_2_, ...), custom_call_target="tpu_custom_call" | custom-call | tf_op jit(solution)/shard_map/close_1/pallas_call | solution.py:335
  (9 shorter events, 0.2 us)
Async XLA Ops:
  0.0 1.2 %slice-start = ((f32[3,2,256,256]{3,2,1,0:T(8,128)}), f32[1,2,256,256]{3,2,1,0:T(8,128)S(1)}, s32[]{:S(2)}) async-start(f32[3,2,256,256]{3,2,1,0:T(8,128)} %param.6), calls=%async_computation | async-start | bytes 1048576 | tf_op jit(solution)/shard_map/slice | solution.py:313
  1.2 6.3 %copy-start.2 = (f32[3,2,256,256]{3,2,1,0:T(8,128)S(1)}, f32[3,2,256,256]{3,2,1,0:T(8,128)}, u32[]{:S(2)}) copy-start(f32[3,2,256,256]{3,2,1,0:T(8,128)} %param.6) | copy-start | bytes 4718596
  1.3 6.4 %copy-start.3 = (f32[1,2,131072]{2,1,0:T(2,128)S(1)}, f32[1,2,131072]{2,1,0:T(2,128)}, u32[]{:S(2)}) copy-start(f32[1,2,131072]{2,1,0:T(2,128)} %param.4) | copy-start | bytes 3145732
  1.8 8.7 %collective-permute-start = (f32[4,2,16,256]{3,2,1,0:T(8,128)S(1)}, f32[4,2,16,256]{3,2,1,0:T(8,128)S(1)}, u32[]{:S(2)}, u32[]{:S(2)}) collective-permute-start(f32[4,2,16,256]{3,2,1,0:T(8,128)S(1)} %get-tuple-element.47), channel_id=1, source_target_pairs={{0,4},{1,5},{2,6},{3,7},{4,0},{5,1},{6,2},{7,3},{8,12},{9,13},{10,... | collective-permute-start | bytes 393224 | tf_op jit(solution)/shard_map/ppermute | solution.py:304
  4.9 10.7 %collective-permute-start.1 = (f32[4,2,16,256]{3,2,1,0:T(8,128)S(1)}, f32[4,2,16,256]{3,2,1,0:T(8,128)S(1)}, u32[]{:S(2)}, u32[]{:S(2)}) collective-permute-start(f32[4,2,16,256]{3,2,1,0:T(8,128)S(1)} %get-tuple-element.48), channel_id=1, source_target_pairs={{0,8},{1,9},{2,10},{3,11},{4,12},{5,13},{6,14},{7,15},{8,0},{9,1},... | collective-permute-start | bytes 393224 | tf_op jit(solution)/shard_map/ppermute | solution.py:304
  7.5 6.2 %copy-start = (f32[3,2,2,256,256]{4,3,2,1,0:T(8,128)S(1)}, f32[3,2,2,256,256]{4,3,2,1,0:T(8,128)}, u32[]{:S(2)}) copy-start(f32[3,2,2,256,256]{4,3,2,1,0:T(8,128)} %table_ref.1) | copy-start | bytes 9437188
  7.7 6.0 %copy-start.1 = (s32[1,3]{1,0:T(1,128)S(1)}, s32[1,3]{1,0:T(1,128)}, u32[]{:S(2)}) copy-start(s32[1,3]{1,0:T(1,128)} %bits_ref.1) | copy-start | bytes 40
  8.3 7.3 %collective-permute-start.2 = (f32[4,2,16,256]{3,2,1,0:T(8,128)S(1)}, f32[4,2,16,256]{3,2,1,0:T(8,128)S(1)}, u32[]{:S(2)}, u32[]{:S(2)}) collective-permute-start(f32[4,2,16,256]{3,2,1,0:T(8,128)S(1)} %get-tuple-element.50), channel_id=1, source_target_pairs={{0,2},{1,3},{2,0},{3,1},{4,6},{5,7},{6,4},{7,5},{8,10},{9,11},{10,... | collective-permute-start | bytes 393224 | tf_op jit(solution)/shard_map/ppermute | solution.py:304
  9.8 5.7 %collective-permute-start.3 = (f32[4,2,16,256]{3,2,1,0:T(8,128)S(1)}, f32[4,2,16,256]{3,2,1,0:T(8,128)S(1)}, u32[]{:S(2)}, u32[]{:S(2)}) collective-permute-start(f32[4,2,16,256]{3,2,1,0:T(8,128)S(1)} %get-tuple-element.51), channel_id=1, source_target_pairs={{0,1},{1,0},{2,3},{3,2},{4,5},{5,4},{6,7},{7,6},{8,9},{9,8},{10,11... | collective-permute-start | bytes 393224 | tf_op jit(solution)/shard_map/ppermute | solution.py:304
  9.9 5.8 %collective-permute-start.4 = (f32[4,2,16,256]{3,2,1,0:T(8,128)S(1)}, f32[4,2,16,256]{3,2,1,0:T(8,128)S(1)}, u32[]{:S(2)}, u32[]{:S(2)}) collective-permute-start(f32[4,2,16,256]{3,2,1,0:T(8,128)S(1)} %get-tuple-element.52), channel_id=1, source_target_pairs={{0,3},{1,2},{2,1},{3,0},{4,7},{5,6},{6,5},{7,4},{8,11},{9,10},{10,... | collective-permute-start | bytes 393224 | tf_op jit(solution)/shard_map/ppermute | solution.py:304
  10.5 8.9 %collective-permute-start.9 = (f32[4,2,16,256]{3,2,1,0:T(8,128)S(1)}, f32[4,2,16,256]{3,2,1,0:T(8,128)S(1)}, u32[]{:S(2)}, u32[]{:S(2)}) collective-permute-start(f32[4,2,16,256]{3,2,1,0:T(8,128)S(1)} %get-tuple-element.59), channel_id=1, source_target_pairs={{0,12},{1,13},{2,14},{3,15},{4,8},{5,9},{6,10},{7,11},{8,4},{9,5},... | collective-permute-start | bytes 393224 | tf_op jit(solution)/shard_map/ppermute | solution.py:304
  15.7 7.8 %collective-permute-start.5 = (f32[4,2,16,256]{3,2,1,0:T(8,128)S(1)}, f32[4,2,16,256]{3,2,1,0:T(8,128)S(1)}, u32[]{:S(2)}, u32[]{:S(2)}) collective-permute-start(f32[4,2,16,256]{3,2,1,0:T(8,128)S(1)} %get-tuple-element.54), channel_id=1, source_target_pairs={{0,4},{1,5},{2,6},{3,7},{4,0},{5,1},{6,2},{7,3},{8,12},{9,13},{10,... | collective-permute-start | bytes 393224 | tf_op jit(solution)/shard_map/ppermute | solution.py:304
  16.2 10.3 %collective-permute-start.6 = (f32[4,2,16,256]{3,2,1,0:T(8,128)S(1)}, f32[4,2,16,256]{3,2,1,0:T(8,128)S(1)}, u32[]{:S(2)}, u32[]{:S(2)}) collective-permute-start(f32[4,2,16,256]{3,2,1,0:T(8,128)S(1)} %get-tuple-element.55), channel_id=1, source_target_pairs={{0,8},{1,9},{2,10},{3,11},{4,12},{5,13},{6,14},{7,15},{8,0},{9,1},... | collective-permute-start | bytes 393224 | tf_op jit(solution)/shard_map/ppermute | solution.py:304
  19.5 7.0 %collective-permute-start.10 = (f32[4,2,16,256]{3,2,1,0:T(8,128)S(1)}, f32[4,2,16,256]{3,2,1,0:T(8,128)S(1)}, u32[]{:S(2)}, u32[]{:S(2)}) collective-permute-start(f32[4,2,16,256]{3,2,1,0:T(8,128)S(1)} %get-tuple-element.61), channel_id=1, source_target_pairs={{0,2},{1,3},{2,0},{3,1},{4,6},{5,7},{6,4},{7,5},{8,10},{9,11},{10,... | collective-permute-start | bytes 393224 | tf_op jit(solution)/shard_map/ppermute | solution.py:304
  21.0 5.5 %collective-permute-start.11 = (f32[4,2,16,256]{3,2,1,0:T(8,128)S(1)}, f32[4,2,16,256]{3,2,1,0:T(8,128)S(1)}, u32[]{:S(2)}, u32[]{:S(2)}) collective-permute-start(f32[4,2,16,256]{3,2,1,0:T(8,128)S(1)} %get-tuple-element.63), channel_id=1, source_target_pairs={{0,1},{1,0},{2,3},{3,2},{4,5},{5,4},{6,7},{7,6},{8,9},{9,8},{10,11... | collective-permute-start | bytes 393224 | tf_op jit(solution)/shard_map/ppermute | solution.py:304
  21.0 5.8 %collective-permute-start.12 = (f32[4,2,16,256]{3,2,1,0:T(8,128)S(1)}, f32[4,2,16,256]{3,2,1,0:T(8,128)S(1)}, u32[]{:S(2)}, u32[]{:S(2)}) collective-permute-start(f32[4,2,16,256]{3,2,1,0:T(8,128)S(1)} %get-tuple-element.64), channel_id=1, source_target_pairs={{0,3},{1,2},{2,1},{3,0},{4,7},{5,6},{6,5},{7,4},{8,11},{9,10},{10,... | collective-permute-start | bytes 393224 | tf_op jit(solution)/shard_map/ppermute | solution.py:304
  23.5 7.2 %collective-permute-start.7 = (f32[4,2,16,256]{3,2,1,0:T(8,128)S(1)}, f32[4,2,16,256]{3,2,1,0:T(8,128)S(1)}, u32[]{:S(2)}, u32[]{:S(2)}) collective-permute-start(f32[4,2,16,256]{3,2,1,0:T(8,128)S(1)} %get-tuple-element.56), channel_id=1, source_target_pairs={{0,12},{1,13},{2,14},{3,15},{4,8},{5,9},{6,10},{7,11},{8,4},{9,5},... | collective-permute-start | bytes 393224 | tf_op jit(solution)/shard_map/ppermute | solution.py:304
  28.0 8.6 %collective-permute-start.13 = (f32[4,2,16,256]{3,2,1,0:T(8,128)S(1)}, f32[4,2,16,256]{3,2,1,0:T(8,128)S(1)}, u32[]{:S(2)}, u32[]{:S(2)}) collective-permute-start(f32[4,2,16,256]{3,2,1,0:T(8,128)S(1)} %get-tuple-element.65), channel_id=1, source_target_pairs={{0,4},{1,5},{2,6},{3,7},{4,0},{5,1},{6,2},{7,3},{8,12},{9,13},{10,... | collective-permute-start | bytes 393224 | tf_op jit(solution)/shard_map/ppermute | solution.py:304
  28.4 9.7 %collective-permute-start.14 = (f32[4,2,16,256]{3,2,1,0:T(8,128)S(1)}, f32[4,2,16,256]{3,2,1,0:T(8,128)S(1)}, u32[]{:S(2)}, u32[]{:S(2)}) collective-permute-start(f32[4,2,16,256]{3,2,1,0:T(8,128)S(1)} %get-tuple-element.66), channel_id=1, source_target_pairs={{0,8},{1,9},{2,10},{3,11},{4,12},{5,13},{6,14},{7,15},{8,0},{9,1},... | collective-permute-start | bytes 393224 | tf_op jit(solution)/shard_map/ppermute | solution.py:304
  31.8 6.3 %collective-permute-start.8 = (f32[4,2,16,256]{3,2,1,0:T(8,128)S(1)}, f32[4,2,16,256]{3,2,1,0:T(8,128)S(1)}, u32[]{:S(2)}, u32[]{:S(2)}) collective-permute-start(f32[4,2,16,256]{3,2,1,0:T(8,128)S(1)} %get-tuple-element.58), channel_id=1, source_target_pairs={{0,2},{1,3},{2,0},{3,1},{4,6},{5,7},{6,4},{7,5},{8,10},{9,11},{10,... | collective-permute-start | bytes 393224 | tf_op jit(solution)/shard_map/ppermute | solution.py:304
  33.4 4.8 %collective-permute-start.15 = (f32[4,2,16,256]{3,2,1,0:T(8,128)S(1)}, f32[4,2,16,256]{3,2,1,0:T(8,128)S(1)}, u32[]{:S(2)}, u32[]{:S(2)}) collective-permute-start(f32[4,2,16,256]{3,2,1,0:T(8,128)S(1)} %get-tuple-element.68), channel_id=1, source_target_pairs={{0,1},{1,0},{2,3},{3,2},{4,5},{5,4},{6,7},{7,6},{8,9},{9,8},{10,11... | collective-permute-start | bytes 393224 | tf_op jit(solution)/shard_map/ppermute | solution.py:304
  33.4 5.8 %collective-permute-start.16 = (f32[4,2,16,256]{3,2,1,0:T(8,128)S(1)}, f32[4,2,16,256]{3,2,1,0:T(8,128)S(1)}, u32[]{:S(2)}, u32[]{:S(2)}) collective-permute-start(f32[4,2,16,256]{3,2,1,0:T(8,128)S(1)} %get-tuple-element.69), channel_id=1, source_target_pairs={{0,3},{1,2},{2,1},{3,0},{4,7},{5,6},{6,5},{7,4},{8,11},{9,10},{10,... | collective-permute-start | bytes 393224 | tf_op jit(solution)/shard_map/ppermute | solution.py:304
  36.6 8.3 %collective-permute-start.20 = (f32[4,2,16,256]{3,2,1,0:T(8,128)S(1)}, f32[4,2,16,256]{3,2,1,0:T(8,128)S(1)}, u32[]{:S(2)}, u32[]{:S(2)}) collective-permute-start(f32[4,2,16,256]{3,2,1,0:T(8,128)S(1)} %get-tuple-element.75), channel_id=1, source_target_pairs={{0,12},{1,13},{2,14},{3,15},{4,8},{5,9},{6,10},{7,11},{8,4},{9,5},... | collective-permute-start | bytes 393224 | tf_op jit(solution)/shard_map/ppermute | solution.py:304
  39.2 7.9 %collective-permute-start.17 = (f32[4,2,16,256]{3,2,1,0:T(8,128)S(1)}, f32[4,2,16,256]{3,2,1,0:T(8,128)S(1)}, u32[]{:S(2)}, u32[]{:S(2)}) collective-permute-start(f32[4,2,16,256]{3,2,1,0:T(8,128)S(1)} %get-tuple-element.71), channel_id=1, source_target_pairs={{0,4},{1,5},{2,6},{3,7},{4,0},{5,1},{6,2},{7,3},{8,12},{9,13},{10,... | collective-permute-start | bytes 393224 | tf_op jit(solution)/shard_map/ppermute | solution.py:304
  40.4 10.2 %collective-permute-start.18 = (f32[4,2,16,256]{3,2,1,0:T(8,128)S(1)}, f32[4,2,16,256]{3,2,1,0:T(8,128)S(1)}, u32[]{:S(2)}, u32[]{:S(2)}) collective-permute-start(f32[4,2,16,256]{3,2,1,0:T(8,128)S(1)} %get-tuple-element.72), channel_id=1, source_target_pairs={{0,8},{1,9},{2,10},{3,11},{4,12},{5,13},{6,14},{7,15},{8,0},{9,1},... | collective-permute-start | bytes 393224 | tf_op jit(solution)/shard_map/ppermute | solution.py:304
  44.9 5.8 %collective-permute-start.21 = (f32[4,2,16,256]{3,2,1,0:T(8,128)S(1)}, f32[4,2,16,256]{3,2,1,0:T(8,128)S(1)}, u32[]{:S(2)}, u32[]{:S(2)}) collective-permute-start(f32[4,2,16,256]{3,2,1,0:T(8,128)S(1)} %get-tuple-element.78), channel_id=1, source_target_pairs={{0,1},{1,0},{2,3},{3,2},{4,5},{5,4},{6,7},{7,6},{8,9},{9,8},{10,11... | collective-permute-start | bytes 393224 | tf_op jit(solution)/shard_map/ppermute | solution.py:304
  45.0 5.7 %collective-permute-start.22 = (f32[4,2,16,256]{3,2,1,0:T(8,128)S(1)}, f32[4,2,16,256]{3,2,1,0:T(8,128)S(1)}, u32[]{:S(2)}, u32[]{:S(2)}) collective-permute-start(f32[4,2,16,256]{3,2,1,0:T(8,128)S(1)} %get-tuple-element.79), channel_id=1, source_target_pairs={{0,3},{1,2},{2,1},{3,0},{4,7},{5,6},{6,5},{7,4},{8,11},{9,10},{10,... | collective-permute-start | bytes 393224 | tf_op jit(solution)/shard_map/ppermute | solution.py:304
  45.0 8.6 %collective-permute-start.23 = (f32[4,2,16,256]{3,2,1,0:T(8,128)S(1)}, f32[4,2,16,256]{3,2,1,0:T(8,128)S(1)}, u32[]{:S(2)}, u32[]{:S(2)}) collective-permute-start(f32[4,2,16,256]{3,2,1,0:T(8,128)S(1)} %get-tuple-element.80), channel_id=1, source_target_pairs={{0,2},{1,3},{2,0},{3,1},{4,6},{5,7},{6,4},{7,5},{8,10},{9,11},{10,... | collective-permute-start | bytes 393224 | tf_op jit(solution)/shard_map/ppermute | solution.py:304
  47.1 7.1 %collective-permute-start.19 = (f32[4,2,16,256]{3,2,1,0:T(8,128)S(1)}, f32[4,2,16,256]{3,2,1,0:T(8,128)S(1)}, u32[]{:S(2)}, u32[]{:S(2)}) collective-permute-start(f32[4,2,16,256]{3,2,1,0:T(8,128)S(1)} %get-tuple-element.73), channel_id=1, source_target_pairs={{0,12},{1,13},{2,14},{3,15},{4,8},{5,9},{6,10},{7,11},{8,4},{9,5},... | collective-permute-start | bytes 393224 | tf_op jit(solution)/shard_map/ppermute | solution.py:304

commit v10 on v9

--- a/solution.py
+++ b/solution.py
@@ -355,7 +355,7 @@
     behind = open_last(lowers[1])
     ahead = send(ahead, uppers[0])
     behind = send(behind, lowers[1])
-    behind = turn(lowers[1], uppers[1], tied(behind, 0, [*ahead[1:3], chain]), "turn_1_in")
+    behind = turn(lowers[1], uppers[1], tied(behind, 0, [chain, *ahead[1:3]]), "turn_1_in")
     behind = send(behind, uppers[1])
     ahead = turn(uppers[0], lowers[0], ahead, "turn_0_in")
     ahead = send(ahead, lowers[0])

time: 55.7 us -> 55.7 us (level)
  no operation moved by 1% of the time
where the time goes in v10:
time: 55.7 us; the launch traced here: 55.6 us
  starting transfers between devices  33.9 us (61%)
  waiting for transfers between devices  12.8 us (23%)
  Pallas kernels  7.24 us (13%)
  local copies, waits for them, and re-layouts  1.43 us (3%)
    ppermute x24, starting transfers between devices, send(): lax.ppermute(value, 'stem', [(i, i ^ step) for i in range(devices)])  33.9 us
    ppermute x24, waiting for transfers between devices, send(): lax.ppermute(value, 'stem', [(i, i ^ step) for i in range(devices)])  12.8 us
    pallas_call x9, Pallas kernels, call(): pl.pallas_call(kernel, out_shape=blocks(out) if isinstance(out, tuple) el...  4.07 us
    pallas_call x1, Pallas kernels, one_slice(): pl.pallas_call(chain_kernel, out_shape=jax.ShapeDtypeStruct((2, low, low)...  1.81 us
    pallas_call x1, Pallas kernels, close_last(): pl.pallas_call(functools.partial(close_last_kernel, layout), out_shape=ja...  1.36 us
    slice x1, local copies, waits for them, and re-layouts, open_first(): packed = jnp.concatenate([laid[0], matrix], axis=0)  1.13 us
  transfers between devices with their start and end apart: 24, of which 9 were waited for; matrix products, arithmetic and copies ran while one was open for 0% of the time, Pallas kernels for 10%

profile of v10, /device:TPU:0, one launch (start us, length us, event | category | flops | bytes accessed | tf_op | source)
XLA Modules:
  0.0 55.6 jit_solution(16459724660654223439)
XLA Ops:
  0.0 1.1 %slice.27 = f32[512,2,128]{2,1,0:T(2,128)S(1)} slice(f32[1024,2,128]{2,1,0:T(2,128)} %bitcast.27), slice={[0:512], [0:2], [0:128]} | slice | bytes 1048576 | tf_op jit(solution)/shard_map/slice | solution.py:315
  1.1 0.1 slice-done
  1.2 0.1 pad_maximum_fusion.packed_ref
  1.3 0.0 copy-start.3
  1.3 0.5 open_0.1
  1.8 3.1 %collective-permute-start = (f32[4,2,16,256]{3,2,1,0:T(8,128)S(1)}, f32[4,2,16,256]{3,2,1,0:T(8,128)S(1)}, u32[]{:S(2)}, u32[]{:S(2)}) collective-permute-start(f32[4,2,16,256]{3,2,1,0:T(8,128)S(1)} %get-tuple-element.47), channel_id=1, source_target_pairs={{0,4},{1,5},{2,6},{3,7},{4,0},{5,1},{6,2},{7,3},{8,12},{9,13},{10,... | collective-permute-start | bytes 393224 | tf_op jit(solution)/shard_map/ppermute | solution.py:304
  4.9 2.6 %collective-permute-start.1 = (f32[4,2,16,256]{3,2,1,0:T(8,128)S(1)}, f32[4,2,16,256]{3,2,1,0:T(8,128)S(1)}, u32[]{:S(2)}, u32[]{:S(2)}) collective-permute-start(f32[4,2,16,256]{3,2,1,0:T(8,128)S(1)} %get-tuple-element.48), channel_id=1, source_target_pairs={{0,8},{1,9},{2,10},{3,11},{4,12},{5,13},{6,14},{7,15},{8,0},{9,1},... | collective-permute-start | bytes 393224 | tf_op jit(solution)/shard_map/ppermute | solution.py:304
  7.5 0.0 copy-done.2
  7.5 0.2 slice_bitcast_fusion
  7.7 0.0 copy-done.3
  7.7 0.0 copy-start.1
  7.8 0.5 open_1.1
  8.3 1.6 %collective-permute-start.2 = (f32[4,2,16,256]{3,2,1,0:T(8,128)S(1)}, f32[4,2,16,256]{3,2,1,0:T(8,128)S(1)}, u32[]{:S(2)}, u32[]{:S(2)}) collective-permute-start(f32[4,2,16,256]{3,2,1,0:T(8,128)S(1)} %get-tuple-element.50), channel_id=1, source_target_pairs={{0,2},{1,3},{2,0},{3,1},{4,6},{5,7},{6,4},{7,5},{8,10},{9,11},{10,... | collective-permute-start | bytes 393224 | tf_op jit(solution)/shard_map/ppermute | solution.py:304
  9.8 0.0 collective-permute-start.3
  9.9 0.6 %collective-permute-start.4 = (f32[4,2,16,256]{3,2,1,0:T(8,128)S(1)}, f32[4,2,16,256]{3,2,1,0:T(8,128)S(1)}, u32[]{:S(2)}, u32[]{:S(2)}) collective-permute-start(f32[4,2,16,256]{3,2,1,0:T(8,128)S(1)} %get-tuple-element.52), channel_id=1, source_target_pairs={{0,3},{1,2},{2,1},{3,0},{4,7},{5,6},{6,5},{7,4},{8,11},{9,10},{10,... | collective-permute-start | bytes 393224 | tf_op jit(solution)/shard_map/ppermute | solution.py:304
  10.5 0.0 collective-permute-done.refs_1_
  10.5 3.2 %collective-permute-start.9 = (f32[4,2,16,256]{3,2,1,0:T(8,128)S(1)}, f32[4,2,16,256]{3,2,1,0:T(8,128)S(1)}, u32[]{:S(2)}, u32[]{:S(2)}) collective-permute-start(f32[4,2,16,256]{3,2,1,0:T(8,128)S(1)} %get-tuple-element.59), channel_id=1, source_target_pairs={{0,12},{1,13},{2,14},{3,15},{4,8},{5,9},{6,10},{7,11},{8,4},{9,5},... | collective-permute-start | bytes 393224 | tf_op jit(solution)/shard_map/ppermute | solution.py:304
  13.7 0.0 copy-done
  13.7 1.8 %low_chain.1.low_table = f32[2,256,256]{2,1,0:T(8,128)S(1)} custom-call(s32[1,3]{1,0:T(1,128)S(1)} %copy-done.1, f32[3,2,2,256,256]{4,3,2,1,0:T(8,128)S(1)} %copy-done), custom_call_target="tpu_custom_call" | custom-call | tf_op jit(solution)/shard_map/low_chain/pallas_call | solution.py:398
  15.6 0.0 collective-permute-done.1.refs_2_
  15.6 0.0 collective-permute-done.2.refs_1_
  15.6 0.0 collective-permute-done.3.refs_2_
  15.6 0.0 collective-permute-done.4.refs_3_
  15.7 0.5 collective-permute-start.5
  16.2 3.2 %collective-permute-start.6 = (f32[4,2,16,256]{3,2,1,0:T(8,128)S(1)}, f32[4,2,16,256]{3,2,1,0:T(8,128)S(1)}, u32[]{:S(2)}, u32[]{:S(2)}) collective-permute-start(f32[4,2,16,256]{3,2,1,0:T(8,128)S(1)} %get-tuple-element.55), channel_id=1, source_target_pairs={{0,8},{1,9},{2,10},{3,11},{4,12},{5,13},{6,14},{7,15},{8,0},{9,1},... | collective-permute-start | bytes 393224 | tf_op jit(solution)/shard_map/ppermute | solution.py:304
  19.4 0.0 collective-permute-done.9.refs_3_
  19.5 1.6 %collective-permute-start.10 = (f32[4,2,16,256]{3,2,1,0:T(8,128)S(1)}, f32[4,2,16,256]{3,2,1,0:T(8,128)S(1)}, u32[]{:S(2)}, u32[]{:S(2)}) collective-permute-start(f32[4,2,16,256]{3,2,1,0:T(8,128)S(1)} %get-tuple-element.61), channel_id=1, source_target_pairs={{0,2},{1,3},{2,0},{3,1},{4,6},{5,7},{6,4},{7,5},{8,10},{9,11},{10,... | collective-permute-start | bytes 393224 | tf_op jit(solution)/shard_map/ppermute | solution.py:304
  21.0 0.0 collective-permute-start.11
  21.0 0.6 %collective-permute-start.12 = (f32[4,2,16,256]{3,2,1,0:T(8,128)S(1)}, f32[4,2,16,256]{3,2,1,0:T(8,128)S(1)}, u32[]{:S(2)}, u32[]{:S(2)}) collective-permute-start(f32[4,2,16,256]{3,2,1,0:T(8,128)S(1)} %get-tuple-element.64), channel_id=1, source_target_pairs={{0,3},{1,2},{2,1},{3,0},{4,7},{5,6},{6,5},{7,4},{8,11},{9,10},{10,... | collective-permute-start | bytes 393224 | tf_op jit(solution)/shard_map/ppermute | solution.py:304
  21.7 1.8 %collective-permute-done.5.refs_1_ = f32[4,2,16,256]{3,2,1,0:T(8,128)S(1)} collective-permute-done((f32[4,2,16,256]{3,2,1,0:T(8,128)S(1)}, f32[4,2,16,256]{3,2,1,0:T(8,128)S(1)}, u32[]{:S(2)}, u32[]{:S(2)}) %collective-permute-start.5) | collective-permute-done | bytes 131104 | tf_op jit(solution)/shard_map/ppermute | solution.py:304
  23.5 2.0 %collective-permute-start.7 = (f32[4,2,16,256]{3,2,1,0:T(8,128)S(1)}, f32[4,2,16,256]{3,2,1,0:T(8,128)S(1)}, u32[]{:S(2)}, u32[]{:S(2)}) collective-permute-start(f32[4,2,16,256]{3,2,1,0:T(8,128)S(1)} %get-tuple-element.56), channel_id=1, source_target_pairs={{0,12},{1,13},{2,14},{3,15},{4,8},{5,9},{6,10},{7,11},{8,4},{9,5},... | collective-permute-start | bytes 393224 | tf_op jit(solution)/shard_map/ppermute | solution.py:304
  25.5 1.0 %collective-permute-done.6.refs_2_ = f32[4,2,16,256]{3,2,1,0:T(8,128)S(1)} collective-permute-done((f32[4,2,16,256]{3,2,1,0:T(8,128)S(1)}, f32[4,2,16,256]{3,2,1,0:T(8,128)S(1)}, u32[]{:S(2)}, u32[]{:S(2)}) %collective-permute-start.6) | collective-permute-done | bytes 131104 | tf_op jit(solution)/shard_map/ppermute | solution.py:304
  26.5 0.0 collective-permute-done.10.refs_1_
  26.5 0.0 collective-permute-done.11.refs_2_
  26.5 0.3 collective-permute-done.12.refs_3_
  26.8 1.2 %middle_0.1 = (f32[4,2,16,256]{3,2,1,0:T(8,128)S(1)}, f32[4,2,16,256]{3,2,1,0:T(8,128)S(1)}, f32[4,2,16,256]{3,2,1,0:T(8,128)S(1)}, f32[4,2,16,256]{3,2,1,0:T(8,128)S(1)}) custom-call(s32[1]{0:T(128)} %bitcast.me_ref, f32[2,256,256]{2,1,0:T(8,128)S(1)} %get-tuple-element.82.table, f32[2,256,256]{2,1,0:T(8,128)S(1)} %low_chain.1.low_table, ...), custom_call_target="tpu_custom_call" | custom-call | tf_op jit(solution)/shard_map/middle_0/pallas_call | solution.py:291
  28.0 0.4 collective-permute-start.13
  28.4 1.7 %collective-permute-start.14 = (f32[4,2,16,256]{3,2,1,0:T(8,128)S(1)}, f32[4,2,16,256]{3,2,1,0:T(8,128)S(1)}, u32[]{:S(2)}, u32[]{:S(2)}) collective-permute-start(f32[4,2,16,256]{3,2,1,0:T(8,128)S(1)} %get-tuple-element.66), channel_id=1, source_target_pairs={{0,8},{1,9},{2,10},{3,11},{4,12},{5,13},{6,14},{7,15},{8,0},{9,1},... | collective-permute-start | bytes 393224 | tf_op jit(solution)/shard_map/ppermute | solution.py:304
  30.1 0.6 %collective-permute-done.7.refs_3_ = f32[4,2,16,256]{3,2,1,0:T(8,128)S(1)} collective-permute-done((f32[4,2,16,256]{3,2,1,0:T(8,128)S(1)}, f32[4,2,16,256]{3,2,1,0:T(8,128)S(1)}, u32[]{:S(2)}, u32[]{:S(2)}) %collective-permute-start.7) | collective-permute-done | bytes 131104 | tf_op jit(solution)/shard_map/ppermute | solution.py:304
  30.7 1.2 %middle_1.1 = (f32[4,2,16,256]{3,2,1,0:T(8,128)S(1)}, f32[4,2,16,256]{3,2,1,0:T(8,128)S(1)}, f32[4,2,16,256]{3,2,1,0:T(8,128)S(1)}, f32[4,2,16,256]{3,2,1,0:T(8,128)S(1)}) custom-call(s32[1]{0:T(128)} %bitcast.me_ref, f32[2,256,256]{2,1,0:T(8,128)S(1)} %get-tuple-element.82.table, f32[2,256,256]{2,1,0:T(8,128)S(1)} %low_chain.1.low_table, ...), custom_call_target="tpu_custom_call" | custom-call | tf_op jit(solution)/shard_map/middle_1/pallas_call | solution.py:291
  31.8 1.5 %collective-permute-start.8 = (f32[4,2,16,256]{3,2,1,0:T(8,128)S(1)}, f32[4,2,16,256]{3,2,1,0:T(8,128)S(1)}, u32[]{:S(2)}, u32[]{:S(2)}) collective-permute-start(f32[4,2,16,256]{3,2,1,0:T(8,128)S(1)} %get-tuple-element.58), channel_id=1, source_target_pairs={{0,2},{1,3},{2,0},{3,1},{4,6},{5,7},{6,4},{7,5},{8,10},{9,11},{10,... | collective-permute-start | bytes 393224 | tf_op jit(solution)/shard_map/ppermute | solution.py:304
  33.4 0.0 collective-permute-start.15
  33.4 0.7 %collective-permute-start.16 = (f32[4,2,16,256]{3,2,1,0:T(8,128)S(1)}, f32[4,2,16,256]{3,2,1,0:T(8,128)S(1)}, u32[]{:S(2)}, u32[]{:S(2)}) collective-permute-start(f32[4,2,16,256]{3,2,1,0:T(8,128)S(1)} %get-tuple-element.69), channel_id=1, source_target_pairs={{0,3},{1,2},{2,1},{3,0},{4,7},{5,6},{6,5},{7,4},{8,11},{9,10},{10,... | collective-permute-start | bytes 393224 | tf_op jit(solution)/shard_map/ppermute | solution.py:304
  34.0 2.5 %collective-permute-done.13.refs_1_ = f32[4,2,16,256]{3,2,1,0:T(8,128)S(1)} collective-permute-done((f32[4,2,16,256]{3,2,1,0:T(8,128)S(1)}, f32[4,2,16,256]{3,2,1,0:T(8,128)S(1)}, u32[]{:S(2)}, u32[]{:S(2)}) %collective-permute-start.13) | collective-permute-done | bytes 131104 | tf_op jit(solution)/shard_map/ppermute | solution.py:304
  36.6 0.4 collective-permute-start.20
  37.0 1.2 %collective-permute-done.14.refs_2_ = f32[4,2,16,256]{3,2,1,0:T(8,128)S(1)} collective-permute-done((f32[4,2,16,256]{3,2,1,0:T(8,128)S(1)}, f32[4,2,16,256]{3,2,1,0:T(8,128)S(1)}, u32[]{:S(2)}, u32[]{:S(2)}) %collective-permute-start.14) | collective-permute-done | bytes 131104 | tf_op jit(solution)/shard_map/ppermute | solution.py:304
  38.1 0.0 collective-permute-done.8.refs_1_
  38.1 0.0 collective-permute-done.15.refs_2_
  38.1 1.0 %collective-permute-done.16.refs_3_ = f32[4,2,16,256]{3,2,1,0:T(8,128)S(1)} collective-permute-done((f32[4,2,16,256]{3,2,1,0:T(8,128)S(1)}, f32[4,2,16,256]{3,2,1,0:T(8,128)S(1)}, u32[]{:S(2)}, u32[]{:S(2)}) %collective-permute-start.16) | collective-permute-done | bytes 131104 | tf_op jit(solution)/shard_map/ppermute | solution.py:304
  39.2 1.2 %collective-permute-start.17 = (f32[4,2,16,256]{3,2,1,0:T(8,128)S(1)}, f32[4,2,16,256]{3,2,1,0:T(8,128)S(1)}, u32[]{:S(2)}, u32[]{:S(2)}) collective-permute-start(f32[4,2,16,256]{3,2,1,0:T(8,128)S(1)} %get-tuple-element.71), channel_id=1, source_target_pairs={{0,4},{1,5},{2,6},{3,7},{4,0},{5,1},{6,2},{7,3},{8,12},{9,13},{10,... | collective-permute-start | bytes 393224 | tf_op jit(solution)/shard_map/ppermute | solution.py:304
  40.4 4.4 %collective-permute-start.18 = (f32[4,2,16,256]{3,2,1,0:T(8,128)S(1)}, f32[4,2,16,256]{3,2,1,0:T(8,128)S(1)}, u32[]{:S(2)}, u32[]{:S(2)}) collective-permute-start(f32[4,2,16,256]{3,2,1,0:T(8,128)S(1)} %get-tuple-element.72), channel_id=1, source_target_pairs={{0,8},{1,9},{2,10},{3,11},{4,12},{5,13},{6,14},{7,15},{8,0},{9,1},... | collective-permute-start | bytes 393224 | tf_op jit(solution)/shard_map/ppermute | solution.py:304
  44.8 0.0 collective-permute-done.20.refs_3_
  44.9 0.1 collective-permute-start.21
  45.0 0.1 collective-permute-start.22
  45.0 2.1 %collective-permute-start.23 = (f32[4,2,16,256]{3,2,1,0:T(8,128)S(1)}, f32[4,2,16,256]{3,2,1,0:T(8,128)S(1)}, u32[]{:S(2)}, u32[]{:S(2)}) collective-permute-start(f32[4,2,16,256]{3,2,1,0:T(8,128)S(1)} %get-tuple-element.80), channel_id=1, source_target_pairs={{0,2},{1,3},{2,0},{3,1},{4,6},{5,7},{6,4},{7,5},{8,10},{9,11},{10,... | collective-permute-start | bytes 393224 | tf_op jit(solution)/shard_map/ppermute | solution.py:304
  47.1 0.0 collective-permute-done.17.refs_1_
  47.1 2.2 %collective-permute-start.19 = (f32[4,2,16,256]{3,2,1,0:T(8,128)S(1)}, f32[4,2,16,256]{3,2,1,0:T(8,128)S(1)}, u32[]{:S(2)}, u32[]{:S(2)}) collective-permute-start(f32[4,2,16,256]{3,2,1,0:T(8,128)S(1)} %get-tuple-element.73), channel_id=1, source_target_pairs={{0,12},{1,13},{2,14},{3,15},{4,8},{5,9},{6,10},{7,11},{8,4},{9,5},... | collective-permute-start | bytes 393224 | tf_op jit(solution)/shard_map/ppermute | solution.py:304
  49.3 1.4 %collective-permute-done.18.refs_2_ = f32[4,2,16,256]{3,2,1,0:T(8,128)S(1)} collective-permute-done((f32[4,2,16,256]{3,2,1,0:T(8,128)S(1)}, f32[4,2,16,256]{3,2,1,0:T(8,128)S(1)}, u32[]{:S(2)}, u32[]{:S(2)}) %collective-permute-start.18) | collective-permute-done | bytes 131104 | tf_op jit(solution)/shard_map/ppermute | solution.py:304
  50.6 0.0 collective-permute-done.21.refs_1_
  50.7 0.0 collective-permute-done.22.refs_2_
  50.7 3.0 %collective-permute-done.23.refs_3_ = f32[4,2,16,256]{3,2,1,0:T(8,128)S(1)} collective-permute-done((f32[4,2,16,256]{3,2,1,0:T(8,128)S(1)}, f32[4,2,16,256]{3,2,1,0:T(8,128)S(1)}, u32[]{:S(2)}, u32[]{:S(2)}) %collective-permute-start.23) | collective-permute-done | bytes 131104 | tf_op jit(solution)/shard_map/ppermute | solution.py:304
  53.6 0.5 close_0.1.refs_4_
  54.2 0.0 collective-permute-done.19.refs_3_
  54.2 1.4 %close_1.1 = f32[2,1024,128]{2,1,0:T(8,128)} custom-call(s32[1]{0:T(128)} %bitcast.me_ref, f32[2,256,256]{2,1,0:T(8,128)S(1)} %get-tuple-element.83.table, f32[4,2,16,256]{3,2,1,0:T(8,128)S(1)} %get-tuple-element.70.refs_0_, f32[4,2,16,256]{3,2,1,0:T(8,128)S(1)} %collective-permute-done.17.refs_1_, f32[4,2,16,256]{3,2,1,0:T(8,128)S(1)} %collective-permute-done.18.refs_2_, ...), custom_call_target="tpu_custom_call" | custom-call | tf_op jit(solution)/shard_map/close_1/pallas_call | solution.py:335
  (9 shorter events, 0.2 us)
Async XLA Ops:
  0.0 1.2 %slice-start = ((f32[3,2,256,256]{3,2,1,0:T(8,128)}), f32[1,2,256,256]{3,2,1,0:T(8,128)S(1)}, s32[]{:S(2)}) async-start(f32[3,2,256,256]{3,2,1,0:T(8,128)} %param.6), calls=%async_computation | async-start | bytes 1048576 | tf_op jit(solution)/shard_map/slice | solution.py:313
  1.2 6.3 %copy-start.2 = (f32[3,2,256,256]{3,2,1,0:T(8,128)S(1)}, f32[3,2,256,256]{3,2,1,0:T(8,128)}, u32[]{:S(2)}) copy-start(f32[3,2,256,256]{3,2,1,0:T(8,128)} %param.6) | copy-start | bytes 4718596
  1.3 6.4 %copy-start.3 = (f32[1,2,131072]{2,1,0:T(2,128)S(1)}, f32[1,2,131072]{2,1,0:T(2,128)}, u32[]{:S(2)}) copy-start(f32[1,2,131072]{2,1,0:T(2,128)} %param.4) | copy-start | bytes 3145732
  1.8 8.7 %collective-permute-start = (f32[4,2,16,256]{3,2,1,0:T(8,128)S(1)}, f32[4,2,16,256]{3,2,1,0:T(8,128)S(1)}, u32[]{:S(2)}, u32[]{:S(2)}) collective-permute-start(f32[4,2,16,256]{3,2,1,0:T(8,128)S(1)} %get-tuple-element.47), channel_id=1, source_target_pairs={{0,4},{1,5},{2,6},{3,7},{4,0},{5,1},{6,2},{7,3},{8,12},{9,13},{10,... | collective-permute-start | bytes 393224 | tf_op jit(solution)/shard_map/ppermute | solution.py:304
  4.9 10.7 %collective-permute-start.1 = (f32[4,2,16,256]{3,2,1,0:T(8,128)S(1)}, f32[4,2,16,256]{3,2,1,0:T(8,128)S(1)}, u32[]{:S(2)}, u32[]{:S(2)}) collective-permute-start(f32[4,2,16,256]{3,2,1,0:T(8,128)S(1)} %get-tuple-element.48), channel_id=1, source_target_pairs={{0,8},{1,9},{2,10},{3,11},{4,12},{5,13},{6,14},{7,15},{8,0},{9,1},... | collective-permute-start | bytes 393224 | tf_op jit(solution)/shard_map/ppermute | solution.py:304
  7.5 6.2 %copy-start = (f32[3,2,2,256,256]{4,3,2,1,0:T(8,128)S(1)}, f32[3,2,2,256,256]{4,3,2,1,0:T(8,128)}, u32[]{:S(2)}) copy-start(f32[3,2,2,256,256]{4,3,2,1,0:T(8,128)} %table_ref.1) | copy-start | bytes 9437188
  7.7 6.0 %copy-start.1 = (s32[1,3]{1,0:T(1,128)S(1)}, s32[1,3]{1,0:T(1,128)}, u32[]{:S(2)}) copy-start(s32[1,3]{1,0:T(1,128)} %bits_ref.1) | copy-start | bytes 40
  8.3 7.3 %collective-permute-start.2 = (f32[4,2,16,256]{3,2,1,0:T(8,128)S(1)}, f32[4,2,16,256]{3,2,1,0:T(8,128)S(1)}, u32[]{:S(2)}, u32[]{:S(2)}) collective-permute-start(f32[4,2,16,256]{3,2,1,0:T(8,128)S(1)} %get-tuple-element.50), channel_id=1, source_target_pairs={{0,2},{1,3},{2,0},{3,1},{4,6},{5,7},{6,4},{7,5},{8,10},{9,11},{10,... | collective-permute-start | bytes 393224 | tf_op jit(solution)/shard_map/ppermute | solution.py:304
  9.8 5.7 %collective-permute-start.3 = (f32[4,2,16,256]{3,2,1,0:T(8,128)S(1)}, f32[4,2,16,256]{3,2,1,0:T(8,128)S(1)}, u32[]{:S(2)}, u32[]{:S(2)}) collective-permute-start(f32[4,2,16,256]{3,2,1,0:T(8,128)S(1)} %get-tuple-element.51), channel_id=1, source_target_pairs={{0,1},{1,0},{2,3},{3,2},{4,5},{5,4},{6,7},{7,6},{8,9},{9,8},{10,11... | collective-permute-start | bytes 393224 | tf_op jit(solution)/shard_map/ppermute | solution.py:304
  9.9 5.8 %collective-permute-start.4 = (f32[4,2,16,256]{3,2,1,0:T(8,128)S(1)}, f32[4,2,16,256]{3,2,1,0:T(8,128)S(1)}, u32[]{:S(2)}, u32[]{:S(2)}) collective-permute-start(f32[4,2,16,256]{3,2,1,0:T(8,128)S(1)} %get-tuple-element.52), channel_id=1, source_target_pairs={{0,3},{1,2},{2,1},{3,0},{4,7},{5,6},{6,5},{7,4},{8,11},{9,10},{10,... | collective-permute-start | bytes 393224 | tf_op jit(solution)/shard_map/ppermute | solution.py:304
  10.5 8.9 %collective-permute-start.9 = (f32[4,2,16,256]{3,2,1,0:T(8,128)S(1)}, f32[4,2,16,256]{3,2,1,0:T(8,128)S(1)}, u32[]{:S(2)}, u32[]{:S(2)}) collective-permute-start(f32[4,2,16,256]{3,2,1,0:T(8,128)S(1)} %get-tuple-element.59), channel_id=1, source_target_pairs={{0,12},{1,13},{2,14},{3,15},{4,8},{5,9},{6,10},{7,11},{8,4},{9,5},... | collective-permute-start | bytes 393224 | tf_op jit(solution)/shard_map/ppermute | solution.py:304
  15.7 7.8 %collective-permute-start.5 = (f32[4,2,16,256]{3,2,1,0:T(8,128)S(1)}, f32[4,2,16,256]{3,2,1,0:T(8,128)S(1)}, u32[]{:S(2)}, u32[]{:S(2)}) collective-permute-start(f32[4,2,16,256]{3,2,1,0:T(8,128)S(1)} %get-tuple-element.54), channel_id=1, source_target_pairs={{0,4},{1,5},{2,6},{3,7},{4,0},{5,1},{6,2},{7,3},{8,12},{9,13},{10,... | collective-permute-start | bytes 393224 | tf_op jit(solution)/shard_map/ppermute | solution.py:304
  16.2 10.3 %collective-permute-start.6 = (f32[4,2,16,256]{3,2,1,0:T(8,128)S(1)}, f32[4,2,16,256]{3,2,1,0:T(8,128)S(1)}, u32[]{:S(2)}, u32[]{:S(2)}) collective-permute-start(f32[4,2,16,256]{3,2,1,0:T(8,128)S(1)} %get-tuple-element.55), channel_id=1, source_target_pairs={{0,8},{1,9},{2,10},{3,11},{4,12},{5,13},{6,14},{7,15},{8,0},{9,1},... | collective-permute-start | bytes 393224 | tf_op jit(solution)/shard_map/ppermute | solution.py:304
  19.5 7.0 %collective-permute-start.10 = (f32[4,2,16,256]{3,2,1,0:T(8,128)S(1)}, f32[4,2,16,256]{3,2,1,0:T(8,128)S(1)}, u32[]{:S(2)}, u32[]{:S(2)}) collective-permute-start(f32[4,2,16,256]{3,2,1,0:T(8,128)S(1)} %get-tuple-element.61), channel_id=1, source_target_pairs={{0,2},{1,3},{2,0},{3,1},{4,6},{5,7},{6,4},{7,5},{8,10},{9,11},{10,... | collective-permute-start | bytes 393224 | tf_op jit(solution)/shard_map/ppermute | solution.py:304
  21.0 5.5 %collective-permute-start.11 = (f32[4,2,16,256]{3,2,1,0:T(8,128)S(1)}, f32[4,2,16,256]{3,2,1,0:T(8,128)S(1)}, u32[]{:S(2)}, u32[]{:S(2)}) collective-permute-start(f32[4,2,16,256]{3,2,1,0:T(8,128)S(1)} %get-tuple-element.63), channel_id=1, source_target_pairs={{0,1},{1,0},{2,3},{3,2},{4,5},{5,4},{6,7},{7,6},{8,9},{9,8},{10,11... | collective-permute-start | bytes 393224 | tf_op jit(solution)/shard_map/ppermute | solution.py:304
  21.0 5.8 %collective-permute-start.12 = (f32[4,2,16,256]{3,2,1,0:T(8,128)S(1)}, f32[4,2,16,256]{3,2,1,0:T(8,128)S(1)}, u32[]{:S(2)}, u32[]{:S(2)}) collective-permute-start(f32[4,2,16,256]{3,2,1,0:T(8,128)S(1)} %get-tuple-element.64), channel_id=1, source_target_pairs={{0,3},{1,2},{2,1},{3,0},{4,7},{5,6},{6,5},{7,4},{8,11},{9,10},{10,... | collective-permute-start | bytes 393224 | tf_op jit(solution)/shard_map/ppermute | solution.py:304
  23.5 7.2 %collective-permute-start.7 = (f32[4,2,16,256]{3,2,1,0:T(8,128)S(1)}, f32[4,2,16,256]{3,2,1,0:T(8,128)S(1)}, u32[]{:S(2)}, u32[]{:S(2)}) collective-permute-start(f32[4,2,16,256]{3,2,1,0:T(8,128)S(1)} %get-tuple-element.56), channel_id=1, source_target_pairs={{0,12},{1,13},{2,14},{3,15},{4,8},{5,9},{6,10},{7,11},{8,4},{9,5},... | collective-permute-start | bytes 393224 | tf_op jit(solution)/shard_map/ppermute | solution.py:304
  28.0 8.6 %collective-permute-start.13 = (f32[4,2,16,256]{3,2,1,0:T(8,128)S(1)}, f32[4,2,16,256]{3,2,1,0:T(8,128)S(1)}, u32[]{:S(2)}, u32[]{:S(2)}) collective-permute-start(f32[4,2,16,256]{3,2,1,0:T(8,128)S(1)} %get-tuple-element.65), channel_id=1, source_target_pairs={{0,4},{1,5},{2,6},{3,7},{4,0},{5,1},{6,2},{7,3},{8,12},{9,13},{10,... | collective-permute-start | bytes 393224 | tf_op jit(solution)/shard_map/ppermute | solution.py:304
  28.4 9.7 %collective-permute-start.14 = (f32[4,2,16,256]{3,2,1,0:T(8,128)S(1)}, f32[4,2,16,256]{3,2,1,0:T(8,128)S(1)}, u32[]{:S(2)}, u32[]{:S(2)}) collective-permute-start(f32[4,2,16,256]{3,2,1,0:T(8,128)S(1)} %get-tuple-element.66), channel_id=1, source_target_pairs={{0,8},{1,9},{2,10},{3,11},{4,12},{5,13},{6,14},{7,15},{8,0},{9,1},... | collective-permute-start | bytes 393224 | tf_op jit(solution)/shard_map/ppermute | solution.py:304
  31.8 6.3 %collective-permute-start.8 = (f32[4,2,16,256]{3,2,1,0:T(8,128)S(1)}, f32[4,2,16,256]{3,2,1,0:T(8,128)S(1)}, u32[]{:S(2)}, u32[]{:S(2)}) collective-permute-start(f32[4,2,16,256]{3,2,1,0:T(8,128)S(1)} %get-tuple-element.58), channel_id=1, source_target_pairs={{0,2},{1,3},{2,0},{3,1},{4,6},{5,7},{6,4},{7,5},{8,10},{9,11},{10,... | collective-permute-start | bytes 393224 | tf_op jit(solution)/shard_map/ppermute | solution.py:304
  33.4 4.8 %collective-permute-start.15 = (f32[4,2,16,256]{3,2,1,0:T(8,128)S(1)}, f32[4,2,16,256]{3,2,1,0:T(8,128)S(1)}, u32[]{:S(2)}, u32[]{:S(2)}) collective-permute-start(f32[4,2,16,256]{3,2,1,0:T(8,128)S(1)} %get-tuple-element.68), channel_id=1, source_target_pairs={{0,1},{1,0},{2,3},{3,2},{4,5},{5,4},{6,7},{7,6},{8,9},{9,8},{10,11... | collective-permute-start | bytes 393224 | tf_op jit(solution)/shard_map/ppermute | solution.py:304
  33.4 5.8 %collective-permute-start.16 = (f32[4,2,16,256]{3,2,1,0:T(8,128)S(1)}, f32[4,2,16,256]{3,2,1,0:T(8,128)S(1)}, u32[]{:S(2)}, u32[]{:S(2)}) collective-permute-start(f32[4,2,16,256]{3,2,1,0:T(8,128)S(1)} %get-tuple-element.69), channel_id=1, source_target_pairs={{0,3},{1,2},{2,1},{3,0},{4,7},{5,6},{6,5},{7,4},{8,11},{9,10},{10,... | collective-permute-start | bytes 393224 | tf_op jit(solution)/shard_map/ppermute | solution.py:304
  36.6 8.3 %collective-permute-start.20 = (f32[4,2,16,256]{3,2,1,0:T(8,128)S(1)}, f32[4,2,16,256]{3,2,1,0:T(8,128)S(1)}, u32[]{:S(2)}, u32[]{:S(2)}) collective-permute-start(f32[4,2,16,256]{3,2,1,0:T(8,128)S(1)} %get-tuple-element.75), channel_id=1, source_target_pairs={{0,12},{1,13},{2,14},{3,15},{4,8},{5,9},{6,10},{7,11},{8,4},{9,5},... | collective-permute-start | bytes 393224 | tf_op jit(solution)/shard_map/ppermute | solution.py:304
  39.2 7.9 %collective-permute-start.17 = (f32[4,2,16,256]{3,2,1,0:T(8,128)S(1)}, f32[4,2,16,256]{3,2,1,0:T(8,128)S(1)}, u32[]{:S(2)}, u32[]{:S(2)}) collective-permute-start(f32[4,2,16,256]{3,2,1,0:T(8,128)S(1)} %get-tuple-element.71), channel_id=1, source_target_pairs={{0,4},{1,5},{2,6},{3,7},{4,0},{5,1},{6,2},{7,3},{8,12},{9,13},{10,... | collective-permute-start | bytes 393224 | tf_op jit(solution)/shard_map/ppermute | solution.py:304
  40.4 10.2 %collective-permute-start.18 = (f32[4,2,16,256]{3,2,1,0:T(8,128)S(1)}, f32[4,2,16,256]{3,2,1,0:T(8,128)S(1)}, u32[]{:S(2)}, u32[]{:S(2)}) collective-permute-start(f32[4,2,16,256]{3,2,1,0:T(8,128)S(1)} %get-tuple-element.72), channel_id=1, source_target_pairs={{0,8},{1,9},{2,10},{3,11},{4,12},{5,13},{6,14},{7,15},{8,0},{9,1},... | collective-permute-start | bytes 393224 | tf_op jit(solution)/shard_map/ppermute | solution.py:304
  44.9 5.8 %collective-permute-start.21 = (f32[4,2,16,256]{3,2,1,0:T(8,128)S(1)}, f32[4,2,16,256]{3,2,1,0:T(8,128)S(1)}, u32[]{:S(2)}, u32[]{:S(2)}) collective-permute-start(f32[4,2,16,256]{3,2,1,0:T(8,128)S(1)} %get-tuple-element.78), channel_id=1, source_target_pairs={{0,1},{1,0},{2,3},{3,2},{4,5},{5,4},{6,7},{7,6},{8,9},{9,8},{10,11... | collective-permute-start | bytes 393224 | tf_op jit(solution)/shard_map/ppermute | solution.py:304
  45.0 5.7 %collective-permute-start.22 = (f32[4,2,16,256]{3,2,1,0:T(8,128)S(1)}, f32[4,2,16,256]{3,2,1,0:T(8,128)S(1)}, u32[]{:S(2)}, u32[]{:S(2)}) collective-permute-start(f32[4,2,16,256]{3,2,1,0:T(8,128)S(1)} %get-tuple-element.79), channel_id=1, source_target_pairs={{0,3},{1,2},{2,1},{3,0},{4,7},{5,6},{6,5},{7,4},{8,11},{9,10},{10,... | collective-permute-start | bytes 393224 | tf_op jit(solution)/shard_map/ppermute | solution.py:304
  45.0 8.6 %collective-permute-start.23 = (f32[4,2,16,256]{3,2,1,0:T(8,128)S(1)}, f32[4,2,16,256]{3,2,1,0:T(8,128)S(1)}, u32[]{:S(2)}, u32[]{:S(2)}) collective-permute-start(f32[4,2,16,256]{3,2,1,0:T(8,128)S(1)} %get-tuple-element.80), channel_id=1, source_target_pairs={{0,2},{1,3},{2,0},{3,1},{4,6},{5,7},{6,4},{7,5},{8,10},{9,11},{10,... | collective-permute-start | bytes 393224 | tf_op jit(solution)/shard_map/ppermute | solution.py:304
  47.1 7.1 %collective-permute-start.19 = (f32[4,2,16,256]{3,2,1,0:T(8,128)S(1)}, f32[4,2,16,256]{3,2,1,0:T(8,128)S(1)}, u32[]{:S(2)}, u32[]{:S(2)}) collective-permute-start(f32[4,2,16,256]{3,2,1,0:T(8,128)S(1)} %get-tuple-element.73), channel_id=1, source_target_pairs={{0,12},{1,13},{2,14},{3,15},{4,8},{5,9},{6,10},{7,11},{8,4},{9,5},... | collective-permute-start | bytes 393224 | tf_op jit(solution)/shard_map/ppermute | solution.py:304
